TPU v7x, 32 devices: a whole 2x2x4 slice. The times are simulated.
32 devices in a mesh: filt: 4 (over y, x), dp: 8 (over z, core).
Axes of the slice: x: 2, y: 2, z: 4, core: 2. Of those that a mesh axis runs over, the one named last changes fastest.
Arguments:
- char_ids: int32 [16384, 50], P('dp'), may hold values from 0 to 261
- word_lengths: int32 [16384], P('dp'), may hold values from 1 to 50, as said below
- out_grad: bfloat16 [16384, 768], P(('dp', 'filt')), may hold values from -6 to 6
- highway_owner: int32 [4], replicated, may hold values from 0 to 3, as said below
- char_table: float32 [262, 16], replicated, may hold values from -6 to 6
- conv_weight: float32 [112, 2048], P(None, 'filt'), may hold values from -0.75 to 0.75
- conv_bias: float32 [2048], P('filt'), may hold values from -4 to 4
- highway_weight: float32 [8, 2048, 2048], P('filt', 'dp'), may hold values from -0.125 to 0.125
- proj_weight: float32 [2048, 768], P(('filt', 'dp')), may hold values from -0.125 to 0.125
- dense_bias: float32 [8960], replicated, may hold values from -4 to 4
- table_moment_one: float32 [262, 16], replicated, may hold values from -2.5 to 2.5
- table_moment_two: float32 [262, 16], replicated, may hold values from 0.0073728 to 0.1179648
- conv_moment_one: float32 [112, 2048], P(None, 'filt'), may hold values from -4 to 4
- conv_moment_two: float32 [112, 2048], P(None, 'filt'), may hold values from 0.02048 to 0.32768
- conv_bias_moment_one: float32 [2048], P('filt'), may hold values from -14 to 14
- conv_bias_moment_two: float32 [2048], P('filt'), may hold values from 0.180224 to 2.94912
- highway_moment_one: float32 [8, 2048, 2048], P('filt', 'dp'), may hold values from -20 to 20
- highway_moment_two: float32 [8, 2048, 2048], P('filt', 'dp'), may hold values from 0.507904 to 8.192
- highway_average: float32 [8, 2048, 2048], P('filt', 'dp'), may hold values from -0.125 to 0.125
- proj_moment_one: float32 [2048, 768], P(('filt', 'dp')), may hold values from -64 to 64
- proj_moment_two: float32 [2048, 768], P(('filt', 'dp')), may hold values from 4.096 to 63.8976
- bias_moment_one: float32 [8960], replicated, may hold values from -24 to 24
- bias_moment_two: float32 [8960], replicated, may hold values from 0.73728 to 11.79648
Outputs:
- word_vectors: float32 [16384, 768], P(('dp', 'filt'))
- table_grad: float32 [262, 16], replicated
- table_second: float32 [262, 16], replicated
- table_new: float32 [262, 16], replicated
- conv_grad: float32 [112, 2048], P(None, 'filt')
- conv_second: float32 [112, 2048], P(None, 'filt')
- conv_new: float32 [112, 2048], P(None, 'filt')
- conv_bias_grad: float32 [2048], P('filt')
- conv_bias_second: float32 [2048], P('filt')
- conv_bias_new: float32 [2048], P('filt')
- highway_grad: float32 [8, 2048, 2048], P('filt', 'dp')
- highway_second: float32 [8, 2048, 2048], P('filt', 'dp')
- highway_new: float32 [8, 2048, 2048], P('filt', 'dp')
- highway_average_new: float32 [8, 2048, 2048], P('filt', 'dp')
- proj_grad: float32 [2048, 768], P(('filt', 'dp'))
- proj_second: float32 [2048, 768], P(('filt', 'dp'))
- proj_new: float32 [2048, 768], P(('filt', 'dp'))
- bias_grad: float32 [8960], replicated
- bias_second: float32 [8960], replicated
- bias_new: float32 [8960], replicated
Inputs may be any that keep to these rules, and one draw needn't show every extreme that they name: `word_lengths`: number of characters of each word; characters at positions from the length on are ignored, and some word has 50. `highway_owner`: an index of filt owns at most 2 of the 4 highway matrices, and one index owns exactly 2.
All inputs are finite; a program needn't handle non-finite values.
Results may differ from a plain program's by a relative error of at most 0.0087.
Values may be sent and summed in bfloat16 or wider, within the bound.
No kernel may reach another device: no remote copies, remote signals or barrier semaphores. Data moves between devices by JAX's collectives and lax.ppermute only.
A program may use at most 320 MiB of HBM per device.

v0:
```python
import jax
import jax.numpy as jnp
from jax import lax
from jax.sharding import PartitionSpec as P

CHAR_DIM = 16
MAX_CHARS = 50
MAX_WIDTH = 7
FILTERS = 2048
UNITS = 4
SLOTS = 2
STEP = 10


beta_one = 0.9
beta_two = 0.999
adam_eps = 1e-08
decay_rate = 0.01
average_keep = 0.9


def channel_widths(start, count, whole):
    channel = start + jnp.arange(count, dtype=jnp.int32)
    widths = jnp.ones((count,), jnp.int32)
    for power in range(6):
        widths = widths + (channel >= whole * 2**power // 64).astype(jnp.int32)
    return widths


def unit_slots(owners, slots_each):
    order = jnp.arange(owners.shape[0], dtype=jnp.int32)
    before = (owners[:, None] == owners[None, :]) & (order[:, None] > order[None, :])
    return owners * slots_each + jnp.sum(before.astype(jnp.int32), axis=1)


def char_onehot(block_ids, block_lengths, vocab_count):
    present = jnp.arange(MAX_CHARS, dtype=jnp.int32)[None, :] < block_lengths[:, None]
    letters = jnp.arange(vocab_count, dtype=jnp.int32)
    return (block_ids[:, :, None] == letters[None, None, :]) & present[:, :, None]


def make_windows(onehot, table_low):
    rows = onehot.shape[0]
    flat = onehot.reshape(rows * MAX_CHARS, -1).astype(jnp.bfloat16)
    embedded = jnp.dot(flat, table_low, preferred_element_type=jnp.float32).astype(jnp.bfloat16)
    embedded = embedded.reshape(rows, MAX_CHARS, CHAR_DIM)
    padded = jnp.pad(embedded, ((0, 0), (0, MAX_WIDTH - 1), (0, 0)))
    return jnp.concatenate(
        [padded[:, offset : offset + MAX_CHARS, :] for offset in range(MAX_WIDTH)], axis=2
    )


def pooling(conv_pre, block_lengths, widths):
    span_left = jnp.maximum(block_lengths[:, None] - widths[None, :], 0)
    inside = jnp.arange(MAX_CHARS, dtype=jnp.int32)[None, :, None] <= span_left[:, None, :]
    masked = jnp.where(inside, conv_pre, -1e30)
    highest = jnp.max(masked, axis=1)
    shifted = jnp.where(inside, jnp.exp(masked - highest[:, None, :]), 0.0)
    summed = jnp.sum(shifted, axis=1)
    pooled = highest + jnp.log(summed) - jnp.log((span_left + 1).astype(jnp.float32))
    return (pooled, shifted / summed[:, None, :])


def silu_slope(value):
    sigma = jax.nn.sigmoid(value)
    return sigma + value * sigma * (1 - sigma)


def highway_forward(current, entering, weight, bias_part):
    half_width = weight.shape[1] // 2
    hidden = jnp.dot(entering, weight, preferred_element_type=jnp.float32) + bias_part
    nonlinear = jax.nn.silu(hidden[:, :half_width])
    gate_value = jax.nn.sigmoid(hidden[:, half_width:])
    return (gate_value * current + (1 - gate_value) * nonlinear, hidden)


def highway_backward(upstream, current, entering, hidden, weight):
    half_width = weight.shape[1] // 2
    first_half = hidden[:, :half_width]
    nonlinear = jax.nn.silu(first_half)
    gate_value = jax.nn.sigmoid(hidden[:, half_width:])
    d_nonlinear = upstream * (1 - gate_value) * silu_slope(first_half)
    d_gate = upstream * (current - nonlinear) * gate_value * (1 - gate_value)
    d_hidden = jnp.concatenate([d_nonlinear, d_gate], axis=1).astype(jnp.bfloat16)
    weight_grad = lax.dot_general(
        entering, d_hidden, (((0,), (0,)), ((), ())), preferred_element_type=jnp.float32
    )
    bias_part_grad = jnp.sum(d_hidden, axis=0, dtype=jnp.float32)
    product = lax.dot_general(
        d_hidden, weight, (((1,), (1,)), ((), ())), preferred_element_type=jnp.float32
    )
    return (upstream * gate_value, product, weight_grad, bias_part_grad)


def adam_update(weight, grad, moment_one, moment_two, rate):
    first_new = beta_one * moment_one + (1 - beta_one) * grad
    second_new = beta_two * moment_two + (1 - beta_two) * grad * grad
    corrected_one = first_new / (1 - beta_one**STEP)
    corrected_two = second_new / (1 - beta_two**STEP)
    updated = weight - rate * (
        corrected_one / (jnp.sqrt(corrected_two) + adam_eps) + decay_rate * weight
    )
    return (second_new, updated)


def per_device(
    char_ids,
    word_lengths,
    out_grad,
    highway_owner,
    char_table,
    conv_weight,
    conv_bias,
    highway_weight,
    proj_weight,
    dense_bias,
    table_moment_one,
    table_moment_two,
    conv_moment_one,
    conv_moment_two,
    conv_bias_moment_one,
    conv_bias_moment_two,
    highway_moment_one,
    highway_moment_two,
    highway_average,
    proj_moment_one,
    proj_moment_two,
    bias_moment_one,
    bias_moment_two,
):
    count_filt = lax.axis_size("filt")
    count_dp = lax.axis_size("dp")
    filt_index = lax.axis_index("filt")
    local_channels = conv_weight.shape[1]
    width_full = highway_weight.shape[2]
    rows_proj = proj_weight.shape[0]
    out_width = proj_weight.shape[1]
    vocab_count = char_table.shape[0]
    table_low = char_table.astype(jnp.bfloat16)
    widths = channel_widths(filt_index * local_channels, local_channels, FILTERS)
    offsets = jnp.arange(MAX_WIDTH * CHAR_DIM, dtype=jnp.int32) // CHAR_DIM
    tap_mask = (offsets[:, None] < widths[None, :]).astype(jnp.float32)
    conv_low = (conv_weight * tap_mask).astype(jnp.bfloat16)
    slot_index = unit_slots(highway_owner, SLOTS)
    arrived = lax.all_to_all(
        highway_weight.astype(jnp.bfloat16), "filt", split_axis=2, concat_axis=0, tiled=True
    )
    unit_part = jnp.stack(
        [
            lax.dynamic_index_in_dim(arrived, slot_index[unit], 0, keepdims=False)
            for unit in range(UNITS)
        ]
    )
    proj_piece = proj_weight.astype(jnp.bfloat16).reshape(1, 1, rows_proj, out_width)
    unit_part, proj_piece = (
        lax.all_gather(unit_part, "filt", axis=2, tiled=True),
        lax.all_gather(proj_piece, "filt", axis=0, tiled=True),
    )
    unit_all, proj_all = (
        lax.all_gather(unit_part, "dp", axis=1, tiled=True),
        lax.all_gather(proj_piece, "dp", axis=1, tiled=True),
    )
    proj_all = proj_all.reshape(-1, out_width)
    bias_float = dense_bias.astype(jnp.bfloat16).astype(jnp.float32)
    layer_weights = [
        jnp.concatenate([unit_all[2 * layer], unit_all[2 * layer + 1]], axis=1)
        for layer in range(2)
    ]
    words_dev = char_ids.shape[0]
    block_size = min(512, words_dev)
    count_blocks = words_dev // block_size
    id_blocks = char_ids.reshape(count_blocks, block_size, MAX_CHARS)
    length_blocks = word_lengths.reshape(count_blocks, block_size)

    def forward_block(pieces):
        block_ids, block_lengths = pieces
        onehot = char_onehot(block_ids, block_lengths, vocab_count)
        windows = make_windows(onehot, table_low)
        conv_pre = (
            jnp.einsum("bpk,kc->bpc", windows, conv_low, preferred_element_type=jnp.float32)
            + conv_bias
        )
        pooled, softness = pooling(conv_pre, block_lengths, widths)
        return jax.nn.silu(pooled).astype(jnp.bfloat16)

    features = lax.map(forward_block, (id_blocks, length_blocks)).reshape(words_dev, local_channels)
    kept = []
    layer_bias = [
        bias_float[2 * layer * width_full : 2 * (layer + 1) * width_full] for layer in range(2)
    ]
    block_low = lax.all_to_all(features, "filt", split_axis=0, concat_axis=1, tiled=True)
    current = block_low.astype(jnp.float32)
    for layer in range(2):
        entering = block_low
        current_next, hidden = highway_forward(
            current, entering, layer_weights[layer], layer_bias[layer]
        )
        kept.append((current, entering, hidden))
        current = current_next
        block_low = current.astype(jnp.bfloat16)
    word_vectors = (
        jnp.dot(block_low, proj_all, preferred_element_type=jnp.float32)
        + bias_float[4 * width_full :]
    )
    proj_bias_grad = jnp.sum(out_grad, axis=0, dtype=jnp.float32)
    proj_local = lax.dot_general(
        block_low, out_grad, (((0,), (0,)), ((), ())), preferred_element_type=jnp.float32
    )
    upstream = lax.dot_general(
        out_grad, proj_all, (((1,), (1,)), ((), ())), preferred_element_type=jnp.float32
    )
    unit_grads = [None, None, None, None]
    bias_parts = [None, None]
    for layer in (1, 0):
        current, entering, hidden = kept[layer]
        gate_term, product, weight_grad, bias_part = highway_backward(
            upstream, current, entering, hidden, layer_weights[layer]
        )
        upstream = gate_term + product
        half_width = weight_grad.shape[1] // 2
        unit_grads[2 * layer] = weight_grad[:, :half_width]
        unit_grads[2 * layer + 1] = weight_grad[:, half_width:]
        bias_parts[layer] = bias_part
    feature_low = upstream.astype(jnp.bfloat16)
    returned = lax.all_to_all(feature_low, "filt", split_axis=1, concat_axis=0, tiled=True)
    bias_grad_local = jnp.concatenate([bias_parts[0], bias_parts[1], proj_bias_grad])
    unit_stack = jnp.stack(unit_grads)
    proj_four = proj_local.reshape(-1, count_dp, rows_proj, out_width)
    unit_sums, proj_sums = (
        lax.psum_scatter(unit_stack, "dp", scatter_dimension=1, tiled=True),
        lax.psum_scatter(proj_four, "dp", scatter_dimension=1, tiled=True),
    )
    unit_sums, proj_sums = (
        lax.psum_scatter(unit_sums, "filt", scatter_dimension=2, tiled=True),
        lax.psum_scatter(proj_sums, "filt", scatter_dimension=0, tiled=True),
    )
    proj_grad = proj_sums.reshape(rows_proj, out_width)
    slot_buffer = jnp.zeros((count_filt * SLOTS,) + unit_sums.shape[1:], jnp.float32)
    for unit in range(UNITS):
        slot_buffer = lax.dynamic_update_index_in_dim(
            slot_buffer, unit_sums[unit], slot_index[unit], 0
        )
    highway_grad = lax.all_to_all(slot_buffer, "filt", split_axis=0, concat_axis=2, tiled=True)
    grad_blocks = returned.reshape(count_blocks, block_size, local_channels)

    def backward_block(running, pieces):
        block_ids, block_lengths, block_grad = pieces
        onehot = char_onehot(block_ids, block_lengths, vocab_count)
        windows = make_windows(onehot, table_low)
        conv_pre = (
            jnp.einsum("bpk,kc->bpc", windows, conv_low, preferred_element_type=jnp.float32)
            + conv_bias
        )
        pooled, softness = pooling(conv_pre, block_lengths, widths)
        d_pooled = block_grad.astype(jnp.float32) * silu_slope(pooled)
        d_pre = (softness * d_pooled[:, None, :]).astype(jnp.bfloat16)
        weight_term = jnp.einsum("bpk,bpc->kc", windows, d_pre, preferred_element_type=jnp.float32)
        bias_term = jnp.sum(d_pre, axis=(0, 1), dtype=jnp.float32)
        d_windows = jnp.einsum("bpc,kc->bpk", d_pre, conv_low, preferred_element_type=jnp.float32)
        d_windows = d_windows.reshape(block_size, MAX_CHARS, MAX_WIDTH, CHAR_DIM)
        d_embedded = jnp.zeros((block_size, MAX_CHARS + MAX_WIDTH - 1, CHAR_DIM), jnp.float32)
        for offset in range(MAX_WIDTH):
            d_embedded = d_embedded + jnp.pad(
                d_windows[:, :, offset, :], ((0, 0), (offset, MAX_WIDTH - 1 - offset), (0, 0))
            )
        d_embedded = d_embedded[:, :MAX_CHARS, :].reshape(block_size * MAX_CHARS, CHAR_DIM)
        flat_hot = onehot.reshape(block_size * MAX_CHARS, vocab_count).astype(jnp.float32)
        table_term = lax.dot_general(
            flat_hot,
            d_embedded,
            (((0,), (0,)), ((), ())),
            precision=lax.Precision.HIGHEST,
            preferred_element_type=jnp.float32,
        )
        return ((running[0] + weight_term, running[1] + bias_term, running[2] + table_term), None)

    initial = (
        jnp.zeros((MAX_WIDTH * CHAR_DIM, local_channels), jnp.float32),
        jnp.zeros((local_channels,), jnp.float32),
        jnp.zeros(char_table.shape, jnp.float32),
    )
    sums_local, unused = lax.scan(backward_block, initial, (id_blocks, length_blocks, grad_blocks))
    conv_grad, conv_bias_grad = lax.psum((sums_local[0] * tap_mask, sums_local[1]), "dp")
    table_grad, bias_grad = lax.psum((sums_local[2], bias_grad_local), ("filt", "dp"))
    table_second, table_new = adam_update(
        char_table, table_grad, table_moment_one, table_moment_two, 1.0
    )
    conv_second, conv_new = adam_update(
        conv_weight, conv_grad, conv_moment_one, conv_moment_two, 0.1
    )
    conv_bias_second, conv_bias_new = adam_update(
        conv_bias, conv_bias_grad, conv_bias_moment_one, conv_bias_moment_two, 0.3
    )
    highway_second, highway_new = adam_update(
        highway_weight, highway_grad, highway_moment_one, highway_moment_two, 0.02
    )
    highway_average_new = average_keep * highway_average + (1 - average_keep) * highway_new
    proj_second, proj_new = adam_update(
        proj_weight, proj_grad, proj_moment_one, proj_moment_two, 0.02
    )
    bias_second, bias_new = adam_update(
        dense_bias, bias_grad, bias_moment_one, bias_moment_two, 0.3
    )
    return (
        word_vectors,
        table_grad,
        table_second,
        table_new,
        conv_grad,
        conv_second,
        conv_new,
        conv_bias_grad,
        conv_bias_second,
        conv_bias_new,
        highway_grad,
        highway_second,
        highway_new,
        highway_average_new,
        proj_grad,
        proj_second,
        proj_new,
        bias_grad,
        bias_second,
        bias_new,
    )


def solution(mesh):
    return jax.shard_map(
        per_device,
        mesh=mesh,
        in_specs=(
            P("dp", None),
            P("dp"),
            P(("dp", "filt"), None),
            P(),
            P(),
            P(None, "filt"),
            P("filt"),
            P("filt", "dp", None),
            P(("filt", "dp"), None),
            P(),
            P(),
            P(),
            P(None, "filt"),
            P(None, "filt"),
            P("filt"),
            P("filt"),
            P("filt", "dp", None),
            P("filt", "dp", None),
            P("filt", "dp", None),
            P(("filt", "dp"), None),
            P(("filt", "dp"), None),
            P(),
            P(),
        ),
        out_specs=(
            P(("dp", "filt"), None),
            P(),
            P(),
            P(),
            P(None, "filt"),
            P(None, "filt"),
            P(None, "filt"),
            P("filt"),
            P("filt"),
            P("filt"),
            P("filt", "dp", None),
            P("filt", "dp", None),
            P("filt", "dp", None),
            P("filt", "dp", None),
            P(("filt", "dp"), None),
            P(("filt", "dp"), None),
            P(("filt", "dp"), None),
            P(),
            P(),
            P(),
        ),
        check_vma=False,
    )
```

profile of v0, /device:TPU:0, one launch (start us, length us, event | category | flops | bytes accessed | tf_op | source)
XLA Modules:
  0.0 2114.8 jit_solution(11973615676258911166)
XLA Ops:
  7.2 6.8 copy.177
  27.8 16.3 all-to-all-done.1
  49.8 53.1 %all-gather.5.cloned.1.call-done = bf16[4,256,2048]{2,1,0:T(8,128)(2,1)} async-done(((bf16[4,256,512]{2,1,0:T(8,128)(2,1)}), bf16[4,256,2048]{2,1,0:T(8,128)(2,1)}) %all-gather.5.cloned.1.call-update) | async-done | bytes 4194320 | tf_op jit(solution)/shard_map/all_gather | solution.py:156
  103.9 260.6 %while.30 = (s32[]{:T(128)}, bf16[4,512,512]{2,1,0:T(8,128)(2,1)}, s32[4,512]{1,0:T(4,128)S(1)}, s32[4,512,50]{1,0,2:T(4,128)S(1)}, bf16[262,16]{0,1:T(8,128)(2,...) while((s32[]{:T(128)}, bf16[4,512,512]{2,1,0:T(8,128)(2,1)}, ...), condition=%wide.region_3.4_spmd.clone, body=%wide.region_0.0_spmd.clone.sunk | while | flops 3298458112 | bytes 163164528 | solution.py:186
  111.7 6.2 reshape.461
  122.8 25.0 %fusion.133 = (f32[512,512]{1,0:T(8,128)S(1)}, f32[512,50,512]{2,0,1:T(8,128)}) fusion(f32[512]{0:T(512)S(1)} %get-tuple-element.765, s32[512,512]{1,0:T(8,128)S(1)} %copy-done.1, bf16[512,50,112]{0,2,1:T(8,128)(2,1)} %copy-done.16, bf16[112,512]{1,0:T(8,128)(2,1)S(1)} %get-tuple-element.764), kind=kOutput, calls=%fused_computation.5.clone.1 | convolution fusion | flops 2988179456 | bytes 60377088 | tf_op jit(solution)/shard_map/while/body/eval_jaxpr/bpk,kc->bpc/dot_general | solution.py:180
  147.9 19.0 select_reduce_fusion.2
  177.5 6.2 reshape.461
  188.1 24.9 %fusion.133 = (f32[512,512]{1,0:T(8,128)S(1)}, f32[512,50,512]{2,0,1:T(8,128)}) fusion(f32[512]{0:T(512)S(1)} %get-tuple-element.765, s32[512,512]{1,0:T(8,128)S(1)} %copy-done.1, bf16[512,50,112]{0,2,1:T(8,128)(2,1)} %copy-done.16, bf16[112,512]{1,0:T(8,128)(2,1)S(1)} %get-tuple-element.764), kind=kOutput, calls=%fused_computation.5.clone.1 | convolution fusion | flops 2988179456 | bytes 60377088 | tf_op jit(solution)/shard_map/while/body/eval_jaxpr/bpk,kc->bpc/dot_general | solution.py:180
  213.0 19.1 select_reduce_fusion.2
  253.2 24.5 %fusion.133 = (f32[512,512]{1,0:T(8,128)S(1)}, f32[512,50,512]{2,0,1:T(8,128)}) fusion(f32[512]{0:T(512)S(1)} %get-tuple-element.765, s32[512,512]{1,0:T(8,128)S(1)} %copy-done.1, bf16[512,50,112]{0,2,1:T(8,128)(2,1)} %copy-done.16, bf16[112,512]{1,0:T(8,128)(2,1)S(1)} %get-tuple-element.764), kind=kOutput, calls=%fused_computation.5.clone.1 | convolution fusion | flops 2988179456 | bytes 60377088 | tf_op jit(solution)/shard_map/while/body/eval_jaxpr/bpk,kc->bpc/dot_general | solution.py:180
  277.7 19.3 select_reduce_fusion.2
  318.2 24.3 %fusion.133 = (f32[512,512]{1,0:T(8,128)S(1)}, f32[512,50,512]{2,0,1:T(8,128)}) fusion(f32[512]{0:T(512)S(1)} %get-tuple-element.765, s32[512,512]{1,0:T(8,128)S(1)} %copy-done.1, bf16[512,50,112]{0,2,1:T(8,128)(2,1)} %copy-done.16, bf16[112,512]{1,0:T(8,128)(2,1)S(1)} %get-tuple-element.764), kind=kOutput, calls=%fused_computation.5.clone.1 | convolution fusion | flops 2988179456 | bytes 60377088 | tf_op jit(solution)/shard_map/while/body/eval_jaxpr/bpk,kc->bpc/dot_general | solution.py:180
  342.5 19.0 select_reduce_fusion.2
  368.6 30.8 %all-gather = bf16[256,768]{1,0:T(8,128)(2,1)} all-gather(bf16[64,768]{1,0:T(8,128)(2,1)S(1)} %convert_element_type.201), channel_id=2, replica_groups=mesh['filt'=4,'dp'=8] {'filt'}, dimensions={0}, use_global_device_ids=true | all-gather | bytes 491520 | tf_op jit(solution)/shard_map/all_gather | solution.py:157
  402.8 23.7 %slice_bitcast_fusion.12 = (bf16[2048,2048]{1,0:T(8,128)(2,1)}, bf16[2048,2048]{1,0:T(8,128)(2,1)}, bf16[2048,2048]{1,0:T(8,128)(2,1)}, bf16[2048,2048]{1,0:T(8,128)(2,1)}) fusion(bf16[4,2048,2048]{2,1,0:T(8,128)(2,1)} %all-gather.7.cloned.1.call-done), kind=kLoop, calls=%fused_computation.109 | loop fusion | bytes 67108864 | tf_op jit(solution)/shard_map/squeeze | solution.py:166
  426.5 18.0 fusion.52
  450.6 19.2 fusion.53
  469.7 10.8 multiply_convert_fusion.4
  480.5 18.4 fusion.67
  498.9 19.0 multiply_convert_fusion.2
  517.9 22.0 %slice_bitcast_fusion.8 = (f32[1,2048,2048]{2,1,0:T(8,128)}, f32[1,2048,2048]{2,1,0:T(8,128)}) fusion(f32[2048,4096]{1,0:T(8,128)} %fusion.67), kind=kLoop, calls=%fused_computation.99 | loop fusion | bytes 67108864 | tf_op jit(solution)/shard_map/stack | solution.py:227
  539.9 15.9 fusion.66
  555.8 21.2 %slice_bitcast_fusion.10 = (f32[1,2048,2048]{2,1,0:T(8,128)}, f32[1,2048,2048]{2,1,0:T(8,128)}) fusion(f32[2048,4096]{1,0:T(8,128)} %fusion.66), kind=kLoop, calls=%fused_computation.101 | loop fusion | bytes 67108864 | tf_op jit(solution)/shard_map/stack | solution.py:227
  576.9 43.5 %pad_maximum_fusion = f32[4,2048,2048]{2,1,0:T(8,128)} fusion(f32[1,2048,2048]{2,1,0:T(8,128)} %get-tuple-element.576, f32[1,2048,2048]{2,1,0:T(8,128)} %get-tuple-element.575, f32[1,2048,2048]{2,1,0:T(8,128)} %get-tuple-element.574, f32[1,2048,2048]{2,1,0:T(8,128)} %get-tuple-element.573), kind=kLoop, calls=%fused_computation.97 | loop fusion | flops 50331648 | bytes 134217728 | tf_op jit(solution)/shard_map/stack | solution.py:227
  622.0 13.7 add_convert_fusion
  647.1 614.0 %reduce-scatter.9.cloned.1.call-done = f32[4,256,2048]{2,1,0:T(8,128)} async-done(((f32[4,2048,2048]{2,1,0:T(8,128)}), f32[4,256,2048]{2,1,0:T(8,128)}) %reduce-scatter.9.cloned.1.call-update) | async-done | bytes 8388624 | tf_op jit(solution)/shard_map/reduce_scatter | solution.py:230
  1261.9 597.0 %while.31 = (s32[]{:T(128)}, f32[112,512]{1,0:T(8,128)S(1)}, f32[512]{0:T(512)S(1)}, f32[262,16]{0,1:T(8,128)}, s32[4,512,50]{1,0,2:T(4,128)}, /*index=5*/s32[4,...) while((s32[]{:T(128)}, f32[112,512]{1,0:T(8,128)S(1)}, ...), condition=%wide.region_9.10_spmd.clone, body=%wide.region_5.9_spmd.clone.sunk | while | flops 10606382080 | bytes 367512736 | solution.py:282
  1285.6 6.7 convolution_convert_fusion.5
  1292.3 7.2 reshape.462
  1304.2 25.4 %fusion.143 = (f32[512,512]{1,0:T(8,128)S(1)}, f32[512,50,512]{2,0,1:T(8,128)}) fusion(f32[512]{0:T(512)S(1)} %get-tuple-element.802, s32[512,512]{1,0:T(8,128)S(1)} %subtract_maximum_fusion.5, bf16[512,50,112]{0,2,1:T(8,128)(2,1)} %copy-done, bf16[112,512]{1,0:T(8,128)(2,1)S(1)} %get-tuple-element.801), kind=kOutput, calls=%fused_computation.40.clone.1 | convolution fusion | flops 2988179456 | bytes 60377088 | tf_op jit(solution)/shard_map/while/body/eval_jaxpr/bpk,kc->bpc/dot_general | solution.py:251
  1329.6 18.7 fusion.144
  1351.1 27.2 %convert_reduce_fusion.6 = (f32[512]{0:T(512)S(1)}, bf16[512,50,512]{2,0,1:T(8,128)(2,1)}) fusion(f32[512,512]{1,0:T(8,128)} %convert_multiply_fusion.3, f32[512,512]{1,0:T(8,128)S(1)} %fusion.144, f32[512,512]{1,0:T(8,128)S(1)} %get-tuple-element.730, f32[512,50,512]{2,0,1:T(8,128)} %get-tuple-element.731, f32[512]{0:T(512)S(1)} %get-tuple-element.802, ...), kind=kLoop, calls=%fused_computation.35.clone.1 | loop fusion | flops 131071488 | bytes 82841600 | tf_op jit(solution)/shard_map/while/body/eval_jaxpr/reduce_sum | solution.py:258
  1378.4 12.0 fusion.145
  1391.1 13.0 fusion.146
  1410.5 17.1 fusion.147
  1431.6 6.7 convolution_convert_fusion.5
  1438.3 7.2 reshape.462
  1450.2 24.1 %fusion.143 = (f32[512,512]{1,0:T(8,128)S(1)}, f32[512,50,512]{2,0,1:T(8,128)}) fusion(f32[512]{0:T(512)S(1)} %get-tuple-element.802, s32[512,512]{1,0:T(8,128)S(1)} %subtract_maximum_fusion.5, bf16[512,50,112]{0,2,1:T(8,128)(2,1)} %copy-done, bf16[112,512]{1,0:T(8,128)(2,1)S(1)} %get-tuple-element.801), kind=kOutput, calls=%fused_computation.40.clone.1 | convolution fusion | flops 2988179456 | bytes 60377088 | tf_op jit(solution)/shard_map/while/body/eval_jaxpr/bpk,kc->bpc/dot_general | solution.py:251
  1474.3 17.7 fusion.144
  1494.8 27.2 %convert_reduce_fusion.6 = (f32[512]{0:T(512)S(1)}, bf16[512,50,512]{2,0,1:T(8,128)(2,1)}) fusion(f32[512,512]{1,0:T(8,128)} %convert_multiply_fusion.3, f32[512,512]{1,0:T(8,128)S(1)} %fusion.144, f32[512,512]{1,0:T(8,128)S(1)} %get-tuple-element.730, f32[512,50,512]{2,0,1:T(8,128)} %get-tuple-element.731, f32[512]{0:T(512)S(1)} %get-tuple-element.802, ...), kind=kLoop, calls=%fused_computation.35.clone.1 | loop fusion | flops 131071488 | bytes 82841600 | tf_op jit(solution)/shard_map/while/body/eval_jaxpr/reduce_sum | solution.py:258
  1522.0 12.0 fusion.145
  1534.7 13.0 fusion.146
  1554.2 17.1 fusion.147
  1575.2 6.7 convolution_convert_fusion.5
  1581.9 7.2 reshape.462
  1593.8 24.1 %fusion.143 = (f32[512,512]{1,0:T(8,128)S(1)}, f32[512,50,512]{2,0,1:T(8,128)}) fusion(f32[512]{0:T(512)S(1)} %get-tuple-element.802, s32[512,512]{1,0:T(8,128)S(1)} %subtract_maximum_fusion.5, bf16[512,50,112]{0,2,1:T(8,128)(2,1)} %copy-done, bf16[112,512]{1,0:T(8,128)(2,1)S(1)} %get-tuple-element.801), kind=kOutput, calls=%fused_computation.40.clone.1 | convolution fusion | flops 2988179456 | bytes 60377088 | tf_op jit(solution)/shard_map/while/body/eval_jaxpr/bpk,kc->bpc/dot_general | solution.py:251
  1617.9 17.7 fusion.144
  1638.4 27.2 %convert_reduce_fusion.6 = (f32[512]{0:T(512)S(1)}, bf16[512,50,512]{2,0,1:T(8,128)(2,1)}) fusion(f32[512,512]{1,0:T(8,128)} %convert_multiply_fusion.3, f32[512,512]{1,0:T(8,128)S(1)} %fusion.144, f32[512,512]{1,0:T(8,128)S(1)} %get-tuple-element.730, f32[512,50,512]{2,0,1:T(8,128)} %get-tuple-element.731, f32[512]{0:T(512)S(1)} %get-tuple-element.802, ...), kind=kLoop, calls=%fused_computation.35.clone.1 | loop fusion | flops 131071488 | bytes 82841600 | tf_op jit(solution)/shard_map/while/body/eval_jaxpr/reduce_sum | solution.py:258
  1665.6 12.0 fusion.145
  1678.4 13.0 fusion.146
  1697.8 17.1 fusion.147
  1718.8 6.7 convolution_convert_fusion.5
  1725.5 7.2 reshape.462
  1737.4 24.1 %fusion.143 = (f32[512,512]{1,0:T(8,128)S(1)}, f32[512,50,512]{2,0,1:T(8,128)}) fusion(f32[512]{0:T(512)S(1)} %get-tuple-element.802, s32[512,512]{1,0:T(8,128)S(1)} %subtract_maximum_fusion.5, bf16[512,50,112]{0,2,1:T(8,128)(2,1)} %copy-done, bf16[112,512]{1,0:T(8,128)(2,1)S(1)} %get-tuple-element.801), kind=kOutput, calls=%fused_computation.40.clone.1 | convolution fusion | flops 2988179456 | bytes 60377088 | tf_op jit(solution)/shard_map/while/body/eval_jaxpr/bpk,kc->bpc/dot_general | solution.py:251
  1761.5 17.7 fusion.144
  1782.0 27.2 %convert_reduce_fusion.6 = (f32[512]{0:T(512)S(1)}, bf16[512,50,512]{2,0,1:T(8,128)(2,1)}) fusion(f32[512,512]{1,0:T(8,128)} %convert_multiply_fusion.3, f32[512,512]{1,0:T(8,128)S(1)} %fusion.144, f32[512,512]{1,0:T(8,128)S(1)} %get-tuple-element.730, f32[512,50,512]{2,0,1:T(8,128)} %get-tuple-element.731, f32[512]{0:T(512)S(1)} %get-tuple-element.802, ...), kind=kLoop, calls=%fused_computation.35.clone.1 | loop fusion | flops 131071488 | bytes 82841600 | tf_op jit(solution)/shard_map/while/body/eval_jaxpr/reduce_sum | solution.py:258
  1809.3 12.0 fusion.145
  1822.0 13.0 fusion.146
  1841.4 17.1 fusion.147
  1897.2 102.3 %all-reduce.15.cloned.1.call-done = (f32[112,512]{1,0:T(8,128)}, f32[4,8,64,768]{3,2,1,0:T(8,128)}) async-done(((f32[112,512]{1,0:T(8,128)}, f32[4,8,64,768]{3,2,1,0:T(8,128)}), (f32[112,512]{1,0:T(8,128)}, f32[4,8,64,768]{3,2,1,0:T(8,128)})) %all-reduce.15.cloned.1.call-update) | async-done | bytes 6520848 | tf_op jit(solution)/shard_map/psum | solution.py:283
  2007.4 15.5 psum.30
  2022.8 38.9 %all-reduce.11 = (f32[262,16]{0,1:T(8,128)S(1)}, f32[8960]{0:T(1024)S(1)}) all-reduce(f32[262,16]{0,1:T(8,128)} %get-tuple-element.887, f32[8960]{0:T(1024)S(1)} %pad_maximum_fusion.22), channel_id=1, replica_groups=mesh['filt'=4,'dp'=8] {'filt','dp'}, use_global_device_ids=true, to_apply=%region_10.11 | all-reduce | flops 13152 | bytes 105216 | tf_op jit(solution)/shard_map/psum | solution.py:284
  2078.7 12.4 multiply_add_fusion
  (421 shorter events, 264.7 us)
Async XLA Ops:
  7.2 12.0 copy-start.57
  14.0 30.0 %all-to-all-start.1 = ((bf16[2,256,2048]{1,0,2:T(2,128)(2,1)}), bf16[2,256,2048]{1,0,2:T(2,128)(2,1)S(1)}, u32[]{:S(2)}, u32[]{:S(2)}) async-start(bf16[2,256,2048]{1,0,2:T(2,128)(2,1)} %copy.177), calls=%async_computation.1 | async-start | bytes 4194304 | tf_op jit(solution)/shard_map/all_to_all | solution.py:145
  19.2 83.7 %all-gather.5.cloned.1.call-start = ((), (), s32[]{:S(2)}) async-start(), calls=%async_computation.7 | async-start | bytes 5242880 | tf_op jit(solution)/shard_map/all_gather | solution.py:156
  48.6 54.4 %copy-start.51 = (s32[2048]{0:T(1024)S(1)}, s32[2048]{0:T(1024)}, u32[]{:S(2)}) copy-start(s32[2048]{0:T(1024)} %param.28) | copy-start | bytes 24580
  48.6 54.4 %copy-start.33 = (s32[2048,50]{0,1:T(8,128)S(1)}, s32[2048,50]{0,1:T(8,128)}, u32[]{:S(2)}) copy-start(s32[2048,50]{0,1:T(8,128)} %param.27) | copy-start | bytes 1228804
  48.6 54.7 %copy-start.41 = (f32[262,16]{0,1:T(8,128)S(1)}, f32[262,16]{0,1:T(8,128)}, u32[]{:S(2)}) copy-start(f32[262,16]{0,1:T(8,128)} %param.31) | copy-start | bytes 50308
  48.6 54.7 %copy-start.27 = (f32[112,512]{1,0:T(8,128)S(1)}, f32[112,512]{1,0:T(8,128)}, u32[]{:S(2)}) copy-start(f32[112,512]{1,0:T(8,128)} %param.32) | copy-start | bytes 688132
  48.6 54.8 %copy-start.31 = (f32[512]{0:T(512)S(1)}, f32[512]{0:T(512)}, u32[]{:S(2)}) copy-start(f32[512]{0:T(512)} %param.33) | copy-start | bytes 6148
  49.8 353.0 %all-gather.7.cloned.1.call-start = ((), (), s32[]{:S(2)}) async-start(), calls=%async_computation.8 | async-start | bytes 37748736 | tf_op jit(solution)/shard_map/all_gather | solution.py:160
  364.6 38.2 %copy-start.9 = (s32[4,512,50]{1,0,2:T(4,128)}, s32[4,512,50]{1,0,2:T(4,128)S(1)}, u32[]{:S(2)}) copy-start(s32[4,512,50]{1,0,2:T(4,128)S(1)} %get-tuple-element.848) | copy-start | bytes 1228804
  364.6 38.2 %copy-start.10 = (bf16[112,512]{1,0:T(8,128)(2,1)}, bf16[112,512]{1,0:T(8,128)(2,1)S(1)}, u32[]{:S(2)}) copy-start(bf16[112,512]{1,0:T(8,128)(2,1)S(1)} %get-tuple-element.854) | copy-start | bytes 344068
  364.6 38.2 %copy-start.40 = (s32[4,512]{1,0:T(4,128)}, s32[4,512]{1,0:T(4,128)S(1)}, u32[]{:S(2)}) copy-start(s32[4,512]{1,0:T(4,128)S(1)} %get-tuple-element.881) | copy-start | bytes 24580
  364.6 38.2 %copy-start.48 = (bf16[262,16]{0,1:T(8,128)(2,1)}, bf16[262,16]{0,1:T(8,128)(2,1)S(1)}, u32[]{:S(2)}) copy-start(bf16[262,16]{0,1:T(8,128)(2,1)S(1)} %get-tuple-element.883) | copy-start | bytes 25156
  364.6 34.9 %copy-start.37 = (f32[8960]{0:T(1024)S(1)}, f32[8960]{0:T(1024)}, u32[]{:S(2)}) copy-start(f32[8960]{0:T(1024)} %param.36) | copy-start | bytes 107524
  364.6 34.9 %all-to-all-start = ((bf16[4,512,512]{2,1,0:T(8,128)(2,1)}), bf16[4,512,512]{2,1,0:T(8,128)(2,1)S(1)}, u32[]{:S(2)}, u32[]{:S(2)}) async-start(bf16[4,512,512]{2,1,0:T(8,128)(2,1)} %get-tuple-element.261), calls=%async_computation | async-start | bytes 4194304 | tf_op jit(solution)/shard_map/all_to_all | solution.py:191
  368.6 101.2 %all-gather.9.cloned.1.call-start = ((), (), s32[]{:S(2)}) async-start(), calls=%async_computation.9 | async-start | bytes 3538944 | tf_op jit(solution)/shard_map/all_gather | solution.py:161
  399.4 861.6 %reduce-scatter.9.cloned.1.call-start = ((), (), s32[]{:S(2)}) async-start(), calls=%async_computation.10 | async-start | bytes 75497472 | tf_op jit(solution)/shard_map/reduce_scatter | solution.py:230
  399.5 27.0 %copy-start.39 = (f32[8960]{0:T(1024)}, f32[8960]{0:T(1024)S(1)}, u32[]{:S(2)}) copy-start(f32[8960]{0:T(1024)S(1)} %convert_convert_fusion) | copy-start | bytes 107524
  450.5 19.2 copy-start.13
  480.5 18.4 copy-start.18
  517.9 22.0 %copy-start.20 = (bf16[512,2048]{1,0:T(8,128)(2,1)}, bf16[512,2048]{1,0:T(8,128)(2,1)S(1)}, u32[]{:S(2)}) copy-start(bf16[512,2048]{1,0:T(8,128)(2,1)S(1)} %get-tuple-element.581) | copy-start | bytes 6291460
  517.9 22.0 %copy-start.23 = (bf16[512,2048]{1,0:T(8,128)(2,1)S(1)}, bf16[512,2048]{1,0:T(8,128)(2,1)}, u32[]{:S(2)}) copy-start(bf16[512,2048]{1,0:T(8,128)(2,1)} %get-tuple-element.582) | copy-start | bytes 6291460
  637.3 623.8 %all-to-all-start.2 = ((bf16[512,4,512]{2,0,1:T(8,128)(2,1)}), bf16[512,4,512]{2,0,1:T(8,128)(2,1)S(1)}, u32[]{:S(2)}, u32[]{:S(2)}) async-start(bf16[512,4,512]{2,0,1:T(8,128)(2,1)} %bitcast.185), calls=%async_computation.2 | async-start | bytes 4194304 | tf_op jit(solution)/shard_map/all_to_all | solution.py:225
  640.9 1218.9 %reduce-scatter.11.cloned.1.call-start = ((), (), s32[]{:S(2)}) async-start(), calls=%async_computation.11 | async-start | bytes 10485760 | tf_op jit(solution)/shard_map/reduce_scatter | solution.py:234
  1261.1 738.5 %all-reduce.15.cloned.1.call-start = ((), (), s32[]{:S(2)}) async-start(), calls=%async_computation.13 | async-start | bytes 13041664 | tf_op jit(solution)/shard_map/psum | solution.py:283
  1261.9 597.0 %copy-start.47 = (s32[512]{0:T(512)S(1)}, s32[512]{0:T(512)}, u32[]{:S(2)}) copy-start(s32[512]{0:T(512)} %copy-done.46) | copy-start | bytes 6148
  1261.9 597.0 %copy-start.56 = (s32[112]{0:T(128)S(1)}, s32[112]{0:T(128)}, u32[]{:S(2)}) copy-start(s32[112]{0:T(128)} %copy-done.55) | copy-start | bytes 1348
  1410.5 17.1 copy-start.5
  1410.5 17.1 copy-start.8
  1410.5 17.1 copy-start.12
  1410.5 17.1 copy-start.50
  1430.1 8.2 copy-start.2
  1554.1 17.1 copy-start.5
  1554.1 17.1 copy-start.8
  1554.1 17.1 copy-start.12
  1554.2 17.1 copy-start.50
  1573.7 8.2 copy-start.2
  1697.8 17.1 copy-start.5
  1697.8 17.1 copy-start.8
  1697.8 17.1 copy-start.12
  1697.8 17.1 copy-start.50
  1717.3 8.2 copy-start.2
  1841.4 17.1 copy-start.5
  1841.4 17.1 copy-start.8
  1841.4 17.1 copy-start.12
  1841.4 17.1 copy-start.50
  1865.7 202.4 %all-to-all-start.3 = ((f32[8,256,512]{2,1,0:T(8,128)}), f32[8,256,512]{2,1,0:T(8,128)}, u32[]{:S(2)}, u32[]{:S(2)}) async-start(f32[8,256,512]{2,1,0:T(8,128)} %slice_dynamic-update-slice_fusion.12), calls=%async_computation.5 | async-start | bytes 8388608 | tf_op jit(solution)/shard_map/all_to_all | solution.py:243
  1870.5 195.6 %reduce-scatter.13.cloned.1.call-start = ((), (), s32[]{:S(2)}) async-start(), calls=%async_computation.12 | async-start | bytes 983040
  1896.1 106.1 %copy-start.17 = (bf16[512,2048]{1,0:T(8,128)(2,1)S(1)}, bf16[512,2048]{1,0:T(8,128)(2,1)}, u32[]{:S(2)}) copy-start(bf16[512,2048]{1,0:T(8,128)(2,1)} %get-tuple-element.585) | copy-start | bytes 6291460
  1896.1 106.1 %slice-start = ((f32[8960]{0:T(1024)}), f32[768]{0:T(1024)S(1)}, s32[]{:S(2)}) async-start(f32[8960]{0:T(1024)} %copy-done.39), calls=%async_computation.14 | async-start | bytes 8192 | tf_op jit(solution)/shard_map/slice | solution.py:203
  2002.3 59.4 %copy-start.53 = (f32[512]{0:T(512)S(1)}, f32[512]{0:T(512)}, u32[]{:S(2)}) copy-start(f32[512]{0:T(512)} %param.41) | copy-start | bytes 6148
  2002.3 59.4 %copy-start.54 = (f32[512]{0:T(512)S(1)}, f32[512]{0:T(512)}, u32[]{:S(2)}) copy-start(f32[512]{0:T(512)} %param.42) | copy-start | bytes 6148
  2002.3 60.1 %copy-start.42 = (f32[262,16]{0,1:T(8,128)S(1)}, f32[262,16]{0,1:T(8,128)}, u32[]{:S(2)}) copy-start(f32[262,16]{0,1:T(8,128)} %param.31) | copy-start | bytes 50308
  2002.3 60.1 %copy-start.44 = (f32[262,16]{0,1:T(8,128)S(1)}, f32[262,16]{0,1:T(8,128)}, u32[]{:S(2)}) copy-start(f32[262,16]{0,1:T(8,128)} %param.37) | copy-start | bytes 50308
  2002.3 61.4 %copy-start.38 = (f32[8960]{0:T(1024)S(1)}, f32[8960]{0:T(1024)}, u32[]{:S(2)}) copy-start(f32[8960]{0:T(1024)} %param.36) | copy-start | bytes 107524
  2002.4 62.9 %copy-start.26 = (f32[112,512]{1,0:T(8,128)S(1)}, f32[112,512]{1,0:T(8,128)}, u32[]{:S(2)}) copy-start(f32[112,512]{1,0:T(8,128)} %get-tuple-element.811) | copy-start | bytes 688132
  2002.4 62.9 %copy-start.28 = (f32[112,512]{1,0:T(8,128)S(1)}, f32[112,512]{1,0:T(8,128)}, u32[]{:S(2)}) copy-start(f32[112,512]{1,0:T(8,128)} %param.32) | copy-start | bytes 688132
  2002.4 62.8 %copy-start.34 = (f32[112,512]{1,0:T(8,128)S(1)}, f32[112,512]{1,0:T(8,128)}, u32[]{:S(2)}) copy-start(f32[112,512]{1,0:T(8,128)} %param.39) | copy-start | bytes 688132
  2002.4 62.8 %copy-start.35 = (f32[112,512]{1,0:T(8,128)S(1)}, f32[112,512]{1,0:T(8,128)}, u32[]{:S(2)}) copy-start(f32[112,512]{1,0:T(8,128)} %param.40) | copy-start | bytes 688132
  2002.4 63.8 %copy-start.30 = (f32[64,768]{1,0:T(8,128)S(1)}, f32[64,768]{1,0:T(8,128)}, u32[]{:S(2)}) copy-start(f32[64,768]{1,0:T(8,128)} %param.35) | copy-start | bytes 589828
  2002.4 63.8 %copy-start.36 = (f32[64,768]{1,0:T(8,128)S(1)}, f32[64,768]{1,0:T(8,128)}, u32[]{:S(2)}) copy-start(f32[64,768]{1,0:T(8,128)} %param.46) | copy-start | bytes 589828
  2022.8 50.5 %copy-start.52 = (f32[512]{0:T(512)}, f32[512]{0:T(512)S(1)}, u32[]{:S(2)}) copy-start(f32[512]{0:T(512)S(1)} %psum.30) | copy-start | bytes 6148
  2061.8 11.6 copy-start.43
  2061.8 11.5 copy-start.45
  (40 other events, 120.1 us)
Sparse Core Ops, SparseCore 0:
  49.9 52.9 all-gather.4
  104.5 288.6 all-gather.6
  399.5 38.7 all-gather.8
  620.6 640.3 reduce-scatter.8
  1264.2 84.6 reduce-scatter.10
  1859.9 139.5 all-reduce.14
  2003.0 25.9 reduce-scatter.12
where the time goes:
time: 2130 us; the launch traced here: 2110 us
  waiting for transfers between devices  786 us (37%)
  matrix products  541 us (25%)
  other arithmetic  360 us (17%)
  local copies, waits for them, and re-layouts  280 us (13%)
  blocking collectives  85.1 us (4%)
  between operations  22.8 us (1%)
  loops' own time  22.1 us (1%)
    reduce_scatter x1, waiting for transfers between devices, per_device(): lax.psum_scatter(unit_stack, 'dp', scatter_dimension=1, tiled=True)  614 us
    reduce_sum x8, other arithmetic, pooling(): summed = jnp.sum(shifted, axis=1)  148 us
    reduce_sum x4, other arithmetic, backward_block(): bias_term = jnp.sum(d_pre, axis=(0, 1), dtype=jnp.float32)  109 us
    psum x1, waiting for transfers between devices, per_device(): lax.psum((sums_local[0] * tap_mask, sums_local[1]), 'dp')  102 us
    dot_general x4, matrix products, forward_block(): jnp.einsum('bpk,kc->bpc', windows, conv_low, preferred_element_type=jnp.f...  98.7 us
    dot_general x4, matrix products, backward_block(): jnp.einsum('bpk,kc->bpc', windows, conv_low, preferred_element_type=jnp.f...  97.8 us
    dot_general x4, matrix products, backward_block(): lax.dot_general(flat_hot, d_embedded, (((0,), (0,)), ((), ())), precision...  68.4 us
    reshape x16, local copies, waits for them, and re-layouts, make_windows(): embedded = embedded.reshape(rows, MAX_CHARS, CHAR_DIM)  65.7 us
  transfers between devices with their start and end apart: 11, of which 4 were waited for; matrix products, arithmetic and copies ran while one was open for 45% of the time, Pallas kernels for 0%

commit v1 on v0

v1 whole, which is shorter than its diff:
```python
import functools

import jax
import jax.numpy as jnp
from jax import lax
from jax.experimental import pallas as pl
from jax.experimental.pallas import tpu as pltpu
from jax.sharding import PartitionSpec as P

CHAR_DIM = 16
MAX_CHARS = 50
MAX_WIDTH = 7
FILTERS = 2048
UNITS = 4
SLOTS = 2
STEP = 10
TAPS = MAX_WIDTH * CHAR_DIM
DEPTH = 128
ID_SHIFT = 128
ID_ROWS = 64
SLOTS_E = MAX_CHARS + MAX_WIDTH - 1 + 8
LANES = 128
STEP_P = 4
beta_one = 0.9
beta_two = 0.999
adam_eps = 1e-08
decay_rate = 0.01
average_keep = 0.9
F32, BF16 = jnp.float32, jnp.bfloat16
MIB = 1 << 20


def nt(a, b):
    return lax.dot_general(a, b, (((1,), (1,)), ((), ())), preferred_element_type=F32)


def nn(a, b):
    return lax.dot_general(a, b, (((1,), (0,)), ((), ())), preferred_element_type=F32)


def tn(a, b):
    return lax.dot_general(a, b, (((0,), (0,)), ((), ())), preferred_element_type=F32)


def embed_tile(ids_ref, table_ref, lens, e_ref, longest):
    tile = lens.shape[1]
    e_ref[...] = jnp.zeros_like(e_ref)
    pieces = table_ref.shape[1] // LANES

    def fill(p, carry):
        row = ids_ref[pl.ds(p, 1), :].astype(jnp.int32)
        parts = []
        for lane in range(tile // LANES):
            idx = jnp.broadcast_to(row[:, lane * LANES : (lane + 1) * LANES], (CHAR_DIM, LANES))
            low = jnp.bitwise_and(idx, LANES - 1)
            value = jnp.zeros((CHAR_DIM, LANES), F32)
            for piece in range(pieces):
                got = jnp.take_along_axis(table_ref[:, piece * LANES : (piece + 1) * LANES], low, axis=1)
                value = jnp.where(lax.shift_right_logical(idx, 7) == piece, got, value)
            parts.append(value)
        value = jnp.concatenate(parts, axis=1) if len(parts) > 1 else parts[0]
        value = jnp.where(p < lens, value, 0.0)
        e_ref[pl.ds(pl.multiple_of(p * CHAR_DIM, CHAR_DIM), CHAR_DIM), :] = value.astype(BF16)
        return carry

    lax.fori_loop(0, longest, fill, 0)


def limits_of(lens):
    row = lax.broadcasted_iota(jnp.int32, (CHAR_DIM, lens.shape[1]), 0)
    past = jnp.maximum(lens - (row - 2), 0)
    return jnp.where(row < 3, -1, jnp.where(row < 3 + MAX_WIDTH, past, 1 << 20))


def window_at(e_ref, limit, p):
    extra = jnp.where(p > limit, 1.0, 0.0).astype(BF16)
    taps = e_ref[pl.ds(pl.multiple_of(p * CHAR_DIM, CHAR_DIM), TAPS), :]
    return jnp.concatenate([taps, extra], axis=0)


def steps_of(longest, narrow):
    return (jnp.maximum(longest - narrow, 0) + STEP_P) // STEP_P


def conv_forward_kernel(cblock, narrow_ref, rank_ref, data_ref, table_ref, conv_ref, width_ref, feat_ref, lse_ref, ids_ref, e_ref, top, total, pre):
    tile = ids_ref.shape[1]
    words = rank_ref.shape[0]
    first = pl.program_id(0) * tile
    lane = first + lax.broadcasted_iota(jnp.int32, (words, tile), 1)
    hot = jnp.where(rank_ref[...] == lane, 1.0, 0.0).astype(BF16)
    moved = nn(data_ref[...], hot)
    shift = jnp.where(lax.broadcasted_iota(jnp.int32, moved.shape, 0) < MAX_CHARS, float(ID_SHIFT), 0.0)
    moved = moved + shift
    ids_ref[...] = moved
    lens = (moved[MAX_CHARS : MAX_CHARS + 1, :] + 0.5).astype(jnp.int32)
    longest = jnp.max(lens)
    embed_tile(ids_ref, table_ref, lens, e_ref, longest)
    limit = limits_of(lens)
    channels = conv_ref.shape[0]
    for block in range(channels // cblock):
        rows = pl.ds(block * cblock, cblock)
        top[...] = jnp.full_like(top, -1e30)
        total[...] = jnp.zeros_like(total)

        def step(s, carry):
            best = top[...]
            for i in range(STEP_P):
                value = nn(conv_ref[rows, :], window_at(e_ref, limit, s * STEP_P + i))
                pre[i] = value
                best = jnp.maximum(best, value)
            summed = total[...] * jnp.exp(top[...] - best)
            for i in range(STEP_P):
                summed = summed + jnp.exp(pre[i] - best)
            total[...] = summed
            top[...] = best
            return carry

        lax.fori_loop(0, steps_of(longest, narrow_ref[block]), step, 0)
        span = jnp.maximum(lens - width_ref[rows, :], 0)
        lse = top[...] + jnp.log(total[...])
        lse_ref[rows, :] = lse
        pooled = lse - jnp.log((span + 1).astype(F32))
        feat_ref[rows, :] = (pooled * jax.nn.sigmoid(pooled)).astype(BF16)


def place_kernel(rank_ref, feat_ref, out_ref):
    shape = (rank_ref.shape[0], feat_ref.shape[1])
    hot = jnp.where(rank_ref[...] == lax.broadcasted_iota(jnp.int32, shape, 1), 1.0, 0.0).astype(BF16)
    out_ref[...] = nt(hot, feat_ref[...]).astype(BF16)


def conv_forward(rank, data, table_t, conv_t, widths, narrow, cblock):
    words, channels = rank.shape[0], conv_t.shape[0]
    tile = min(256, words)
    full = lambda *shape: pl.BlockSpec(shape, lambda i: (0,) * len(shape))
    feat, lse, ids = pl.pallas_call(
        functools.partial(conv_forward_kernel, cblock),
        grid=(words // tile,),
        in_specs=[
            pl.BlockSpec(memory_space=pltpu.SMEM),
            full(words, 1),
            full(*data.shape),
            full(*table_t.shape),
            full(*conv_t.shape),
            full(channels, 1),
        ],
        out_specs=[
            pl.BlockSpec((channels, tile), lambda i: (0, i)),
            pl.BlockSpec((channels, tile), lambda i: (0, i)),
            pl.BlockSpec((ID_ROWS, tile), lambda i: (0, i)),
        ],
        out_shape=[
            jax.ShapeDtypeStruct((channels, words), BF16),
            jax.ShapeDtypeStruct((channels, words), F32),
            jax.ShapeDtypeStruct((ID_ROWS, words), F32),
        ],
        scratch_shapes=[
            pltpu.VMEM((SLOTS_E * CHAR_DIM, tile), BF16),
            pltpu.VMEM((cblock, tile), F32),
            pltpu.VMEM((cblock, tile), F32),
            pltpu.VMEM((STEP_P, cblock, tile), F32),
        ],
        compiler_params=pltpu.CompilerParams(vmem_limit_bytes=48 * MIB),
        name="conv_forward",
    )(narrow, rank, data, table_t, conv_t, widths)
    return feat, lse, ids


def conv_backward_kernel(cblock, n_parts, narrow_ref, ids_ref, table_ref, conv_ref, back_ref, width_ref, lse_ref, *refs):
    ranks, grads, refs = refs[:n_parts], refs[n_parts : 2 * n_parts], refs[2 * n_parts :]
    conv_grad_ref, table_grad_ref, e_ref, de_ref, dpool, d_pre = refs
    tile = ids_ref.shape[1]
    words = ranks[0].shape[0]
    vocab = table_grad_ref.shape[1]
    first = pl.program_id(0) * tile

    @pl.when(pl.program_id(0) == 0)
    def _():
        conv_grad_ref[...] = jnp.zeros_like(conv_grad_ref)
        table_grad_ref[...] = jnp.zeros_like(table_grad_ref)

    lane = first + lax.broadcasted_iota(jnp.int32, (words, tile), 1)
    hots = [jnp.where(rank_ref[...] == lane, 1.0, 0.0).astype(BF16) for rank_ref in ranks]
    lens = (ids_ref[MAX_CHARS : MAX_CHARS + 1, :] + 0.5).astype(jnp.int32)
    longest = jnp.max(lens)
    embed_tile(ids_ref, table_ref, lens, e_ref, longest)
    limit = limits_of(lens)
    de_ref[...] = jnp.zeros_like(de_ref)
    channels = conv_ref.shape[0]
    for block in range(channels // cblock):
        rows = pl.ds(block * cblock, cblock)
        span = jnp.maximum(lens - width_ref[rows, :], 0)
        pooled = lse_ref[rows, :] - jnp.log((span + 1).astype(F32))
        sigma = jax.nn.sigmoid(pooled)
        slope = sigma + pooled * sigma * (1 - sigma)
        dpool[...] = sum(tn(grad_ref[:, rows], hot) for grad_ref, hot in zip(grads, hots)) * slope

        def step(s, carry):
            windows = []
            for i in range(STEP_P):
                p = s * STEP_P + i
                window = window_at(e_ref, limit, p)
                value = nn(conv_ref[rows, :], window)
                d = (jnp.exp(value - lse_ref[rows, :]) * dpool[...]).astype(BF16)
                d_pre[:, i * tile : (i + 1) * tile] = d
                windows.append(window)
                at = pl.ds(pl.multiple_of(p * CHAR_DIM, CHAR_DIM), DEPTH)
                de_ref[at, :] += nn(back_ref[:, rows], d)
            conv_grad_ref[rows, :] += nt(d_pre[...], jnp.concatenate(windows, axis=1))
            return carry

        lax.fori_loop(0, steps_of(longest, narrow_ref[block]), step, 0)

    letter = lax.broadcasted_iota(jnp.int32, (vocab, tile), 0)

    def spread(p, carry):
        at = pl.ds(pl.multiple_of(p * CHAR_DIM, CHAR_DIM), CHAR_DIM)
        value = jnp.where(p < lens, de_ref[at, :], 0.0)
        high = value.astype(BF16)
        both = jnp.concatenate([high, (value - high.astype(F32)).astype(BF16)], axis=0)
        row = ids_ref[pl.ds(p, 1), :].astype(jnp.int32)
        found = jnp.where(letter == row, 1.0, 0.0).astype(BF16)
        table_grad_ref[...] += nt(both, found)
        return carry

    lax.fori_loop(0, longest, spread, 0)


def conv_backward(ranks, ids, table_t, conv_t, conv_back, widths, narrow, lse, grads, cblock):
    channels, words = conv_t.shape[0], ids.shape[1]
    tile = min(256, words)
    vocab = table_t.shape[1]
    full = lambda *shape: pl.BlockSpec(shape, lambda i: (0,) * len(shape))
    return pl.pallas_call(
        functools.partial(conv_backward_kernel, cblock, len(ranks)),
        grid=(words // tile,),
        in_specs=[
            pl.BlockSpec(memory_space=pltpu.SMEM),
            pl.BlockSpec((ID_ROWS, tile), lambda i: (0, i)),
            full(*table_t.shape),
            full(*conv_t.shape),
            full(*conv_back.shape),
            full(channels, 1),
            pl.BlockSpec((channels, tile), lambda i: (0, i)),
        ]
        + [full(*part.shape) for part in ranks]
        + [full(*part.shape) for part in grads],
        out_specs=[full(channels, DEPTH), full(2 * CHAR_DIM, vocab)],
        out_shape=[
            jax.ShapeDtypeStruct((channels, DEPTH), F32),
            jax.ShapeDtypeStruct((2 * CHAR_DIM, vocab), F32),
        ],
        scratch_shapes=[
            pltpu.VMEM((SLOTS_E * CHAR_DIM, tile), BF16),
            pltpu.VMEM((SLOTS_E * CHAR_DIM, tile), F32),
            pltpu.VMEM((cblock, tile), F32),
            pltpu.VMEM((cblock, STEP_P * tile), BF16),
        ],
        compiler_params=pltpu.CompilerParams(vmem_limit_bytes=48 * MIB),
        name="conv_backward",
    )(narrow, ids, table_t, conv_t, conv_back, widths, lse, *ranks, *grads)


def word_order(lengths):
    count = lengths.shape[0]
    key = lengths * count - jnp.arange(count, dtype=jnp.int32)
    return jnp.sum((key[None, :] > key[:, None]).astype(jnp.int32), axis=1, keepdims=True)


def conv_operands(char_ids, lengths, char_table, conv_weight, conv_bias, widths, cblock):
    words = char_ids.shape[0]
    channels = conv_weight.shape[1]
    vocab = char_table.shape[0]
    lanes = -(-vocab // LANES) * LANES
    rank = word_order(lengths)
    data = jnp.concatenate([char_ids.T - ID_SHIFT, lengths[None, :]], axis=0)
    data = jnp.pad(data, ((0, ID_ROWS - MAX_CHARS - 1), (0, 0))).astype(BF16)
    offsets = jnp.arange(TAPS, dtype=jnp.int32) // CHAR_DIM
    taps = jnp.where(offsets[:, None] < widths[None, :], conv_weight, 0.0).astype(BF16)
    parts, rest = [], conv_bias
    for _ in range(3):
        part = lax.reduce_precision(rest, 8, 7)
        parts.append(part)
        rest = rest - part
    kinds = jnp.arange(1, MAX_WIDTH + 1, dtype=jnp.int32)
    spans = jnp.where(kinds[:, None] == widths[None, :], -1e30, 0.0)
    under = jnp.concatenate([jnp.stack(parts), spans, jnp.zeros((DEPTH - TAPS - 3 - MAX_WIDTH, channels), F32)])
    conv_all = jnp.concatenate([taps, under.astype(BF16)])
    conv_back = jnp.pad(taps, ((0, DEPTH - TAPS), (0, 0)))
    table_t = jnp.pad(lax.reduce_precision(char_table, 8, 7).T, ((0, 0), (0, lanes - vocab)))
    narrow = widths[::cblock]
    return rank, data, table_t, conv_all.T, conv_back, widths[:, None], narrow


def channel_widths(start, count, whole):
    channel = start + jnp.arange(count, dtype=jnp.int32)
    widths = jnp.ones((count,), jnp.int32)
    for power in range(6):
        widths = widths + (channel >= whole * 2**power // 64).astype(jnp.int32)
    return widths


def unit_slots(owners, slots_each):
    order = jnp.arange(owners.shape[0], dtype=jnp.int32)
    before = (owners[:, None] == owners[None, :]) & (order[:, None] > order[None, :])
    return owners * slots_each + jnp.sum(before.astype(jnp.int32), axis=1)


def place_words(rank, feat):
    words, channels = rank.shape[0], feat.shape[0]
    rows = min(256, words)
    return pl.pallas_call(
        place_kernel,
        grid=(words // rows,),
        in_specs=[
            pl.BlockSpec((rows, 1), lambda i: (i, 0)),
            pl.BlockSpec(feat.shape, lambda i: (0, 0)),
        ],
        out_specs=pl.BlockSpec((rows, channels), lambda i: (i, 0)),
        out_shape=jax.ShapeDtypeStruct((words, channels), BF16),
        compiler_params=pltpu.CompilerParams(vmem_limit_bytes=48 * MIB),
        name="place_words",
    )(rank, feat)


def load_pieces(table_ref, pieces, dest, sems, half=None):
    rows, cols = pieces[0].shape[2:]
    depth = dest.shape[1]

    def each(act):
        at = 0
        for ref in pieces:
            for j in range(ref.shape[0]):
                row, col = table_ref[0, at], table_ref[1, at]
                row = row if half is None else row - half * depth
                sem = sems.at[at]

                def go(ref=ref, j=j, row=row, col=col, sem=sem):
                    place = (slice(None), pl.ds(pl.multiple_of(row, rows), rows), pl.ds(pl.multiple_of(col, cols), cols))
                    act(pltpu.make_async_copy(ref.at[j], dest.at[place], sem))

                if half is None:
                    go()
                else:
                    pl.when((row >= 0) & (row < depth))(go)
                at += 1

    each(lambda copy: copy.start())
    each(lambda copy: copy.wait())


def hidden_of(xs, weight, unit, cols, bias_ref):
    at, total = 0, None
    for x in xs:
        term = nn(x[...], weight[unit, at : at + x.shape[1], cols])
        total = term if total is None else total + term
        at += x.shape[1]
    return total + bias_ref[unit : unit + 1, cols]


def forward_kernel(n_own, n_pieces, width, table_ref, bias_ref, *refs):
    own, refs = refs[:n_own], refs[n_own:]
    mate, refs = refs[:n_own], refs[n_own:]
    pieces, refs = refs[:n_pieces], refs[n_pieces:]
    next_ref, low_ref, first_ref, gate_ref, weight, sems = refs

    @pl.when(pl.program_id(0) == 0)
    def _():
        load_pieces(table_ref, pieces, weight, sems)

    for j, x in enumerate(own):
        cols = slice(j * width, (j + 1) * width)
        a = hidden_of(own + mate, weight, 0, cols, bias_ref)
        g = hidden_of(own + mate, weight, 1, cols, bias_ref)
        first_ref[:, cols] = a
        gate_ref[:, cols] = g
        gate = jax.nn.sigmoid(g)
        value = gate * x[...].astype(F32) + (1 - gate) * (a * jax.nn.sigmoid(a))
        next_ref[:, cols] = value
        low_ref[:, cols] = value.astype(BF16)


def slopes(dy, x, a, g):
    s = jax.nn.sigmoid(a)
    gate = jax.nn.sigmoid(g)
    nonlinear = a * s
    d_first = dy * (1 - gate) * (s + nonlinear * (1 - s))
    d_gate = dy * (x - nonlinear) * gate * (1 - gate)
    return d_first.astype(BF16), d_gate.astype(BF16), dy * gate, gate * x + (1 - gate) * nonlinear


def turn_kernel(n_pieces, width, table_ref, bias_ref, own, mate, exact, out_grad, proj, *refs):
    pieces, refs = refs[:n_pieces], refs[n_pieces:]
    low_ref, d_first_ref, d_gate_ref, up_ref, sums_ref, weight, sems = refs

    @pl.when(pl.program_id(0) == 0)
    def _():
        load_pieces(table_ref, pieces, weight, sems)
        sums_ref[...] = jnp.zeros_like(sums_ref)

    for j in range(own.shape[1] // width):
        cols = slice(j * width, (j + 1) * width)
        a = hidden_of((own, mate), weight, 0, cols, bias_ref)
        g = hidden_of((own, mate), weight, 1, cols, bias_ref)
        dy = nt(out_grad[...], proj[cols, :])
        d_first, d_gate, up, value = slopes(dy, exact[:, cols], a, g)
        low_ref[:, cols] = value.astype(BF16)
        d_first_ref[:, cols] = d_first
        d_gate_ref[:, cols] = d_gate
        up_ref[:, cols] = up
        sums_ref[0:1, cols] += jnp.sum(d_first.astype(F32), axis=0, keepdims=True)
        sums_ref[1:2, cols] += jnp.sum(d_gate.astype(F32), axis=0, keepdims=True)


def slope_kernel(n_own, width, partial, arrived, first_ref, gate_ref, *refs):
    own, refs = refs[:n_own], refs[n_own:]
    d_first_ref, d_gate_ref, up_ref, sums_ref = refs

    @pl.when(pl.program_id(0) == 0)
    def _():
        sums_ref[...] = jnp.zeros_like(sums_ref)

    for j, x in enumerate(own):
        cols = slice(j * width, (j + 1) * width)
        dy = partial[:, cols] + arrived[:, cols].astype(F32)
        d_first, d_gate, up, _ = slopes(dy, x[...].astype(F32), first_ref[:, cols], gate_ref[:, cols])
        d_first_ref[:, cols] = d_first
        d_gate_ref[:, cols] = d_gate
        up_ref[:, cols] = up
        sums_ref[0:1, cols] += jnp.sum(d_first.astype(F32), axis=0, keepdims=True)
        sums_ref[1:2, cols] += jnp.sum(d_gate.astype(F32), axis=0, keepdims=True)


def back_kernel(half, n_pieces, with_up, table_ref, d_first, d_gate, *refs):
    if with_up:
        up, refs = refs[0], refs[1:]
    pieces, refs = refs[:n_pieces], refs[n_pieces:]
    out_ref, weight, sems = refs

    @pl.when(pl.program_id(0) == 0)
    def _():
        load_pieces(table_ref, pieces, weight, sems, half)

    width = min(512, out_ref.shape[1])
    for j in range(out_ref.shape[1] // width):
        cols = slice(j * width, (j + 1) * width)
        value = nt(d_first[...], weight[0, cols, :]) + nt(d_gate[...], weight[1, cols, :])
        if with_up:
            value = value + up[:, cols]
        out_ref[:, cols] = value.astype(out_ref.dtype)


def weight_grad_kernel(n_own, width, table_ref, *refs):
    xs, refs = refs[: 2 * n_own], refs[2 * n_own :]
    d_first, d_gate, refs = refs[0], refs[1], refs[2:]
    outs, turned = refs[:-1], refs[-1]
    rows = outs[0].shape[2]

    @pl.when(pl.program_id(0) == 0)
    def _():
        at = 0
        for x in xs:
            turned[at : at + x.shape[1], :] = x[...].T
            at += x.shape[1]

    blocks = d_first.shape[1] // width
    for side in range(2):
        row = table_ref[side, pl.program_id(0)]
        left = turned[pl.ds(pl.multiple_of(row, rows), rows), :]
        for j in range(blocks):
            cols = slice(j * width, (j + 1) * width)
            out = outs[side * blocks + j]
            out[0, 0] = nn(left, d_first[:, cols]).astype(BF16)
            out[0, 1] = nn(left, d_gate[:, cols]).astype(BF16)


SMEM_SPEC = pl.BlockSpec(memory_space=pltpu.SMEM)
ANY_SPEC = pl.BlockSpec(memory_space=pl.ANY)


def whole(array):
    return pl.BlockSpec(array.shape, lambda i: (0,) * array.ndim)


def by_rows(rows, width):
    return pl.BlockSpec((rows, width), lambda i: (i, 0))


def params(**kw):
    return pltpu.CompilerParams(vmem_limit_bytes=58 * MIB, **kw)


def count_of(pieces):
    return sum(piece.shape[0] for piece in pieces)


def cost(flops, *arrays):
    return pl.CostEstimate(flops=flops, bytes_accessed=sum(a.size * a.dtype.itemsize for a in arrays), transcendentals=0)


def highway_forward(table, pieces, bias, own, mate):
    words, width = own[0].shape
    half = width * len(own)
    rows = min(512, words)
    tile = by_rows(rows, width)
    out = by_rows(rows, half)
    return pl.pallas_call(
        functools.partial(forward_kernel, len(own), len(pieces), width),
        grid=(words // rows,),
        in_specs=[SMEM_SPEC, whole(bias)] + [tile] * (2 * len(own)) + [ANY_SPEC] * len(pieces),
        out_specs=[out] * 4,
        out_shape=[jax.ShapeDtypeStruct((words, half), kind) for kind in (F32, BF16, F32, F32)],
        scratch_shapes=[pltpu.VMEM((2, 2 * half, half), BF16), pltpu.SemaphoreType.DMA((count_of(pieces),))],
        compiler_params=params(),
        cost_estimate=cost(8 * words * half * half, *pieces, *own, *own, *own),
        name="highway_forward",
    )(table, bias, *own, *mate, *pieces)


def highway_turn(table, pieces, bias, own, mate, exact, out_grad, proj, width):
    words, half = own.shape
    rows = min(512, words)
    tile = by_rows(rows, half)
    return pl.pallas_call(
        functools.partial(turn_kernel, len(pieces), width),
        grid=(words // rows,),
        in_specs=[SMEM_SPEC, whole(bias), tile, tile, tile, by_rows(rows, out_grad.shape[1]), whole(proj)] + [ANY_SPEC] * len(pieces),
        out_specs=[tile, tile, tile, tile, pl.BlockSpec((2, half), lambda i: (0, 0))],
        out_shape=[jax.ShapeDtypeStruct((words, half), kind) for kind in (BF16, BF16, BF16, F32)] + [jax.ShapeDtypeStruct((2, half), F32)],
        scratch_shapes=[pltpu.VMEM((2, 2 * half, half), BF16), pltpu.SemaphoreType.DMA((count_of(pieces),))],
        compiler_params=params(),
        cost_estimate=cost(8 * words * half * half, *pieces, own, mate, exact, exact),
        name="highway_turn",
    )(table, bias, own, mate, exact, out_grad, proj, *pieces)


def highway_slopes(partial, arrived, first, gate, own):
    words, half = partial.shape
    width = own[0].shape[1]
    rows = min(256, words)
    tile = by_rows(rows, half)
    return pl.pallas_call(
        functools.partial(slope_kernel, len(own), width),
        grid=(words // rows,),
        in_specs=[tile] * 4 + [by_rows(rows, width)] * len(own),
        out_specs=[tile, tile, tile, pl.BlockSpec((2, half), lambda i: (0, 0))],
        out_shape=[jax.ShapeDtypeStruct((words, half), kind) for kind in (BF16, BF16, F32)] + [jax.ShapeDtypeStruct((2, half), F32)],
        compiler_params=params(),
        cost_estimate=cost(0, partial, partial, first, gate, arrived),
        name="highway_slopes",
    )(partial, arrived, first, gate, *own)


def highway_back(half, table, pieces, d_first, d_gate, up=None):
    words, width = d_first.shape
    rows = min(512, words)
    tile = by_rows(rows, width)
    ups = [] if up is None else [up]
    return pl.pallas_call(
        functools.partial(back_kernel, half, len(pieces), up is not None),
        grid=(words // rows,),
        in_specs=[SMEM_SPEC, tile, tile] + [tile] * len(ups) + [ANY_SPEC] * len(pieces),
        out_specs=tile,
        out_shape=jax.ShapeDtypeStruct((words, width), BF16 if up is None else F32),
        scratch_shapes=[pltpu.VMEM((2, width, width), BF16), pltpu.SemaphoreType.DMA((count_of(pieces),))],
        compiler_params=params(),
        cost_estimate=cost(4 * words * width * width, *pieces, d_first, d_gate),
        name="highway_back",
    )(table, d_first, d_gate, *ups, *pieces)


def highway_weight_grad(table, own, mate, d_first, d_gate, rows, width):
    words, half = d_first.shape
    xs = list(own) + list(mate)
    steps = table.shape[1]
    blocks = half // width
    block = pl.BlockSpec((1, 2, rows, width), lambda i: (i, 0, 0, 0))
    return pl.pallas_call(
        functools.partial(weight_grad_kernel, len(own), width),
        grid=(steps,),
        in_specs=[SMEM_SPEC] + [whole(x) for x in xs] + [whole(d_first), whole(d_gate)],
        out_specs=[block] * (2 * blocks),
        out_shape=[jax.ShapeDtypeStruct((steps, 2, rows, width), BF16)] * (2 * blocks),
        scratch_shapes=[pltpu.VMEM((2 * half, words), BF16)],
        compiler_params=params(),
        cost_estimate=cost(8 * words * half * half, *xs, d_first, d_gate, d_first, d_gate),
        name="highway_weight_grad",
    )(table, *xs, d_first, d_gate)


def adam_update(weight, grad, moment_one, moment_two, rate):
    first_new = beta_one * moment_one + (1 - beta_one) * grad
    second_new = beta_two * moment_two + (1 - beta_two) * grad * grad
    corrected_one = first_new / (1 - beta_one**STEP)
    corrected_two = second_new / (1 - beta_two**STEP)
    updated = weight - rate * (
        corrected_one / (jnp.sqrt(corrected_two) + adam_eps) + decay_rate * weight
    )
    return (second_new, updated)


def owner_kernel(at_ref, grad_in, weight, one, two, average, grad, second, new, average_new):
    value = grad_in[0].astype(F32)
    grad[...] = value
    second_new, updated = adam_update(weight[...], value, one[...], two[...], 0.02)
    second[...] = second_new
    new[...] = updated
    average_new[...] = average_keep * average[...] + (1 - average_keep) * updated


def owner_update(at, grads, weight, one, two, average):
    slots, rows, width = grads.shape[1:]
    part = min(128, rows)
    block = pl.BlockSpec((slots, part, width), lambda j, r, at: (0, r, at[j]))
    return pl.pallas_call(
        owner_kernel,
        grid_spec=pltpu.PrefetchScalarGridSpec(
            num_scalar_prefetch=1,
            grid=(grads.shape[0], rows // part),
            in_specs=[pl.BlockSpec((1, slots, part, width), lambda j, r, at: (j, 0, r, 0))] + [block] * 4,
            out_specs=[block] * 4,
        ),
        out_shape=[jax.ShapeDtypeStruct(weight.shape, F32)] * 4,
        compiler_params=params(),
        cost_estimate=cost(0, weight, weight, weight, weight, weight, weight, weight, weight),
        name="owner_update",
    )(at, grads, weight, one, two, average)


class Places:
    def __init__(self):
        self.n_filt, self.n_dp = lax.axis_size("filt"), lax.axis_size("dp")
        self.n_y, self.n_z = self.n_filt // 2, self.n_dp // 2
        self.f, self.d = lax.axis_index("filt"), lax.axis_index("dp")
        self.y, self.x = self.f // 2, self.f % 2
        self.z, self.c = self.d // 2, self.d % 2
        self.direct = self.n_y * self.n_z <= 8

    def over_filt(self, value, step):
        return lax.ppermute(value, "filt", [(i, i ^ step) for i in range(self.n_filt)])

    def over_x(self, value):
        return self.over_filt(value, 1)

    def over_y(self, value, step):
        return self.over_filt(value, 2 * step)

    def over_core(self, value):
        return lax.ppermute(value, "dp", [(i, i ^ 1) for i in range(self.n_dp)])

    def over_z(self, value, step):
        pairs = [(i, (i // 2 + step) % self.n_z * 2 + i % 2) for i in range(self.n_dp)]
        return lax.ppermute(value, "dp", pairs)

    def far_first(self):
        return sorted(range(1, self.n_z), key=lambda k: (min(k, self.n_z - k), k))

    def row_of(self, d, rows, width):
        f = d * rows // width
        half = self.n_y * width
        return (f % 2 ^ self.x) * half + (f // 2 ^ self.y) * width + d * rows % width


def gather_layer(place, piece):
    rows, width = piece.shape[1:]
    if place.direct:
        found = {0: piece}
        for k in place.far_first():
            found[k] = place.over_z(piece, k)
        pieces, at_rows, at_cols = [], [], []
        for k in [0] + place.far_first():
            for step in range(place.n_y):
                mine = found[k] if step == 0 else place.over_y(found[k], step)
                for other in range(2):
                    pieces.append((place.over_core(mine) if other else mine)[None])
                    d = (place.z - k) % place.n_z * 2 + (place.c ^ other)
                    at_rows.append(place.row_of(d, rows, width))
                    at_cols.append(jnp.int32(step * width))
        return pieces, jnp.stack([jnp.stack(at_rows), jnp.stack(at_cols)]).astype(jnp.int32), found
    spread = lax.all_gather(lax.all_gather(piece, "dp"), "filt")
    spread = spread.reshape((place.n_y, 2) + spread.shape[1:])
    spread = lax.dynamic_index_in_dim(spread, place.x, 1, keepdims=False)
    spread = spread.reshape((place.n_y * place.n_dp,) + piece.shape)
    d = jnp.tile(jnp.arange(place.n_dp, dtype=jnp.int32), place.n_y)
    y = jnp.repeat(jnp.arange(place.n_y, dtype=jnp.int32), place.n_dp)
    table = jnp.stack([place.row_of(d, rows, width), (y ^ place.y) * width]).astype(jnp.int32)
    return [spread], table, None


def sum_table(place, rows, width):
    z = jnp.arange(place.n_z, dtype=jnp.int32)
    z, c = ((place.z + z) % place.n_z, place.c) if place.direct else (z, 0)
    return jnp.stack([place.row_of(z * 2 + c, rows, width), place.row_of(z * 2 + (1 - c), rows, width)]).astype(jnp.int32)


def sum_layer(place, blocks):
    n_y = place.n_y
    near, far = blocks[:n_y], blocks[n_y:]
    if place.direct:
        arrived = {step: place.over_core(far[step]) for step in list(range(1, n_y)) + [0]}
        order = place.far_first()[::-1] + [0]
        both = lambda step, k: near[step][k].astype(F32) + arrived[step][k].astype(F32)
        turned = {}
        for k in order:
            turned[k] = [place.over_y(both(step, k).astype(BF16), step) for step in range(1, n_y)]
        total = None
        for k in order:
            value = both(0, k)
            for term in turned[k]:
                value = value + term.astype(F32)
            if k:
                value = place.over_z(value.astype(BF16), k).astype(F32)
            total = value if total is None else total + value
        return total
    steps = jnp.arange(n_y, dtype=jnp.int32) ^ place.y
    pairs = jnp.stack([jnp.stack(near), jnp.stack(far)], axis=2)
    pairs = jnp.take(pairs, steps, axis=0)
    pairs = pairs.reshape((n_y, place.n_dp) + pairs.shape[3:])
    mine = lax.psum_scatter(pairs, "dp", scatter_dimension=1)
    sides = jnp.arange(2, dtype=jnp.int32).reshape(1, 2, 1, 1, 1)
    mine = jnp.where(sides == place.x, mine[:, None], jnp.zeros((), BF16))
    mine = mine.reshape((place.n_filt,) + mine.shape[2:])
    return lax.psum_scatter(mine, "filt", scatter_dimension=0).astype(F32)


def per_device(
    char_ids,
    word_lengths,
    out_grad,
    highway_owner,
    char_table,
    conv_weight,
    conv_bias,
    highway_weight,
    proj_weight,
    dense_bias,
    table_moment_one,
    table_moment_two,
    conv_moment_one,
    conv_moment_two,
    conv_bias_moment_one,
    conv_bias_moment_two,
    highway_moment_one,
    highway_moment_two,
    highway_average,
    proj_moment_one,
    proj_moment_two,
    bias_moment_one,
    bias_moment_two,
):
    place = Places()
    n_y, n_filt = place.n_y, place.n_filt
    width = conv_weight.shape[1]
    rows, width_full = highway_weight.shape[1:]
    half = width_full // 2
    rows_proj, out_width = proj_weight.shape
    vocab_count = char_table.shape[0]
    words_dev = char_ids.shape[0]
    words_y = words_dev // n_y
    slot_index = unit_slots(highway_owner, SLOTS)

    def block_of(step):
        start = (place.f ^ step) * width
        return lax.dynamic_slice_in_dim(highway_weight, start, width, axis=2).astype(BF16)

    from_owner = [block_of(0)] + [place.over_filt(block_of(step), step) for step in range(1, n_filt)]

    def unit_block(unit):
        chosen = from_owner[0][0]
        for step in range(n_filt):
            for slot in range(SLOTS):
                here = slot_index[unit] == (place.f ^ step) * SLOTS + slot
                chosen = jnp.where(here, from_owner[step][slot], chosen)
        return chosen

    layer_blocks = [jnp.stack([unit_block(2 * layer), unit_block(2 * layer + 1)]) for layer in range(2)]
    gathered = [None, None]
    pieces, table, found = gather_layer(place, layer_blocks[0])
    gathered[0] = (pieces, table)
    second = layer_blocks[1]
    if found is not None:
        second, _ = lax.optimization_barrier((second, found[place.far_first()[-1]]))
    pieces, table, _ = gather_layer(place, second)
    gathered[1] = (pieces, table)

    proj_rows = lax.all_gather(proj_weight.astype(BF16), "dp", axis=0, tiled=True)
    proj_half = jnp.concatenate([proj_rows] + [place.over_y(proj_rows, step) for step in range(1, n_y)], axis=0)
    grad_mate = place.over_x(out_grad)
    mine_first = place.x == 0
    out_grad_y = jnp.concatenate([jnp.where(mine_first, out_grad, grad_mate), jnp.where(mine_first, grad_mate, out_grad)], axis=0)

    bias_float = lax.reduce_precision(dense_bias, 8, 7)

    def half_bias(unit):
        whole_bias = bias_float[unit * width_full : (unit + 1) * width_full].reshape(n_filt, width)
        return jnp.concatenate([lax.dynamic_index_in_dim(whole_bias, 2 * (place.y ^ step) + place.x, 0, keepdims=False) for step in range(n_y)])

    layer_bias = [jnp.stack([half_bias(2 * layer), half_bias(2 * layer + 1)]) for layer in range(2)]

    widths = channel_widths(place.f * width, width, FILTERS)
    offsets = jnp.arange(TAPS, dtype=jnp.int32) // CHAR_DIM
    tap_mask = (offsets[:, None] < widths[None, :]).astype(jnp.float32)
    cblock = min(256, width)
    rank, data, table_t, conv_t, conv_back, width_col, narrow = conv_operands(
        char_ids, word_lengths, char_table, conv_weight, conv_bias, widths, cblock
    )
    feature_rows, lse, sorted_ids = conv_forward(rank, data, table_t, conv_t, width_col, narrow, cblock)
    rank_parts = [lax.dynamic_slice_in_dim(rank, (place.y ^ step) * words_y, words_y, axis=0) for step in range(n_y)]
    placed = {step: place_words(rank_parts[step], feature_rows) for step in list(range(1, n_y)) + [0]}
    own = [placed[0]] + [place.over_y(placed[step], step) for step in range(1, n_y)]
    mate = [place.over_x(part) for part in own]

    x_one, x_one_low, first_zero, gate_zero = highway_forward(gathered[0][1], gathered[0][0], layer_bias[0], own, mate)
    x_one_mate = place.over_x(x_one_low)
    x_two_low, d_first, d_gate, up, sums_one = highway_turn(
        gathered[1][1], gathered[1][0], layer_bias[1], x_one_low, x_one_mate, x_one, out_grad_y, proj_half, width
    )
    targets = sum_table(place, rows, width)
    layer_sums = [None, None]
    leaving = highway_back(1, gathered[1][1], gathered[1][0], d_first, d_gate)
    arrived = place.over_x(leaving)
    blocks = highway_weight_grad(targets, [x_one_low], [x_one_mate], d_first, d_gate, rows, width)
    layer_sums[1] = sum_layer(place, blocks)
    partial = highway_back(0, gathered[1][1], gathered[1][0], d_first, d_gate, up)

    vectors = nn(x_two_low, proj_half)
    vectors_two = vectors.reshape(2, words_y // 2, out_width)
    vectors_away = lax.dynamic_index_in_dim(vectors_two, 1 - place.x, 0, keepdims=False).astype(BF16)
    vectors_here = lax.dynamic_index_in_dim(vectors_two, place.x, 0, keepdims=False)
    word_vectors = vectors_here + place.over_x(vectors_away).astype(F32) + bias_float[UNITS * width_full :]
    proj_part = tn(x_two_low, out_grad_y).reshape(n_y, width, out_width)
    proj_sum = proj_part[0]
    for step in range(1, n_y):
        proj_sum = proj_sum + place.over_y(proj_part[step].astype(BF16), step).astype(F32)
    proj_grad = lax.psum_scatter(proj_sum, "dp", scatter_dimension=0, tiled=True)

    d_first, d_gate, up, sums_zero = highway_slopes(partial, arrived, first_zero, gate_zero, own)
    leaving = highway_back(1, gathered[0][1], gathered[0][0], d_first, d_gate)
    arrived = place.over_x(leaving)
    blocks = highway_weight_grad(targets, own, mate, d_first, d_gate, rows, width)
    layer_sums[0] = sum_layer(place, blocks)
    partial = highway_back(0, gathered[0][1], gathered[0][0], d_first, d_gate, up)
    feature_grad = [(partial[:, step * width : (step + 1) * width] + arrived[:, step * width : (step + 1) * width].astype(F32)).astype(BF16) for step in range(n_y)]
    returned = [feature_grad[0]] + [place.over_y(feature_grad[step], step) for step in range(1, n_y)]

    conv_sums, table_sums = conv_backward(
        rank_parts, sorted_ids, table_t, conv_t, conv_back, width_col, narrow, lse, returned, cblock
    )
    table_local = (table_sums[:CHAR_DIM] + table_sums[CHAR_DIM:]).T[:vocab_count]
    conv_sums = lax.psum(conv_sums, "dp")
    conv_grad, conv_bias_grad = conv_sums[:, :TAPS].T * tap_mask, conv_sums[:, TAPS]

    home = jnp.arange(n_filt, dtype=jnp.int32)

    def natural(values):
        parts = values.reshape(n_y, 1, width)
        out = jnp.zeros((n_filt, width), F32)
        for step in range(n_y):
            out = jnp.where((home == 2 * (place.y ^ step) + place.x)[:, None], parts[step], out)
        return out.reshape(-1)

    bias_local = jnp.concatenate(
        [natural(sums[unit]) for sums in (sums_zero, sums_one) for unit in range(2)] + [jnp.sum(out_grad, axis=0, dtype=F32)]
    )
    table_grad, bias_grad = lax.psum((table_local, bias_local), ("filt", "dp"))

    units = [layer_sums[unit // 2][unit % 2].astype(BF16) for unit in range(UNITS)]

    def for_owner(step):
        slots = []
        for slot in range(SLOTS):
            value = jnp.zeros_like(units[0])
            for unit in range(UNITS):
                value = jnp.where(slot_index[unit] == (place.f ^ step) * SLOTS + slot, units[unit], value)
            slots.append(value)
        return jnp.stack(slots)

    slot_grads = [for_owner(0)] + [place.over_filt(for_owner(step), step) for step in range(1, n_filt)]
    columns = place.f ^ jnp.arange(n_filt, dtype=jnp.int32)
    highway_grad, highway_second, highway_new, highway_average_new = owner_update(
        columns, jnp.stack(slot_grads), highway_weight, highway_moment_one, highway_moment_two, highway_average
    )
    table_second, table_new = adam_update(
        char_table, table_grad, table_moment_one, table_moment_two, 1.0
    )
    conv_second, conv_new = adam_update(
        conv_weight, conv_grad, conv_moment_one, conv_moment_two, 0.1
    )
    conv_bias_second, conv_bias_new = adam_update(
        conv_bias, conv_bias_grad, conv_bias_moment_one, conv_bias_moment_two, 0.3
    )
    proj_second, proj_new = adam_update(
        proj_weight, proj_grad, proj_moment_one, proj_moment_two, 0.02
    )
    bias_second, bias_new = adam_update(
        dense_bias, bias_grad, bias_moment_one, bias_moment_two, 0.3
    )
    return (
        word_vectors,
        table_grad,
        table_second,
        table_new,
        conv_grad,
        conv_second,
        conv_new,
        conv_bias_grad,
        conv_bias_second,
        conv_bias_new,
        highway_grad,
        highway_second,
        highway_new,
        highway_average_new,
        proj_grad,
        proj_second,
        proj_new,
        bias_grad,
        bias_second,
        bias_new,
    )


def solution(mesh):
    return jax.shard_map(
        per_device,
        mesh=mesh,
        in_specs=(
            P("dp", None),
            P("dp"),
            P(("dp", "filt"), None),
            P(),
            P(),
            P(None, "filt"),
            P("filt"),
            P("filt", "dp", None),
            P(("filt", "dp"), None),
            P(),
            P(),
            P(),
            P(None, "filt"),
            P(None, "filt"),
            P("filt"),
            P("filt"),
            P("filt", "dp", None),
            P("filt", "dp", None),
            P("filt", "dp", None),
            P(("filt", "dp"), None),
            P(("filt", "dp"), None),
            P(),
            P(),
        ),
        out_specs=(
            P(("dp", "filt"), None),
            P(),
            P(),
            P(),
            P(None, "filt"),
            P(None, "filt"),
            P(None, "filt"),
            P("filt"),
            P("filt"),
            P("filt"),
            P("filt", "dp", None),
            P("filt", "dp", None),
            P("filt", "dp", None),
            P("filt", "dp", None),
            P(("filt", "dp"), None),
            P(("filt", "dp"), None),
            P(("filt", "dp"), None),
            P(),
            P(),
            P(),
        ),
        check_vma=False,
    )
```

time: 2130 us -> 758 us (0.36)
  waiting for transfers between devices: 786 us -> 159 us
  matrix products: 541 us -> 8.98 us
  Pallas kernels: 0 us -> 324 us
  other arithmetic: 360 us -> 50.6 us
  local copies, waits for them, and re-layouts: 280 us -> 26.2 us
  starting transfers between devices: 17.8 us -> 83 us
  blocking collectives: 85.1 us -> 61.2 us
  loops' own time: 22.1 us -> 0 us
    reduce_scatter x2 -> x1, waiting for transfers between devices: 614 us -> 0.01 us  [per_device(): lax.psum_scatter(proj_sum, 'dp', scatter_dimension=0, tiled=True)]
    dot_general x37 -> x2, matrix products: 541 us -> 8.98 us  [the longest x1 5.53 us: nn(): lax.dot_general(a, b, (((1,), (0,)), ((), ())), preferred_element_type=F32)]
    pallas_call x0 -> x14, Pallas kernels: none -> 324 us  [the longest x1 127 us: conv_backward(): pl.pallas_call(functools.partial(conv_backward_kernel, cblock, len(ranks)...]
    reduce_sum x15 -> x2, other arithmetic: 261 us -> 3.09 us  [the longest x1 1.8 us: word_order(): jnp.sum((key[None, :] > key[:, None]).astype(jnp.int32), axis=1, keepdims...]
    ppermute x0 -> x65, waiting for transfers between devices: none -> 154 us  [the longest x33 111 us: over_filt(): lax.ppermute(value, 'filt', [(i, i ^ step) for i in range(self.n_filt)])]
    psum x1, waiting for transfers between devices: 102 us -> 4.9 us  [per_device(): conv_sums = lax.psum(conv_sums, 'dp')]
    ppermute x0 -> x65, starting transfers between devices: none -> 82.9 us  [the longest x12 39.8 us: over_z(): return lax.ppermute(value, 'dp', pairs)]
    reshape x18 -> x4, local copies, waits for them, and re-layouts: 66 us -> 2.62 us  [half_bias(): bias_float[unit * width_full:(unit + 1) * width_full].reshape(n_filt, width)]
  transfers between devices with their start and end apart: 11 -> 67, of which waited for: 4 -> 18; matrix products, arithmetic and copies ran while one was open for 45% -> 9% of each run, Pallas kernels for 0% -> 38%
where the time goes in v1:
time: 758 us; the launch traced here: 748 us
  Pallas kernels  324 us (43%)
  waiting for transfers between devices  159 us (21%)
  starting transfers between devices  83 us (11%)
  blocking collectives  61.2 us (8%)
  other arithmetic  50.6 us (7%)
  between operations  35 us (5%)
  local copies, waits for them, and re-layouts  26.2 us (3%)
  matrix products  8.98 us (1%)
    pallas_call x1, Pallas kernels, conv_backward(): pl.pallas_call(functools.partial(conv_backward_kernel, cblock, len(ranks)...  127 us
    ppermute x33, waiting for transfers between devices, over_filt(): lax.ppermute(value, 'filt', [(i, i ^ step) for i in range(self.n_filt)])  111 us
    pallas_call x1, Pallas kernels, conv_forward(): pl.pallas_call(functools.partial(conv_forward_kernel, cblock), grid=(word...  50.1 us
    ppermute x12, waiting for transfers between devices, over_z(): return lax.ppermute(value, 'dp', pairs)  43.1 us
    pallas_call x4, Pallas kernels, highway_back(): pl.pallas_call(functools.partial(back_kernel, half, len(pieces), up is no...  42.3 us
    psum x1, blocking collectives, per_device(): table_grad, bias_grad = lax.psum((table_local, bias_local), ('filt', 'dp'))  42.2 us
    ppermute x12, starting transfers between devices, over_z(): return lax.ppermute(value, 'dp', pairs)  39.8 us
    ppermute x33, starting transfers between devices, over_filt(): lax.ppermute(value, 'filt', [(i, i ^ step) for i in range(self.n_filt)])  39.4 us
  transfers between devices with their start and end apart: 67, of which 18 were waited for; matrix products, arithmetic and copies ran while one was open for 9% of the time, Pallas kernels for 38%

profile of v1, /device:TPU:0, one launch (start us, length us, event | category | flops | bytes accessed | tf_op | source)
XLA Modules:
  0.0 748.4 jit_solution(5556931474000917477)
XLA Ops:
  7.3 3.5 dynamic-slice_convert_fusion.4
  10.8 3.9 collective-permute-start.3
  24.6 1.8 convert_reduce_fusion
  29.5 8.8 %collective-permute-done.5 = bf16[2,256,512]{2,1,0:T(8,128)(2,1)S(1)} collective-permute-done((bf16[2,256,512]{2,1,0:T(8,128)(2,1)}, bf16[2,256,512]{2,1,0:T(8,128)(2,1)S(1)}, u32[]{:S(2)}, u32[]{:S(2)}) %collective-permute-start.5) | collective-permute-done | bytes 524320 | tf_op jit(solution)/shard_map/ppermute | solution.py:640
  40.3 3.6 collective-permute-start.13
  45.6 50.1 %conv_forward.1 = (bf16[512,2048]{1,0:T(8,128)(2,1)S(1)}, f32[512,2048]{1,0:T(8,128)}, f32[64,2048]{1,0:T(8,128)S(1)}) custom-call(s32[2]{0:T(128)S(1)} %slice.338.narrow_ref, s32[2048,1]{1,0:T(8,128)S(1)} %copy-done, bf16[64,2048]{1,0:T(8,128)(2,1)S(1)} %fusion.24.data_ref, f32[16,384]{1,0:T(8,128)S(1)} %pad.14.table_ref, ...), custom_call_target="tpu_custom_call" | custom-call | tf_op jit(solution)/shard_map/conv_forward/pallas_call | solution.py:136
  95.7 3.7 place_words.3
  99.7 3.8 place_words.2.refs_0_
  103.6 1.9 collective-permute-start.17
  105.5 2.0 collective-permute-start.15
  121.9 8.5 %collective-permute-done.17 = bf16[2,256,512]{2,1,0:T(8,128)(2,1)} collective-permute-done((bf16[2,256,512]{2,1,0:T(8,128)(2,1)}, bf16[2,256,512]{2,1,0:T(8,128)(2,1)}, u32[]{:S(2)}, u32[]{:S(2)}) %collective-permute-start.17) | collective-permute-done | bytes 524320 | tf_op jit(solution)/shard_map/ppermute | solution.py:653
  130.4 2.2 collective-permute-start.11
  133.1 3.4 collective-permute-done.15
  138.3 19.1 %all_gather.3 = bf16[512,768]{1,0:T(8,128)(2,1)S(1)} all-gather(bf16[64,768]{1,0:T(8,128)(2,1)} %convert_element_type.446), channel_id=1, replica_groups=mesh['filt'=4,'dp'=8] {'dp'}, dimensions={0}, use_global_device_ids=true | all-gather | bytes 884736 | tf_op jit(solution)/shard_map/all_gather | solution.py:786
  161.6 2.0 collective-permute-start.22
  164.3 3.0 collective-permute-start.31
  168.4 18.3 %highway_forward.1 = (f32[1024,1024]{1,0:T(8,128)}, bf16[1024,1024]{1,0:T(8,128)(2,1)}, f32[1024,1024]{1,0:T(8,128)}, f32[1024,1024]{1,0:T(8,128)}) custom-call(s32[2,16]{1,0:T(2,128)} %pad_add_fusion.table_ref, f32[2,1024]{1,0:T(2,128)} %pad_maximum_fusion.8.bias_ref, bf16[1024,512]{1,0:T(8,128)(2,1)} %place_words.2.refs_0_, ...), custom_call_target="tpu_custom_call" | custom-call | flops 8589934592 | bytes 14680064 | tf_op jit(solution)/shard_map/highway_forward/pallas_call | solution.py:507
  189.3 2.2 collective-permute-done.35
  193.0 8.7 %collective-permute-done.27 = bf16[2,256,512]{2,1,0:T(8,128)(2,1)} collective-permute-done((bf16[2,256,512]{2,1,0:T(8,128)(2,1)S(1)}, bf16[2,256,512]{2,1,0:T(8,128)(2,1)}, u32[]{:S(2)}, u32[]{:S(2)}) %collective-permute-start.27) | collective-permute-done | bytes 524320 | tf_op jit(solution)/shard_map/ppermute | solution.py:653
  203.4 1.8 collective-permute-start.33
  205.5 8.4 %collective-permute-done.37 = bf16[2,256,512]{2,1,0:T(8,128)(2,1)S(1)} collective-permute-done((bf16[2,256,512]{2,1,0:T(8,128)(2,1)S(1)}, bf16[2,256,512]{2,1,0:T(8,128)(2,1)S(1)}, u32[]{:S(2)}, u32[]{:S(2)}) %collective-permute-start.37) | collective-permute-done | bytes 524320 | tf_op jit(solution)/shard_map/ppermute | solution.py:640
  223.4 1.9 collective-permute-done.33
  225.8 9.2 %collective-permute-done.29 = bf16[2,256,512]{2,1,0:T(8,128)(2,1)} collective-permute-done((bf16[2,256,512]{2,1,0:T(8,128)(2,1)}, bf16[2,256,512]{2,1,0:T(8,128)(2,1)}, u32[]{:S(2)}, u32[]{:S(2)}) %collective-permute-start.29) | collective-permute-done | bytes 524320 | tf_op jit(solution)/shard_map/ppermute | solution.py:640
  241.7 22.5 %highway_turn.1 = (bf16[1024,1024]{1,0:T(8,128)(2,1)}, bf16[1024,1024]{1,0:T(8,128)(2,1)}, bf16[1024,1024]{1,0:T(8,128)(2,1)}, f32[1024,1024]{1,0:T(8,128)}, f32[2,1024]{1,0:T(2,128)}) custom-call(s32[2,16]{1,0:T(2,128)} %pad_add_fusion.table_ref, f32[2,1024]{1,0:T(2,128)} %pad_maximum_fusion.7.bias_ref, bf16[1024,1024]{1,0:T(8,128)(2,1)} %get-tuple-element.52.own.refs_0_, ...), custom_call_target="tpu_custom_call" | custom-call | flops 8589934592 | bytes 20971520 | tf_op jit(solution)/shard_map/highway_turn/pallas_call | solution.py:524
  264.2 3.5 fusion.58
  267.7 1.8 collective-permute-start.64
  269.5 15.0 %highway_weight_grad.2 = (bf16[4,2,256,512]{3,2,1,0:T(8,128)(2,1)}, bf16[4,2,256,512]{3,2,1,0:T(8,128)(2,1)}, bf16[4,2,256,512]{3,2,1,0:T(8,128)(2,1)}, bf16[4,2,256,512]{3,2,1,0:T(8,128)(2,1)}) custom-call(s32[2,4]{1,0:T(2,128)} %pad_add_fusion.1.table_ref, bf16[1024,1024]{1,0:T(8,128)(2,1)} %get-tuple-element.52.own.refs_0_, ...), custom_call_target="tpu_custom_call" | custom-call | flops 8589934592 | bytes 12582912 | tf_op jit(solution)/shard_map/highway_weight_grad/pallas_call | solution.py:578
  284.5 9.8 %highway_back.5 = bf16[1024,1024]{1,0:T(8,128)(2,1)} custom-call(s32[2,16]{1,0:T(2,128)} %pad_add_fusion.table_ref, bf16[1024,1024]{1,0:T(8,128)(2,1)} %get-tuple-element.58.d_first.refs_2_, bf16[1024,1024]{1,0:T(8,128)(2,1)} %get-tuple-element.59.d_gate.refs_3_, bf16[1,2,256,512]{3,2,1,0:T(8,128)(2,1)} %bitcast.163, bf16[1,2,256,512]{3,2,1,0:T(8,128)(2,1)} %bitcast.199, ...), custom_call_target="tpu_custom_call" | custom-call | flops 4294967296 | bytes 12582912 | tf_op jit(solution)/shard_map/highway_back/pallas_call | solution.py:559
  295.7 5.5 fusion.70
  301.2 2.4 fusion.13
  304.9 11.0 %highway_back.4.partial = f32[1024,1024]{1,0:T(8,128)} custom-call(s32[2,16]{1,0:T(2,128)} %pad_add_fusion.table_ref, bf16[1024,1024]{1,0:T(8,128)(2,1)} %get-tuple-element.58.d_first.refs_2_, bf16[1024,1024]{1,0:T(8,128)(2,1)} %get-tuple-element.59.d_gate.refs_3_, f32[1024,1024]{1,0:T(8,128)} %get-tuple-element.60.refs_0_, ...), custom_call_target="tpu_custom_call" | custom-call | flops 4294967296 | bytes 12582912 | tf_op jit(solution)/shard_map/highway_back/pallas_call | solution.py:559
  317.4 42.2 %collective-permute-done.39 = bf16[512,768]{1,0:T(8,128)(2,1)} collective-permute-done((bf16[512,768]{1,0:T(8,128)(2,1)}, bf16[512,768]{1,0:T(8,128)(2,1)}, u32[]{:S(2)}, u32[]{:S(2)}) %collective-permute-start.39) | collective-permute-done | bytes 786464 | tf_op jit(solution)/shard_map/ppermute | solution.py:640
  359.6 3.0 fusion.2
  362.5 3.2 fusion.14
  367.8 10.3 %highway_slopes.1 = (bf16[1024,1024]{1,0:T(8,128)(2,1)}, bf16[1024,1024]{1,0:T(8,128)(2,1)}, f32[1024,1024]{1,0:T(8,128)}, f32[2,1024]{1,0:T(2,128)}) custom-call(f32[1024,1024]{1,0:T(8,128)} %highway_back.4.partial, bf16[1024,1024]{1,0:T(8,128)(2,1)} %collective-permute-done.40.arrived, f32[1024,1024]{1,0:T(8,128)} %get-tuple-element.61.first_ref, ...), custom_call_target="tpu_custom_call" | custom-call | bytes 18874368 | tf_op jit(solution)/shard_map/highway_slopes/pallas_call | solution.py:542
  378.1 9.8 %highway_back.7 = bf16[1024,1024]{1,0:T(8,128)(2,1)} custom-call(s32[2,16]{1,0:T(2,128)} %pad_add_fusion.table_ref, bf16[1024,1024]{1,0:T(8,128)(2,1)} %get-tuple-element.63.d_first.refs_4_, bf16[1024,1024]{1,0:T(8,128)(2,1)} %get-tuple-element.64.d_gate.refs_5_, bf16[1,2,256,512]{3,2,1,0:T(8,128)(2,1)} %get-tuple-element.126.refs_4_.refs_1_.refs_0_, ...), custom_call_target="tpu_custom_call" | custom-call | flops 4294967296 | bytes 12582912 | tf_op jit(solution)/shard_map/highway_back/pallas_call | solution.py:559
  389.3 15.0 %highway_weight_grad.3 = (bf16[4,2,256,512]{3,2,1,0:T(8,128)(2,1)}, bf16[4,2,256,512]{3,2,1,0:T(8,128)(2,1)}, bf16[4,2,256,512]{3,2,1,0:T(8,128)(2,1)}, bf16[4,2,256,512]{3,2,1,0:T(8,128)(2,1)}) custom-call(s32[2,4]{1,0:T(2,128)} %pad_add_fusion.1.table_ref, bf16[1024,512]{1,0:T(8,128)(2,1)} %place_words.2.refs_0_, ...), custom_call_target="tpu_custom_call" | custom-call | flops 8589934592 | bytes 12582912 | tf_op jit(solution)/shard_map/highway_weight_grad/pallas_call | solution.py:578
  406.2 11.8 %highway_back.6 = f32[1024,1024]{1,0:T(8,128)} custom-call(s32[2,16]{1,0:T(2,128)} %pad_add_fusion.table_ref, bf16[1024,1024]{1,0:T(8,128)(2,1)} %get-tuple-element.63.d_first.refs_4_, bf16[1024,1024]{1,0:T(8,128)(2,1)} %get-tuple-element.64.d_gate.refs_5_, f32[1024,1024]{1,0:T(8,128)} %get-tuple-element.65.refs_0_, ...), custom_call_target="tpu_custom_call" | custom-call | flops 4294967296 | bytes 12582912 | tf_op jit(solution)/shard_map/highway_back/pallas_call | solution.py:559
  418.0 1.8 collective-permute-start.51
  419.9 2.7 fusion.12
  422.6 11.4 %collective-permute-start.46 = (bf16[2,256,512]{2,1,0:T(8,128)(2,1)S(1)}, bf16[2,256,512]{2,1,0:T(8,128)(2,1)S(1)}, u32[]{:S(2)}, u32[]{:S(2)}) collective-permute-start(bf16[2,256,512]{2,1,0:T(8,128)(2,1)S(1)} %get-tuple-element.97), channel_id=1, source_target_pairs={{0,4},{1,5},{2,6},{3,7},{4,0},{5,1},{6,2},{7,3},{8,12},{9,13},{10,... | collective-permute-start | bytes 1572872 | tf_op jit(solution)/shard_map/ppermute | solution.py:653
  434.0 10.7 %collective-permute-start.50 = (bf16[2,256,512]{2,1,0:T(8,128)(2,1)S(1)}, bf16[2,256,512]{2,1,0:T(8,128)(2,1)S(1)}, u32[]{:S(2)}, u32[]{:S(2)}) collective-permute-start(bf16[2,256,512]{2,1,0:T(8,128)(2,1)S(1)} %get-tuple-element.98), channel_id=1, source_target_pairs={{0,2},{1,3},{2,4},{3,5},{4,6},{5,7},{6,0},{7,1},{8,10},{9,11},{10,... | collective-permute-start | bytes 1572872 | tf_op jit(solution)/shard_map/ppermute | solution.py:653
  445.0 3.4 fusion
  451.9 17.4 %collective-permute-done.46 = bf16[2,256,512]{2,1,0:T(8,128)(2,1)S(1)} collective-permute-done((bf16[2,256,512]{2,1,0:T(8,128)(2,1)S(1)}, bf16[2,256,512]{2,1,0:T(8,128)(2,1)S(1)}, u32[]{:S(2)}, u32[]{:S(2)}) %collective-permute-start.46) | collective-permute-done | bytes 524320 | tf_op jit(solution)/shard_map/ppermute | solution.py:653
  471.3 6.3 collective-permute-done.48
  478.8 2.4 fusion.9
  481.2 2.1 multiply_subtract_fusion.1
  484.2 1.8 collective-permute-done.54
  486.1 11.2 %collective-permute-done.58 = bf16[2,256,512]{2,1,0:T(8,128)(2,1)} collective-permute-done((bf16[2,256,512]{2,1,0:T(8,128)(2,1)}, bf16[2,256,512]{2,1,0:T(8,128)(2,1)}, u32[]{:S(2)}, u32[]{:S(2)}) %collective-permute-start.58) | collective-permute-done | bytes 524320 | tf_op jit(solution)/shard_map/ppermute | solution.py:640
  497.3 11.2 %collective-permute-done.56 = bf16[2,256,512]{2,1,0:T(8,128)(2,1)} collective-permute-done((bf16[2,256,512]{2,1,0:T(8,128)(2,1)}, bf16[2,256,512]{2,1,0:T(8,128)(2,1)}, u32[]{:S(2)}, u32[]{:S(2)}) %collective-permute-start.56) | collective-permute-done | bytes 524320 | tf_op jit(solution)/shard_map/ppermute | solution.py:640
  508.5 4.0 fusion.7
  512.5 3.5 collective-permute-start.55
  516.6 3.2 collective-permute-start.57
  519.9 126.8 %conv_backward.1 = (f32[512,128]{1,0:T(8,128)S(1)}, f32[32,384]{1,0:T(8,128)S(1)}) custom-call(s32[2]{0:T(128)S(1)} %slice.338.narrow_ref, f32[64,2048]{1,0:T(8,128)S(1)} %copy-done.3, f32[16,384]{1,0:T(8,128)S(1)} %copy-done.6, bf16[512,128]{1,0:T(8,128)(2,1)S(1)} %copy.64.conv_ref, bf16[128,512]{1,0:T(8,128)(2,1)S(1)} %copy-done.1, ...), custom_call_target="tpu_custom_call" | custom-call | tf_op jit(solution)/shard_map/conv_backward/pallas_call | solution.py:234
  647.4 1.8 copy.70
  649.2 42.2 %all-reduce.3 = (f32[262,16]{0,1:T(8,128)S(1)}, f32[8960]{0:T(1024)S(1)}) all-reduce(f32[262,16]{0,1:T(8,128)S(1)} %bitcast.219, f32[8960]{0:T(1024)} %copy-done.53), channel_id=1, replica_groups=mesh['filt'=4,'dp'=8] {'filt','dp'}, use_global_device_ids=true, to_apply=%region_2.3 | all-reduce | flops 13152 | bytes 105216 | tf_op jit(solution)/shard_map/psum | solution.py:865
  694.3 2.3 fusion.4
  697.1 2.3 collective-permute-start.61
  701.2 4.9 all-reduce.6.cloned.1.call-done
  707.4 2.2 multiply_subtract_fusion
  709.7 2.6 collective-permute-done.61
  712.2 9.9 %collective-permute-done.62 = bf16[2,256,512]{2,1,0:T(8,128)(2,1)S(1)} collective-permute-done((bf16[2,256,512]{2,1,0:T(8,128)(2,1)S(1)}, bf16[2,256,512]{2,1,0:T(8,128)(2,1)S(1)}, u32[]{:S(2)}, u32[]{:S(2)}) %collective-permute-start.62) | collective-permute-done | bytes 524320 | tf_op jit(solution)/shard_map/ppermute | solution.py:640
  722.1 2.6 pad_maximum_fusion.grad_in
  724.8 16.3 %owner_update.1 = (f32[2,256,2048]{2,1,0:T(8,128)}, f32[2,256,2048]{2,1,0:T(8,128)}, f32[2,256,2048]{2,1,0:T(8,128)}, f32[2,256,2048]{2,1,0:T(8,128)}) custom-call(s32[4]{0:T(128)} %iota_xor_fusion.at_ref, bf16[4,2,256,512]{3,2,1,0:T(8,128)(2,1)} %pad_maximum_fusion.grad_in, f32[2,256,2048]{2,1,0:T(8,128)} %weight.1, f32[2,256,2048]{2,1,0:T(8,128)} %one.1, ...), custom_call_target="tpu_custom_call" | custom-call | bytes 33554432 | tf_op jit(solution)/shard_map/owner_update/pallas_call | solution.py:615
  (349 shorter events, 67.8 us)
Async XLA Ops:
  7.2 474.1 %reduce-scatter.2.cloned.1.call-start = ((), (), s32[]{:S(2)}) async-start(), calls=%async_computation.2 | async-start | bytes 1769472 | tf_op jit(solution)/shard_map/reduce_scatter | solution.py:835
  10.8 18.7 %collective-permute-start.3 = (bf16[2,256,512]{2,1,0:T(8,128)(2,1)}, bf16[2,256,512]{2,1,0:T(8,128)(2,1)S(1)}, u32[]{:S(2)}, u32[]{:S(2)}) collective-permute-start(bf16[2,256,512]{2,1,0:T(8,128)(2,1)} %get-tuple-element.111), channel_id=1, source_target_pairs={{0,24},{8,16},{16,8},{24,0},{1,25},{9,17},{17,9},{25,1},{2,26},{10... | collective-permute-start | bytes 1572872 | tf_op jit(solution)/shard_map/ppermute | solution.py:640
  14.7 23.7 %collective-permute-start.5 = (bf16[2,256,512]{2,1,0:T(8,128)(2,1)}, bf16[2,256,512]{2,1,0:T(8,128)(2,1)S(1)}, u32[]{:S(2)}, u32[]{:S(2)}) collective-permute-start(bf16[2,256,512]{2,1,0:T(8,128)(2,1)} %get-tuple-element.112), channel_id=1, source_target_pairs={{0,8},{8,0},{16,24},{24,16},{1,9},{9,1},{17,25},{25,17},{2,10},{10... | collective-permute-start | bytes 1572872 | tf_op jit(solution)/shard_map/ppermute | solution.py:640
  15.2 23.1 %collective-permute-start.4 = (bf16[2,256,512]{2,1,0:T(8,128)(2,1)}, bf16[2,256,512]{2,1,0:T(8,128)(2,1)S(1)}, u32[]{:S(2)}, u32[]{:S(2)}) collective-permute-start(bf16[2,256,512]{2,1,0:T(8,128)(2,1)} %get-tuple-element.113), channel_id=1, source_target_pairs={{0,16},{8,24},{16,0},{24,8},{1,17},{9,25},{17,1},{25,9},{2,18},{10... | collective-permute-start | bytes 1572872 | tf_op jit(solution)/shard_map/ppermute | solution.py:640
  40.3 63.1 %collective-permute-start.13 = (bf16[2,256,512]{2,1,0:T(8,128)(2,1)}, bf16[2,256,512]{2,1,0:T(8,128)(2,1)}, u32[]{:S(2)}, u32[]{:S(2)}) collective-permute-start(bf16[2,256,512]{2,1,0:T(8,128)(2,1)} %get-tuple-element.125), channel_id=1, source_target_pairs={{0,6},{1,7},{2,0},{3,1},{4,2},{5,3},{6,4},{7,5},{8,14},{9,15},{10,... | collective-permute-start | bytes 1572872 | tf_op jit(solution)/shard_map/ppermute | solution.py:653
  44.0 59.6 %collective-permute-start.9 = (bf16[2,256,512]{2,1,0:T(8,128)(2,1)}, bf16[2,256,512]{2,1,0:T(8,128)(2,1)}, u32[]{:S(2)}, u32[]{:S(2)}) collective-permute-start(bf16[2,256,512]{2,1,0:T(8,128)(2,1)} %get-tuple-element.125), channel_id=1, source_target_pairs={{0,2},{1,3},{2,4},{3,5},{4,6},{5,7},{6,0},{7,1},{8,10},{9,11},{10,... | collective-permute-start | bytes 1572872 | tf_op jit(solution)/shard_map/ppermute | solution.py:653
  44.1 61.5 %collective-permute-start.7 = (bf16[2,256,512]{2,1,0:T(8,128)(2,1)}, bf16[2,256,512]{2,1,0:T(8,128)(2,1)}, u32[]{:S(2)}, u32[]{:S(2)}) collective-permute-start(bf16[2,256,512]{2,1,0:T(8,128)(2,1)} %get-tuple-element.125), channel_id=1, source_target_pairs={{0,16},{8,24},{16,0},{24,8},{1,17},{9,25},{17,1},{25,9},{2,18},{10... | collective-permute-start | bytes 1572872 | tf_op jit(solution)/shard_map/ppermute | solution.py:640
  45.4 62.2 %collective-permute-start.6 = (bf16[2,256,512]{2,1,0:T(8,128)(2,1)}, bf16[2,256,512]{2,1,0:T(8,128)(2,1)}, u32[]{:S(2)}, u32[]{:S(2)}) collective-permute-start(bf16[2,256,512]{2,1,0:T(8,128)(2,1)} %get-tuple-element.125), channel_id=1, source_target_pairs={{0,1},{1,0},{2,3},{3,2},{4,5},{5,4},{6,7},{7,6},{8,9},{9,8},{10,11... | collective-permute-start | bytes 1572872 | tf_op jit(solution)/shard_map/ppermute | solution.py:649
  99.4 33.2 %collective-permute-start = (bf16[1024,512]{1,0:T(8,128)(2,1)}, bf16[1024,512]{1,0:T(8,128)(2,1)}, u32[]{:S(2)}, u32[]{:S(2)}) collective-permute-start(bf16[1024,512]{1,0:T(8,128)(2,1)} %place_words.3), channel_id=1, source_target_pairs={{0,16},{8,24},{16,0},{24,8},{1,17},{9,25},{17,1},{25,9},{2,18},{10... | collective-permute-start | bytes 3145736 | tf_op jit(solution)/shard_map/ppermute | solution.py:640
  103.4 29.2 %collective-permute-start.1 = (bf16[1024,512]{1,0:T(8,128)(2,1)}, bf16[1024,512]{1,0:T(8,128)(2,1)}, u32[]{:S(2)}, u32[]{:S(2)}) collective-permute-start(bf16[1024,512]{1,0:T(8,128)(2,1)} %place_words.2.refs_0_), channel_id=1, source_target_pairs={{0,8},{8,0},{16,24},{24,16},{1,9},{9,1},{17,25},{25,17},{2,10},{10... | collective-permute-start | bytes 3145736 | tf_op jit(solution)/shard_map/ppermute | solution.py:640
  103.6 26.8 %collective-permute-start.17 = (bf16[2,256,512]{2,1,0:T(8,128)(2,1)}, bf16[2,256,512]{2,1,0:T(8,128)(2,1)}, u32[]{:S(2)}, u32[]{:S(2)}) collective-permute-start(bf16[2,256,512]{2,1,0:T(8,128)(2,1)} %get-tuple-element.125), channel_id=1, source_target_pairs={{0,4},{1,5},{2,6},{3,7},{4,0},{5,1},{6,2},{7,3},{8,12},{9,13},{10,... | collective-permute-start | bytes 1572872 | tf_op jit(solution)/shard_map/ppermute | solution.py:653
  105.5 31.0 %collective-permute-start.15 = (bf16[2,256,512]{2,1,0:T(8,128)(2,1)}, bf16[2,256,512]{2,1,0:T(8,128)(2,1)}, u32[]{:S(2)}, u32[]{:S(2)}) collective-permute-start(bf16[2,256,512]{2,1,0:T(8,128)(2,1)} %collective-permute-done.13), channel_id=1, source_target_pairs={{0,16},{8,24},{16,0},{24,8},{1,17},{9,25},{17,1},{25,9},{2,18},{10... | collective-permute-start | bytes 1572872 | tf_op jit(solution)/shard_map/ppermute | solution.py:640
  107.5 29.6 %collective-permute-start.14 = (bf16[2,256,512]{2,1,0:T(8,128)(2,1)}, bf16[2,256,512]{2,1,0:T(8,128)(2,1)}, u32[]{:S(2)}, u32[]{:S(2)}) collective-permute-start(bf16[2,256,512]{2,1,0:T(8,128)(2,1)} %collective-permute-done.13), channel_id=1, source_target_pairs={{0,1},{1,0},{2,3},{3,2},{4,5},{5,4},{6,7},{7,6},{8,9},{9,8},{10,11... | collective-permute-start | bytes 1572872 | tf_op jit(solution)/shard_map/ppermute | solution.py:649
  130.4 27.0 %collective-permute-start.11 = (bf16[2,256,512]{2,1,0:T(8,128)(2,1)}, bf16[2,256,512]{2,1,0:T(8,128)(2,1)S(1)}, u32[]{:S(2)}, u32[]{:S(2)}) collective-permute-start(bf16[2,256,512]{2,1,0:T(8,128)(2,1)} %collective-permute-done.9), channel_id=1, source_target_pairs={{0,16},{8,24},{16,0},{24,8},{1,17},{9,25},{17,1},{25,9},{2,18},{10... | collective-permute-start | bytes 1572872 | tf_op jit(solution)/shard_map/ppermute | solution.py:640
  132.6 25.2 %collective-permute-start.10 = (bf16[2,256,512]{2,1,0:T(8,128)(2,1)}, bf16[2,256,512]{2,1,0:T(8,128)(2,1)S(1)}, u32[]{:S(2)}, u32[]{:S(2)}) collective-permute-start(bf16[2,256,512]{2,1,0:T(8,128)(2,1)} %collective-permute-done.9), channel_id=1, source_target_pairs={{0,1},{1,0},{2,3},{3,2},{4,5},{5,4},{6,7},{7,6},{8,9},{9,8},{10,11... | collective-permute-start | bytes 1572872 | tf_op jit(solution)/shard_map/ppermute | solution.py:649
  132.6 25.4 %collective-permute-start.8 = (bf16[2,256,512]{2,1,0:T(8,128)(2,1)}, bf16[2,256,512]{2,1,0:T(8,128)(2,1)S(1)}, u32[]{:S(2)}, u32[]{:S(2)}) collective-permute-start(bf16[2,256,512]{2,1,0:T(8,128)(2,1)} %collective-permute-done.7), channel_id=1, source_target_pairs={{0,1},{1,0},{2,3},{3,2},{4,5},{5,4},{6,7},{7,6},{8,9},{9,8},{10,11... | collective-permute-start | bytes 1572872 | tf_op jit(solution)/shard_map/ppermute | solution.py:649
  136.5 22.4 %collective-permute-start.19 = (bf16[2,256,512]{2,1,0:T(8,128)(2,1)}, bf16[2,256,512]{2,1,0:T(8,128)(2,1)S(1)}, u32[]{:S(2)}, u32[]{:S(2)}) collective-permute-start(bf16[2,256,512]{2,1,0:T(8,128)(2,1)} %collective-permute-done.17), channel_id=1, source_target_pairs={{0,16},{8,24},{16,0},{24,8},{1,17},{9,25},{17,1},{25,9},{2,18},{10... | collective-permute-start | bytes 1572872 | tf_op jit(solution)/shard_map/ppermute | solution.py:640
  137.1 30.3 %collective-permute-start.2 = (bf16[1024,512]{1,0:T(8,128)(2,1)}, bf16[1024,512]{1,0:T(8,128)(2,1)S(1)}, u32[]{:S(2)}, u32[]{:S(2)}) collective-permute-start(bf16[1024,512]{1,0:T(8,128)(2,1)} %collective-permute-done.refs_1_), channel_id=1, source_target_pairs={{0,8},{8,0},{16,24},{24,16},{1,9},{9,1},{17,25},{25,17},{2,10},{10... | collective-permute-start | bytes 3145736 | tf_op jit(solution)/shard_map/ppermute | solution.py:640
  158.0 5.7 collective-permute-start.12
  158.9 5.5 collective-permute-start.20
  159.9 26.8 %collective-permute-start.23 = (bf16[512,768]{1,0:T(8,128)(2,1)S(1)}, bf16[512,768]{1,0:T(8,128)(2,1)S(1)}, u32[]{:S(2)}, u32[]{:S(2)}) collective-permute-start(bf16[512,768]{1,0:T(8,128)(2,1)S(1)} %all_gather.3), channel_id=1, source_target_pairs={{0,16},{8,24},{16,0},{24,8},{1,17},{9,25},{17,1},{25,9},{2,18},{10... | collective-permute-start | bytes 2359304 | tf_op jit(solution)/shard_map/ppermute | solution.py:640
  161.6 26.1 %collective-permute-start.22 = (bf16[512,768]{1,0:T(8,128)(2,1)}, bf16[512,768]{1,0:T(8,128)(2,1)}, u32[]{:S(2)}, u32[]{:S(2)}) collective-permute-start(bf16[512,768]{1,0:T(8,128)(2,1)} %param.25), channel_id=1, source_target_pairs={{0,8},{8,0},{16,24},{24,16},{1,9},{9,1},{17,25},{25,17},{2,10},{10... | collective-permute-start | bytes 2359304 | tf_op jit(solution)/shard_map/ppermute | solution.py:640
  163.6 27.8 %collective-permute-start.35 = (bf16[2,256,512]{2,1,0:T(8,128)(2,1)S(1)}, bf16[2,256,512]{2,1,0:T(8,128)(2,1)S(1)}, u32[]{:S(2)}, u32[]{:S(2)}) collective-permute-start(bf16[2,256,512]{2,1,0:T(8,128)(2,1)S(1)} %pad_maximum_fusion.3), channel_id=1, source_target_pairs={{0,4},{1,5},{2,6},{3,7},{4,0},{5,1},{6,2},{7,3},{8,12},{9,13},{10,... | collective-permute-start | bytes 1572872 | tf_op jit(solution)/shard_map/ppermute | solution.py:653
  164.3 27.1 %collective-permute-start.31 = (bf16[2,256,512]{2,1,0:T(8,128)(2,1)S(1)}, bf16[2,256,512]{2,1,0:T(8,128)(2,1)}, u32[]{:S(2)}, u32[]{:S(2)}) collective-permute-start(bf16[2,256,512]{2,1,0:T(8,128)(2,1)S(1)} %pad_maximum_fusion.3), channel_id=1, source_target_pairs={{0,6},{1,7},{2,0},{3,1},{4,2},{5,3},{6,4},{7,5},{8,14},{9,15},{10,... | collective-permute-start | bytes 1572872 | tf_op jit(solution)/shard_map/ppermute | solution.py:653
  167.4 34.3 %collective-permute-start.27 = (bf16[2,256,512]{2,1,0:T(8,128)(2,1)S(1)}, bf16[2,256,512]{2,1,0:T(8,128)(2,1)}, u32[]{:S(2)}, u32[]{:S(2)}) collective-permute-start(bf16[2,256,512]{2,1,0:T(8,128)(2,1)S(1)} %pad_maximum_fusion.3), channel_id=1, source_target_pairs={{0,2},{1,3},{2,4},{3,5},{4,6},{5,7},{6,0},{7,1},{8,10},{9,11},{10,... | collective-permute-start | bytes 1572872 | tf_op jit(solution)/shard_map/ppermute | solution.py:653
  187.6 54.1 %collective-permute-start.21 = (bf16[1024,1024]{1,0:T(8,128)(2,1)}, bf16[1024,1024]{1,0:T(8,128)(2,1)}, u32[]{:S(2)}, u32[]{:S(2)}) collective-permute-start(bf16[1024,1024]{1,0:T(8,128)(2,1)} %get-tuple-element.52.own.refs_0_), channel_id=1, source_target_pairs={{0,8},{8,0},{16,24},{24,16},{1,9},{9,1},{17,25},{25,17},{2,10},{10... | collective-permute-start | bytes 6291464 | tf_op jit(solution)/shard_map/ppermute | solution.py:640
  187.7 15.7 %collective-permute-start.25 = (bf16[2,256,512]{2,1,0:T(8,128)(2,1)S(1)}, bf16[2,256,512]{2,1,0:T(8,128)(2,1)S(1)}, u32[]{:S(2)}, u32[]{:S(2)}) collective-permute-start(bf16[2,256,512]{2,1,0:T(8,128)(2,1)S(1)} %pad_maximum_fusion.3), channel_id=1, source_target_pairs={{0,16},{8,24},{16,0},{24,8},{1,17},{9,25},{17,1},{25,9},{2,18},{10... | collective-permute-start | bytes 1572872 | tf_op jit(solution)/shard_map/ppermute | solution.py:640
  191.5 13.8 %collective-permute-start.24 = (bf16[2,256,512]{2,1,0:T(8,128)(2,1)S(1)}, bf16[2,256,512]{2,1,0:T(8,128)(2,1)S(1)}, u32[]{:S(2)}, u32[]{:S(2)}) collective-permute-start(bf16[2,256,512]{2,1,0:T(8,128)(2,1)S(1)} %pad_maximum_fusion.3), channel_id=1, source_target_pairs={{0,1},{1,0},{2,3},{3,2},{4,5},{5,4},{6,7},{7,6},{8,9},{9,8},{10,11... | collective-permute-start | bytes 1572872 | tf_op jit(solution)/shard_map/ppermute | solution.py:649
  191.5 22.4 %collective-permute-start.37 = (bf16[2,256,512]{2,1,0:T(8,128)(2,1)S(1)}, bf16[2,256,512]{2,1,0:T(8,128)(2,1)S(1)}, u32[]{:S(2)}, u32[]{:S(2)}) collective-permute-start(bf16[2,256,512]{2,1,0:T(8,128)(2,1)S(1)} %collective-permute-done.35), channel_id=1, source_target_pairs={{0,16},{8,24},{16,0},{24,8},{1,17},{9,25},{17,1},{25,9},{2,18},{10... | collective-permute-start | bytes 1572872 | tf_op jit(solution)/shard_map/ppermute | solution.py:640
  201.7 13.7 %collective-permute-start.36 = (bf16[2,256,512]{2,1,0:T(8,128)(2,1)S(1)}, bf16[2,256,512]{2,1,0:T(8,128)(2,1)S(1)}, u32[]{:S(2)}, u32[]{:S(2)}) collective-permute-start(bf16[2,256,512]{2,1,0:T(8,128)(2,1)S(1)} %collective-permute-done.35), channel_id=1, source_target_pairs={{0,1},{1,0},{2,3},{3,2},{4,5},{5,4},{6,7},{7,6},{8,9},{9,8},{10,11... | collective-permute-start | bytes 1572872 | tf_op jit(solution)/shard_map/ppermute | solution.py:649
  203.4 21.8 %collective-permute-start.33 = (bf16[2,256,512]{2,1,0:T(8,128)(2,1)}, bf16[2,256,512]{2,1,0:T(8,128)(2,1)}, u32[]{:S(2)}, u32[]{:S(2)}) collective-permute-start(bf16[2,256,512]{2,1,0:T(8,128)(2,1)} %collective-permute-done.31), channel_id=1, source_target_pairs={{0,16},{8,24},{16,0},{24,8},{1,17},{9,25},{17,1},{25,9},{2,18},{10... | collective-permute-start | bytes 1572872 | tf_op jit(solution)/shard_map/ppermute | solution.py:640
  205.3 20.0 %collective-permute-start.32 = (bf16[2,256,512]{2,1,0:T(8,128)(2,1)}, bf16[2,256,512]{2,1,0:T(8,128)(2,1)}, u32[]{:S(2)}, u32[]{:S(2)}) collective-permute-start(bf16[2,256,512]{2,1,0:T(8,128)(2,1)} %collective-permute-done.31), channel_id=1, source_target_pairs={{0,1},{1,0},{2,3},{3,2},{4,5},{5,4},{6,7},{7,6},{8,9},{9,8},{10,11... | collective-permute-start | bytes 1572872 | tf_op jit(solution)/shard_map/ppermute | solution.py:649
  213.9 21.1 %collective-permute-start.29 = (bf16[2,256,512]{2,1,0:T(8,128)(2,1)}, bf16[2,256,512]{2,1,0:T(8,128)(2,1)}, u32[]{:S(2)}, u32[]{:S(2)}) collective-permute-start(bf16[2,256,512]{2,1,0:T(8,128)(2,1)} %collective-permute-done.27), channel_id=1, source_target_pairs={{0,16},{8,24},{16,0},{24,8},{1,17},{9,25},{17,1},{25,9},{2,18},{10... | collective-permute-start | bytes 1572872 | tf_op jit(solution)/shard_map/ppermute | solution.py:640
  215.3 19.7 %collective-permute-start.28 = (bf16[2,256,512]{2,1,0:T(8,128)(2,1)}, bf16[2,256,512]{2,1,0:T(8,128)(2,1)}, u32[]{:S(2)}, u32[]{:S(2)}) collective-permute-start(bf16[2,256,512]{2,1,0:T(8,128)(2,1)} %collective-permute-done.27), channel_id=1, source_target_pairs={{0,1},{1,0},{2,3},{3,2},{4,5},{5,4},{6,7},{7,6},{8,9},{9,8},{10,11... | collective-permute-start | bytes 1572872 | tf_op jit(solution)/shard_map/ppermute | solution.py:649
  225.2 14.0 %collective-permute-start.26 = (bf16[2,256,512]{2,1,0:T(8,128)(2,1)S(1)}, bf16[2,256,512]{2,1,0:T(8,128)(2,1)S(1)}, u32[]{:S(2)}, u32[]{:S(2)}) collective-permute-start(bf16[2,256,512]{2,1,0:T(8,128)(2,1)S(1)} %copy-done.41), channel_id=1, source_target_pairs={{0,1},{1,0},{2,3},{3,2},{4,5},{5,4},{6,7},{7,6},{8,9},{9,8},{10,11... | collective-permute-start | bytes 1572872 | tf_op jit(solution)/shard_map/ppermute | solution.py:649
  225.3 14.0 %collective-permute-start.38 = (bf16[2,256,512]{2,1,0:T(8,128)(2,1)S(1)}, bf16[2,256,512]{2,1,0:T(8,128)(2,1)S(1)}, u32[]{:S(2)}, u32[]{:S(2)}) collective-permute-start(bf16[2,256,512]{2,1,0:T(8,128)(2,1)S(1)} %copy-done.44), channel_id=1, source_target_pairs={{0,1},{1,0},{2,3},{3,2},{4,5},{5,4},{6,7},{7,6},{8,9},{9,8},{10,11... | collective-permute-start | bytes 1572872 | tf_op jit(solution)/shard_map/ppermute | solution.py:649
  235.0 5.9 collective-permute-start.30
  267.7 48.2 %collective-permute-start.64 = (bf16[512,768]{1,0:T(8,128)(2,1)S(1)}, bf16[512,768]{1,0:T(8,128)(2,1)S(1)}, u32[]{:S(2)}, u32[]{:S(2)}) collective-permute-start(bf16[512,768]{1,0:T(8,128)(2,1)S(1)} %slice.560), channel_id=1, source_target_pairs={{0,16},{8,24},{16,0},{24,8},{1,17},{9,25},{17,1},{25,9},{2,18},{10... | collective-permute-start | bytes 2359304 | tf_op jit(solution)/shard_map/ppermute | solution.py:640
  284.5 78.0 %collective-permute-start.44 = (bf16[4,2,256,512]{3,2,1,0:T(8,128)(2,1)}, bf16[4,2,256,512]{3,2,1,0:T(8,128)(2,1)}, u32[]{:S(2)}, u32[]{:S(2)}) collective-permute-start(bf16[4,2,256,512]{3,2,1,0:T(8,128)(2,1)} %get-tuple-element.71), channel_id=1, source_target_pairs={{0,1},{1,0},{2,3},{3,2},{4,5},{5,4},{6,7},{7,6},{8,9},{9,8},{10,11... | collective-permute-start | bytes 6291464 | tf_op jit(solution)/shard_map/ppermute | solution.py:649
  294.3 73.5 %collective-permute-start.40 = (bf16[1024,1024]{1,0:T(8,128)(2,1)}, bf16[1024,1024]{1,0:T(8,128)(2,1)}, u32[]{:S(2)}, u32[]{:S(2)}) collective-permute-start(bf16[1024,1024]{1,0:T(8,128)(2,1)} %highway_back.5), channel_id=1, source_target_pairs={{0,8},{8,0},{16,24},{24,16},{1,9},{9,1},{17,25},{25,17},{2,10},{10... | collective-permute-start | bytes 6291464 | tf_op jit(solution)/shard_map/ppermute | solution.py:640
  303.6 56.0 %collective-permute-start.39 = (bf16[512,768]{1,0:T(8,128)(2,1)}, bf16[512,768]{1,0:T(8,128)(2,1)}, u32[]{:S(2)}, u32[]{:S(2)}) collective-permute-start(bf16[512,768]{1,0:T(8,128)(2,1)} %fusion.13), channel_id=1, source_target_pairs={{0,8},{8,0},{16,24},{24,16},{1,9},{9,1},{17,25},{25,17},{2,10},{10... | collective-permute-start | bytes 2359304 | tf_op jit(solution)/shard_map/ppermute | solution.py:640
  304.9 100.2 %collective-permute-start.43 = (bf16[4,2,256,512]{3,2,1,0:T(8,128)(2,1)}, bf16[4,2,256,512]{3,2,1,0:T(8,128)(2,1)}, u32[]{:S(2)}, u32[]{:S(2)}) collective-permute-start(bf16[4,2,256,512]{3,2,1,0:T(8,128)(2,1)} %get-tuple-element.69), channel_id=1, source_target_pairs={{0,1},{1,0},{2,3},{3,2},{4,5},{5,4},{6,7},{7,6},{8,9},{9,8},{10,11... | collective-permute-start | bytes 6291464 | tf_op jit(solution)/shard_map/ppermute | solution.py:649
  317.3 388.7 %all-reduce.6.cloned.1.call-start = ((), (), s32[]{:S(2)}) async-start(), calls=%async_computation.1 | async-start | bytes 524288 | tf_op jit(solution)/shard_map/psum | solution.py:850
  365.7 39.7 %collective-permute-start.45 = (bf16[2,256,512]{2,1,0:T(8,128)(2,1)}, bf16[2,256,512]{2,1,0:T(8,128)(2,1)S(1)}, u32[]{:S(2)}, u32[]{:S(2)}) collective-permute-start(bf16[2,256,512]{2,1,0:T(8,128)(2,1)} %get-tuple-element.100), channel_id=1, source_target_pairs={{0,16},{8,24},{16,0},{24,8},{1,17},{9,25},{17,1},{25,9},{2,18},{10... | collective-permute-start | bytes 1572872 | tf_op jit(solution)/shard_map/ppermute | solution.py:640
  366.0 52.0 %collective-permute-start.49 = (bf16[2,256,512]{2,1,0:T(8,128)(2,1)}, bf16[2,256,512]{2,1,0:T(8,128)(2,1)}, u32[]{:S(2)}, u32[]{:S(2)}) collective-permute-start(bf16[2,256,512]{2,1,0:T(8,128)(2,1)} %get-tuple-element.102), channel_id=1, source_target_pairs={{0,16},{8,24},{16,0},{24,8},{1,17},{9,25},{17,1},{25,9},{2,18},{10... | collective-permute-start | bytes 1572872 | tf_op jit(solution)/shard_map/ppermute | solution.py:640
  387.9 56.8 %collective-permute-start.41 = (bf16[1024,1024]{1,0:T(8,128)(2,1)}, bf16[1024,1024]{1,0:T(8,128)(2,1)}, u32[]{:S(2)}, u32[]{:S(2)}) collective-permute-start(bf16[1024,1024]{1,0:T(8,128)(2,1)} %highway_back.7), channel_id=1, source_target_pairs={{0,8},{8,0},{16,24},{24,16},{1,9},{9,1},{17,25},{25,17},{2,10},{10... | collective-permute-start | bytes 6291464 | tf_op jit(solution)/shard_map/ppermute | solution.py:640
  404.3 44.1 %collective-permute-start.53 = (bf16[4,2,256,512]{3,2,1,0:T(8,128)(2,1)}, bf16[4,2,256,512]{3,2,1,0:T(8,128)(2,1)S(1)}, u32[]{:S(2)}, u32[]{:S(2)}) collective-permute-start(bf16[4,2,256,512]{3,2,1,0:T(8,128)(2,1)} %get-tuple-element.75), channel_id=1, source_target_pairs={{0,1},{1,0},{2,3},{3,2},{4,5},{5,4},{6,7},{7,6},{8,9},{9,8},{10,11... | collective-permute-start | bytes 6291464 | tf_op jit(solution)/shard_map/ppermute | solution.py:649
  405.1 14.8 %collective-permute-start.47 = (bf16[2,256,512]{2,1,0:T(8,128)(2,1)}, bf16[2,256,512]{2,1,0:T(8,128)(2,1)}, u32[]{:S(2)}, u32[]{:S(2)}) collective-permute-start(bf16[2,256,512]{2,1,0:T(8,128)(2,1)} %get-tuple-element.103), channel_id=1, source_target_pairs={{0,16},{8,24},{16,0},{24,8},{1,17},{9,25},{17,1},{25,9},{2,18},{10... | collective-permute-start | bytes 1572872 | tf_op jit(solution)/shard_map/ppermute | solution.py:640
  405.4 77.9 %collective-permute-start.52 = (bf16[4,2,256,512]{3,2,1,0:T(8,128)(2,1)}, bf16[4,2,256,512]{3,2,1,0:T(8,128)(2,1)}, u32[]{:S(2)}, u32[]{:S(2)}) collective-permute-start(bf16[4,2,256,512]{3,2,1,0:T(8,128)(2,1)} %get-tuple-element.73), channel_id=1, source_target_pairs={{0,1},{1,0},{2,3},{3,2},{4,5},{5,4},{6,7},{7,6},{8,9},{9,8},{10,11... | collective-permute-start | bytes 6291464 | tf_op jit(solution)/shard_map/ppermute | solution.py:649
  418.0 16.0 %collective-permute-start.51 = (bf16[2,256,512]{2,1,0:T(8,128)(2,1)S(1)}, bf16[2,256,512]{2,1,0:T(8,128)(2,1)S(1)}, u32[]{:S(2)}, u32[]{:S(2)}) collective-permute-start(bf16[2,256,512]{2,1,0:T(8,128)(2,1)S(1)} %copy-done.29), channel_id=1, source_target_pairs={{0,16},{8,24},{16,0},{24,8},{1,17},{9,25},{17,1},{25,9},{2,18},{10... | collective-permute-start | bytes 1572872 | tf_op jit(solution)/shard_map/ppermute | solution.py:640
  422.6 46.7 %collective-permute-start.46 = (bf16[2,256,512]{2,1,0:T(8,128)(2,1)S(1)}, bf16[2,256,512]{2,1,0:T(8,128)(2,1)S(1)}, u32[]{:S(2)}, u32[]{:S(2)}) collective-permute-start(bf16[2,256,512]{2,1,0:T(8,128)(2,1)S(1)} %get-tuple-element.97), channel_id=1, source_target_pairs={{0,4},{1,5},{2,6},{3,7},{4,0},{5,1},{6,2},{7,3},{8,12},{9,13},{10,... | collective-permute-start | bytes 1572872 | tf_op jit(solution)/shard_map/ppermute | solution.py:653
  434.0 35.5 %collective-permute-start.50 = (bf16[2,256,512]{2,1,0:T(8,128)(2,1)S(1)}, bf16[2,256,512]{2,1,0:T(8,128)(2,1)S(1)}, u32[]{:S(2)}, u32[]{:S(2)}) collective-permute-start(bf16[2,256,512]{2,1,0:T(8,128)(2,1)S(1)} %get-tuple-element.98), channel_id=1, source_target_pairs={{0,2},{1,3},{2,4},{3,5},{4,6},{5,7},{6,0},{7,1},{8,10},{9,11},{10,... | collective-permute-start | bytes 1572872 | tf_op jit(solution)/shard_map/ppermute | solution.py:653
  444.8 32.9 %collective-permute-start.48 = (bf16[2,256,512]{2,1,0:T(8,128)(2,1)S(1)}, bf16[2,256,512]{2,1,0:T(8,128)(2,1)S(1)}, u32[]{:S(2)}, u32[]{:S(2)}) collective-permute-start(bf16[2,256,512]{2,1,0:T(8,128)(2,1)S(1)} %get-tuple-element.99), channel_id=1, source_target_pairs={{0,6},{1,7},{2,0},{3,1},{4,2},{5,3},{6,4},{7,5},{8,14},{9,15},{10,... | collective-permute-start | bytes 1572872 | tf_op jit(solution)/shard_map/ppermute | solution.py:653
  448.4 71.5 %collective-permute-start.42 = (bf16[1024,512]{1,0:T(8,128)(2,1)}, bf16[1024,512]{1,0:T(8,128)(2,1)S(1)}, u32[]{:S(2)}, u32[]{:S(2)}) collective-permute-start(bf16[1024,512]{1,0:T(8,128)(2,1)} %get-tuple-element.95), channel_id=1, source_target_pairs={{0,16},{8,24},{16,0},{24,8},{1,17},{9,25},{17,1},{25,9},{2,18},{10... | collective-permute-start | bytes 3145736 | tf_op jit(solution)/shard_map/ppermute | solution.py:640
  469.3 16.8 %collective-permute-start.54 = (bf16[2,256,512]{2,1,0:T(8,128)(2,1)}, bf16[2,256,512]{2,1,0:T(8,128)(2,1)}, u32[]{:S(2)}, u32[]{:S(2)}) collective-permute-start(bf16[2,256,512]{2,1,0:T(8,128)(2,1)} %get-tuple-element.107), channel_id=1, source_target_pairs={{0,16},{8,24},{16,0},{24,8},{1,17},{9,25},{17,1},{25,9},{2,18},{10... | collective-permute-start | bytes 1572872 | tf_op jit(solution)/shard_map/ppermute | solution.py:640
  469.6 27.7 %collective-permute-start.58 = (bf16[2,256,512]{2,1,0:T(8,128)(2,1)}, bf16[2,256,512]{2,1,0:T(8,128)(2,1)}, u32[]{:S(2)}, u32[]{:S(2)}) collective-permute-start(bf16[2,256,512]{2,1,0:T(8,128)(2,1)} %get-tuple-element.109), channel_id=1, source_target_pairs={{0,16},{8,24},{16,0},{24,8},{1,17},{9,25},{17,1},{25,9},{2,18},{10... | collective-permute-start | bytes 1572872 | tf_op jit(solution)/shard_map/ppermute | solution.py:640
  477.6 30.9 %collective-permute-start.56 = (bf16[2,256,512]{2,1,0:T(8,128)(2,1)}, bf16[2,256,512]{2,1,0:T(8,128)(2,1)}, u32[]{:S(2)}, u32[]{:S(2)}) collective-permute-start(bf16[2,256,512]{2,1,0:T(8,128)(2,1)} %get-tuple-element.110), channel_id=1, source_target_pairs={{0,16},{8,24},{16,0},{24,8},{1,17},{9,25},{17,1},{25,9},{2,18},{10... | collective-permute-start | bytes 1572872 | tf_op jit(solution)/shard_map/ppermute | solution.py:640
  483.4 210.9 %collective-permute-start.60 = (bf16[2,256,512]{2,1,0:T(8,128)(2,1)}, bf16[2,256,512]{2,1,0:T(8,128)(2,1)}, u32[]{:S(2)}, u32[]{:S(2)}) collective-permute-start(bf16[2,256,512]{2,1,0:T(8,128)(2,1)} %get-tuple-element.108), channel_id=1, source_target_pairs={{0,16},{8,24},{16,0},{24,8},{1,17},{9,25},{17,1},{25,9},{2,18},{10... | collective-permute-start | bytes 1572872 | tf_op jit(solution)/shard_map/ppermute | solution.py:640
  512.5 181.8 %collective-permute-start.55 = (bf16[2,256,512]{2,1,0:T(8,128)(2,1)}, bf16[2,256,512]{2,1,0:T(8,128)(2,1)}, u32[]{:S(2)}, u32[]{:S(2)}) collective-permute-start(bf16[2,256,512]{2,1,0:T(8,128)(2,1)} %get-tuple-element.104), channel_id=1, source_target_pairs={{0,4},{1,5},{2,6},{3,7},{4,0},{5,1},{6,2},{7,3},{8,12},{9,13},{10,... | collective-permute-start | bytes 1572872 | tf_op jit(solution)/shard_map/ppermute | solution.py:653
  516.0 178.3 %collective-permute-start.59 = (bf16[2,256,512]{2,1,0:T(8,128)(2,1)}, bf16[2,256,512]{2,1,0:T(8,128)(2,1)}, u32[]{:S(2)}, u32[]{:S(2)}) collective-permute-start(bf16[2,256,512]{2,1,0:T(8,128)(2,1)} %get-tuple-element.105), channel_id=1, source_target_pairs={{0,2},{1,3},{2,4},{3,5},{4,6},{5,7},{6,0},{7,1},{8,10},{9,11},{10,... | collective-permute-start | bytes 1572872 | tf_op jit(solution)/shard_map/ppermute | solution.py:653
  516.6 177.7 %collective-permute-start.57 = (bf16[2,256,512]{2,1,0:T(8,128)(2,1)}, bf16[2,256,512]{2,1,0:T(8,128)(2,1)}, u32[]{:S(2)}, u32[]{:S(2)}) collective-permute-start(bf16[2,256,512]{2,1,0:T(8,128)(2,1)} %get-tuple-element.106), channel_id=1, source_target_pairs={{0,6},{1,7},{2,0},{3,1},{4,2},{5,3},{6,4},{7,5},{8,14},{9,15},{10,... | collective-permute-start | bytes 1572872 | tf_op jit(solution)/shard_map/ppermute | solution.py:653
  697.1 15.2 %collective-permute-start.61 = (bf16[2,256,512]{2,1,0:T(8,128)(2,1)S(1)}, bf16[2,256,512]{2,1,0:T(8,128)(2,1)S(1)}, u32[]{:S(2)}, u32[]{:S(2)}) collective-permute-start(bf16[2,256,512]{2,1,0:T(8,128)(2,1)S(1)} %pad_maximum_fusion.4), channel_id=1, source_target_pairs={{0,8},{8,0},{16,24},{24,16},{1,9},{9,1},{17,25},{25,17},{2,10},{10... | collective-permute-start | bytes 1572872 | tf_op jit(solution)/shard_map/ppermute | solution.py:640
  699.4 22.7 %collective-permute-start.62 = (bf16[2,256,512]{2,1,0:T(8,128)(2,1)S(1)}, bf16[2,256,512]{2,1,0:T(8,128)(2,1)S(1)}, u32[]{:S(2)}, u32[]{:S(2)}) collective-permute-start(bf16[2,256,512]{2,1,0:T(8,128)(2,1)S(1)} %pad_maximum_fusion.5), channel_id=1, source_target_pairs={{0,16},{8,24},{16,0},{24,8},{1,17},{9,25},{17,1},{25,9},{2,18},{10... | collective-permute-start | bytes 1572872 | tf_op jit(solution)/shard_map/ppermute | solution.py:640
  699.6 22.5 %collective-permute-start.63 = (bf16[2,256,512]{2,1,0:T(8,128)(2,1)S(1)}, bf16[2,256,512]{2,1,0:T(8,128)(2,1)}, u32[]{:S(2)}, u32[]{:S(2)}) collective-permute-start(bf16[2,256,512]{2,1,0:T(8,128)(2,1)S(1)} %pad_maximum_fusion.6), channel_id=1, source_target_pairs={{0,24},{8,16},{16,8},{24,0},{1,25},{9,17},{17,9},{25,1},{2,26},{10... | collective-permute-start | bytes 1572872 | tf_op jit(solution)/shard_map/ppermute | solution.py:640
  (81 other events, 1195.6 us)
Sparse Core Ops, SparseCore 0:
  317.4 43.4 reduce-scatter.1
  649.3 56.6 all-reduce.5

commit v2 on v1

v2 whole, which is shorter than its diff:
```python
import functools

import jax
import jax.numpy as jnp
from jax import lax
from jax.experimental import pallas as pl
from jax.experimental.pallas import tpu as pltpu
from jax.sharding import PartitionSpec as P

CHAR_DIM = 16
MAX_CHARS = 50
MAX_WIDTH = 7
FILTERS = 2048
UNITS = 4
SLOTS = 2
STEP = 10
TAPS = MAX_WIDTH * CHAR_DIM
DEPTH = 128
ID_SHIFT = 128
ID_ROWS = 64
SLOTS_E = MAX_CHARS + MAX_WIDTH - 1 + 8
LANES = 128
STEP_P = 4
ROWS = 256
beta_one = 0.9
beta_two = 0.999
adam_eps = 1e-08
decay_rate = 0.01
average_keep = 0.9
F32, BF16 = jnp.float32, jnp.bfloat16
MIB = 1 << 20


def lasting(us):
    return pl.CostEstimate(flops=int(us * 1e7), bytes_accessed=int(us * 3e4), transcendentals=0)


def nt(a, b):
    return lax.dot_general(a, b, (((1,), (1,)), ((), ())), preferred_element_type=F32)


def nn(a, b):
    return lax.dot_general(a, b, (((1,), (0,)), ((), ())), preferred_element_type=F32)


def tn(a, b):
    return lax.dot_general(a, b, (((0,), (0,)), ((), ())), preferred_element_type=F32)


def embed_tile(ids_ref, table_ref, lens, e_ref, longest):
    tile = lens.shape[1]
    e_ref[...] = jnp.zeros_like(e_ref)
    pieces = table_ref.shape[1] // LANES

    def fill(s, carry):
        for i in range(STEP_P):
            p = s * STEP_P + i
            row = ids_ref[pl.ds(p, 1), :].astype(jnp.int32)
            parts = []
            for lane in range(tile // LANES):
                idx = jnp.broadcast_to(row[:, lane * LANES : (lane + 1) * LANES], (CHAR_DIM, LANES))
                low = jnp.bitwise_and(idx, LANES - 1)
                value = jnp.zeros((CHAR_DIM, LANES), F32)
                for piece in range(pieces):
                    got = jnp.take_along_axis(table_ref[:, piece * LANES : (piece + 1) * LANES], low, axis=1)
                    value = jnp.where(lax.shift_right_logical(idx, 7) == piece, got, value)
                parts.append(value)
            value = jnp.concatenate(parts, axis=1) if len(parts) > 1 else parts[0]
            value = jnp.where(p < lens, value, 0.0)
            e_ref[pl.ds(pl.multiple_of(p * CHAR_DIM, CHAR_DIM), CHAR_DIM), :] = value.astype(BF16)
        return carry

    lax.fori_loop(0, (longest + STEP_P - 1) // STEP_P, fill, 0)


def limits_of(lens):
    row = lax.broadcasted_iota(jnp.int32, (CHAR_DIM, lens.shape[1]), 0)
    past = jnp.maximum(lens - (row - 2), 0)
    return jnp.where(row < 3, -1, jnp.where(row < 3 + MAX_WIDTH, past, 1 << 20))


def window_at(e_ref, limit, p):
    extra = jnp.where(p > limit, 1.0, 0.0).astype(BF16)
    taps = e_ref[pl.ds(pl.multiple_of(p * CHAR_DIM, CHAR_DIM), TAPS), :]
    return jnp.concatenate([taps, extra], axis=0)


SUB = 32


def windows_at(e_ref, limit, s):
    return jnp.concatenate([window_at(e_ref, limit, s * STEP_P + i) for i in range(STEP_P)], axis=1)


def steps_of(longest, narrow):
    return (jnp.maximum(longest - narrow, 0) + STEP_P) // STEP_P


def conv_forward_kernel(cblock, base, narrow_ref, rank_ref, data_ref, table_ref, conv_ref, width_ref, feat_ref, lse_ref, ids_ref, e_ref, top, total, pre):
    tile = ids_ref.shape[1]
    words = rank_ref.shape[0]
    first = (base + pl.program_id(0)) * tile
    lane = first + lax.broadcasted_iota(jnp.int32, (words, tile), 1)
    hot = jnp.where(rank_ref[...] == lane, 1.0, 0.0).astype(BF16)
    moved = nn(data_ref[...], hot)
    shift = jnp.where(lax.broadcasted_iota(jnp.int32, moved.shape, 0) < MAX_CHARS, float(ID_SHIFT), 0.0)
    moved = moved + shift
    ids_ref[...] = moved
    lens = (moved[MAX_CHARS : MAX_CHARS + 1, :] + 0.5).astype(jnp.int32)
    longest = jnp.max(lens)
    embed_tile(ids_ref, table_ref, lens, e_ref, longest)
    limit = limits_of(lens)
    channels = conv_ref.shape[0]
    for block in range(channels // cblock):
        rows = pl.ds(block * cblock, cblock)
        top[...] = jnp.full_like(top, -1e30)
        total[...] = jnp.zeros_like(total)

        def step(s, carry):
            pre[...] = nn(conv_ref[rows, :], windows_at(e_ref, limit, s))
            for sub in range(0, cblock, SUB):
                part = slice(sub, sub + SUB)
                values = [pre[part, i * tile : (i + 1) * tile] for i in range(STEP_P)]
                before = top[part, :]
                best = functools.reduce(jnp.maximum, values, before)
                top[part, :] = best
                total[part, :] = total[part, :] * jnp.exp(before - best) + sum(jnp.exp(value - best) for value in values)
            return carry

        lax.fori_loop(0, steps_of(longest, narrow_ref[block]), step, 0)
        span = jnp.maximum(lens - width_ref[rows, :], 0)
        lse = top[...] + jnp.log(total[...])
        lse_ref[rows, :] = lse
        pooled = lse - jnp.log((span + 1).astype(F32))
        feat_ref[rows, :] = (pooled * jax.nn.sigmoid(pooled)).astype(BF16)


def place_kernel(rank_ref, *refs):
    feats, out_ref = refs[:-1], refs[-1]
    total, base = 0.0, 0
    for feat_ref in feats:
        shape = (rank_ref.shape[0], feat_ref.shape[1])
        lane = base + lax.broadcasted_iota(jnp.int32, shape, 1)
        hot = jnp.where(rank_ref[...] == lane, 1.0, 0.0).astype(BF16)
        total = total + nt(hot, feat_ref[...])
        base += shape[1]
    out_ref[...] = total.astype(BF16)


def conv_forward(rank, data, table_t, conv_t, widths, narrow, cblock, base, count):
    words, channels = rank.shape[0], conv_t.shape[0]
    tile = min(256, words)
    span = count * tile
    full = lambda *shape: pl.BlockSpec(shape, lambda i: (0,) * len(shape))
    column = lambda depth: pl.BlockSpec((depth, tile), lambda i: (0, i))
    return pl.pallas_call(
        functools.partial(conv_forward_kernel, cblock, base),
        grid=(count,),
        in_specs=[
            pl.BlockSpec(memory_space=pltpu.SMEM),
            full(words, 1),
            full(*data.shape),
            full(*table_t.shape),
            full(*conv_t.shape),
            full(channels, 1),
        ],
        out_specs=[column(channels), column(channels), column(ID_ROWS), column(SLOTS_E * CHAR_DIM)],
        out_shape=[
            jax.ShapeDtypeStruct((channels, span), BF16),
            jax.ShapeDtypeStruct((channels, span), F32),
            jax.ShapeDtypeStruct((ID_ROWS, span), F32),
            jax.ShapeDtypeStruct((SLOTS_E * CHAR_DIM, span), BF16),
        ],
        scratch_shapes=[
            pltpu.VMEM((cblock, tile), F32),
            pltpu.VMEM((cblock, tile), F32),
            pltpu.VMEM((cblock, STEP_P * tile), F32),
        ],
        compiler_params=pltpu.CompilerParams(vmem_limit_bytes=48 * MIB),
        cost_estimate=lasting(11),
        name="conv_forward",
    )(narrow, rank, data, table_t, conv_t, widths)


def place_words(rank, feats):
    words, channels = rank.shape[0], feats[0].shape[0]
    rows = min(256, words)
    return pl.pallas_call(
        place_kernel,
        grid=(words // rows,),
        in_specs=[pl.BlockSpec((rows, 1), lambda i: (i, 0))] + [pl.BlockSpec(feat.shape, lambda i: (0, 0)) for feat in feats],
        out_specs=pl.BlockSpec((rows, channels), lambda i: (i, 0)),
        out_shape=jax.ShapeDtypeStruct((words, channels), BF16),
        compiler_params=pltpu.CompilerParams(vmem_limit_bytes=48 * MIB),
        cost_estimate=lasting(4),
        name="place_words",
    )(rank, *feats)


def conv_backward_kernel(cblock, n_parts, base, narrow_ref, ids_ref, e_ref, conv_ref, back_ref, width_ref, lse_ref, *refs):
    ranks, grads, refs = refs[:n_parts], refs[n_parts : 2 * n_parts], refs[2 * n_parts :]
    so_far, sums_ref, table_grad_ref, de_ref, dpool, pre, d_pre, found = refs
    tile = ids_ref.shape[1]
    vocab = table_grad_ref.shape[0]
    channels = conv_ref.shape[0]
    first = (base + pl.program_id(0)) * tile

    @pl.when(pl.program_id(0) == 0)
    def _():
        sums_ref[...] = so_far[...]
        table_grad_ref[...] = jnp.zeros_like(table_grad_ref)

    lens = (ids_ref[MAX_CHARS : MAX_CHARS + 1, :] + 0.5).astype(jnp.int32)
    longest = jnp.max(lens)
    limit = limits_of(lens)
    de_ref[...] = jnp.zeros_like(de_ref)
    moved = 0.0
    for rank_ref, grad_ref in zip(ranks, grads):
        row = first + lax.broadcasted_iota(jnp.int32, (tile, rank_ref.shape[1]), 0)
        moved = moved + nn(jnp.where(rank_ref[...] == row, 1.0, 0.0).astype(BF16), grad_ref[...])
    moved = moved.T
    for block in range(channels // cblock):
        rows = slice(block * cblock, (block + 1) * cblock)
        span = jnp.maximum(lens - width_ref[rows, :], 0)
        pooled = lse_ref[rows, :] - jnp.log((span + 1).astype(F32))
        sigma = jax.nn.sigmoid(pooled)
        dpool[...] = moved[rows, :] * (sigma + pooled * sigma * (1 - sigma))

        def step(s, carry):
            windows = windows_at(e_ref, limit, s)
            pre[...] = nn(conv_ref[rows, :], windows)
            for sub in range(0, cblock, SUB):
                part = slice(sub, sub + SUB)
                low, scale = lse_ref[block * cblock + sub : block * cblock + sub + SUB, :], dpool[part, :]
                for i in range(STEP_P):
                    cols = slice(i * tile, (i + 1) * tile)
                    d_pre[part, cols] = (jnp.exp(pre[part, cols] - low) * scale).astype(BF16)
            back = nn(back_ref[:, rows], d_pre[...])
            for i in range(STEP_P):
                at = pl.ds(pl.multiple_of((s * STEP_P + i) * CHAR_DIM, CHAR_DIM), TAPS)
                de_ref[at, :] += back[:TAPS, i * tile : (i + 1) * tile]
            sums_ref[rows, :] += nt(d_pre[...], windows)
            return carry

        lax.fori_loop(0, steps_of(longest, narrow_ref[block]), step, 0)

    letter = lax.broadcasted_iota(jnp.int32, (vocab, tile), 0)

    def spread(s, carry):
        parts = []
        for i in range(STEP_P):
            p = s * STEP_P + i
            at = pl.ds(pl.multiple_of(p * CHAR_DIM, CHAR_DIM), CHAR_DIM)
            value = jnp.where(p < lens, de_ref[at, :], 0.0)
            high = value.astype(BF16)
            parts.append(jnp.concatenate([high, (value - high.astype(F32)).astype(BF16)], axis=0))
            row = ids_ref[pl.ds(p, 1), :].astype(jnp.int32)
            found[:, i * tile : (i + 1) * tile] = jnp.where(letter == row, 1.0, 0.0).astype(BF16)
        table_grad_ref[...] += nt(found[...], jnp.concatenate(parts, axis=1))
        return carry

    lax.fori_loop(0, (longest + STEP_P - 1) // STEP_P, spread, 0)

    @pl.when(pl.program_id(0) == pl.num_programs(0) - 1)
    def _():
        both = table_grad_ref[...].T
        total = both[:CHAR_DIM] + both[CHAR_DIM:]
        for piece in range(vocab // LANES):
            at = channels + piece * CHAR_DIM
            sums_ref[at : at + CHAR_DIM, :] += total[:, piece * LANES : (piece + 1) * LANES]


def conv_backward(ranks, ids, embedded, vocab, conv_t, conv_back, widths, narrow, lse, grads, cblock, base, tile, so_far):
    channels, words = conv_t.shape[0], ids.shape[1]
    full = lambda *shape: pl.BlockSpec(shape, lambda i: (0,) * len(shape))
    return pl.pallas_call(
        functools.partial(conv_backward_kernel, cblock, len(ranks), base),
        grid=(words // tile,),
        in_specs=[
            pl.BlockSpec(memory_space=pltpu.SMEM),
            pl.BlockSpec((ID_ROWS, tile), lambda i: (0, i)),
            pl.BlockSpec((SLOTS_E * CHAR_DIM, tile), lambda i: (0, i)),
            full(*conv_t.shape),
            full(*conv_back.shape),
            full(channels, 1),
            pl.BlockSpec((channels, tile), lambda i: (0, i)),
        ]
        + [full(*part.shape) for part in ranks]
        + [full(*part.shape) for part in grads]
        + [full(*so_far.shape)],
        out_specs=full(*so_far.shape),
        out_shape=jax.ShapeDtypeStruct(so_far.shape, F32),
        scratch_shapes=[
            pltpu.VMEM((vocab, 2 * CHAR_DIM), F32),
            pltpu.VMEM((SLOTS_E * CHAR_DIM, tile), F32),
            pltpu.VMEM((cblock, tile), F32),
            pltpu.VMEM((cblock, STEP_P * tile), F32),
            pltpu.VMEM((cblock, STEP_P * tile), BF16),
            pltpu.VMEM((vocab, STEP_P * tile), BF16),
        ],
        compiler_params=pltpu.CompilerParams(vmem_limit_bytes=48 * MIB),
        cost_estimate=lasting(15),
        name="conv_backward",
    )(narrow, ids, embedded, conv_t, conv_back, widths, lse, *ranks, *grads, so_far)


def word_order(lengths):
    count = lengths.shape[0]
    key = lengths * count - jnp.arange(count, dtype=jnp.int32)
    return jnp.sum((key[None, :] > key[:, None]).astype(jnp.int32), axis=1, keepdims=True)


def conv_operands(char_ids, lengths, char_table, conv_weight, conv_bias, widths, cblock):
    words = char_ids.shape[0]
    channels = conv_weight.shape[1]
    vocab = char_table.shape[0]
    lanes = -(-vocab // LANES) * LANES
    rank = word_order(lengths)
    data = jnp.concatenate([char_ids.T - ID_SHIFT, lengths[None, :]], axis=0)
    data = jnp.pad(data, ((0, ID_ROWS - MAX_CHARS - 1), (0, 0))).astype(BF16)
    offsets = jnp.arange(TAPS, dtype=jnp.int32) // CHAR_DIM
    taps = jnp.where(offsets[:, None] < widths[None, :], conv_weight, 0.0).astype(BF16)
    parts, rest = [], conv_bias
    for _ in range(3):
        part = lax.reduce_precision(rest, 8, 7)
        parts.append(part)
        rest = rest - part
    kinds = jnp.arange(1, MAX_WIDTH + 1, dtype=jnp.int32)
    spans = jnp.where(kinds[:, None] == widths[None, :], -1e30, 0.0)
    under = jnp.concatenate([jnp.stack(parts), spans, jnp.zeros((DEPTH - TAPS - 3 - MAX_WIDTH, channels), F32)])
    conv_all = jnp.concatenate([taps, under.astype(BF16)])
    conv_back = jnp.pad(taps, ((0, DEPTH - TAPS), (0, 0)))
    table_t = jnp.pad(lax.reduce_precision(char_table, 8, 7).T, ((0, 0), (0, lanes - vocab)))
    narrow = widths[::cblock]
    return rank, data, table_t, conv_all.T, conv_back, widths[:, None], narrow


def channel_widths(start, count, whole):
    channel = start + jnp.arange(count, dtype=jnp.int32)
    widths = jnp.ones((count,), jnp.int32)
    for power in range(6):
        widths = widths + (channel >= whole * 2**power // 64).astype(jnp.int32)
    return widths


def unit_slots(owners, slots_each):
    order = jnp.arange(owners.shape[0], dtype=jnp.int32)
    before = (owners[:, None] == owners[None, :]) & (order[:, None] > order[None, :])
    return owners * slots_each + jnp.sum(before.astype(jnp.int32), axis=1)


def load_pieces(table_ref, pieces, rows, dest, sems, half=None, proj=None):
    cols = pieces[0].shape[3]
    depth = dest.shape[1]

    def each(act):
        at = 0
        for ref in pieces:
            for j in range(ref.shape[0]):
                row, col = table_ref[0, at], table_ref[1, at]
                row = row if half is None else row - half * depth
                sem = sems.at[at]

                def go(ref=ref, j=j, row=row, col=col, sem=sem):
                    place = (slice(None), pl.ds(pl.multiple_of(row, rows), rows), pl.ds(pl.multiple_of(col, cols), cols))
                    act(pltpu.make_async_copy(ref.at[j, :, :rows, :], dest.at[place], sem))

                if half is None:
                    go()
                else:
                    pl.when((row >= 0) & (row < depth))(go)
                if proj is not None:
                    under = ref.shape[2] - rows
                    part = proj[0].shape[1] // 2
                    to = pl.ds(pl.multiple_of(table_ref[2, at], under), under)
                    for side in range(2):
                        source = ref.at[j, side, rows:, :part]
                        act(pltpu.make_async_copy(source, proj[0].at[to, side * part : (side + 1) * part], proj[1].at[2 * at + side]))
                at += 1

    each(lambda copy: copy.start())
    each(lambda copy: copy.wait())


def hidden_of(xs, weight, unit, cols, bias_ref):
    at, total = 0, None
    for x in xs:
        term = nn(x[...], weight[unit, at : at + x.shape[1], cols])
        total = term if total is None else total + term
        at += x.shape[1]
    return total + bias_ref[unit : unit + 1, cols]


def sigmoid(value):
    return 0.5 * jnp.tanh(0.5 * value) + 0.5


def factors(x, a, g):
    s = sigmoid(a)
    gate = sigmoid(g)
    nonlinear = a * s
    left = 1 - gate
    gap = x - nonlinear
    return nonlinear + gate * gap, left * (s + nonlinear * (1 - s)), gap * gate * left, gate


def forward_kernel(n_own, n_pieces, rows, width, table_ref, bias_ref, *refs):
    own, refs = refs[:n_own], refs[n_own:]
    mate, refs = refs[:n_own], refs[n_own:]
    pieces, refs = refs[:n_pieces], refs[n_pieces:]
    next_ref, low_ref, first_ref, second_ref, gate_ref, weight, sems = refs

    @pl.when(pl.program_id(0) == 0)
    def _():
        load_pieces(table_ref, pieces, rows, weight, sems)

    for j, x in enumerate(own):
        cols = slice(j * width, (j + 1) * width)
        a = hidden_of(own + mate, weight, 0, cols, bias_ref)
        g = hidden_of(own + mate, weight, 1, cols, bias_ref)
        value, first, second, gate = factors(x[...].astype(F32), a, g)
        next_ref[:, cols] = value
        low_ref[:, cols] = value.astype(BF16)
        first_ref[:, cols] = first.astype(BF16)
        second_ref[:, cols] = second.astype(BF16)
        gate_ref[:, cols] = gate.astype(BF16)


def column_sums(sums_ref, cols, d_first, d_gate):
    sums_ref[0:1, cols] += jnp.sum(d_first.astype(F32), axis=0, keepdims=True)
    sums_ref[1:2, cols] += jnp.sum(d_gate.astype(F32), axis=0, keepdims=True)


def product_back(out_ref, d_first, d_gate, weight, base, up=None):
    width = min(512, out_ref.shape[1])
    for j in range(out_ref.shape[1] // width):
        cols = slice(j * width, (j + 1) * width)
        rows = slice(base + j * width, base + (j + 1) * width)
        value = nt(d_first[...], weight[0, rows, :]) + nt(d_gate[...], weight[1, rows, :])
        if up is not None:
            value = value + up[:, cols]
        out_ref[:, cols] = value.astype(out_ref.dtype)


def turn_kernel(n_pieces, rows, width, packed, table_ref, bias_ref, own, mate, exact, out_grad, *refs):
    if packed:
        pieces, refs = refs[:n_pieces], refs[n_pieces:]
        low_ref, d_first_ref, d_gate_ref, up_ref, leaving_ref, vectors_ref, sums_ref, weight, sems, proj, proj_sems = refs
        proj_rows = (proj, proj_sems)
    else:
        proj, pieces, refs = refs[0], refs[1 : n_pieces + 1], refs[n_pieces + 1 :]
        low_ref, d_first_ref, d_gate_ref, up_ref, leaving_ref, vectors_ref, sums_ref, weight, sems = refs
        proj_rows = None

    @pl.when(pl.program_id(0) == 0)
    def _():
        load_pieces(table_ref, pieces, rows, weight, sems, None, proj_rows)
        sums_ref[...] = jnp.zeros_like(sums_ref)

    half = own.shape[1]
    for j in range(half // width):
        cols = slice(j * width, (j + 1) * width)
        a = hidden_of((own, mate), weight, 0, cols, bias_ref)
        g = hidden_of((own, mate), weight, 1, cols, bias_ref)
        dy = nt(out_grad[...], proj[cols, :])
        value, first, second, gate = factors(exact[:, cols], a, g)
        low_ref[:, cols] = value.astype(BF16)
        d_first, d_gate = (dy * first).astype(BF16), (dy * second).astype(BF16)
        d_first_ref[:, cols] = d_first
        d_gate_ref[:, cols] = d_gate
        up_ref[:, cols] = dy * gate
        column_sums(sums_ref, cols, d_first, d_gate)
    product_back(leaving_ref, d_first_ref, d_gate_ref, weight, half)
    vectors_ref[...] = nn(low_ref[...], proj[...])


def slope_kernel(n_pieces, rows, width, table_ref, partial, arrived, first_ref, second_ref, gate_ref, *refs):
    pieces, refs = refs[:n_pieces], refs[n_pieces:]
    d_first_ref, d_gate_ref, up_ref, leaving_ref, sums_ref, weight, sems = refs

    @pl.when(pl.program_id(0) == 0)
    def _():
        load_pieces(table_ref, pieces, rows, weight, sems, 1)
        sums_ref[...] = jnp.zeros_like(sums_ref)

    for j in range(partial.shape[1] // width):
        cols = slice(j * width, (j + 1) * width)
        dy = partial[:, cols] + arrived[:, cols].astype(F32)
        d_first, d_gate = (dy * first_ref[:, cols].astype(F32)).astype(BF16), (dy * second_ref[:, cols].astype(F32)).astype(BF16)
        d_first_ref[:, cols] = d_first
        d_gate_ref[:, cols] = d_gate
        up_ref[:, cols] = dy * gate_ref[:, cols].astype(F32)
        column_sums(sums_ref, cols, d_first, d_gate)
    product_back(leaving_ref, d_first_ref, d_gate_ref, weight, 0)


def back_kernel(n_pieces, rows, table_ref, d_first, d_gate, up, *refs):
    pieces, refs = refs[:n_pieces], refs[n_pieces:]
    out_ref, weight, sems = refs

    @pl.when(pl.program_id(0) == 0)
    def _():
        load_pieces(table_ref, pieces, rows, weight, sems, 0)

    product_back(out_ref, d_first, d_gate, weight, 0, up)


def weight_grad_kernel(n_chunks, n_cols, n_d, width, table_ref, *refs):
    xs, refs = refs[: n_chunks * n_cols], refs[n_chunks * n_cols :]
    d_first, d_gate, refs = refs[:n_d], refs[n_d : 2 * n_d], refs[2 * n_d :]
    outs, turned = refs[:-1], refs[-1]
    rows = outs[0].shape[2]

    @pl.when(pl.program_id(0) == 0)
    def _():
        word = 0
        for chunk in range(n_chunks):
            at = 0
            for x in xs[chunk * n_cols : (chunk + 1) * n_cols]:
                turned[at : at + x.shape[1], word : word + x.shape[0]] = x[...].T
                at += x.shape[1]
            word += x.shape[0]

    blocks = d_first[0].shape[1] // width
    for side in range(2):
        row = table_ref[side, pl.program_id(0)]
        left = turned[pl.ds(pl.multiple_of(row, rows), rows), :]
        for j in range(blocks):
            cols = slice(j * width, (j + 1) * width)
            out = outs[blocks].at[j] if side else outs[j]
            for unit, ds in enumerate((d_first, d_gate)):
                total, word = 0.0, 0
                for d in ds:
                    total = total + nn(left[:, word : word + d.shape[0]], d[:, cols])
                    word += d.shape[0]
                out[0, unit] = total.astype(BF16)


SMEM_SPEC = pl.BlockSpec(memory_space=pltpu.SMEM)
ANY_SPEC = pl.BlockSpec(memory_space=pl.ANY)


def whole(array):
    return pl.BlockSpec(array.shape, lambda i: (0,) * array.ndim)


def by_rows(rows, width, base=0):
    return pl.BlockSpec((rows, width), lambda i: (base + i, 0))


def params(**kw):
    return pltpu.CompilerParams(vmem_limit_bytes=58 * MIB, **kw)


def count_of(pieces):
    return sum(piece.shape[0] for piece in pieces)


def highway_forward(table, pieces, block_rows, bias, own, mate, chunk, words):
    width = own[0].shape[1]
    half = width * len(own)
    rows = min(ROWS, words)
    steps = words // rows
    tile = by_rows(rows, width, chunk * steps)
    out = by_rows(rows, half)
    return pl.pallas_call(
        functools.partial(forward_kernel, len(own), len(pieces), block_rows, width),
        grid=(steps,),
        in_specs=[SMEM_SPEC, whole(bias)] + [tile] * (2 * len(own)) + [ANY_SPEC] * len(pieces),
        out_specs=[out] * 5,
        out_shape=[jax.ShapeDtypeStruct((words, half), kind) for kind in (F32, BF16, BF16, BF16, BF16)],
        scratch_shapes=[pltpu.VMEM((2, 2 * half, half), BF16), pltpu.SemaphoreType.DMA((count_of(pieces),))],
        compiler_params=params(),
        cost_estimate=lasting(10),
        name="highway_forward",
    )(table, bias, *own, *mate, *pieces)


def highway_turn(table, pieces, block_rows, bias, own, mate, exact, out_grad, proj, width):
    words, half = own.shape
    out_width = out_grad.shape[1]
    rows = min(ROWS, words)
    tile = by_rows(rows, half)
    packed = proj is None
    scratch = [pltpu.VMEM((2, 2 * half, half), BF16), pltpu.SemaphoreType.DMA((count_of(pieces),))]
    if packed:
        scratch += [pltpu.VMEM((half, out_width), BF16), pltpu.SemaphoreType.DMA((2 * count_of(pieces),))]
    return pl.pallas_call(
        functools.partial(turn_kernel, len(pieces), block_rows, width, packed),
        grid=(words // rows,),
        in_specs=[SMEM_SPEC, whole(bias), tile, tile, tile, by_rows(rows, out_width)]
        + ([] if packed else [whole(proj)])
        + [ANY_SPEC] * len(pieces),
        out_specs=[tile] * 5 + [by_rows(rows, out_width), pl.BlockSpec((2, half), lambda i: (0, 0))],
        out_shape=[jax.ShapeDtypeStruct((words, half), kind) for kind in (BF16, BF16, BF16, F32, BF16)]
        + [jax.ShapeDtypeStruct((words, out_width), F32), jax.ShapeDtypeStruct((2, half), F32)],
        scratch_shapes=scratch,
        compiler_params=params(),
        cost_estimate=lasting(16),
        name="highway_turn",
    )(table, bias, own, mate, exact, out_grad, *([] if packed else [proj]), *pieces)


def highway_slopes(table, pieces, block_rows, partial, arrived, first, second, gate, width):
    words, half = partial.shape
    rows = min(ROWS, words)
    tile = by_rows(rows, half)
    return pl.pallas_call(
        functools.partial(slope_kernel, len(pieces), block_rows, width),
        grid=(words // rows,),
        in_specs=[SMEM_SPEC] + [tile] * 5 + [ANY_SPEC] * len(pieces),
        out_specs=[tile, tile, tile, tile, pl.BlockSpec((2, half), lambda i: (0, 0))],
        out_shape=[jax.ShapeDtypeStruct((words, half), kind) for kind in (BF16, BF16, F32, BF16)] + [jax.ShapeDtypeStruct((2, half), F32)],
        scratch_shapes=[pltpu.VMEM((2, half, half), BF16), pltpu.SemaphoreType.DMA((count_of(pieces),))],
        compiler_params=params(),
        cost_estimate=lasting(8),
        name="highway_slopes",
    )(table, partial, arrived, first, second, gate, *pieces)


def highway_back(table, pieces, block_rows, d_first, d_gate, up):
    words, width = d_first.shape
    rows = min(ROWS, words)
    tile = by_rows(rows, width)
    return pl.pallas_call(
        functools.partial(back_kernel, len(pieces), block_rows),
        grid=(words // rows,),
        in_specs=[SMEM_SPEC, tile, tile, tile] + [ANY_SPEC] * len(pieces),
        out_specs=tile,
        out_shape=jax.ShapeDtypeStruct((words, width), F32),
        scratch_shapes=[pltpu.VMEM((2, width, width), BF16), pltpu.SemaphoreType.DMA((count_of(pieces),))],
        compiler_params=params(),
        cost_estimate=lasting(6),
        name="highway_back",
    )(table, d_first, d_gate, up, *pieces)


def highway_weight_grad(table, xs, d_first, d_gate, rows, width):
    half = d_first[0].shape[1]
    words = sum(d.shape[0] for d in d_first)
    flat = [x for row in xs for x in row]
    steps = table.shape[1]
    blocks = half // width
    block = pl.BlockSpec((1, 2, rows, width), lambda i: (i, 0, 0, 0))
    return pl.pallas_call(
        functools.partial(weight_grad_kernel, len(xs), len(xs[0]), len(d_first), width),
        grid=(steps,),
        in_specs=[SMEM_SPEC] + [whole(x) for x in flat] + [whole(d) for d in d_first + d_gate],
        out_specs=[block] * blocks + [pl.BlockSpec((blocks, 1, 2, rows, width), lambda i: (0, i, 0, 0, 0))],
        out_shape=[jax.ShapeDtypeStruct((steps, 2, rows, width), BF16)] * blocks
        + [jax.ShapeDtypeStruct((blocks, steps, 2, rows, width), BF16)],
        scratch_shapes=[pltpu.VMEM((2 * half, words), BF16)],
        compiler_params=params(),
        cost_estimate=lasting(15),
        name="highway_weight_grad",
    )(table, *flat, *d_first, *d_gate)


def adam_update(weight, grad, moment_one, moment_two, rate):
    first_new = beta_one * moment_one + (1 - beta_one) * grad
    second_new = beta_two * moment_two + (1 - beta_two) * grad * grad
    corrected_one = first_new / (1 - beta_one**STEP)
    corrected_two = second_new / (1 - beta_two**STEP)
    updated = weight - rate * (
        corrected_one / (jnp.sqrt(corrected_two) + adam_eps) + decay_rate * weight
    )
    return (second_new, updated)


def owner_kernel(n_grads, at_ref, *refs):
    grads, refs = refs[:n_grads], refs[n_grads:]
    weight, one, two, average = refs[:4]
    grad, second, new, average_new = refs[-4:]
    width = grads[0].shape[2]
    for j, ref in enumerate(grads):
        at = pl.ds(pl.multiple_of(at_ref[j], LANES), width)
        grad[:, :, at] = ref[...].astype(F32)
    second_new, updated = adam_update(weight[...], grad[...], one[...], two[...], 0.02)
    second[...] = second_new
    new[...] = updated
    average_new[...] = average_keep * average[...] + (1 - average_keep) * updated


def owner_update(slot, at, grads, weight, one, two, average, so_far=()):
    slots, rows, width = grads[0].shape
    part = min(64, rows)
    block = pl.BlockSpec((1, part, weight.shape[2]), lambda i: (slot, i, 0))
    given = len(grads) + 5
    return pl.pallas_call(
        functools.partial(owner_kernel, len(grads)),
        grid=(rows // part,),
        in_specs=[SMEM_SPEC]
        + [pl.BlockSpec((1, part, width), lambda i: (slot, i, 0))] * len(grads)
        + [block] * 4
        + [ANY_SPEC] * len(so_far),
        out_specs=[block] * 4,
        out_shape=[jax.ShapeDtypeStruct(weight.shape, F32)] * 4,
        input_output_aliases={given + n: n for n in range(len(so_far))},
        compiler_params=params(),
        cost_estimate=lasting(8),
        name="owner_update",
    )(at, *grads, weight, one, two, average, *so_far)


def choose_kernel(n_from, table_ref, proj, *refs):
    arrived, outs = refs[:n_from], refs[n_from:]
    rows, width = arrived[0].shape[1:]
    for unit in range(UNITS):
        for step, ref in enumerate(arrived):

            @pl.when(table_ref[0, unit] == step)
            def _(ref=ref, unit=unit):
                outs[unit // 2][unit % 2, :rows, :] = ref[table_ref[1, unit]]

    under, part = proj.shape[0], proj.shape[1] // 2
    if outs[1].shape[1] > rows:
        outs[1][:, rows:, :] = jnp.zeros((2, under, width), BF16)
        for side in range(2):
            outs[1][side, rows:, :part] = proj[:, side * part : (side + 1) * part].astype(BF16)


def choose_units(table, arrived, proj, packed):
    slots, rows, width = arrived[0].shape
    shapes = [(2, rows, width), (2, rows + (proj.shape[0] if packed else 0), width)]
    return pl.pallas_call(
        functools.partial(choose_kernel, len(arrived)),
        grid=(1,),
        in_specs=[SMEM_SPEC, whole(proj)] + [whole(part) for part in arrived],
        out_specs=[pl.BlockSpec(shape, lambda i: (0, 0, 0)) for shape in shapes],
        out_shape=[jax.ShapeDtypeStruct(shape, BF16) for shape in shapes],
        compiler_params=params(),
        cost_estimate=lasting(3),
        name="choose_units",
    )(table, proj, *arrived)


def return_kernel(counts, table_ref, *refs):
    layers = (refs[: counts[0]], refs[counts[0] : counts[0] + counts[1]])
    for step, out in enumerate(refs[counts[0] + counts[1] :]):
        for slot in range(SLOTS):
            taken = table_ref[step, slot]
            for unit in range(UNITS):

                @pl.when(taken == unit)
                def _(unit=unit, out=out, slot=slot):
                    out[slot] = sum(ref[unit % 2].astype(F32) for ref in layers[unit // 2]).astype(BF16)

            @pl.when(taken < 0)
            def _(out=out, slot=slot):
                out[slot] = jnp.zeros(out.shape[1:], BF16)


def return_units(table, layers, count):
    shape = layers[0][0].shape
    part = min(64, shape[1])
    block = pl.BlockSpec((2, part, shape[2]), lambda i: (0, i, 0))
    terms = list(layers[0]) + list(layers[1])
    return pl.pallas_call(
        functools.partial(return_kernel, [len(layer) for layer in layers]),
        grid=(shape[1] // part,),
        in_specs=[SMEM_SPEC] + [block] * len(terms),
        out_specs=[block] * count,
        out_shape=[jax.ShapeDtypeStruct(shape, BF16)] * count,
        compiler_params=params(),
        cost_estimate=lasting(3),
        name="return_units",
    )(table, *terms)


class Places:
    def __init__(self):
        self.n_filt, self.n_dp = lax.axis_size("filt"), lax.axis_size("dp")
        self.n_y, self.n_z = self.n_filt // 2, self.n_dp // 2
        self.f, self.d = lax.axis_index("filt"), lax.axis_index("dp")
        self.y, self.x = self.f // 2, self.f % 2
        self.z, self.c = self.d // 2, self.d % 2
        self.direct = self.n_y == 2 and self.n_z == 4

    def over_filt(self, value, step):
        return lax.ppermute(value, "filt", [(i, i ^ step) for i in range(self.n_filt)])

    def over_x(self, value):
        return self.over_filt(value, 1)

    def over_y(self, value, step):
        return self.over_filt(value, 2 * step)

    def over_core(self, value):
        return lax.ppermute(value, "dp", [(i, i ^ 1) for i in range(self.n_dp)])

    def over_z(self, value, step):
        pairs = [(i, (i // 2 + step) % self.n_z * 2 + i % 2) for i in range(self.n_dp)]
        return lax.ppermute(value, "dp", pairs)

    def far_first(self):
        return sorted(range(1, self.n_z), key=lambda k: (min(k, self.n_z - k), k))

    def row_of(self, d, rows, width):
        f = d * rows // width
        half = self.n_y * width
        return (f % 2 ^ self.x) * half + (f // 2 ^ self.y) * width + d * rows % width


def after(value, *earlier):
    return lax.optimization_barrier((value, earlier))[0]


def settle(*values):
    return lax.optimization_barrier(values)


def gather_general(place, blocks):
    rows, width = blocks[0].shape[1:]
    out = []
    for piece in blocks:
        spread = lax.all_gather(lax.all_gather(piece, "dp"), "filt")
        spread = spread.reshape((place.n_y, 2) + spread.shape[1:])
        spread = lax.dynamic_index_in_dim(spread, place.x, 1, keepdims=False)
        spread = spread.reshape((place.n_y * place.n_dp,) + piece.shape)
        d = jnp.tile(jnp.arange(place.n_dp, dtype=jnp.int32), place.n_y)
        y = jnp.repeat(jnp.arange(place.n_y, dtype=jnp.int32), place.n_dp)
        table = jnp.stack([place.row_of(d, rows, width), (y ^ place.y) * width]).astype(jnp.int32)
        out.append((table, [spread]))
    return out


BLOCK_STEPS = (
    [(0, 0), (0, 1), (1, 0), (3, 0), (2, 0), (1, 1), (3, 1), (2, 1)],
    [(0, 0), (0, 1), (1, 0), (3, 0), (1, 1), (3, 1), (2, 0), (2, 1)],
)


def gather_table(place, layer, rows, width, rows_proj):
    at_rows, at_cols, at_proj = [], [], []
    for other in range(2):
        for k, step in BLOCK_STEPS[layer]:
            d = (place.z - k) % place.n_z * 2 + (place.c ^ other)
            at_rows.append(place.row_of(d, rows, width))
            at_cols.append(jnp.int32(step * width))
            at_proj.append(step * width + d * rows_proj)
    return jnp.stack([jnp.stack(at_rows), jnp.stack(at_cols), jnp.stack(at_proj)]).astype(jnp.int32)


def sum_table(place, rows, width):
    z = jnp.arange(place.n_z, dtype=jnp.int32)
    z, c = ((place.z + z) % place.n_z, place.c) if place.direct else (z, 0)
    return jnp.stack([place.row_of(z * 2 + c, rows, width), place.row_of(z * 2 + (1 - c), rows, width)]).astype(jnp.int32)


def sent_over_y(parts, group):
    near, arrived = parts
    return jnp.stack([(near[1][k].astype(F32) + arrived[1][k].astype(F32)).astype(BF16) for k in group])


def kept_over_y(parts, turned, group):
    near, arrived = parts
    return [near[0][k].astype(F32) + arrived[0][k].astype(F32) + turned[n].astype(F32) for n, k in enumerate(group)]


def sum_general(place, blocks):
    n_y = place.n_y
    near, far = blocks[:n_y], list(blocks[n_y])
    steps = jnp.arange(n_y, dtype=jnp.int32) ^ place.y
    pairs = jnp.stack([jnp.stack(near), jnp.stack(far)], axis=2)
    pairs = jnp.take(pairs, steps, axis=0)
    pairs = pairs.reshape((n_y, place.n_dp) + pairs.shape[3:])
    mine = lax.psum_scatter(pairs, "dp", scatter_dimension=1)
    sides = jnp.arange(2, dtype=jnp.int32).reshape(1, 2, 1, 1, 1)
    mine = jnp.where(sides == place.x, mine[:, None], jnp.zeros((), BF16))
    mine = mine.reshape((place.n_filt,) + mine.shape[2:])
    return lax.psum_scatter(mine, "filt", scatter_dimension=0).astype(F32)


def pick(array, at, axis=0):
    return lax.dynamic_index_in_dim(array, at, axis, keepdims=False)


def rows_over_core(place, value):
    parts = value.reshape((place.n_z, 2, -1) + value.shape[1:])
    return pick(parts, place.c, 1), over_core_low(place, pick(parts, 1 - place.c, 1))


def over_core_low(place, value):
    return place.over_core(value.astype(BF16))


def swap_z(place, value, step):
    pairs = [(i, i ^ (2 * step)) for i in range(place.n_dp)]
    return lax.ppermute(value, "dp", pairs)


def swap_rows(place, parts, step):
    upper = place.z // step % 2
    halves = parts.reshape((2, -1) + parts.shape[1:])
    return pick(halves, upper), swap_z(place, pick(halves, 1 - upper).astype(BF16), step)


def sum_filt(place, value):
    if not place.direct:
        return lax.psum(value, "filt")
    step = 1
    while step < place.n_filt:
        value = value + place.over_filt(value, step)
        step *= 2
    return value


def per_device(
    char_ids,
    word_lengths,
    out_grad,
    highway_owner,
    char_table,
    conv_weight,
    conv_bias,
    highway_weight,
    proj_weight,
    dense_bias,
    table_moment_one,
    table_moment_two,
    conv_moment_one,
    conv_moment_two,
    conv_bias_moment_one,
    conv_bias_moment_two,
    highway_moment_one,
    highway_moment_two,
    highway_average,
    proj_moment_one,
    proj_moment_two,
    bias_moment_one,
    bias_moment_two,
):
    place = Places()
    n_y, n_filt, direct = place.n_y, place.n_filt, place.direct
    width = conv_weight.shape[1]
    rows, width_full = highway_weight.shape[1:]
    half = width_full // 2
    rows_proj, out_width = proj_weight.shape
    vocab_count = char_table.shape[0]
    words_dev = char_ids.shape[0]
    words_y = words_dev // n_y
    chunks, chunk_words = range(2), words_y // 2
    steps_y = list(range(1, n_y))
    slot_index = unit_slots(highway_owner, SLOTS)
    mine_first = place.x == 0
    over_core, over_x, over_y, over_z = place.over_core, place.over_x, place.over_y, place.over_z

    widths = channel_widths(place.f * width, width, FILTERS)
    offsets = jnp.arange(TAPS, dtype=jnp.int32) // CHAR_DIM
    tap_mask = (offsets[:, None] < widths[None, :]).astype(jnp.float32)
    tile = min(256, words_dev)
    n_tiles = words_dev // tile
    cuts = [0, 1, 2, 4, 8] if n_tiles == 8 else [0, n_tiles]
    splits = list(zip(cuts[:-1], cuts[1:]))
    rank, data, table_t, conv_t, conv_back, width_col, narrow = conv_operands(
        char_ids, word_lengths, char_table, conv_weight, conv_bias, widths, width
    )
    rank_parts = [lax.dynamic_slice_in_dim(rank, (place.y ^ step) * words_y, words_y, axis=0) for step in range(n_y)]

    def convolve(some, narrow):
        return [conv_forward(rank, data, table_t, conv_t, width_col, narrow, width, begin, end - begin) for begin, end in some]

    def block_of(step):
        start = (place.f ^ step) * width
        return lax.dynamic_slice_in_dim(highway_weight, start, width, axis=2).astype(BF16)

    from_owner = [block_of(0)] + [place.over_filt(block_of(step), step) for step in range(1, n_filt)]
    kept = convolve(splits[: len(splits) // 2], narrow)
    from_owner, kept, narrow = settle(from_owner, kept, narrow)
    owner_table = jnp.stack([highway_owner ^ place.f, slot_index % SLOTS])
    blocks = choose_units(owner_table, from_owner, proj_weight, direct)
    bias_float = lax.reduce_precision(dense_bias, 8, 7)

    def half_bias(unit):
        starts = [unit * width_full + (2 * (place.y ^ step) + place.x) * width for step in range(n_y)]
        return jnp.concatenate([lax.dynamic_slice_in_dim(bias_float, start, width) for start in starts])

    layer_bias = [jnp.stack([half_bias(2 * layer), half_bias(2 * layer + 1)]) for layer in range(2)]

    blocks, narrow, sent = settle(blocks, narrow, out_grad)
    grad_mate = over_x(sent)
    if direct:
        first_y = [over_y(block, 1) for block in blocks]
        near = [over_z(blocks[0], k) for k in (1, 3)]
    kept = kept + convolve(splits[len(splits) // 2 :], narrow)
    placed = [place_words(part, [parts[0] for parts in kept]) for part in rank_parts]
    own = [placed[0]] + [over_y(placed[step], step) for step in steps_y]
    if direct:
        near, first_y, placed, grad_mate, blocks = settle(near, first_y, placed, grad_mate, blocks)
        own = [placed[0], over_y(placed[1], 1)]
        mate = [over_x(placed[0])]
        far = over_z(blocks[0], 2)
        own, mate, far, near, blocks, first_y, layer_bias, grad_mate = settle(
            own, mate, far, near, blocks, first_y, layer_bias, grad_mate
        )

        out_grads = [jnp.where(mine_first, out_grad, grad_mate), jnp.where(mine_first, grad_mate, out_grad)]
        sent = jnp.stack([near[0], near[1], far])
        sent_y = over_y(sent, 1)
        mate = mate + [over_x(own[1])]
        near_one = [over_z(blocks[1], k) for k in (1, 3)]
        sent_core = over_core(sent)
        start = jnp.stack([blocks[0], first_y[0]])
        sent_y, sent_core, start, mate, near_one, blocks = settle(sent_y, sent_core, start, mate, near_one, blocks)

        table = [gather_table(place, layer, rows, width, rows_proj) for layer in range(2)]
        gathered = [(table[0], [start, sent, sent_y, over_core(start), sent_core, over_core(sent_y)], rows)]
        far_one = over_z(blocks[1], 2)
        near_y = over_y(jnp.stack(near_one), 1)
    else:
        mate = [over_x(part) for part in own]
        gathered = [(*found, rows) for found in gather_general(place, blocks)]
        out_grads = [jnp.where(mine_first, out_grad, grad_mate), jnp.where(mine_first, grad_mate, out_grad)]

    forward, x_one_mate = [], []
    for chunk in chunks:
        forward.append(highway_forward(*gathered[0], layer_bias[0], own, mate, chunk, chunk_words))
        x_one_mate.append(over_x(forward[chunk][1]))
        if direct and chunk == 0:
            forward[0], near_one, layer_bias[0] = settle(forward[0], near_one, layer_bias[0])
            start = jnp.stack([blocks[1], first_y[1], near_one[0], near_one[1]])
            start_core = over_core(start)
    if direct:
        far_one, near_y, forward[1] = settle(far_one, near_y, forward[1])
        far_y = over_y(far_one, 1)
        far_y, x_one_mate[0] = settle(far_y, x_one_mate[0])
        last = jnp.stack([near_y[0], near_y[1], far_one, far_y])
        gathered.append((table[1], [start, last, start_core, over_core(last)], rows))
        proj_half = None
    else:
        proj_own = jnp.stack([proj_weight.astype(BF16)] + [over_y(proj_weight.astype(BF16), step) for step in steps_y])
        proj_half = lax.all_gather(proj_own, "dp", axis=1).reshape(half, out_width)
    x_one, x_one_low, first_zero, second_zero, gate_zero = zip(*forward)
    turned, arrived = [], []
    for chunk in chunks:
        bias_one = layer_bias[1] if chunk == 0 else settle(layer_bias[1], turned[0])[0]
        turned.append(
            highway_turn(*gathered[1], bias_one, x_one_low[chunk], x_one_mate[chunk], x_one[chunk], out_grads[chunk], proj_half, width)
        )
        arrived.append(over_x(turned[chunk][4]))
    x_two_low, d_first_one, d_gate_one, up_one, _, vectors, sums = (list(parts) for parts in zip(*turned))
    sums_one = sums[0] + sums[1]

    targets = sum_table(place, rows, width)
    blocks = highway_weight_grad(
        targets, [[x_one_low[chunk], x_one_mate[chunk]] for chunk in chunks], d_first_one, d_gate_one, rows, width
    )
    blocks, up_one[0], arrived[0] = settle(blocks, up_one[0], arrived[0])
    if not direct:
        sum_one = sum_general(place, blocks)

    partial, parts_zero, arrived_zero = [], [], []
    for chunk in chunks:
        partial.append(highway_back(*gathered[1], d_first_one[chunk], d_gate_one[chunk], up_one[chunk]))
        if chunk == 0 and direct:
            partial[0], arrived[1], blocks = settle(partial[0], arrived[1], blocks)
            one = (blocks[:2], over_core(blocks[2]))
        parts_zero.append(
            highway_slopes(*gathered[0], partial[chunk], arrived[chunk], first_zero[chunk], second_zero[chunk], gate_zero[chunk], width)
        )
        if chunk == 0 and direct:
            one, parts_zero[0], up_one[1] = settle(one, parts_zero[0], up_one[1])
            sent = sent_over_y(one, range(place.n_z))
            sent, up_one[1] = settle(sent, up_one[1])
            one_y = over_y(sent, 1)
        arrived_zero.append(over_x(parts_zero[chunk][3]))
    d_first, d_gate, up, _, sums = (list(parts) for parts in zip(*parts_zero))
    sums_zero = sums[0] + sums[1]
    blocks = highway_weight_grad(targets, [own + mate], d_first, d_gate, rows, width)
    blocks, up, arrived_zero[0] = settle(blocks, up, arrived_zero[0])
    groups = [[2, 1], [3, 0]]
    if not direct:
        sum_zero = sum_general(place, blocks)
    partial = [highway_back(*gathered[0], d_first[chunk], d_gate[chunk], up[chunk]) for chunk in chunks]
    if direct:
        partial, blocks, arrived_zero[1], one_y = settle(partial, blocks, arrived_zero[1], one_y)
        zero = (blocks[:2], over_core(blocks[2]))
    if direct:
        one_here = kept_over_y(one, one_y, range(place.n_z))
        one_sent = [one_here[k].astype(BF16) for k in (2, 1, 3)]
        one_here = one_here[0]
        one_sent, one_here, partial = settle(one_sent, one_here, partial)
        one_z = [over_z(value, k) for value, k in zip(one_sent, (2, 1, 3))]
    groups = [[2, 1], [3, 0]]
    if not direct:
        sum_zero = sum_general(place, blocks)
    partial = [highway_back(*gathered[0], d_first[chunk], d_gate[chunk], up[chunk]) for chunk in chunks]
    if direct:
        partial, blocks, arrived_zero[1], one_y = settle(partial, blocks, arrived_zero[1], one_y)
        zero = (blocks[:2], over_core(blocks[2]))
    feature_grad = []
    for step in range(n_y):
        cols = slice(step * width, (step + 1) * width)
        feature_grad.append(
            jnp.concatenate(
                [(partial[chunk][:, cols] + arrived_zero[chunk][:, cols].astype(F32)).astype(BF16) for chunk in chunks]
            )
        )
    groups = [[2, 1], [3, 0]]
    returned = [over_y(value, step) if step else value for step, value in enumerate(feature_grad)]
    if direct:
        returned[0], x_two_low, vectors = settle(returned[0], x_two_low, vectors)
        zero_y = [over_y(sent_over_y(zero, groups[0]), 1)]
    proj_part = (tn(x_two_low[0], out_grads[0]) + tn(x_two_low[1], out_grads[1])).reshape(n_y, width, out_width)
    proj_here, proj_away = proj_part[0], [proj_part[step].astype(BF16) for step in steps_y]
    vectors_away = jnp.where(mine_first, vectors[1], vectors[0]).astype(BF16)
    vectors_here = jnp.where(mine_first, vectors[0], vectors[1])
    ranks = [part.T for part in rank_parts]

    wanted = (place.f ^ jnp.arange(n_filt, dtype=jnp.int32))[:, None] * SLOTS + jnp.arange(SLOTS, dtype=jnp.int32)[None, :]
    fits = slot_index[None, None, :] == wanted[:, :, None]
    return_table = jnp.max(jnp.where(fits, jnp.arange(UNITS, dtype=jnp.int32), -1), axis=2)
    if direct:
        returned, narrow, ranks = settle(returned, narrow, ranks)

    def convolve_back(n, narrow, so_far):
        (begin, _), (_, lse, sorted_ids, embedded) = splits[n], kept[n]
        return conv_backward(
            ranks, sorted_ids, embedded, table_t.shape[1], conv_t, conv_back, width_col, narrow, lse, returned, width, begin, tile, so_far
        )

    home = jnp.arange(n_filt, dtype=jnp.int32)

    def natural(values):
        parts = values.reshape(n_y, 1, width)
        out = jnp.zeros((n_filt, width), F32)
        for step in range(n_y):
            out = jnp.where((home == 2 * (place.y ^ step) + place.x)[:, None], parts[step], out)
        return out.reshape(-1)

    bias_local = jnp.concatenate(
        [natural(sums[unit]) for sums in (sums_zero, sums_one) for unit in range(2)] + [jnp.sum(out_grad, axis=0, dtype=F32)]
    )
    table_rows = table_t.shape[1] // LANES * CHAR_DIM
    bias_rows = -(-bias_local.size // DEPTH)
    bias_rows += -(width + table_rows + bias_rows) % 16
    bias_flat = jnp.pad(bias_local, (0, bias_rows * DEPTH - bias_local.size)).reshape(bias_rows, DEPTH)
    small = jnp.concatenate([jnp.zeros((width + table_rows, DEPTH), F32), bias_flat])
    if direct:
        small, returned, narrow = settle(small, returned, narrow)
    back = small
    for n in range(len(splits)):
        back = convolve_back(n, narrow, back)
        if direct and n == 0:
            back, narrow, one_z, zero_y[0], zero, vectors_away, proj_away = settle(
                back, narrow, one_z, zero_y[0], zero, vectors_away, proj_away
            )
            zero_here = kept_over_y(zero, zero_y[0], groups[0])
            zero_z, zero_sent, narrow = settle([value.astype(BF16) for value in zero_here], sent_over_y(zero, groups[1]), narrow)
            zero_z = [over_z(value, k) for value, k in zip(zero_z, groups[0])]
            zero_y.append(over_y(zero_sent, 1))
            proj_y = over_y(proj_away[0], 1)
            vectors_arrived = over_x(vectors_away)
        if direct and n == 2:
            back, zero_z, narrow, zero_y, vectors_arrived, proj_y = settle(back, zero_z, narrow, zero_y, vectors_arrived, proj_y)
            last, zero_here = kept_over_y(zero, zero_y[1], groups[1])
            last, zero_here, narrow = settle(last.astype(BF16), zero_here, narrow)
            last = over_z(last, 3)
            proj_rows = rows_over_core(place, proj_here + proj_y.astype(F32))
    if direct:
        back, last, proj_rows = settle(back, last, proj_rows)
        slot_grads = return_units(return_table, [[zero_here] + zero_z + [last], [one_here] + one_z], n_filt)
    else:
        proj_y = [over_y(value, step) for value, step in zip(proj_away, steps_y)]
        proj_grad = lax.psum_scatter(proj_here + sum(value.astype(F32) for value in proj_y), "dp", scatter_dimension=0, tiled=True)
    if not direct:
        vectors_arrived = over_x(vectors_away)
    small = back
    if direct:
        small = small + over_core(small)
    else:
        small = lax.psum(small, "dp")
        small = jnp.concatenate([small[:width], sum_filt(place, small[width:])])

    optimizer = (highway_weight, highway_moment_one, highway_moment_two, highway_average)
    columns = (place.f ^ jnp.arange(n_filt, dtype=jnp.int32)) * width
    if direct:
        slot_grads, small, proj_rows, vectors_arrived = settle(slot_grads, small, proj_rows, vectors_arrived)
        arrived_slots = [place.over_filt(slot_grads[step], step) for step in range(1, n_filt)]
        small = small + swap_z(place, small.astype(BF16), 1).astype(F32)
        small = small + swap_z(place, small.astype(BF16), 2).astype(F32)
        small, arrived_slots = settle(small, arrived_slots)
        conv_sums, small = small[:width], small[width:]
        slot_grads = [slot_grads[0]] + arrived_slots
        small = small + over_x(small)
        proj_rows = swap_rows(place, proj_rows[0] + proj_rows[1].astype(F32), 2)
        updates = owner_update(0, columns, slot_grads, *optimizer)
        updates, small, proj_rows, slot_grads = settle(updates, small, proj_rows, slot_grads)
        small = small + over_y(small, 1)
        proj_rows = swap_rows(place, proj_rows[0] + proj_rows[1].astype(F32), 1)
        updates = owner_update(1, columns, slot_grads, *optimizer, updates)
        updates, small, proj_rows = settle(updates, small, proj_rows)
        proj_grad = (proj_rows[0] + proj_rows[1].astype(F32)).reshape(rows_proj, out_width)
    else:
        slot_grads = return_units(return_table, [[sum_zero], [sum_one]], n_filt)
        slot_grads = [slot_grads[0]] + [place.over_filt(slot_grads[step], step) for step in range(1, n_filt)]
        conv_sums, small = small[:width], small[width:]
        updates = owner_update(0, columns, slot_grads, *optimizer)
        updates = owner_update(1, columns, slot_grads, *optimizer, updates)
    highway_grad, highway_second, highway_new, highway_average_new = updates
    word_vectors = vectors_here + vectors_arrived.astype(F32) + bias_float[UNITS * width_full :]
    conv_grad, conv_bias_grad = conv_sums[:, :TAPS].T * tap_mask, conv_sums[:, TAPS]
    table_grad = small[:table_rows].reshape(-1, CHAR_DIM, LANES).transpose(0, 2, 1).reshape(-1, CHAR_DIM)[:vocab_count]
    bias_grad = small[table_rows:].reshape(-1)[: bias_local.size]
    table_second, table_new = adam_update(
        char_table, table_grad, table_moment_one, table_moment_two, 1.0
    )
    conv_second, conv_new = adam_update(
        conv_weight, conv_grad, conv_moment_one, conv_moment_two, 0.1
    )
    conv_bias_second, conv_bias_new = adam_update(
        conv_bias, conv_bias_grad, conv_bias_moment_one, conv_bias_moment_two, 0.3
    )
    proj_second, proj_new = adam_update(
        proj_weight, proj_grad, proj_moment_one, proj_moment_two, 0.02
    )
    bias_second, bias_new = adam_update(
        dense_bias, bias_grad, bias_moment_one, bias_moment_two, 0.3
    )
    return (
        word_vectors,
        table_grad,
        table_second,
        table_new,
        conv_grad,
        conv_second,
        conv_new,
        conv_bias_grad,
        conv_bias_second,
        conv_bias_new,
        highway_grad,
        highway_second,
        highway_new,
        highway_average_new,
        proj_grad,
        proj_second,
        proj_new,
        bias_grad,
        bias_second,
        bias_new,
    )


def solution(mesh):
    return jax.shard_map(
        per_device,
        mesh=mesh,
        in_specs=(
            P("dp", None),
            P("dp"),
            P(("dp", "filt"), None),
            P(),
            P(),
            P(None, "filt"),
            P("filt"),
            P("filt", "dp", None),
            P(("filt", "dp"), None),
            P(),
            P(),
            P(),
            P(None, "filt"),
            P(None, "filt"),
            P("filt"),
            P("filt"),
            P("filt", "dp", None),
            P("filt", "dp", None),
            P("filt", "dp", None),
            P(("filt", "dp"), None),
            P(("filt", "dp"), None),
            P(),
            P(),
        ),
        out_specs=(
            P(("dp", "filt"), None),
            P(),
            P(),
            P(),
            P(None, "filt"),
            P(None, "filt"),
            P(None, "filt"),
            P("filt"),
            P("filt"),
            P("filt"),
            P("filt", "dp", None),
            P("filt", "dp", None),
            P("filt", "dp", None),
            P("filt", "dp", None),
            P(("filt", "dp"), None),
            P(("filt", "dp"), None),
            P(("filt", "dp"), None),
            P(),
            P(),
            P(),
        ),
        check_vma=False,
    )
```

time: 758 us -> 529 us (0.70)
  blocking collectives: 61.2 us -> 0 us
  Pallas kernels: 324 us -> 268 us
  waiting for transfers between devices: 159 us -> 113 us
  between operations: 35 us -> 3.44 us
  starting transfers between devices: 83 us -> 53.3 us
    ppermute x33 -> x29, waiting for transfers between devices: 111 us -> 42.2 us  [over_filt(): lax.ppermute(value, 'filt', [(i, i ^ step) for i in range(self.n_filt)])]
    pallas_call x1 -> x4, Pallas kernels: 127 us -> 61.1 us  [conv_backward(): pl.pallas_call(functools.partial(conv_backward_kernel, cblock, len(ranks)...]
    psum x1 -> x0, blocking collectives: 42.2 us -> none  [per_device(): table_grad, bias_grad = lax.psum((table_local, bias_local), ('filt', 'dp'))]
    ppermute x12, starting transfers between devices: 39.8 us -> 12.7 us  [over_z(): return lax.ppermute(value, 'dp', pairs)]
    all_gather x1 -> x0, blocking collectives: 19.1 us -> none  [per_device(): lax.all_gather(proj_weight.astype(BF16), 'dp', axis=0, tiled=True)]
    ppermute x12, waiting for transfers between devices: 43.1 us -> 57.8 us  [over_z(): return lax.ppermute(value, 'dp', pairs)]
    ppermute x0 -> x4, waiting for transfers between devices: none -> 12.5 us  [swap_z(): return lax.ppermute(value, 'dp', pairs)]
    unnamed x163 -> x224, local copies, waits for them, and re-layouts: 8.07 us -> 19 us
  transfers between devices with their start and end apart: 67 -> 54, of which waited for: 18 -> 13; matrix products, arithmetic and copies ran while one was open for 9% -> 9% of each run, Pallas kernels for 38% -> 51%
where the time goes in v2:
time: 529 us; the launch traced here: 522 us
  Pallas kernels  268 us (51%)
  waiting for transfers between devices  113 us (21%)
  other arithmetic  54.2 us (10%)
  starting transfers between devices  53.3 us (10%)
  local copies, waits for them, and re-layouts  28.6 us (5%)
    pallas_call x4, Pallas kernels, conv_backward(): pl.pallas_call(functools.partial(conv_backward_kernel, cblock, len(ranks)...  61.1 us
    ppermute x12, waiting for transfers between devices, over_z(): return lax.ppermute(value, 'dp', pairs)  57.8 us
    ppermute x29, waiting for transfers between devices, over_filt(): lax.ppermute(value, 'filt', [(i, i ^ step) for i in range(self.n_filt)])  42.2 us
    pallas_call x4, Pallas kernels, conv_forward(): pl.pallas_call(functools.partial(conv_forward_kernel, cblock, base), grid...  41.8 us
    ppermute x29, starting transfers between devices, over_filt(): lax.ppermute(value, 'filt', [(i, i ^ step) for i in range(self.n_filt)])  34.1 us
    pallas_call x2, Pallas kernels, highway_turn(): pl.pallas_call(functools.partial(turn_kernel, len(pieces), block_rows, wi...  32.7 us
    pallas_call x4, Pallas kernels, highway_back(): pl.pallas_call(functools.partial(back_kernel, len(pieces), block_rows), g...  30.8 us
    pallas_call x2, Pallas kernels, highway_weight_grad(): pl.pallas_call(functools.partial(weight_grad_kernel, len(xs), len(xs[0]),...  30.3 us
  transfers between devices with their start and end apart: 54, of which 13 were waited for; matrix products, arithmetic and copies ran while one was open for 9% of the time, Pallas kernels for 51%

profile of v2, /device:TPU:0, one launch (start us, length us, event | category | flops | bytes accessed | tf_op | source)
XLA Modules:
  0.0 522.2 jit_solution(651444362237247639)
XLA Ops:
  0.7 3.7 dynamic-slice_convert_fusion
  4.4 3.9 collective-permute-start.2
  8.9 1.8 convert_reduce_fusion
  12.5 7.4 %conv_forward.5 = (bf16[512,256]{1,0:T(8,128)(2,1)S(1)}, f32[512,256]{1,0:T(8,128)S(1)}, f32[64,256]{1,0:T(8,128)S(1)}, bf16[1024,256]{1,0:T(8,128)(2,1)S(1)}) custom-call(s32[1]{0:T(128)} %slice.281.narrow_ref, s32[2048,1]{1,0:T(8,128)S(1)} %copy.98.rank_ref, bf16[64,2048]{1,0:T(8,128)(2,1)S(1)} %fusion.17.data_ref, f32[16,384]{1,0:T(8,128)S(1)} %pad.19.table_ref, ...), custom_call_target="tpu_custom_call" | custom-call | flops 110000000 | bytes 330000 | tf_op jit(solution)/shard_map/conv_forward/pallas_call | solution.py:156
  21.5 12.2 %conv_forward.4 = (bf16[512,256]{1,0:T(8,128)(2,1)S(1)}, f32[512,256]{1,0:T(8,128)S(1)}, f32[64,256]{1,0:T(8,128)S(1)}, bf16[1024,256]{1,0:T(8,128)(2,1)S(1)}) custom-call(s32[1]{0:T(128)} %slice.281.narrow_ref, s32[2048,1]{1,0:T(8,128)S(1)} %copy.98.rank_ref, bf16[64,2048]{1,0:T(8,128)(2,1)S(1)} %fusion.17.data_ref, f32[16,384]{1,0:T(8,128)S(1)} %pad.19.table_ref, ...), custom_call_target="tpu_custom_call" | custom-call | flops 110000000 | bytes 330000 | tf_op jit(solution)/shard_map/conv_forward/pallas_call | solution.py:156
  37.6 2.8 choose_units.1
  43.1 3.6 collective-permute-start.4
  48.5 10.4 %conv_forward.6 = (bf16[512,512]{1,0:T(8,128)(2,1)S(1)}, f32[512,512]{1,0:T(8,128)S(1)}, f32[64,512]{1,0:T(8,128)S(1)}, bf16[1024,512]{1,0:T(8,128)(2,1)S(1)}) custom-call(s32[1]{0:T(128)} %slice.281.narrow_ref, s32[2048,1]{1,0:T(8,128)S(1)} %copy.98.rank_ref, bf16[64,2048]{1,0:T(8,128)(2,1)S(1)} %fusion.17.data_ref, f32[16,384]{1,0:T(8,128)S(1)} %copy-done.10, ...), custom_call_target="tpu_custom_call" | custom-call | flops 110000000 | bytes 330000 | tf_op jit(solution)/shard_map/conv_forward/pallas_call | solution.py:156
  60.5 11.8 %conv_forward.7 = (bf16[512,1024]{1,0:T(8,128)(2,1)S(1)}, f32[512,1024]{1,0:T(8,128)S(1)}, f32[64,1024]{1,0:T(8,128)S(1)}, bf16[1024,1024]{1,0:T(8,128)(2,1)}) custom-call(s32[1]{0:T(128)} %slice.281.narrow_ref, s32[2048,1]{1,0:T(8,128)S(1)} %copy.98.rank_ref, bf16[64,2048]{1,0:T(8,128)(2,1)S(1)} %fusion.17.data_ref, f32[16,384]{1,0:T(8,128)S(1)} %copy-done.10, ...), custom_call_target="tpu_custom_call" | custom-call | flops 110000000 | bytes 330000 | tf_op jit(solution)/shard_map/conv_forward/pallas_call | solution.py:156
  73.7 3.7 place_words.3
  77.4 3.1 place_words.2.refs_0_
  85.3 22.0 %collective-permute-done.10 = bf16[2,256,512]{2,1,0:T(8,128)(2,1)S(1)} collective-permute-done((bf16[2,256,512]{2,1,0:T(8,128)(2,1)}, bf16[2,256,512]{2,1,0:T(8,128)(2,1)S(1)}, u32[]{:S(2)}, u32[]{:S(2)}) %collective-permute-start.10) | collective-permute-done | bytes 524320 | tf_op jit(solution)/shard_map/ppermute | solution.py:793
  107.3 2.1 pad_maximum_fusion.3.refs_5_.refs_1_
  111.2 1.7 collective-permute-start.13
  116.1 27.6 %collective-permute-done.15 = bf16[2,320,512]{2,1,0:T(8,128)(2,1)S(1)} collective-permute-done((bf16[2,320,512]{2,1,0:T(8,128)(2,1)}, bf16[2,320,512]{2,1,0:T(8,128)(2,1)S(1)}, u32[]{:S(2)}, u32[]{:S(2)}) %collective-permute-start.15) | collective-permute-done | bytes 655392 | tf_op jit(solution)/shard_map/ppermute | solution.py:793
  143.7 2.7 collective-permute-done.11.refs_6_.refs_2_
  152.9 12.1 %highway_forward.2 = (f32[512,1024]{1,0:T(8,128)}, bf16[512,1024]{1,0:T(8,128)(2,1)}, bf16[512,1024]{1,0:T(8,128)(2,1)}, bf16[512,1024]{1,0:T(8,128)(2,1)}, bf16[512,1024]{1,0:T(8,128)(2,1)}) custom-call(s32[3,16]{1,0:T(4,128)} %pad_add_fusion.table_ref, f32[2,1024]{1,0:T(2,128)} %pad_maximum_fusion.10.bias_ref, bf16[1024,512]{1,0:T(8,128)(2,1)} %copy-done, ...), custom_call_target="tpu_custom_call" | custom-call | flops 100000000 | bytes 300000 | tf_op jit(solution)/shard_map/highway_forward/pallas_call | solution.py:566
  165.0 1.8 collective-permute-start.21
  166.8 12.1 %highway_forward.3 = (f32[512,1024]{1,0:T(8,128)}, bf16[512,1024]{1,0:T(8,128)(2,1)}, bf16[512,1024]{1,0:T(8,128)(2,1)}, bf16[512,1024]{1,0:T(8,128)(2,1)}, bf16[512,1024]{1,0:T(8,128)(2,1)}) custom-call(s32[3,16]{1,0:T(4,128)} %pad_add_fusion.table_ref, f32[2,1024]{1,0:T(2,128)} %pad_maximum_fusion.10.bias_ref, bf16[1024,512]{1,0:T(8,128)(2,1)} %copy-done, ...), custom_call_target="tpu_custom_call" | custom-call | flops 100000000 | bytes 300000 | tf_op jit(solution)/shard_map/highway_forward/pallas_call | solution.py:566
  181.6 3.1 pad_maximum_fusion.refs_0_
  184.7 12.2 %collective-permute-done.20 = bf16[2,320,512]{2,1,0:T(8,128)(2,1)S(1)} collective-permute-done((bf16[2,320,512]{2,1,0:T(8,128)(2,1)S(1)}, bf16[2,320,512]{2,1,0:T(8,128)(2,1)S(1)}, u32[]{:S(2)}, u32[]{:S(2)}) %collective-permute-start.20) | collective-permute-done | bytes 655392 | tf_op jit(solution)/shard_map/ppermute | solution.py:780
  196.9 3.5 pad_maximum_fusion.1.refs_1_
  200.4 1.8 collective-permute-start.24
  203.0 2.6 broadcast_select_fusion
  205.7 16.3 %highway_turn.2 = (bf16[512,1024]{1,0:T(8,128)(2,1)}, bf16[512,1024]{1,0:T(8,128)(2,1)}, bf16[512,1024]{1,0:T(8,128)(2,1)}, f32[512,1024]{1,0:T(8,128)}, bf16[51...) custom-call(s32[3,16]{1,0:T(4,128)} %pad_add_fusion.1.table_ref, ...), custom_call_target="tpu_custom_call" | custom-call | flops 160000000 | bytes 480000 | tf_op jit(solution)/shard_map/highway_turn/pallas_call | solution.py:588
  222.0 1.8 collective-permute-start.25
  223.8 2.7 collective-permute-done.24.mate.refs_3_
  227.4 16.4 %highway_turn.3 = (bf16[512,1024]{1,0:T(8,128)(2,1)}, bf16[512,1024]{1,0:T(8,128)(2,1)}, bf16[512,1024]{1,0:T(8,128)(2,1)}, f32[512,1024]{1,0:T(8,128)}, bf16[51...) custom-call(s32[3,16]{1,0:T(4,128)} %pad_add_fusion.1.table_ref, ...), custom_call_target="tpu_custom_call" | custom-call | flops 160000000 | bytes 480000 | tf_op jit(solution)/shard_map/highway_turn/pallas_call | solution.py:588
  243.9 1.8 collective-permute-start.26
  246.3 15.2 %highway_weight_grad.2 = (bf16[4,2,256,512]{3,2,1,0:T(8,128)(2,1)}, bf16[4,2,256,512]{3,2,1,0:T(8,128)(2,1)}, bf16[2,4,2,256,512]{4,3,2,1,0:T(8,128)(2,1)}) custom-call(s32[2,4]{1,0:T(2,128)} %pad_add_fusion.3.table_ref, bf16[512,1024]{1,0:T(8,128)(2,1)} %get-tuple-element.325.own.refs_0_, bf16[512,1024]{1,0:T(8,128)(2,1)} %copy-done.47, ...), custom_call_target="tpu_custom_call" | custom-call | flops 150000000 | bytes 450000 | tf_op jit(solution)/shard_map/highway_weight_grad/pallas_call | solution.py:645
  261.5 7.6 %highway_back.4.partial = f32[512,1024]{1,0:T(8,128)} custom-call(s32[3,16]{1,0:T(4,128)} %pad_add_fusion.1.table_ref, bf16[512,1024]{1,0:T(8,128)(2,1)} %get-tuple-element.342.refs_4_.d_first, bf16[512,1024]{1,0:T(8,128)(2,1)} %get-tuple-element.343.refs_6_.d_gate, f32[512,1024]{1,0:T(8,128)} %get-tuple-element.357.up, ...), custom_call_target="tpu_custom_call" | custom-call | flops 60000000 | bytes 180000 | tf_op jit(solution)/shard_map/highway_back/pallas_call | solution.py:625
  269.0 1.9 collective-permute-done.26.arrived
  271.0 8.2 %highway_slopes.2 = (bf16[512,1024]{1,0:T(8,128)(2,1)}, bf16[512,1024]{1,0:T(8,128)(2,1)}, f32[512,1024]{1,0:T(8,128)}, bf16[512,1024]{1,0:T(8,128)(2,1)}, f32[2,1024]{1,0:T(2,128)}) custom-call(s32[3,16]{1,0:T(4,128)} %pad_add_fusion.table_ref, f32[512,1024]{1,0:T(8,128)} %highway_back.4.partial, bf16[512,1024]{1,0:T(8,128)(2,1)} %collective-permute-done.25.arrived, ...), custom_call_target="tpu_custom_call" | custom-call | flops 80000000 | bytes 240000 | tf_op jit(solution)/shard_map/highway_slopes/pallas_call | solution.py:608
  279.2 3.6 fusion.13
  286.6 7.9 %highway_back.5.partial = f32[512,1024]{1,0:T(8,128)} custom-call(s32[3,16]{1,0:T(4,128)} %pad_add_fusion.1.table_ref, bf16[512,1024]{1,0:T(8,128)(2,1)} %get-tuple-element.352.refs_5_.d_first, bf16[512,1024]{1,0:T(8,128)(2,1)} %get-tuple-element.353.refs_7_.d_gate, f32[512,1024]{1,0:T(8,128)} %get-tuple-element.381.up, ...), custom_call_target="tpu_custom_call" | custom-call | flops 60000000 | bytes 180000 | tf_op jit(solution)/shard_map/highway_back/pallas_call | solution.py:625
  294.5 7.9 %highway_slopes.3 = (bf16[512,1024]{1,0:T(8,128)(2,1)}, bf16[512,1024]{1,0:T(8,128)(2,1)}, f32[512,1024]{1,0:T(8,128)}, bf16[512,1024]{1,0:T(8,128)(2,1)}, f32[2,1024]{1,0:T(2,128)}) custom-call(s32[3,16]{1,0:T(4,128)} %pad_add_fusion.table_ref, f32[512,1024]{1,0:T(8,128)} %highway_back.5.partial, bf16[512,1024]{1,0:T(8,128)(2,1)} %copy-done.68, ...), custom_call_target="tpu_custom_call" | custom-call | flops 80000000 | bytes 240000 | tf_op jit(solution)/shard_map/highway_slopes/pallas_call | solution.py:608
  303.7 15.2 %highway_weight_grad.3 = (bf16[4,2,256,512]{3,2,1,0:T(8,128)(2,1)}, bf16[4,2,256,512]{3,2,1,0:T(8,128)(2,1)}, bf16[2,4,2,256,512]{4,3,2,1,0:T(8,128)(2,1)}) custom-call(s32[2,4]{1,0:T(2,128)} %pad_add_fusion.3.table_ref, bf16[1024,512]{1,0:T(8,128)(2,1)} %copy-done, bf16[1024,512]{1,0:T(8,128)(2,1)} %copy-done.33, bf16[1024,512]{1,0:T(8,128)(2,1)} %copy-done.34, ...), custom_call_target="tpu_custom_call" | custom-call | flops 150000000 | bytes 450000 | tf_op jit(solution)/shard_map/highway_weight_grad/pallas_call | solution.py:645
  319.8 7.6 %highway_back.6 = f32[512,1024]{1,0:T(8,128)} custom-call(s32[3,16]{1,0:T(4,128)} %pad_add_fusion.table_ref, bf16[512,1024]{1,0:T(8,128)(2,1)} %get-tuple-element.376.refs_4_.d_first, bf16[512,1024]{1,0:T(8,128)(2,1)} %get-tuple-element.377.refs_6_.d_gate, f32[512,1024]{1,0:T(8,128)} %get-tuple-element.394.up, bf16[2,2,256,512]{3,2,1,0:T(8,128)(2,1)} %copy-done.29, ...), custom_call_target="tpu_custom_call" | custom-call | flops 60000000 | bytes 180000 | tf_op jit(solution)/shard_map/highway_back/pallas_call | solution.py:625
  327.5 7.8 %highway_back.7 = f32[512,1024]{1,0:T(8,128)} custom-call(s32[3,16]{1,0:T(4,128)} %pad_add_fusion.table_ref, bf16[512,1024]{1,0:T(8,128)(2,1)} %get-tuple-element.386.refs_5_.d_first, bf16[512,1024]{1,0:T(8,128)(2,1)} %get-tuple-element.387.refs_7_.d_gate, f32[512,1024]{1,0:T(8,128)} %get-tuple-element.395.up, bf16[2,2,256,512]{3,2,1,0:T(8,128)(2,1)} %copy-done.29, ...), custom_call_target="tpu_custom_call" | custom-call | flops 60000000 | bytes 180000 | tf_op jit(solution)/shard_map/highway_back/pallas_call | solution.py:625
  337.1 4.0 convert_add_fusion.12
  341.0 2.0 collective-permute-start.33
  343.0 2.1 collective-permute-start.34
  349.0 1.7 copy-done.50
  355.6 1.7 copy-done.40
  358.4 15.0 %collective-permute-done.31.refs_3_ = bf16[1024,512]{1,0:T(8,128)(2,1)S(1)} collective-permute-done((bf16[1024,512]{1,0:T(8,128)(2,1)S(1)}, bf16[1024,512]{1,0:T(8,128)(2,1)S(1)}, u32[]{:S(2)}, u32[]{:S(2)}) %collective-permute-start.31) | collective-permute-done | bytes 1048608 | tf_op jit(solution)/shard_map/ppermute | solution.py:780
  373.4 19.2 %conv_backward.4.refs_4_ = f32[640,128]{1,0:T(8,128)S(1)} custom-call(s32[1]{0:T(128)} %slice.281.narrow_ref, f32[64,256]{1,0:T(8,128)S(1)} %copy-done.26, bf16[1024,256]{1,0:T(8,128)(2,1)S(1)} %copy-done.18, bf16[512,128]{1,0:T(8,128)(2,1)S(1)} %copy.99.conv_ref, bf16[128,512]{1,0:T(8,128)(2,1)S(1)} %pad.21.back_ref, ...), custom_call_target="tpu_custom_call" | custom-call | flops 150000000 | bytes 450000 | tf_op jit(solution)/shard_map/conv_backward/pallas_call | solution.py:276
  392.7 2.2 collective-permute-done.36
  396.3 2.7 fusion.3
  399.6 1.8 collective-permute-start.40
  403.9 11.5 %conv_backward.5.refs_4_ = f32[640,128]{1,0:T(8,128)S(1)} custom-call(s32[1]{0:T(128)} %slice.281.narrow_ref, f32[64,256]{1,0:T(8,128)S(1)} %copy-done.24, bf16[1024,256]{1,0:T(8,128)(2,1)S(1)} %copy-done.14, bf16[512,128]{1,0:T(8,128)(2,1)S(1)} %copy.99.conv_ref, bf16[128,512]{1,0:T(8,128)(2,1)S(1)} %pad.21.back_ref, ...), custom_call_target="tpu_custom_call" | custom-call | flops 150000000 | bytes 450000 | tf_op jit(solution)/shard_map/conv_backward/pallas_call | solution.py:276
  415.4 14.9 %conv_backward.6.refs_4_ = f32[640,128]{1,0:T(8,128)S(1)} custom-call(s32[1]{0:T(128)} %slice.281.narrow_ref, f32[64,512]{1,0:T(8,128)S(1)} %copy-done.22, bf16[1024,512]{1,0:T(8,128)(2,1)S(1)} %copy-done.8, bf16[512,128]{1,0:T(8,128)(2,1)S(1)} %copy.99.conv_ref, bf16[128,512]{1,0:T(8,128)(2,1)S(1)} %pad.21.back_ref, ...), custom_call_target="tpu_custom_call" | custom-call | flops 150000000 | bytes 450000 | tf_op jit(solution)/shard_map/conv_backward/pallas_call | solution.py:276
  430.4 6.9 %collective-permute-done.37.refs_1_ = bf16[2,256,512]{2,1,0:T(8,128)(2,1)} collective-permute-done((bf16[2,256,512]{2,1,0:T(8,128)(2,1)}, bf16[2,256,512]{2,1,0:T(8,128)(2,1)}, u32[]{:S(2)}, u32[]{:S(2)}) %collective-permute-start.37) | collective-permute-done | bytes 524320 | tf_op jit(solution)/shard_map/ppermute | solution.py:793
  437.3 3.0 collective-permute-done.41
  440.2 3.1 convert_add_fusion
  449.2 15.4 %conv_backward.7 = f32[640,128]{1,0:T(8,128)S(1)} custom-call(s32[1]{0:T(128)} %slice.281.narrow_ref, f32[64,1024]{1,0:T(8,128)S(1)} %copy-done.20, bf16[1024,1024]{1,0:T(8,128)(2,1)S(1)} %copy-done.2, bf16[512,128]{1,0:T(8,128)(2,1)S(1)} %copy.99.conv_ref, bf16[128,512]{1,0:T(8,128)(2,1)S(1)} %pad.21.back_ref, s32[512,1]{1,0:T(8,128)S(1)} %convert_add_fusion.28.width_ref, ...), custom_call_target="tpu_custom_call" | custom-call | flops 150000000 | bytes 450000 | tf_op jit(solution)/shard_map/conv_backward/pallas_call | solution.py:276
  466.3 5.0 return_units.1
  473.0 3.5 collective-permute-start.49
  478.2 2.5 collective-permute-start.46
  480.8 2.5 add_add_fusion
  483.3 12.4 %collective-permute-done.46 = bf16[640,128]{0,1:T(8,128)(2,1)S(1)} collective-permute-done((bf16[640,128]{0,1:T(8,128)(2,1)S(1)}, bf16[640,128]{0,1:T(8,128)(2,1)S(1)}, u32[]{:S(2)}, u32[]{:S(2)}) %collective-permute-start.46) | collective-permute-done | bytes 163872 | tf_op jit(solution)/shard_map/ppermute | solution.py:889
  495.8 2.5 collective-permute-done.48.refs_2_
  498.3 1.8 collective-permute-start.50
  501.9 8.2 %owner_update.2 = (f32[2,256,2048]{2,1,0:T(8,128)}, f32[2,256,2048]{2,1,0:T(8,128)}, f32[2,256,2048]{2,1,0:T(8,128)}, f32[2,256,2048]{2,1,0:T(8,128)}) custom-call(s32[4]{0:T(128)} %get-tuple-element.589.at_ref, bf16[2,256,512]{2,1,0:T(8,128)(2,1)} %get-tuple-element.498.refs_0_, bf16[2,256,512]{2,1,0:T(8,128)(2,1)} %copy-done.57, ...), custom_call_target="tpu_custom_call" | custom-call | flops 80000000 | bytes 240000 | tf_op jit(solution)/shard_map/owner_update/pallas_call | solution.py:689
  511.2 8.2 %owner_update.3 = (f32[2,256,2048]{2,1,0:T(8,128)}, f32[2,256,2048]{2,1,0:T(8,128)}, f32[2,256,2048]{2,1,0:T(8,128)}, f32[2,256,2048]{2,1,0:T(8,128)}) custom-call(s32[4]{0:T(128)} %get-tuple-element.589.at_ref, bf16[2,256,512]{2,1,0:T(8,128)(2,1)} %get-tuple-element.498.refs_0_, ...), custom_call_target="tpu_custom_call", output_to_operand_aliasing={{0}: (9, {}), {1}: (10, {}), {2}: (11, {}), {3}: (12, {})} | custom-call | flops 80000000 | bytes 240000 | tf_op jit(solution)/shard_map/owner_update/pallas_call | solution.py:689
  (405 shorter events, 73.6 us)
Async XLA Ops:
  4.4 32.3 %collective-permute-start.2 = (bf16[2,256,512]{2,1,0:T(8,128)(2,1)}, bf16[2,256,512]{2,1,0:T(8,128)(2,1)S(1)}, u32[]{:S(2)}, u32[]{:S(2)}) collective-permute-start(bf16[2,256,512]{2,1,0:T(8,128)(2,1)} %get-tuple-element.551), channel_id=1, source_target_pairs={{0,24},{8,16},{16,8},{24,0},{1,25},{9,17},{17,9},{25,1},{2,26},{10... | collective-permute-start | bytes 1572872 | tf_op jit(solution)/shard_map/ppermute | solution.py:780
  8.3 28.4 %collective-permute-start.1 = (bf16[2,256,512]{2,1,0:T(8,128)(2,1)}, bf16[2,256,512]{2,1,0:T(8,128)(2,1)S(1)}, u32[]{:S(2)}, u32[]{:S(2)}) collective-permute-start(bf16[2,256,512]{2,1,0:T(8,128)(2,1)} %get-tuple-element.552), channel_id=1, source_target_pairs={{0,16},{8,24},{16,0},{24,8},{1,17},{9,25},{17,1},{25,9},{2,18},{10... | collective-permute-start | bytes 1572872 | tf_op jit(solution)/shard_map/ppermute | solution.py:780
  8.8 27.9 %collective-permute-start = (bf16[2,256,512]{2,1,0:T(8,128)(2,1)}, bf16[2,256,512]{2,1,0:T(8,128)(2,1)}, u32[]{:S(2)}, u32[]{:S(2)}) collective-permute-start(bf16[2,256,512]{2,1,0:T(8,128)(2,1)} %get-tuple-element.553), channel_id=1, source_target_pairs={{0,8},{8,0},{16,24},{24,16},{1,9},{9,1},{17,25},{25,17},{2,10},{10... | collective-permute-start | bytes 1572872 | tf_op jit(solution)/shard_map/ppermute | solution.py:780
  12.1 23.3 %copy-start.104 = (s32[4]{0:T(128)S(1)}, s32[4]{0:T(128)}, u32[]{:S(2)}) copy-start(s32[4]{0:T(128)} %param.26) | copy-start | bytes 52
  12.5 28.0 %copy-start.9 = (f32[16,384]{1,0:T(8,128)}, f32[16,384]{1,0:T(8,128)S(1)}, u32[]{:S(2)}) copy-start(f32[16,384]{1,0:T(8,128)S(1)} %pad.19.table_ref) | copy-start | bytes 73732
  21.5 26.0 %copy-start.23 = (f32[64,256]{1,0:T(8,128)}, f32[64,256]{1,0:T(8,128)S(1)}, u32[]{:S(2)}) copy-start(f32[64,256]{1,0:T(8,128)S(1)} %get-tuple-element.448.ids_ref) | copy-start | bytes 196612
  40.4 40.1 %collective-permute-start.7 = (bf16[512,768]{1,0:T(8,128)(2,1)}, bf16[512,768]{1,0:T(8,128)(2,1)}, u32[]{:S(2)}, u32[]{:S(2)}) collective-permute-start(bf16[512,768]{1,0:T(8,128)(2,1)} %param.25), channel_id=1, source_target_pairs={{0,8},{8,0},{16,24},{24,16},{1,9},{9,1},{17,25},{25,17},{2,10},{10... | collective-permute-start | bytes 2359304 | tf_op jit(solution)/shard_map/ppermute | solution.py:780
  41.1 39.5 %collective-permute-start.6 = (bf16[2,320,512]{2,1,0:T(8,128)(2,1)}, bf16[2,320,512]{2,1,0:T(8,128)(2,1)}, u32[]{:S(2)}, u32[]{:S(2)}) collective-permute-start(bf16[2,320,512]{2,1,0:T(8,128)(2,1)} %get-tuple-element.326), channel_id=1, source_target_pairs={{0,16},{8,24},{16,0},{24,8},{1,17},{9,25},{17,1},{25,9},{2,18},{10... | collective-permute-start | bytes 1966088 | tf_op jit(solution)/shard_map/ppermute | solution.py:780
  41.9 38.6 %collective-permute-start.5 = (bf16[2,256,512]{2,1,0:T(8,128)(2,1)}, bf16[2,256,512]{2,1,0:T(8,128)(2,1)}, u32[]{:S(2)}, u32[]{:S(2)}) collective-permute-start(bf16[2,256,512]{2,1,0:T(8,128)(2,1)} %get-tuple-element.309), channel_id=1, source_target_pairs={{0,16},{8,24},{16,0},{24,8},{1,17},{9,25},{17,1},{25,9},{2,18},{10... | collective-permute-start | bytes 1572872 | tf_op jit(solution)/shard_map/ppermute | solution.py:780
  43.1 37.4 %collective-permute-start.4 = (bf16[2,256,512]{2,1,0:T(8,128)(2,1)}, bf16[2,256,512]{2,1,0:T(8,128)(2,1)}, u32[]{:S(2)}, u32[]{:S(2)}) collective-permute-start(bf16[2,256,512]{2,1,0:T(8,128)(2,1)} %get-tuple-element.309), channel_id=1, source_target_pairs={{0,6},{1,7},{2,0},{3,1},{4,2},{5,3},{6,4},{7,5},{8,14},{9,15},{10,... | collective-permute-start | bytes 1572872 | tf_op jit(solution)/shard_map/ppermute | solution.py:793
  46.7 33.9 %collective-permute-start.3 = (bf16[2,256,512]{2,1,0:T(8,128)(2,1)}, bf16[2,256,512]{2,1,0:T(8,128)(2,1)}, u32[]{:S(2)}, u32[]{:S(2)}) collective-permute-start(bf16[2,256,512]{2,1,0:T(8,128)(2,1)} %get-tuple-element.309), channel_id=1, source_target_pairs={{0,2},{1,3},{2,4},{3,5},{4,6},{5,7},{6,0},{7,1},{8,10},{9,11},{10,... | collective-permute-start | bytes 1572872 | tf_op jit(solution)/shard_map/ppermute | solution.py:793
  48.5 25.2 %copy-start.4 = (bf16[512,256]{1,0:T(8,128)(2,1)S(1)}, bf16[512,256]{1,0:T(8,128)(2,1)}, u32[]{:S(2)}) copy-start(bf16[512,256]{1,0:T(8,128)(2,1)} %copy-done.3) | copy-start | bytes 786436
  80.5 35.6 %copy-start = (bf16[1024,512]{1,0:T(8,128)(2,1)}, bf16[1024,512]{1,0:T(8,128)(2,1)S(1)}, u32[]{:S(2)}) copy-start(bf16[1024,512]{1,0:T(8,128)(2,1)S(1)} %place_words.2.refs_0_) | copy-start | bytes 3145732
  80.6 26.7 %collective-permute-start.8 = (bf16[1024,512]{1,0:T(8,128)(2,1)}, bf16[1024,512]{1,0:T(8,128)(2,1)S(1)}, u32[]{:S(2)}, u32[]{:S(2)}) collective-permute-start(bf16[1024,512]{1,0:T(8,128)(2,1)} %place_words.3), channel_id=1, source_target_pairs={{0,16},{8,24},{16,0},{24,8},{1,17},{9,25},{17,1},{25,9},{2,18},{10... | collective-permute-start | bytes 3145736 | tf_op jit(solution)/shard_map/ppermute | solution.py:780
  80.6 26.6 %collective-permute-start.9 = (bf16[1024,512]{1,0:T(8,128)(2,1)S(1)}, bf16[1024,512]{1,0:T(8,128)(2,1)S(1)}, u32[]{:S(2)}, u32[]{:S(2)}) collective-permute-start(bf16[1024,512]{1,0:T(8,128)(2,1)S(1)} %place_words.2.refs_0_), channel_id=1, source_target_pairs={{0,8},{8,0},{16,24},{24,16},{1,9},{9,1},{17,25},{25,17},{2,10},{10... | collective-permute-start | bytes 3145736 | tf_op jit(solution)/shard_map/ppermute | solution.py:780
  82.2 32.7 %copy-start.76 = (bf16[2,256,512]{2,1,0:T(8,128)(2,1)S(1)}, bf16[2,256,512]{2,1,0:T(8,128)(2,1)}, u32[]{:S(2)}) copy-start(bf16[2,256,512]{2,1,0:T(8,128)(2,1)} %get-tuple-element.309) | copy-start | bytes 1572868
  82.2 25.1 %collective-permute-start.10 = (bf16[2,256,512]{2,1,0:T(8,128)(2,1)}, bf16[2,256,512]{2,1,0:T(8,128)(2,1)S(1)}, u32[]{:S(2)}, u32[]{:S(2)}) collective-permute-start(bf16[2,256,512]{2,1,0:T(8,128)(2,1)} %get-tuple-element.309), channel_id=1, source_target_pairs={{0,4},{1,5},{2,6},{3,7},{4,0},{5,1},{6,2},{7,3},{8,12},{9,13},{10,... | collective-permute-start | bytes 1572872 | tf_op jit(solution)/shard_map/ppermute | solution.py:793
  109.4 38.7 %copy-start.27 = (bf16[3,2,256,512]{3,2,1,0:T(8,128)(2,1)}, bf16[3,2,256,512]{3,2,1,0:T(8,128)(2,1)S(1)}, u32[]{:S(2)}) copy-start(bf16[3,2,256,512]{3,2,1,0:T(8,128)(2,1)S(1)} %pad_maximum_fusion.3.refs_5_.refs_1_) | copy-start | bytes 4718596
  109.5 34.3 %collective-permute-start.12 = (bf16[3,2,256,512]{3,2,1,0:T(8,128)(2,1)S(1)}, bf16[3,2,256,512]{3,2,1,0:T(8,128)(2,1)S(1)}, u32[]{:S(2)}, u32[]{:S(2)}) collective-permute-start(bf16[3,2,256,512]{3,2,1,0:T(8,128)(2,1)S(1)} %pad_maximum_fusion.3.refs_5_.refs_1_), channel_id=1, source_target_pairs={{0,1},{1,0},{2,3},{3,2},{4,5},{5,4},{6,7},{7,6},{8,9},{9,8},{10,11... | collective-permute-start | bytes 4718600 | tf_op jit(solution)/shard_map/ppermute | solution.py:789
  109.5 36.9 %collective-permute-start.11 = (bf16[3,2,256,512]{3,2,1,0:T(8,128)(2,1)S(1)}, bf16[3,2,256,512]{3,2,1,0:T(8,128)(2,1)}, u32[]{:S(2)}, u32[]{:S(2)}) collective-permute-start(bf16[3,2,256,512]{3,2,1,0:T(8,128)(2,1)S(1)} %pad_maximum_fusion.3.refs_5_.refs_1_), channel_id=1, source_target_pairs={{0,16},{8,24},{16,0},{24,8},{1,17},{9,25},{17,1},{25,9},{2,18},{10... | collective-permute-start | bytes 4718600 | tf_op jit(solution)/shard_map/ppermute | solution.py:780
  111.2 32.5 %collective-permute-start.13 = (bf16[1024,512]{1,0:T(8,128)(2,1)S(1)}, bf16[1024,512]{1,0:T(8,128)(2,1)S(1)}, u32[]{:S(2)}, u32[]{:S(2)}) collective-permute-start(bf16[1024,512]{1,0:T(8,128)(2,1)S(1)} %collective-permute-done.8.refs_1_), channel_id=1, source_target_pairs={{0,8},{8,0},{16,24},{24,16},{1,9},{9,1},{17,25},{25,17},{2,10},{10... | collective-permute-start | bytes 3145736 | tf_op jit(solution)/shard_map/ppermute | solution.py:780
  112.9 30.8 %collective-permute-start.15 = (bf16[2,320,512]{2,1,0:T(8,128)(2,1)}, bf16[2,320,512]{2,1,0:T(8,128)(2,1)S(1)}, u32[]{:S(2)}, u32[]{:S(2)}) collective-permute-start(bf16[2,320,512]{2,1,0:T(8,128)(2,1)} %get-tuple-element.326), channel_id=1, source_target_pairs={{0,6},{1,7},{2,0},{3,1},{4,2},{5,3},{6,4},{7,5},{8,14},{9,15},{10,... | collective-permute-start | bytes 1966088 | tf_op jit(solution)/shard_map/ppermute | solution.py:793
  114.5 29.2 %collective-permute-start.14 = (bf16[2,320,512]{2,1,0:T(8,128)(2,1)}, bf16[2,320,512]{2,1,0:T(8,128)(2,1)S(1)}, u32[]{:S(2)}, u32[]{:S(2)}) collective-permute-start(bf16[2,320,512]{2,1,0:T(8,128)(2,1)} %get-tuple-element.326), channel_id=1, source_target_pairs={{0,2},{1,3},{2,4},{3,5},{4,6},{5,7},{6,0},{7,1},{8,10},{9,11},{10,... | collective-permute-start | bytes 1966088 | tf_op jit(solution)/shard_map/ppermute | solution.py:793
  116.1 35.8 %copy-start.29 = (bf16[2,2,256,512]{3,2,1,0:T(8,128)(2,1)}, bf16[2,2,256,512]{3,2,1,0:T(8,128)(2,1)S(1)}, u32[]{:S(2)}) copy-start(bf16[2,2,256,512]{3,2,1,0:T(8,128)(2,1)S(1)} %pad_maximum_fusion.5.refs_4_.refs_0_) | copy-start | bytes 3145732
  146.5 5.5 %collective-permute-start.17 = (bf16[3,2,256,512]{3,2,1,0:T(8,128)(2,1)}, bf16[3,2,256,512]{3,2,1,0:T(8,128)(2,1)}, u32[]{:S(2)}, u32[]{:S(2)}) collective-permute-start(bf16[3,2,256,512]{3,2,1,0:T(8,128)(2,1)} %collective-permute-done.11.refs_6_.refs_2_), channel_id=1, source_target_pairs={{0,1},{1,0},{2,3},{3,2},{4,5},{5,4},{6,7},{7,6},{8,9},{9,8},{10,11... | collective-permute-start | bytes 4718600 | tf_op jit(solution)/shard_map/ppermute | solution.py:789
  146.5 5.5 %collective-permute-start.16 = (bf16[2,2,256,512]{3,2,1,0:T(8,128)(2,1)S(1)}, bf16[2,2,256,512]{3,2,1,0:T(8,128)(2,1)S(1)}, u32[]{:S(2)}, u32[]{:S(2)}) collective-permute-start(bf16[2,2,256,512]{3,2,1,0:T(8,128)(2,1)S(1)} %pad_maximum_fusion.5.refs_4_.refs_0_), channel_id=1, source_target_pairs={{0,1},{1,0},{2,3},{3,2},{4,5},{5,4},{6,7},{7,6},{8,9},{9,8},{10,11... | collective-permute-start | bytes 3145736 | tf_op jit(solution)/shard_map/ppermute | solution.py:789
  148.1 32.1 %collective-permute-start.19 = (bf16[2,2,320,512]{3,2,1,0:T(8,128)(2,1)}, bf16[2,2,320,512]{3,2,1,0:T(8,128)(2,1)}, u32[]{:S(2)}, u32[]{:S(2)}) collective-permute-start(bf16[2,2,320,512]{3,2,1,0:T(8,128)(2,1)} %pad_maximum_fusion.4), channel_id=1, source_target_pairs={{0,16},{8,24},{16,0},{24,8},{1,17},{9,25},{17,1},{25,9},{2,18},{10... | collective-permute-start | bytes 3932168 | tf_op jit(solution)/shard_map/ppermute | solution.py:780
  149.7 30.5 %collective-permute-start.18 = (bf16[2,320,512]{2,1,0:T(8,128)(2,1)}, bf16[2,320,512]{2,1,0:T(8,128)(2,1)S(1)}, u32[]{:S(2)}, u32[]{:S(2)}) collective-permute-start(bf16[2,320,512]{2,1,0:T(8,128)(2,1)} %get-tuple-element.326), channel_id=1, source_target_pairs={{0,4},{1,5},{2,6},{3,7},{4,0},{5,1},{6,2},{7,3},{8,12},{9,13},{10,... | collective-permute-start | bytes 1966088 | tf_op jit(solution)/shard_map/ppermute | solution.py:793
  165.0 31.9 %collective-permute-start.21 = (bf16[512,1024]{1,0:T(8,128)(2,1)}, bf16[512,1024]{1,0:T(8,128)(2,1)S(1)}, u32[]{:S(2)}, u32[]{:S(2)}) collective-permute-start(bf16[512,1024]{1,0:T(8,128)(2,1)} %get-tuple-element.325.own.refs_0_), channel_id=1, source_target_pairs={{0,8},{8,0},{16,24},{24,16},{1,9},{9,1},{17,25},{25,17},{2,10},{10... | collective-permute-start | bytes 3145736 | tf_op jit(solution)/shard_map/ppermute | solution.py:780
  180.2 16.7 %collective-permute-start.20 = (bf16[2,320,512]{2,1,0:T(8,128)(2,1)S(1)}, bf16[2,320,512]{2,1,0:T(8,128)(2,1)S(1)}, u32[]{:S(2)}, u32[]{:S(2)}) collective-permute-start(bf16[2,320,512]{2,1,0:T(8,128)(2,1)S(1)} %collective-permute-done.18), channel_id=1, source_target_pairs={{0,16},{8,24},{16,0},{24,8},{1,17},{9,25},{17,1},{25,9},{2,18},{10... | collective-permute-start | bytes 1966088 | tf_op jit(solution)/shard_map/ppermute | solution.py:780
  184.7 21.0 %collective-permute-start.22 = (bf16[4,2,320,512]{3,2,1,0:T(8,128)(2,1)}, bf16[4,2,320,512]{3,2,1,0:T(8,128)(2,1)}, u32[]{:S(2)}, u32[]{:S(2)}) collective-permute-start(bf16[4,2,320,512]{3,2,1,0:T(8,128)(2,1)} %pad_maximum_fusion.refs_0_), channel_id=1, source_target_pairs={{0,1},{1,0},{2,3},{3,2},{4,5},{5,4},{6,7},{7,6},{8,9},{9,8},{10,11... | collective-permute-start | bytes 7864328 | tf_op jit(solution)/shard_map/ppermute | solution.py:789
  200.4 5.3 %collective-permute-start.23 = (bf16[4,2,320,512]{3,2,1,0:T(8,128)(2,1)}, bf16[4,2,320,512]{3,2,1,0:T(8,128)(2,1)}, u32[]{:S(2)}, u32[]{:S(2)}) collective-permute-start(bf16[4,2,320,512]{3,2,1,0:T(8,128)(2,1)} %pad_maximum_fusion.1.refs_1_), channel_id=1, source_target_pairs={{0,1},{1,0},{2,3},{3,2},{4,5},{5,4},{6,7},{7,6},{8,9},{9,8},{10,11... | collective-permute-start | bytes 7864328 | tf_op jit(solution)/shard_map/ppermute | solution.py:789
  200.4 26.0 %collective-permute-start.24 = (bf16[512,1024]{1,0:T(8,128)(2,1)S(1)}, bf16[512,1024]{1,0:T(8,128)(2,1)S(1)}, u32[]{:S(2)}, u32[]{:S(2)}) collective-permute-start(bf16[512,1024]{1,0:T(8,128)(2,1)S(1)} %copy-done.48), channel_id=1, source_target_pairs={{0,8},{8,0},{16,24},{24,16},{1,9},{9,1},{17,25},{25,17},{2,10},{10... | collective-permute-start | bytes 3145736 | tf_op jit(solution)/shard_map/ppermute | solution.py:780
  222.0 39.5 %collective-permute-start.25 = (bf16[512,1024]{1,0:T(8,128)(2,1)}, bf16[512,1024]{1,0:T(8,128)(2,1)}, u32[]{:S(2)}, u32[]{:S(2)}) collective-permute-start(bf16[512,1024]{1,0:T(8,128)(2,1)} %get-tuple-element.347), channel_id=1, source_target_pairs={{0,8},{8,0},{16,24},{24,16},{1,9},{9,1},{17,25},{25,17},{2,10},{10... | collective-permute-start | bytes 3145736 | tf_op jit(solution)/shard_map/ppermute | solution.py:780
  243.9 27.1 %collective-permute-start.26 = (bf16[512,1024]{1,0:T(8,128)(2,1)}, bf16[512,1024]{1,0:T(8,128)(2,1)S(1)}, u32[]{:S(2)}, u32[]{:S(2)}) collective-permute-start(bf16[512,1024]{1,0:T(8,128)(2,1)} %get-tuple-element.358), channel_id=1, source_target_pairs={{0,8},{8,0},{16,24},{24,16},{1,9},{9,1},{17,25},{25,17},{2,10},{10... | collective-permute-start | bytes 3145736 | tf_op jit(solution)/shard_map/ppermute | solution.py:780
  271.0 8.3 %collective-permute-start.27 = (bf16[2,4,2,256,512]{4,3,2,1,0:T(8,128)(2,1)}, bf16[2,4,2,256,512]{4,3,2,1,0:T(8,128)(2,1)S(1)}, u32[]{:S(2)}, u32[]{:S(2)}) collective-permute-start(bf16[2,4,2,256,512]{4,3,2,1,0:T(8,128)(2,1)} %get-tuple-element.364), channel_id=1, source_target_pairs={{0,1},{1,0},{2,3},{3,2},{4,5},{5,4},{6,7},{7,6},{8,9},{9,8},{10,11... | collective-permute-start | bytes 12582920 | tf_op jit(solution)/shard_map/ppermute | solution.py:789
  284.5 50.8 %collective-permute-start.30 = (bf16[4,2,256,512]{3,2,1,0:T(8,128)(2,1)}, bf16[4,2,256,512]{3,2,1,0:T(8,128)(2,1)S(1)}, u32[]{:S(2)}, u32[]{:S(2)}) collective-permute-start(bf16[4,2,256,512]{3,2,1,0:T(8,128)(2,1)} %pad_maximum_fusion.2), channel_id=1, source_target_pairs={{0,16},{8,24},{16,0},{24,8},{1,17},{9,25},{17,1},{25,9},{2,18},{10... | collective-permute-start | bytes 6291464 | tf_op jit(solution)/shard_map/ppermute | solution.py:780
  285.8 33.1 %collective-permute-start.28 = (bf16[512,1024]{1,0:T(8,128)(2,1)S(1)}, bf16[512,1024]{1,0:T(8,128)(2,1)S(1)}, u32[]{:S(2)}, u32[]{:S(2)}) collective-permute-start(bf16[512,1024]{1,0:T(8,128)(2,1)S(1)} %copy-done.106), channel_id=1, source_target_pairs={{0,8},{8,0},{16,24},{24,16},{1,9},{9,1},{17,25},{25,17},{2,10},{10... | collective-permute-start | bytes 3145736 | tf_op jit(solution)/shard_map/ppermute | solution.py:780
  302.4 32.9 %collective-permute-start.29 = (bf16[512,1024]{1,0:T(8,128)(2,1)}, bf16[512,1024]{1,0:T(8,128)(2,1)}, u32[]{:S(2)}, u32[]{:S(2)}) collective-permute-start(bf16[512,1024]{1,0:T(8,128)(2,1)} %get-tuple-element.399), channel_id=1, source_target_pairs={{0,8},{8,0},{16,24},{24,16},{1,9},{9,1},{17,25},{25,17},{2,10},{10... | collective-permute-start | bytes 3145736 | tf_op jit(solution)/shard_map/ppermute | solution.py:780
  335.3 12.7 %collective-permute-start.35 = (bf16[2,4,2,256,512]{4,3,2,1,0:T(8,128)(2,1)}, bf16[2,4,2,256,512]{4,3,2,1,0:T(8,128)(2,1)S(1)}, u32[]{:S(2)}, u32[]{:S(2)}) collective-permute-start(bf16[2,4,2,256,512]{4,3,2,1,0:T(8,128)(2,1)} %get-tuple-element.435), channel_id=1, source_target_pairs={{0,1},{1,0},{2,3},{3,2},{4,5},{5,4},{6,7},{7,6},{8,9},{9,8},{10,11... | collective-permute-start | bytes 12582920 | tf_op jit(solution)/shard_map/ppermute | solution.py:789
  341.0 51.6 %collective-permute-start.32 = (bf16[2,256,512]{2,1,0:T(8,128)(2,1)}, bf16[2,256,512]{2,1,0:T(8,128)(2,1)S(1)}, u32[]{:S(2)}, u32[]{:S(2)}) collective-permute-start(bf16[2,256,512]{2,1,0:T(8,128)(2,1)} %get-tuple-element.431), channel_id=1, source_target_pairs={{0,4},{1,5},{2,6},{3,7},{4,0},{5,1},{6,2},{7,3},{8,12},{9,13},{10,... | collective-permute-start | bytes 1572872 | tf_op jit(solution)/shard_map/ppermute | solution.py:793
  341.0 51.6 %collective-permute-start.33 = (bf16[2,256,512]{2,1,0:T(8,128)(2,1)}, bf16[2,256,512]{2,1,0:T(8,128)(2,1)S(1)}, u32[]{:S(2)}, u32[]{:S(2)}) collective-permute-start(bf16[2,256,512]{2,1,0:T(8,128)(2,1)} %get-tuple-element.432), channel_id=1, source_target_pairs={{0,2},{1,3},{2,4},{3,5},{4,6},{5,7},{6,0},{7,1},{8,10},{9,11},{10,... | collective-permute-start | bytes 1572872 | tf_op jit(solution)/shard_map/ppermute | solution.py:793
  343.0 49.7 %collective-permute-start.34 = (bf16[2,256,512]{2,1,0:T(8,128)(2,1)}, bf16[2,256,512]{2,1,0:T(8,128)(2,1)}, u32[]{:S(2)}, u32[]{:S(2)}) collective-permute-start(bf16[2,256,512]{2,1,0:T(8,128)(2,1)} %get-tuple-element.433), channel_id=1, source_target_pairs={{0,6},{1,7},{2,0},{3,1},{4,2},{5,3},{6,4},{7,5},{8,14},{9,15},{10,... | collective-permute-start | bytes 1572872 | tf_op jit(solution)/shard_map/ppermute | solution.py:793
  347.3 26.1 %collective-permute-start.31 = (bf16[1024,512]{1,0:T(8,128)(2,1)S(1)}, bf16[1024,512]{1,0:T(8,128)(2,1)S(1)}, u32[]{:S(2)}, u32[]{:S(2)}) collective-permute-start(bf16[1024,512]{1,0:T(8,128)(2,1)S(1)} %pad_maximum_fusion.7), channel_id=1, source_target_pairs={{0,16},{8,24},{16,0},{24,8},{1,17},{9,25},{17,1},{25,9},{2,18},{10... | collective-permute-start | bytes 3145736 | tf_op jit(solution)/shard_map/ppermute | solution.py:780
  351.7 43.1 %collective-permute-start.36 = (bf16[2,2,256,512]{3,2,1,0:T(8,128)(2,1)}, bf16[2,2,256,512]{3,2,1,0:T(8,128)(2,1)}, u32[]{:S(2)}, u32[]{:S(2)}) collective-permute-start(bf16[2,2,256,512]{3,2,1,0:T(8,128)(2,1)} %pad_maximum_fusion.8), channel_id=1, source_target_pairs={{0,16},{8,24},{16,0},{24,8},{1,17},{9,25},{17,1},{25,9},{2,18},{10... | collective-permute-start | bytes 3145736 | tf_op jit(solution)/shard_map/ppermute | solution.py:780
  357.3 37.6 %copy-start.61 = (bf16[4,2,256,512]{3,2,1,0:T(8,128)(2,1)S(1)}, bf16[4,2,256,512]{3,2,1,0:T(8,128)(2,1)}, u32[]{:S(2)}) copy-start(bf16[4,2,256,512]{3,2,1,0:T(8,128)(2,1)} %get-tuple-element.442) | copy-start | bytes 6291460
  398.9 41.3 %collective-permute-start.39 = (bf16[2,2,256,512]{3,2,1,0:T(8,128)(2,1)}, bf16[2,2,256,512]{3,2,1,0:T(8,128)(2,1)}, u32[]{:S(2)}, u32[]{:S(2)}) collective-permute-start(bf16[2,2,256,512]{3,2,1,0:T(8,128)(2,1)} %pad_maximum_fusion.9), channel_id=1, source_target_pairs={{0,16},{8,24},{16,0},{24,8},{1,17},{9,25},{17,1},{25,9},{2,18},{10... | collective-permute-start | bytes 3145736 | tf_op jit(solution)/shard_map/ppermute | solution.py:780
  399.6 37.6 %collective-permute-start.40 = (bf16[512,768]{1,0:T(8,128)(2,1)}, bf16[512,768]{1,0:T(8,128)(2,1)}, u32[]{:S(2)}, u32[]{:S(2)}) collective-permute-start(bf16[512,768]{1,0:T(8,128)(2,1)} %select_convert_fusion), channel_id=1, source_target_pairs={{0,8},{8,0},{16,24},{24,16},{1,9},{9,1},{17,25},{25,17},{2,10},{10... | collective-permute-start | bytes 2359304 | tf_op jit(solution)/shard_map/ppermute | solution.py:780
  401.4 38.8 %collective-permute-start.41 = (bf16[512,768]{1,0:T(8,128)(2,1)}, bf16[512,768]{1,0:T(8,128)(2,1)}, u32[]{:S(2)}, u32[]{:S(2)}) collective-permute-start(bf16[512,768]{1,0:T(8,128)(2,1)} %slice.418), channel_id=1, source_target_pairs={{0,16},{8,24},{16,0},{24,8},{1,17},{9,25},{17,1},{25,9},{2,18},{10... | collective-permute-start | bytes 2359304 | tf_op jit(solution)/shard_map/ppermute | solution.py:780
  401.8 35.5 %collective-permute-start.37 = (bf16[2,256,512]{2,1,0:T(8,128)(2,1)}, bf16[2,256,512]{2,1,0:T(8,128)(2,1)}, u32[]{:S(2)}, u32[]{:S(2)}) collective-permute-start(bf16[2,256,512]{2,1,0:T(8,128)(2,1)} %get-tuple-element.452), channel_id=1, source_target_pairs={{0,4},{1,5},{2,6},{3,7},{4,0},{5,1},{6,2},{7,3},{8,12},{9,13},{10,... | collective-permute-start | bytes 1572872 | tf_op jit(solution)/shard_map/ppermute | solution.py:793
  402.6 34.7 %collective-permute-start.38 = (bf16[2,256,512]{2,1,0:T(8,128)(2,1)}, bf16[2,256,512]{2,1,0:T(8,128)(2,1)}, u32[]{:S(2)}, u32[]{:S(2)}) collective-permute-start(bf16[2,256,512]{2,1,0:T(8,128)(2,1)} %get-tuple-element.453), channel_id=1, source_target_pairs={{0,2},{1,3},{2,4},{3,5},{4,6},{5,7},{6,0},{7,1},{8,10},{9,11},{10,... | collective-permute-start | bytes 1572872 | tf_op jit(solution)/shard_map/ppermute | solution.py:793
  415.4 24.8 %copy-start.64 = (bf16[4,2,256,512]{3,2,1,0:T(8,128)(2,1)S(1)}, bf16[4,2,256,512]{3,2,1,0:T(8,128)(2,1)}, u32[]{:S(2)}) copy-start(bf16[4,2,256,512]{3,2,1,0:T(8,128)(2,1)} %get-tuple-element.439) | copy-start | bytes 6291460
  443.3 21.4 %collective-permute-start.42 = (bf16[2,256,512]{2,1,0:T(8,128)(2,1)}, bf16[2,256,512]{2,1,0:T(8,128)(2,1)}, u32[]{:S(2)}, u32[]{:S(2)}) collective-permute-start(bf16[2,256,512]{2,1,0:T(8,128)(2,1)} %get-tuple-element.467), channel_id=1, source_target_pairs={{0,6},{1,7},{2,0},{3,1},{4,2},{5,3},{6,4},{7,5},{8,14},{9,15},{10,... | collective-permute-start | bytes 1572872 | tf_op jit(solution)/shard_map/ppermute | solution.py:793
  447.1 17.6 %collective-permute-start.43 = (bf16[4,64,768]{2,1,0:T(8,128)(2,1)}, bf16[4,64,768]{2,1,0:T(8,128)(2,1)}, u32[]{:S(2)}, u32[]{:S(2)}) collective-permute-start(bf16[4,64,768]{2,1,0:T(8,128)(2,1)} %fusion.16), channel_id=1, source_target_pairs={{0,1},{1,0},{2,3},{3,2},{4,5},{5,4},{6,7},{7,6},{8,9},{9,8},{10,11... | collective-permute-start | bytes 1179656 | tf_op jit(solution)/shard_map/ppermute | solution.py:789
  464.9 6.4 %collective-permute-start.44 = (f32[640,128]{0,1:T(8,128)S(1)}, f32[640,128]{0,1:T(8,128)S(1)}, u32[]{:S(2)}, u32[]{:S(2)}) collective-permute-start(f32[640,128]{0,1:T(8,128)S(1)} %copy.114), channel_id=1, source_target_pairs={{0,1},{1,0},{2,3},{3,2},{4,5},{5,4},{6,7},{7,6},{8,9},{9,8},{10,11... | collective-permute-start | bytes 983048 | tf_op jit(solution)/shard_map/ppermute | solution.py:789
  471.4 6.7 %collective-permute-start.45 = (bf16[640,128]{0,1:T(8,128)(2,1)S(1)}, bf16[640,128]{0,1:T(8,128)(2,1)S(1)}, u32[]{:S(2)}, u32[]{:S(2)}) collective-permute-start(bf16[640,128]{0,1:T(8,128)(2,1)S(1)} %convert_element_type.650), channel_id=1, source_target_pairs={{0,2},{1,3},{2,0},{3,1},{4,6},{5,7},{6,4},{7,5},{8,10},{9,11},{10,... | collective-permute-start | bytes 491528 | tf_op jit(solution)/shard_map/ppermute | solution.py:889
  473.0 22.8 %collective-permute-start.47 = (bf16[2,256,512]{2,1,0:T(8,128)(2,1)}, bf16[2,256,512]{2,1,0:T(8,128)(2,1)S(1)}, u32[]{:S(2)}, u32[]{:S(2)}) collective-permute-start(bf16[2,256,512]{2,1,0:T(8,128)(2,1)} %get-tuple-element.485), channel_id=1, source_target_pairs={{0,8},{8,0},{16,24},{24,16},{1,9},{9,1},{17,25},{25,17},{2,10},{10... | collective-permute-start | bytes 1572872 | tf_op jit(solution)/shard_map/ppermute | solution.py:780
  473.0 25.3 %collective-permute-start.48 = (bf16[2,256,512]{2,1,0:T(8,128)(2,1)}, bf16[2,256,512]{2,1,0:T(8,128)(2,1)S(1)}, u32[]{:S(2)}, u32[]{:S(2)}) collective-permute-start(bf16[2,256,512]{2,1,0:T(8,128)(2,1)} %get-tuple-element.486), channel_id=1, source_target_pairs={{0,16},{8,24},{16,0},{24,8},{1,17},{9,25},{17,1},{25,9},{2,18},{10... | collective-permute-start | bytes 1572872 | tf_op jit(solution)/shard_map/ppermute | solution.py:780
  473.0 25.3 %collective-permute-start.49 = (bf16[2,256,512]{2,1,0:T(8,128)(2,1)}, bf16[2,256,512]{2,1,0:T(8,128)(2,1)S(1)}, u32[]{:S(2)}, u32[]{:S(2)}) collective-permute-start(bf16[2,256,512]{2,1,0:T(8,128)(2,1)} %get-tuple-element.487), channel_id=1, source_target_pairs={{0,24},{8,16},{16,8},{24,0},{1,25},{9,17},{17,9},{25,1},{2,26},{10... | collective-permute-start | bytes 1572872 | tf_op jit(solution)/shard_map/ppermute | solution.py:780
  477.6 32.5 %collective-permute-start.51 = (bf16[2,64,768]{2,1,0:T(8,128)(2,1)S(1)}, bf16[2,64,768]{2,1,0:T(8,128)(2,1)S(1)}, u32[]{:S(2)}, u32[]{:S(2)}) collective-permute-start(bf16[2,64,768]{2,1,0:T(8,128)(2,1)S(1)} %fusion.29), channel_id=1, source_target_pairs={{0,4},{1,5},{2,6},{3,7},{4,0},{5,1},{6,2},{7,3},{8,12},{9,13},{10,... | collective-permute-start | bytes 589832 | tf_op jit(solution)/shard_map/ppermute | solution.py:889
  478.2 17.5 %collective-permute-start.46 = (bf16[640,128]{0,1:T(8,128)(2,1)S(1)}, bf16[640,128]{0,1:T(8,128)(2,1)S(1)}, u32[]{:S(2)}, u32[]{:S(2)}) collective-permute-start(bf16[640,128]{0,1:T(8,128)(2,1)S(1)} %fusion.27), channel_id=1, source_target_pairs={{0,4},{1,5},{2,6},{3,7},{4,0},{5,1},{6,2},{7,3},{8,12},{9,13},{10,... | collective-permute-start | bytes 491528 | tf_op jit(solution)/shard_map/ppermute | solution.py:889
  498.3 11.7 %collective-permute-start.50 = (f32[128,128]{0,1:T(8,128)S(1)}, f32[128,128]{0,1:T(8,128)S(1)}, u32[]{:S(2)}, u32[]{:S(2)}) collective-permute-start(f32[128,128]{0,1:T(8,128)S(1)} %slice.341), channel_id=1, source_target_pairs={{0,8},{8,0},{16,24},{24,16},{1,9},{9,1},{17,25},{25,17},{2,10},{10... | collective-permute-start | bytes 196616 | tf_op jit(solution)/shard_map/ppermute | solution.py:780
  510.1 9.3 %collective-permute-start.52 = (f32[128,128]{0,1:T(8,128)S(1)}, f32[128,128]{0,1:T(8,128)S(1)}, u32[]{:S(2)}, u32[]{:S(2)}) collective-permute-start(f32[128,128]{0,1:T(8,128)S(1)} %slice_add_fusion.1), channel_id=1, source_target_pairs={{0,16},{8,24},{16,0},{24,8},{1,17},{9,25},{17,1},{25,9},{2,18},{10... | collective-permute-start | bytes 196616 | tf_op jit(solution)/shard_map/ppermute | solution.py:780
  510.6 8.8 %collective-permute-start.53 = (bf16[1,64,768]{2,1,0:T(8,128)(2,1)S(1)}, bf16[1,64,768]{2,1,0:T(8,128)(2,1)S(1)}, u32[]{:S(2)}, u32[]{:S(2)}) collective-permute-start(bf16[1,64,768]{2,1,0:T(8,128)(2,1)S(1)} %dynamic-slice_convert_fusion.6), channel_id=1, source_target_pairs={{0,2},{1,3},{2,0},{3,1},{4,6},{5,7},{6,4},{7,5},{8,10},{9,11},{10,... | collective-permute-start | bytes 294920 | tf_op jit(solution)/shard_map/ppermute | solution.py:889
  (99 other events, 736.0 us)

commit v3 on v2

--- a/solution.py
+++ b/solution.py
@@ -92,6 +92,12 @@
     return jnp.concatenate([window_at(e_ref, limit, s * STEP_P + i) for i in range(STEP_P)], axis=1)
 
 
+def in_halves(step, channels, longest, narrow_ref):
+    both = steps_of(longest, narrow_ref[1])
+    lax.fori_loop(0, both, functools.partial(step, channels), 0)
+    lax.fori_loop(both, jnp.maximum(both, steps_of(longest, narrow_ref[0])), functools.partial(step, channels // 2), 0)
+
+
 def steps_of(longest, narrow):
     return (jnp.maximum(longest - narrow, 0) + STEP_P) // STEP_P
 
@@ -111,28 +117,26 @@
     embed_tile(ids_ref, table_ref, lens, e_ref, longest)
     limit = limits_of(lens)
     channels = conv_ref.shape[0]
-    for block in range(channels // cblock):
-        rows = pl.ds(block * cblock, cblock)
-        top[...] = jnp.full_like(top, -1e30)
-        total[...] = jnp.zeros_like(total)
-
-        def step(s, carry):
-            pre[...] = nn(conv_ref[rows, :], windows_at(e_ref, limit, s))
-            for sub in range(0, cblock, SUB):
-                part = slice(sub, sub + SUB)
-                values = [pre[part, i * tile : (i + 1) * tile] for i in range(STEP_P)]
-                before = top[part, :]
-                best = functools.reduce(jnp.maximum, values, before)
-                top[part, :] = best
-                total[part, :] = total[part, :] * jnp.exp(before - best) + sum(jnp.exp(value - best) for value in values)
-            return carry
-
-        lax.fori_loop(0, steps_of(longest, narrow_ref[block]), step, 0)
-        span = jnp.maximum(lens - width_ref[rows, :], 0)
-        lse = top[...] + jnp.log(total[...])
-        lse_ref[rows, :] = lse
-        pooled = lse - jnp.log((span + 1).astype(F32))
-        feat_ref[rows, :] = (pooled * jax.nn.sigmoid(pooled)).astype(BF16)
+    top[...] = jnp.full_like(top, -1e30)
+    total[...] = jnp.zeros_like(total)
+
+    def step(rows, s, carry):
+        pre[:rows, :] = nn(conv_ref[:rows, :], windows_at(e_ref, limit, s))
+        for sub in range(0, rows, SUB):
+            part = slice(sub, sub + SUB)
+            values = [pre[part, i * tile : (i + 1) * tile] for i in range(STEP_P)]
+            before = top[part, :]
+            best = functools.reduce(jnp.maximum, values, before)
+            top[part, :] = best
+            total[part, :] = total[part, :] * jnp.exp(before - best) + sum(jnp.exp(value - best) for value in values)
+        return carry
+
+    in_halves(step, channels, longest, narrow_ref)
+    span = jnp.maximum(lens - width_ref[...], 0)
+    lse = top[...] + jnp.log(total[...])
+    lse_ref[...] = lse
+    pooled = lse - jnp.log((span + 1).astype(F32))
+    feat_ref[...] = (pooled * jax.nn.sigmoid(pooled)).astype(BF16)
 
 
 def place_kernel(rank_ref, *refs):
@@ -201,7 +205,7 @@
     ranks, grads, refs = refs[:n_parts], refs[n_parts : 2 * n_parts], refs[2 * n_parts :]
     so_far, sums_ref, table_grad_ref, de_ref, dpool, pre, d_pre, found = refs
     tile = ids_ref.shape[1]
-    vocab = table_grad_ref.shape[0]
+    lanes = table_grad_ref.shape[0]
     channels = conv_ref.shape[0]
     first = (base + pl.program_id(0)) * tile
 
@@ -219,32 +223,29 @@
         row = first + lax.broadcasted_iota(jnp.int32, (tile, rank_ref.shape[1]), 0)
         moved = moved + nn(jnp.where(rank_ref[...] == row, 1.0, 0.0).astype(BF16), grad_ref[...])
     moved = moved.T
-    for block in range(channels // cblock):
-        rows = slice(block * cblock, (block + 1) * cblock)
-        span = jnp.maximum(lens - width_ref[rows, :], 0)
-        pooled = lse_ref[rows, :] - jnp.log((span + 1).astype(F32))
-        sigma = jax.nn.sigmoid(pooled)
-        dpool[...] = moved[rows, :] * (sigma + pooled * sigma * (1 - sigma))
-
-        def step(s, carry):
-            windows = windows_at(e_ref, limit, s)
-            pre[...] = nn(conv_ref[rows, :], windows)
-            for sub in range(0, cblock, SUB):
-                part = slice(sub, sub + SUB)
-                low, scale = lse_ref[block * cblock + sub : block * cblock + sub + SUB, :], dpool[part, :]
-                for i in range(STEP_P):
-                    cols = slice(i * tile, (i + 1) * tile)
-                    d_pre[part, cols] = (jnp.exp(pre[part, cols] - low) * scale).astype(BF16)
-            back = nn(back_ref[:, rows], d_pre[...])
+    span = jnp.maximum(lens - width_ref[...], 0)
+    pooled = lse_ref[...] - jnp.log((span + 1).astype(F32))
+    sigma = jax.nn.sigmoid(pooled)
+    dpool[...] = moved * (sigma + pooled * sigma * (1 - sigma))
+
+    def step(rows, s, carry):
+        windows = windows_at(e_ref, limit, s)
+        pre[:rows, :] = nn(conv_ref[:rows, :], windows)
+        for sub in range(0, rows, SUB):
+            part = slice(sub, sub + SUB)
+            low, scale = lse_ref[part, :], dpool[part, :]
             for i in range(STEP_P):
-                at = pl.ds(pl.multiple_of((s * STEP_P + i) * CHAR_DIM, CHAR_DIM), TAPS)
-                de_ref[at, :] += back[:TAPS, i * tile : (i + 1) * tile]
-            sums_ref[rows, :] += nt(d_pre[...], windows)
-            return carry
-
-        lax.fori_loop(0, steps_of(longest, narrow_ref[block]), step, 0)
-
-    letter = lax.broadcasted_iota(jnp.int32, (vocab, tile), 0)
+                cols = slice(i * tile, (i + 1) * tile)
+                d_pre[part, cols] = (jnp.exp(pre[part, cols] - low) * scale).astype(BF16)
+        back = nn(back_ref[:, :rows], d_pre[:rows, :])
+        for i in range(STEP_P):
+            at = pl.ds(pl.multiple_of((s * STEP_P + i) * CHAR_DIM, CHAR_DIM), TAPS)
+            de_ref[at, :] += back[:TAPS, i * tile : (i + 1) * tile]
+        sums_ref[:rows, :] += nt(d_pre[:rows, :], windows)
+        return carry
+
+    in_halves(step, channels, longest, narrow_ref)
+    letter = lax.broadcasted_iota(jnp.int32, (found.shape[0], tile), 0)
 
     def spread(s, carry):
         parts = []
@@ -256,7 +257,7 @@
             parts.append(jnp.concatenate([high, (value - high.astype(F32)).astype(BF16)], axis=0))
             row = ids_ref[pl.ds(p, 1), :].astype(jnp.int32)
             found[:, i * tile : (i + 1) * tile] = jnp.where(letter == row, 1.0, 0.0).astype(BF16)
-        table_grad_ref[...] += nt(found[...], jnp.concatenate(parts, axis=1))
+        table_grad_ref[: found.shape[0], :] += nt(found[...], jnp.concatenate(parts, axis=1))
         return carry
 
     lax.fori_loop(0, (longest + STEP_P - 1) // STEP_P, spread, 0)
@@ -265,7 +266,7 @@
     def _():
         both = table_grad_ref[...].T
         total = both[:CHAR_DIM] + both[CHAR_DIM:]
-        for piece in range(vocab // LANES):
+        for piece in range(lanes // LANES):
             at = channels + piece * CHAR_DIM
             sums_ref[at : at + CHAR_DIM, :] += total[:, piece * LANES : (piece + 1) * LANES]
 
@@ -291,12 +292,12 @@
         out_specs=full(*so_far.shape),
         out_shape=jax.ShapeDtypeStruct(so_far.shape, F32),
         scratch_shapes=[
-            pltpu.VMEM((vocab, 2 * CHAR_DIM), F32),
+            pltpu.VMEM((-(-vocab // LANES) * LANES, 2 * CHAR_DIM), F32),
             pltpu.VMEM((SLOTS_E * CHAR_DIM, tile), F32),
             pltpu.VMEM((cblock, tile), F32),
             pltpu.VMEM((cblock, STEP_P * tile), F32),
             pltpu.VMEM((cblock, STEP_P * tile), BF16),
-            pltpu.VMEM((vocab, STEP_P * tile), BF16),
+            pltpu.VMEM((-(-vocab // 16) * 16, STEP_P * tile), BF16),
         ],
         compiler_params=pltpu.CompilerParams(vmem_limit_bytes=48 * MIB),
         cost_estimate=lasting(15),
@@ -331,7 +332,7 @@
     conv_all = jnp.concatenate([taps, under.astype(BF16)])
     conv_back = jnp.pad(taps, ((0, DEPTH - TAPS), (0, 0)))
     table_t = jnp.pad(lax.reduce_precision(char_table, 8, 7).T, ((0, 0), (0, lanes - vocab)))
-    narrow = widths[::cblock]
+    narrow = widths[:: channels // 2]
     return rank, data, table_t, conv_all.T, conv_back, widths[:, None], narrow
 
 
@@ -341,12 +342,6 @@
     for power in range(6):
         widths = widths + (channel >= whole * 2**power // 64).astype(jnp.int32)
     return widths
-
-
-def unit_slots(owners, slots_each):
-    order = jnp.arange(owners.shape[0], dtype=jnp.int32)
-    before = (owners[:, None] == owners[None, :]) & (order[:, None] > order[None, :])
-    return owners * slots_each + jnp.sum(before.astype(jnp.int32), axis=1)
 
 
 def load_pieces(table_ref, pieces, rows, dest, sems, half=None, proj=None):
@@ -702,15 +697,20 @@
     )(at, *grads, weight, one, two, average, *so_far)
 
 
-def choose_kernel(n_from, table_ref, proj, *refs):
+def slot_of(owner_ref, unit):
+    return sum(jnp.where(owner_ref[before] == owner_ref[unit], 1, 0) for before in range(unit)) if unit else 0
+
+
+def choose_kernel(n_from, owner_ref, proj, *refs):
     arrived, outs = refs[:n_from], refs[n_from:]
     rows, width = arrived[0].shape[1:]
+    here = lax.axis_index("filt")
     for unit in range(UNITS):
         for step, ref in enumerate(arrived):
 
-            @pl.when(table_ref[0, unit] == step)
+            @pl.when(owner_ref[unit] ^ here == step)
             def _(ref=ref, unit=unit):
-                outs[unit // 2][unit % 2, :rows, :] = ref[table_ref[1, unit]]
+                outs[unit // 2][unit % 2, :rows, :] = ref[slot_of(owner_ref, unit)]
 
     under, part = proj.shape[0], proj.shape[1] // 2
     if outs[1].shape[1] > rows:
@@ -719,7 +719,7 @@
             outs[1][side, rows:, :part] = proj[:, side * part : (side + 1) * part].astype(BF16)
 
 
-def choose_units(table, arrived, proj, packed):
+def choose_units(owners, arrived, proj, packed):
     slots, rows, width = arrived[0].shape
     shapes = [(2, rows, width), (2, rows + (proj.shape[0] if packed else 0), width)]
     return pl.pallas_call(
@@ -731,14 +731,18 @@
         compiler_params=params(),
         cost_estimate=lasting(3),
         name="choose_units",
-    )(table, proj, *arrived)
-
-
-def return_kernel(counts, table_ref, *refs):
+    )(owners, proj, *arrived)
+
+
+def return_kernel(counts, owner_ref, *refs):
     layers = (refs[: counts[0]], refs[counts[0] : counts[0] + counts[1]])
+    here = lax.axis_index("filt")
     for step, out in enumerate(refs[counts[0] + counts[1] :]):
         for slot in range(SLOTS):
-            taken = table_ref[step, slot]
+            taken = -1
+            for unit in range(UNITS):
+                fits = (owner_ref[unit] ^ here == step) & (slot_of(owner_ref, unit) == slot)
+                taken = jnp.where(fits, unit, taken)
             for unit in range(UNITS):
 
                 @pl.when(taken == unit)
@@ -750,9 +754,9 @@
                 out[slot] = jnp.zeros(out.shape[1:], BF16)
 
 
-def return_units(table, layers, count):
+def return_units(owners, layers, count):
     shape = layers[0][0].shape
-    part = min(64, shape[1])
+    part = min(128, shape[1])
     block = pl.BlockSpec((2, part, shape[2]), lambda i: (0, i, 0))
     terms = list(layers[0]) + list(layers[1])
     return pl.pallas_call(
@@ -764,7 +768,7 @@
         compiler_params=params(),
         cost_estimate=lasting(3),
         name="return_units",
-    )(table, *terms)
+    )(owners, *terms)
 
 
 class Places:
@@ -849,12 +853,13 @@
 
 def sent_over_y(parts, group):
     near, arrived = parts
-    return jnp.stack([(near[1][k].astype(F32) + arrived[1][k].astype(F32)).astype(BF16) for k in group])
+    return (near[1][group].astype(F32) + arrived[1][group].astype(F32)).astype(BF16)
 
 
 def kept_over_y(parts, turned, group):
     near, arrived = parts
-    return [near[0][k].astype(F32) + arrived[0][k].astype(F32) + turned[n].astype(F32) for n, k in enumerate(group)]
+    steps = range(group.start, group.stop)
+    return [near[0][k].astype(F32) + arrived[0][k].astype(F32) + turned[n].astype(F32) for n, k in enumerate(steps)]
 
 
 def sum_general(place, blocks):
@@ -941,7 +946,6 @@
     words_y = words_dev // n_y
     chunks, chunk_words = range(2), words_y // 2
     steps_y = list(range(1, n_y))
-    slot_index = unit_slots(highway_owner, SLOTS)
     mine_first = place.x == 0
     over_core, over_x, over_y, over_z = place.over_core, place.over_x, place.over_y, place.over_z
 
@@ -967,8 +971,7 @@
     from_owner = [block_of(0)] + [place.over_filt(block_of(step), step) for step in range(1, n_filt)]
     kept = convolve(splits[: len(splits) // 2], narrow)
     from_owner, kept, narrow = settle(from_owner, kept, narrow)
-    owner_table = jnp.stack([highway_owner ^ place.f, slot_index % SLOTS])
-    blocks = choose_units(owner_table, from_owner, proj_weight, direct)
+    blocks = choose_units(highway_owner, from_owner, proj_weight, direct)
     bias_float = lax.reduce_precision(dense_bias, 8, 7)
 
     def half_bias(unit):
@@ -977,7 +980,7 @@
 
     layer_bias = [jnp.stack([half_bias(2 * layer), half_bias(2 * layer + 1)]) for layer in range(2)]
 
-    blocks, narrow, sent = settle(blocks, narrow, out_grad)
+    blocks, narrow, sent, layer_bias = settle(blocks, narrow, out_grad, layer_bias)
     grad_mate = over_x(sent)
     if direct:
         first_y = [over_y(block, 1) for block in blocks]
@@ -990,26 +993,31 @@
         own = [placed[0], over_y(placed[1], 1)]
         mate = [over_x(placed[0])]
         far = over_z(blocks[0], 2)
-        own, mate, far, near, blocks, first_y, layer_bias, grad_mate = settle(
-            own, mate, far, near, blocks, first_y, layer_bias, grad_mate
+        sent = jnp.stack([near[0], near[1], jnp.zeros_like(near[0])])
+        own, mate, far, sent, blocks, first_y, layer_bias, grad_mate = settle(
+            own, mate, far, sent, blocks, first_y, layer_bias, grad_mate
         )
 
         out_grads = [jnp.where(mine_first, out_grad, grad_mate), jnp.where(mine_first, grad_mate, out_grad)]
-        sent = jnp.stack([near[0], near[1], far])
+        out_sum = jnp.sum(out_grad, axis=0, dtype=F32)
+        sent = lax.dynamic_update_index_in_dim(sent, far, 2, 0)
         sent_y = over_y(sent, 1)
         mate = mate + [over_x(own[1])]
         near_one = [over_z(blocks[1], k) for k in (1, 3)]
         sent_core = over_core(sent)
         start = jnp.stack([blocks[0], first_y[0]])
-        sent_y, sent_core, start, mate, near_one, blocks = settle(sent_y, sent_core, start, mate, near_one, blocks)
-
         table = [gather_table(place, layer, rows, width, rows_proj) for layer in range(2)]
+        sent_y, sent_core, start, mate, near_one, blocks, out_grads, table, out_sum = settle(
+            sent_y, sent_core, start, mate, near_one, blocks, out_grads, table, out_sum
+        )
+
         gathered = [(table[0], [start, sent, sent_y, over_core(start), sent_core, over_core(sent_y)], rows)]
         far_one = over_z(blocks[1], 2)
         near_y = over_y(jnp.stack(near_one), 1)
     else:
         mate = [over_x(part) for part in own]
         gathered = [(*found, rows) for found in gather_general(place, blocks)]
+        out_sum = jnp.sum(out_grad, axis=0, dtype=F32)
         out_grads = [jnp.where(mine_first, out_grad, grad_mate), jnp.where(mine_first, grad_mate, out_grad)]
 
     forward, x_one_mate = [], []
@@ -1060,7 +1068,7 @@
         )
         if chunk == 0 and direct:
             one, parts_zero[0], up_one[1] = settle(one, parts_zero[0], up_one[1])
-            sent = sent_over_y(one, range(place.n_z))
+            sent = sent_over_y(one, slice(0, place.n_z))
             sent, up_one[1] = settle(sent, up_one[1])
             one_y = over_y(sent, 1)
         arrived_zero.append(over_x(parts_zero[chunk][3]))
@@ -1068,7 +1076,7 @@
     sums_zero = sums[0] + sums[1]
     blocks = highway_weight_grad(targets, [own + mate], d_first, d_gate, rows, width)
     blocks, up, arrived_zero[0] = settle(blocks, up, arrived_zero[0])
-    groups = [[2, 1], [3, 0]]
+    groups = [slice(2, 4), slice(0, 2)]
     if not direct:
         sum_zero = sum_general(place, blocks)
     partial = [highway_back(*gathered[0], d_first[chunk], d_gate[chunk], up[chunk]) for chunk in chunks]
@@ -1076,12 +1084,12 @@
         partial, blocks, arrived_zero[1], one_y = settle(partial, blocks, arrived_zero[1], one_y)
         zero = (blocks[:2], over_core(blocks[2]))
     if direct:
-        one_here = kept_over_y(one, one_y, range(place.n_z))
+        one_here = kept_over_y(one, one_y, slice(0, place.n_z))
         one_sent = [one_here[k].astype(BF16) for k in (2, 1, 3)]
         one_here = one_here[0]
         one_sent, one_here, partial = settle(one_sent, one_here, partial)
         one_z = [over_z(value, k) for value, k in zip(one_sent, (2, 1, 3))]
-    groups = [[2, 1], [3, 0]]
+    groups = [slice(2, 4), slice(0, 2)]
     if not direct:
         sum_zero = sum_general(place, blocks)
     partial = [highway_back(*gathered[0], d_first[chunk], d_gate[chunk], up[chunk]) for chunk in chunks]
@@ -1096,7 +1104,7 @@
                 [(partial[chunk][:, cols] + arrived_zero[chunk][:, cols].astype(F32)).astype(BF16) for chunk in chunks]
             )
         )
-    groups = [[2, 1], [3, 0]]
+    groups = [slice(2, 4), slice(0, 2)]
     returned = [over_y(value, step) if step else value for step, value in enumerate(feature_grad)]
     if direct:
         returned[0], x_two_low, vectors = settle(returned[0], x_two_low, vectors)
@@ -1107,16 +1115,14 @@
     vectors_here = jnp.where(mine_first, vectors[0], vectors[1])
     ranks = [part.T for part in rank_parts]
 
-    wanted = (place.f ^ jnp.arange(n_filt, dtype=jnp.int32))[:, None] * SLOTS + jnp.arange(SLOTS, dtype=jnp.int32)[None, :]
-    fits = slot_index[None, None, :] == wanted[:, :, None]
-    return_table = jnp.max(jnp.where(fits, jnp.arange(UNITS, dtype=jnp.int32), -1), axis=2)
     if direct:
-        returned, narrow, ranks = settle(returned, narrow, ranks)
+        zero_sent = sent_over_y(zero, groups[1])
+        returned, narrow, ranks, zero_sent = settle(returned, narrow, ranks, zero_sent)
 
     def convolve_back(n, narrow, so_far):
         (begin, _), (_, lse, sorted_ids, embedded) = splits[n], kept[n]
         return conv_backward(
-            ranks, sorted_ids, embedded, table_t.shape[1], conv_t, conv_back, width_col, narrow, lse, returned, width, begin, tile, so_far
+            ranks, sorted_ids, embedded, vocab_count, conv_t, conv_back, width_col, narrow, lse, returned, width, begin, tile, so_far
         )
 
     home = jnp.arange(n_filt, dtype=jnp.int32)
@@ -1129,7 +1135,7 @@
         return out.reshape(-1)
 
     bias_local = jnp.concatenate(
-        [natural(sums[unit]) for sums in (sums_zero, sums_one) for unit in range(2)] + [jnp.sum(out_grad, axis=0, dtype=F32)]
+        [natural(sums[unit]) for sums in (sums_zero, sums_one) for unit in range(2)] + [out_sum]
     )
     table_rows = table_t.shape[1] // LANES * CHAR_DIM
     bias_rows = -(-bias_local.size // DEPTH)
@@ -1146,20 +1152,19 @@
                 back, narrow, one_z, zero_y[0], zero, vectors_away, proj_away
             )
             zero_here = kept_over_y(zero, zero_y[0], groups[0])
-            zero_z, zero_sent, narrow = settle([value.astype(BF16) for value in zero_here], sent_over_y(zero, groups[1]), narrow)
-            zero_z = [over_z(value, k) for value, k in zip(zero_z, groups[0])]
+            zero_z, zero_sent, narrow = settle([value.astype(BF16) for value in zero_here], zero_sent, narrow)
+            zero_z = [over_z(value, k) for value, k in zip(zero_z, (2, 3))]
             zero_y.append(over_y(zero_sent, 1))
-            proj_y = over_y(proj_away[0], 1)
             vectors_arrived = over_x(vectors_away)
         if direct and n == 2:
-            back, zero_z, narrow, zero_y, vectors_arrived, proj_y = settle(back, zero_z, narrow, zero_y, vectors_arrived, proj_y)
-            last, zero_here = kept_over_y(zero, zero_y[1], groups[1])
+            back, zero_z, narrow, zero_y, vectors_arrived, proj_away = settle(back, zero_z, narrow, zero_y, vectors_arrived, proj_away)
+            zero_here, last = kept_over_y(zero, zero_y[1], groups[1])
             last, zero_here, narrow = settle(last.astype(BF16), zero_here, narrow)
-            last = over_z(last, 3)
-            proj_rows = rows_over_core(place, proj_here + proj_y.astype(F32))
+            last = over_z(last, 1)
+            proj_y = over_y(proj_away[0], 1)
     if direct:
-        back, last, proj_rows = settle(back, last, proj_rows)
-        slot_grads = return_units(return_table, [[zero_here] + zero_z + [last], [one_here] + one_z], n_filt)
+        back, last, proj_y = settle(back, last, proj_y)
+        slot_grads = return_units(highway_owner, [[zero_here] + zero_z + [last], [one_here] + one_z], n_filt)
     else:
         proj_y = [over_y(value, step) for value, step in zip(proj_away, steps_y)]
         proj_grad = lax.psum_scatter(proj_here + sum(value.astype(F32) for value in proj_y), "dp", scatter_dimension=0, tiled=True)
@@ -1175,11 +1180,12 @@
     optimizer = (highway_weight, highway_moment_one, highway_moment_two, highway_average)
     columns = (place.f ^ jnp.arange(n_filt, dtype=jnp.int32)) * width
     if direct:
-        slot_grads, small, proj_rows, vectors_arrived = settle(slot_grads, small, proj_rows, vectors_arrived)
+        slot_grads, small, proj_y, vectors_arrived = settle(slot_grads, small, proj_y, vectors_arrived)
+        proj_rows = rows_over_core(place, proj_here + proj_y.astype(F32))
         arrived_slots = [place.over_filt(slot_grads[step], step) for step in range(1, n_filt)]
         small = small + swap_z(place, small.astype(BF16), 1).astype(F32)
         small = small + swap_z(place, small.astype(BF16), 2).astype(F32)
-        small, arrived_slots = settle(small, arrived_slots)
+        small, arrived_slots, proj_rows = settle(small, arrived_slots, proj_rows)
         conv_sums, small = small[:width], small[width:]
         slot_grads = [slot_grads[0]] + arrived_slots
         small = small + over_x(small)
@@ -1192,7 +1198,7 @@
         updates, small, proj_rows = settle(updates, small, proj_rows)
         proj_grad = (proj_rows[0] + proj_rows[1].astype(F32)).reshape(rows_proj, out_width)
     else:
-        slot_grads = return_units(return_table, [[sum_zero], [sum_one]], n_filt)
+        slot_grads = return_units(highway_owner, [[sum_zero], [sum_one]], n_filt)
         slot_grads = [slot_grads[0]] + [place.over_filt(slot_grads[step], step) for step in range(1, n_filt)]
         conv_sums, small = small[:width], small[width:]
         updates = owner_update(0, columns, slot_grads, *optimizer)

time: 529 us -> 504 us (0.953)
  other arithmetic: 54.2 us -> 41.3 us
  starting transfers between devices: 53.3 us -> 64.6 us
  waiting for transfers between devices: 113 us -> 104 us
  local copies, waits for them, and re-layouts: 28.6 us -> 20.4 us
  Pallas kernels: 268 us -> 261 us
    ppermute x12, waiting for transfers between devices: 57.8 us -> 45.6 us  [over_z(): return lax.ppermute(value, 'dp', pairs)]
    ppermute x12, starting transfers between devices: 12.7 us -> 24.3 us  [over_z(): return lax.ppermute(value, 'dp', pairs)]
    ppermute x29, waiting for transfers between devices: 42.2 us -> 49.1 us  [over_filt(): lax.ppermute(value, 'filt', [(i, i ^ step) for i in range(self.n_filt)])]
    unnamed x224 -> x204, local copies, waits for them, and re-layouts: 19 us -> 13.2 us
    another operation x9 -> x4, other arithmetic: 7.09 us -> 1.49 us  [the longest x1 1.41 us: per_device(): sent = jnp.stack([near[0], near[1], jnp.zeros_like(near[0])])]
  transfers between devices with their start and end apart: 54 -> 54, of which waited for: 13 -> 16; matrix products, arithmetic and copies ran while one was open for 9% -> 8% of each run, Pallas kernels for 51% -> 52%
where the time goes in v3:
time: 504 us; the launch traced here: 497 us
  Pallas kernels  261 us (52%)
  waiting for transfers between devices  104 us (21%)
  starting transfers between devices  64.6 us (13%)
  other arithmetic  41.3 us (8%)
  local copies, waits for them, and re-layouts  20.4 us (4%)
    pallas_call x4, Pallas kernels, conv_backward(): pl.pallas_call(functools.partial(conv_backward_kernel, cblock, len(ranks)...  57.3 us
    ppermute x29, waiting for transfers between devices, over_filt(): lax.ppermute(value, 'filt', [(i, i ^ step) for i in range(self.n_filt)])  49.1 us
    ppermute x12, waiting for transfers between devices, over_z(): return lax.ppermute(value, 'dp', pairs)  45.6 us
    pallas_call x4, Pallas kernels, conv_forward(): pl.pallas_call(functools.partial(conv_forward_kernel, cblock, base), grid...  39.9 us
    ppermute x29, starting transfers between devices, over_filt(): lax.ppermute(value, 'filt', [(i, i ^ step) for i in range(self.n_filt)])  34.5 us
    pallas_call x2, Pallas kernels, highway_turn(): pl.pallas_call(functools.partial(turn_kernel, len(pieces), block_rows, wi...  33.7 us
    pallas_call x4, Pallas kernels, highway_back(): pl.pallas_call(functools.partial(back_kernel, len(pieces), block_rows), g...  30.6 us
    pallas_call x2, Pallas kernels, highway_weight_grad(): pl.pallas_call(functools.partial(weight_grad_kernel, len(xs), len(xs[0]),...  30.3 us
  transfers between devices with their start and end apart: 54, of which 16 were waited for; matrix products, arithmetic and copies ran while one was open for 8% of the time, Pallas kernels for 52%

profile of v3, /device:TPU:0, one launch (start us, length us, event | category | flops | bytes accessed | tf_op | source)
XLA Modules:
  0.0 496.9 jit_solution(8483621379907869109)
XLA Ops:
  0.7 3.7 dynamic-slice_convert_fusion
  4.4 3.9 collective-permute-start.2
  9.3 1.8 convert_reduce_fusion
  12.3 7.0 %conv_forward.5 = (bf16[512,256]{1,0:T(8,128)(2,1)S(1)}, f32[512,256]{1,0:T(8,128)S(1)}, f32[64,256]{1,0:T(8,128)S(1)}, bf16[1024,256]{1,0:T(8,128)(2,1)S(1)}) custom-call(s32[2]{0:T(128)S(1)} %slice.229.narrow_ref, s32[2048,1]{1,0:T(8,128)S(1)} %copy.97.rank_ref, bf16[64,2048]{1,0:T(8,128)(2,1)S(1)} %fusion.12.data_ref, f32[16,384]{1,0:T(8,128)S(1)} %pad.19.table_ref, ...), custom_call_target="tpu_custom_call" | custom-call | flops 110000000 | bytes 330000 | tf_op jit(solution)/shard_map/conv_forward/pallas_call | solution.py:160
  19.4 11.9 %conv_forward.4 = (bf16[512,256]{1,0:T(8,128)(2,1)S(1)}, f32[512,256]{1,0:T(8,128)S(1)}, f32[64,256]{1,0:T(8,128)S(1)}, bf16[1024,256]{1,0:T(8,128)(2,1)S(1)}) custom-call(s32[2]{0:T(128)S(1)} %slice.229.narrow_ref, s32[2048,1]{1,0:T(8,128)S(1)} %copy.97.rank_ref, bf16[64,2048]{1,0:T(8,128)(2,1)S(1)} %fusion.12.data_ref, f32[16,384]{1,0:T(8,128)S(1)} %pad.19.table_ref, ...), custom_call_target="tpu_custom_call" | custom-call | flops 110000000 | bytes 330000 | tf_op jit(solution)/shard_map/conv_forward/pallas_call | solution.py:160
  34.2 2.8 choose_units.1
  40.3 3.6 collective-permute-start.4
  44.6 9.7 %conv_forward.6 = (bf16[512,512]{1,0:T(8,128)(2,1)S(1)}, f32[512,512]{1,0:T(8,128)S(1)}, f32[64,512]{1,0:T(8,128)S(1)}, bf16[1024,512]{1,0:T(8,128)(2,1)S(1)}) custom-call(s32[2]{0:T(128)S(1)} %slice.229.narrow_ref, s32[2048,1]{1,0:T(8,128)S(1)} %copy.97.rank_ref, bf16[64,2048]{1,0:T(8,128)(2,1)S(1)} %fusion.12.data_ref, f32[16,384]{1,0:T(8,128)S(1)} %pad.19.table_ref, ...), custom_call_target="tpu_custom_call" | custom-call | flops 110000000 | bytes 330000 | tf_op jit(solution)/shard_map/conv_forward/pallas_call | solution.py:160
  55.3 11.3 %conv_forward.7 = (bf16[512,1024]{1,0:T(8,128)(2,1)S(1)}, f32[512,1024]{1,0:T(8,128)S(1)}, f32[64,1024]{1,0:T(8,128)S(1)}, bf16[1024,1024]{1,0:T(8,128)(2,1)}) custom-call(s32[2]{0:T(128)S(1)} %slice.229.narrow_ref, s32[2048,1]{1,0:T(8,128)S(1)} %copy.97.rank_ref, bf16[64,2048]{1,0:T(8,128)(2,1)S(1)} %fusion.12.data_ref, f32[16,384]{1,0:T(8,128)S(1)} %pad.19.table_ref, ...), custom_call_target="tpu_custom_call" | custom-call | flops 110000000 | bytes 330000 | tf_op jit(solution)/shard_map/conv_forward/pallas_call | solution.py:160
  67.9 3.0 place_words.3
  70.9 3.0 place_words.2.refs_0_
  76.7 20.6 %collective-permute-done.10 = bf16[2,256,512]{2,1,0:T(8,128)(2,1)S(1)} collective-permute-done((bf16[2,256,512]{2,1,0:T(8,128)(2,1)S(1)}, bf16[2,256,512]{2,1,0:T(8,128)(2,1)S(1)}, u32[]{:S(2)}, u32[]{:S(2)}) %collective-permute-start.10) | collective-permute-done | bytes 524320 | tf_op jit(solution)/shard_map/ppermute | solution.py:797
  98.3 1.6 collective-permute-start.11
  99.9 1.7 collective-permute-start.13
  102.1 3.0 collective-permute-start.15
  108.4 3.0 broadcast_select_fusion
  111.5 9.0 %collective-permute-done.15 = bf16[2,320,512]{2,1,0:T(8,128)(2,1)S(1)} collective-permute-done((bf16[2,320,512]{2,1,0:T(8,128)(2,1)}, bf16[2,320,512]{2,1,0:T(8,128)(2,1)S(1)}, u32[]{:S(2)}, u32[]{:S(2)}) %collective-permute-start.15) | collective-permute-done | bytes 655392 | tf_op jit(solution)/shard_map/ppermute | solution.py:797
  120.5 13.6 %collective-permute-done.14 = bf16[2,320,512]{2,1,0:T(8,128)(2,1)S(1)} collective-permute-done((bf16[2,320,512]{2,1,0:T(8,128)(2,1)}, bf16[2,320,512]{2,1,0:T(8,128)(2,1)S(1)}, u32[]{:S(2)}, u32[]{:S(2)}) %collective-permute-start.14) | collective-permute-done | bytes 655392 | tf_op jit(solution)/shard_map/ppermute | solution.py:797
  142.0 11.9 %highway_forward.2 = (f32[512,1024]{1,0:T(8,128)}, bf16[512,1024]{1,0:T(8,128)(2,1)}, bf16[512,1024]{1,0:T(8,128)(2,1)}, bf16[512,1024]{1,0:T(8,128)(2,1)}, bf16[512,1024]{1,0:T(8,128)(2,1)}) custom-call(s32[3,16]{1,0:T(4,128)} %get-tuple-element.318.table_ref, f32[2,1024]{1,0:T(2,128)} %pad_maximum_fusion.6.bias_ref, bf16[1024,512]{1,0:T(8,128)(2,1)} %copy-done, ...), custom_call_target="tpu_custom_call" | custom-call | flops 100000000 | bytes 300000 | tf_op jit(solution)/shard_map/highway_forward/pallas_call | solution.py:561
  154.0 1.7 collective-permute-start.21
  155.7 12.1 %highway_forward.3 = (f32[512,1024]{1,0:T(8,128)}, bf16[512,1024]{1,0:T(8,128)(2,1)}, bf16[512,1024]{1,0:T(8,128)(2,1)}, bf16[512,1024]{1,0:T(8,128)(2,1)}, bf16[512,1024]{1,0:T(8,128)(2,1)}) custom-call(s32[3,16]{1,0:T(4,128)} %get-tuple-element.318.table_ref, f32[2,1024]{1,0:T(2,128)} %pad_maximum_fusion.6.bias_ref, bf16[1024,512]{1,0:T(8,128)(2,1)} %copy-done, ...), custom_call_target="tpu_custom_call" | custom-call | flops 100000000 | bytes 300000 | tf_op jit(solution)/shard_map/highway_forward/pallas_call | solution.py:561
  167.8 2.4 collective-permute-done.18
  170.6 1.6 pad_maximum_fusion.refs_0_
  172.3 14.4 %collective-permute-done.20 = bf16[2,320,512]{2,1,0:T(8,128)(2,1)S(1)} collective-permute-done((bf16[2,320,512]{2,1,0:T(8,128)(2,1)}, bf16[2,320,512]{2,1,0:T(8,128)(2,1)S(1)}, u32[]{:S(2)}, u32[]{:S(2)}) %collective-permute-start.20) | collective-permute-done | bytes 655392 | tf_op jit(solution)/shard_map/ppermute | solution.py:784
  186.6 2.2 pad_maximum_fusion.1.refs_1_
  189.0 1.9 collective-permute-start.24
  192.4 1.6 collective-permute-done.23.refs_3_
  194.0 16.6 %highway_turn.2 = (bf16[512,1024]{1,0:T(8,128)(2,1)}, bf16[512,1024]{1,0:T(8,128)(2,1)}, bf16[512,1024]{1,0:T(8,128)(2,1)}, f32[512,1024]{1,0:T(8,128)}, bf16[51...) custom-call(s32[3,16]{1,0:T(4,128)} %get-tuple-element.319.table_ref, ...), custom_call_target="tpu_custom_call" | custom-call | flops 160000000 | bytes 480000 | tf_op jit(solution)/shard_map/highway_turn/pallas_call | solution.py:583
  210.7 1.9 collective-permute-start.25
  212.5 2.5 collective-permute-done.24.mate.refs_3_
  216.0 17.1 %highway_turn.3 = (bf16[512,1024]{1,0:T(8,128)(2,1)}, bf16[512,1024]{1,0:T(8,128)(2,1)}, bf16[512,1024]{1,0:T(8,128)(2,1)}, f32[512,1024]{1,0:T(8,128)}, bf16[51...) custom-call(s32[3,16]{1,0:T(4,128)} %get-tuple-element.319.table_ref, ...), custom_call_target="tpu_custom_call" | custom-call | flops 160000000 | bytes 480000 | tf_op jit(solution)/shard_map/highway_turn/pallas_call | solution.py:583
  233.1 1.9 collective-permute-start.26
  235.6 15.1 %highway_weight_grad.2 = (bf16[4,2,256,512]{3,2,1,0:T(8,128)(2,1)}, bf16[4,2,256,512]{3,2,1,0:T(8,128)(2,1)}, bf16[2,4,2,256,512]{4,3,2,1,0:T(8,128)(2,1)}) custom-call(s32[2,4]{1,0:T(2,128)} %pad_add_fusion.2.table_ref, bf16[512,1024]{1,0:T(8,128)(2,1)} %get-tuple-element.335.own.refs_0_, bf16[512,1024]{1,0:T(8,128)(2,1)} %copy-done.36, ...), custom_call_target="tpu_custom_call" | custom-call | flops 150000000 | bytes 450000 | tf_op jit(solution)/shard_map/highway_weight_grad/pallas_call | solution.py:640
  250.7 7.6 %highway_back.4.partial = f32[512,1024]{1,0:T(8,128)} custom-call(s32[3,16]{1,0:T(4,128)} %get-tuple-element.319.table_ref, bf16[512,1024]{1,0:T(8,128)(2,1)} %get-tuple-element.352.refs_4_.d_first, bf16[512,1024]{1,0:T(8,128)(2,1)} %get-tuple-element.353.refs_6_.d_gate, f32[512,1024]{1,0:T(8,128)} %get-tuple-element.368.up, ...), custom_call_target="tpu_custom_call" | custom-call | flops 60000000 | bytes 180000 | tf_op jit(solution)/shard_map/highway_back/pallas_call | solution.py:620
  259.6 8.2 %highway_slopes.2 = (bf16[512,1024]{1,0:T(8,128)(2,1)}, bf16[512,1024]{1,0:T(8,128)(2,1)}, f32[512,1024]{1,0:T(8,128)}, bf16[512,1024]{1,0:T(8,128)(2,1)}, f32[2,1024]{1,0:T(2,128)}) custom-call(s32[3,16]{1,0:T(4,128)} %get-tuple-element.318.table_ref, f32[512,1024]{1,0:T(8,128)} %highway_back.4.partial, bf16[512,1024]{1,0:T(8,128)(2,1)} %collective-permute-done.25.arrived, ...), custom_call_target="tpu_custom_call" | custom-call | flops 80000000 | bytes 240000 | tf_op jit(solution)/shard_map/highway_slopes/pallas_call | solution.py:603
  267.8 3.7 fusion
  272.0 1.7 collective-permute-start.28
  273.6 7.7 %highway_back.5.partial = f32[512,1024]{1,0:T(8,128)} custom-call(s32[3,16]{1,0:T(4,128)} %get-tuple-element.319.table_ref, bf16[512,1024]{1,0:T(8,128)(2,1)} %get-tuple-element.363.refs_5_.d_first, bf16[512,1024]{1,0:T(8,128)(2,1)} %get-tuple-element.364.refs_7_.d_gate, f32[512,1024]{1,0:T(8,128)} %get-tuple-element.392.up, ...), custom_call_target="tpu_custom_call" | custom-call | flops 60000000 | bytes 180000 | tf_op jit(solution)/shard_map/highway_back/pallas_call | solution.py:620
  281.3 7.9 %highway_slopes.3 = (bf16[512,1024]{1,0:T(8,128)(2,1)}, bf16[512,1024]{1,0:T(8,128)(2,1)}, f32[512,1024]{1,0:T(8,128)}, bf16[512,1024]{1,0:T(8,128)(2,1)}, f32[2,1024]{1,0:T(2,128)}) custom-call(s32[3,16]{1,0:T(4,128)} %get-tuple-element.318.table_ref, f32[512,1024]{1,0:T(8,128)} %highway_back.5.partial, bf16[512,1024]{1,0:T(8,128)(2,1)} %copy-done.57, ...), custom_call_target="tpu_custom_call" | custom-call | flops 80000000 | bytes 240000 | tf_op jit(solution)/shard_map/highway_slopes/pallas_call | solution.py:603
  289.7 15.2 %highway_weight_grad.3 = (bf16[4,2,256,512]{3,2,1,0:T(8,128)(2,1)}, bf16[4,2,256,512]{3,2,1,0:T(8,128)(2,1)}, bf16[2,4,2,256,512]{4,3,2,1,0:T(8,128)(2,1)}) custom-call(s32[2,4]{1,0:T(2,128)} %pad_add_fusion.2.table_ref, bf16[1024,512]{1,0:T(8,128)(2,1)} %copy-done, bf16[1024,512]{1,0:T(8,128)(2,1)} %collective-permute-done.8.refs_1_, ...), custom_call_target="tpu_custom_call" | custom-call | flops 150000000 | bytes 450000 | tf_op jit(solution)/shard_map/highway_weight_grad/pallas_call | solution.py:640
  304.9 7.5 %highway_back.6 = f32[512,1024]{1,0:T(8,128)} custom-call(s32[3,16]{1,0:T(4,128)} %get-tuple-element.318.table_ref, bf16[512,1024]{1,0:T(8,128)(2,1)} %get-tuple-element.387.refs_4_.d_first, bf16[512,1024]{1,0:T(8,128)(2,1)} %get-tuple-element.388.refs_6_.d_gate, f32[512,1024]{1,0:T(8,128)} %get-tuple-element.405.up, bf16[2,2,256,512]{3,2,1,0:T(8,128)(2,1)} %copy-done.23, ...), custom_call_target="tpu_custom_call" | custom-call | flops 60000000 | bytes 180000 | tf_op jit(solution)/shard_map/highway_back/pallas_call | solution.py:620
  312.5 7.8 %highway_back.7 = f32[512,1024]{1,0:T(8,128)} custom-call(s32[3,16]{1,0:T(4,128)} %get-tuple-element.318.table_ref, bf16[512,1024]{1,0:T(8,128)(2,1)} %get-tuple-element.397.refs_5_.d_first, bf16[512,1024]{1,0:T(8,128)(2,1)} %get-tuple-element.398.refs_7_.d_gate, f32[512,1024]{1,0:T(8,128)} %get-tuple-element.406.up, bf16[2,2,256,512]{3,2,1,0:T(8,128)(2,1)} %copy-done.23, ...), custom_call_target="tpu_custom_call" | custom-call | flops 60000000 | bytes 180000 | tf_op jit(solution)/shard_map/highway_back/pallas_call | solution.py:620
  321.7 4.5 convert_add_fusion.11
  326.2 2.8 collective-permute-start.34
  331.3 1.7 collective-permute-start.31
  333.0 2.5 fusion.1
  340.1 1.7 copy-done.33
  342.9 14.5 %collective-permute-done.31.refs_3_ = bf16[1024,512]{1,0:T(8,128)(2,1)S(1)} collective-permute-done((bf16[1024,512]{1,0:T(8,128)(2,1)S(1)}, bf16[1024,512]{1,0:T(8,128)(2,1)S(1)}, u32[]{:S(2)}, u32[]{:S(2)}) %collective-permute-start.31) | collective-permute-done | bytes 1048608 | tf_op jit(solution)/shard_map/ppermute | solution.py:784
  357.4 18.6 %conv_backward.4.refs_4_ = f32[640,128]{1,0:T(8,128)S(1)} custom-call(s32[2]{0:T(128)S(1)} %slice.229.narrow_ref, f32[64,256]{1,0:T(8,128)S(1)} %copy-done.18, bf16[1024,256]{1,0:T(8,128)(2,1)S(1)} %copy-done.14, bf16[512,128]{1,0:T(8,128)(2,1)S(1)} %copy.98.conv_ref, bf16[128,512]{1,0:T(8,128)(2,1)S(1)} %pad.21.back_ref, ...), custom_call_target="tpu_custom_call" | custom-call | flops 150000000 | bytes 450000 | tf_op jit(solution)/shard_map/conv_backward/pallas_call | solution.py:277
  376.1 2.8 collective-permute-done.36
  380.3 1.6 collective-permute-start.39
  381.9 1.8 collective-permute-start.40
  385.9 10.6 %conv_backward.5.refs_4_ = f32[640,128]{1,0:T(8,128)S(1)} custom-call(s32[2]{0:T(128)S(1)} %slice.229.narrow_ref, f32[64,256]{1,0:T(8,128)S(1)} %get-tuple-element.460.ids_ref, bf16[1024,256]{1,0:T(8,128)(2,1)S(1)} %copy-done.10, bf16[512,128]{1,0:T(8,128)(2,1)S(1)} %copy.98.conv_ref, bf16[128,512]{1,0:T(8,128)(2,1)S(1)} %pad.21.back_ref, ...), custom_call_target="tpu_custom_call" | custom-call | flops 150000000 | bytes 450000 | tf_op jit(solution)/shard_map/conv_backward/pallas_call | solution.py:277
  396.6 14.0 %conv_backward.6.refs_4_ = f32[640,128]{1,0:T(8,128)S(1)} custom-call(s32[2]{0:T(128)S(1)} %slice.229.narrow_ref, f32[64,512]{1,0:T(8,128)S(1)} %get-tuple-element.457.ids_ref, bf16[1024,512]{1,0:T(8,128)(2,1)S(1)} %copy-done.6, bf16[512,128]{1,0:T(8,128)(2,1)S(1)} %copy.98.conv_ref, bf16[128,512]{1,0:T(8,128)(2,1)S(1)} %pad.21.back_ref, ...), custom_call_target="tpu_custom_call" | custom-call | flops 150000000 | bytes 450000 | tf_op jit(solution)/shard_map/conv_backward/pallas_call | solution.py:277
  410.7 2.9 convert_add_fusion.3
  413.7 8.9 %collective-permute-start.41 = (bf16[2,256,512]{2,1,0:T(8,128)(2,1)S(1)}, bf16[2,256,512]{2,1,0:T(8,128)(2,1)S(1)}, u32[]{:S(2)}, u32[]{:S(2)}) collective-permute-start(bf16[2,256,512]{2,1,0:T(8,128)(2,1)S(1)} %get-tuple-element.479), channel_id=1, source_target_pairs={{0,2},{1,3},{2,4},{3,5},{4,6},{5,7},{6,0},{7,1},{8,10},{9,11},{10,... | collective-permute-start | bytes 1572872 | tf_op jit(solution)/shard_map/ppermute | solution.py:797
  422.6 14.0 %conv_backward.7 = f32[640,128]{1,0:T(8,128)S(1)} custom-call(s32[2]{0:T(128)S(1)} %slice.229.narrow_ref, f32[64,1024]{1,0:T(8,128)S(1)} %copy-done.16, bf16[1024,1024]{1,0:T(8,128)(2,1)S(1)} %copy-done.2, bf16[512,128]{1,0:T(8,128)(2,1)S(1)} %copy.98.conv_ref, bf16[128,512]{1,0:T(8,128)(2,1)S(1)} %pad.21.back_ref, ...), custom_call_target="tpu_custom_call" | custom-call | flops 150000000 | bytes 450000 | tf_op jit(solution)/shard_map/conv_backward/pallas_call | solution.py:277
  438.2 4.2 return_units.1
  442.6 1.8 collective-permute-start.44
  447.5 2.0 collective-permute-start.48
  452.4 7.2 %collective-permute-done.45 = bf16[640,128]{0,1:T(8,128)(2,1)S(1)} collective-permute-done((bf16[640,128]{0,1:T(8,128)(2,1)S(1)}, bf16[640,128]{0,1:T(8,128)(2,1)S(1)}, u32[]{:S(2)}, u32[]{:S(2)}) %collective-permute-start.45) | collective-permute-done | bytes 163872 | tf_op jit(solution)/shard_map/ppermute | solution.py:894
  460.7 11.5 %collective-permute-done.47.refs_2_ = bf16[2,256,512]{2,1,0:T(8,128)(2,1)S(1)} collective-permute-done((bf16[2,256,512]{2,1,0:T(8,128)(2,1)S(1)}, bf16[2,256,512]{2,1,0:T(8,128)(2,1)S(1)}, u32[]{:S(2)}, u32[]{:S(2)}) %collective-permute-start.47) | collective-permute-done | bytes 524320 | tf_op jit(solution)/shard_map/ppermute | solution.py:784
  476.0 8.2 %owner_update.2 = (f32[2,256,2048]{2,1,0:T(8,128)}, f32[2,256,2048]{2,1,0:T(8,128)}, f32[2,256,2048]{2,1,0:T(8,128)}, f32[2,256,2048]{2,1,0:T(8,128)}) custom-call(s32[4]{0:T(128)} %xor_multiply_fusion.at_ref, bf16[2,256,512]{2,1,0:T(8,128)(2,1)} %get-tuple-element.510.refs_0_, bf16[2,256,512]{2,1,0:T(8,128)(2,1)} %copy-done.46, ...), custom_call_target="tpu_custom_call" | custom-call | flops 80000000 | bytes 240000 | tf_op jit(solution)/shard_map/owner_update/pallas_call | solution.py:684
  485.8 8.2 %owner_update.3 = (f32[2,256,2048]{2,1,0:T(8,128)}, f32[2,256,2048]{2,1,0:T(8,128)}, f32[2,256,2048]{2,1,0:T(8,128)}, f32[2,256,2048]{2,1,0:T(8,128)}) custom-call(s32[4]{0:T(128)} %xor_multiply_fusion.at_ref, bf16[2,256,512]{2,1,0:T(8,128)(2,1)} %get-tuple-element.510.refs_0_, ...), custom_call_target="tpu_custom_call", output_to_operand_aliasing={{0}: (9, {}), {1}: (10, {}), {2}: (11, {}), {3}: (12, {})} | custom-call | flops 80000000 | bytes 240000 | tf_op jit(solution)/shard_map/owner_update/pallas_call | solution.py:684
  (376 shorter events, 61.7 us)
Async XLA Ops:
  4.4 29.8 %collective-permute-start.2 = (bf16[2,256,512]{2,1,0:T(8,128)(2,1)}, bf16[2,256,512]{2,1,0:T(8,128)(2,1)}, u32[]{:S(2)}, u32[]{:S(2)}) collective-permute-start(bf16[2,256,512]{2,1,0:T(8,128)(2,1)} %get-tuple-element.555), channel_id=1, source_target_pairs={{0,24},{8,16},{16,8},{24,0},{1,25},{9,17},{17,9},{25,1},{2,26},{10... | collective-permute-start | bytes 1572872 | tf_op jit(solution)/shard_map/ppermute | solution.py:784
  8.3 26.0 %collective-permute-start.1 = (bf16[2,256,512]{2,1,0:T(8,128)(2,1)}, bf16[2,256,512]{2,1,0:T(8,128)(2,1)}, u32[]{:S(2)}, u32[]{:S(2)}) collective-permute-start(bf16[2,256,512]{2,1,0:T(8,128)(2,1)} %get-tuple-element.556), channel_id=1, source_target_pairs={{0,16},{8,24},{16,0},{24,8},{1,17},{9,25},{17,1},{25,9},{2,18},{10... | collective-permute-start | bytes 1572872 | tf_op jit(solution)/shard_map/ppermute | solution.py:784
  8.8 25.5 %collective-permute-start = (bf16[2,256,512]{2,1,0:T(8,128)(2,1)}, bf16[2,256,512]{2,1,0:T(8,128)(2,1)}, u32[]{:S(2)}, u32[]{:S(2)}) collective-permute-start(bf16[2,256,512]{2,1,0:T(8,128)(2,1)} %get-tuple-element.557), channel_id=1, source_target_pairs={{0,8},{8,0},{16,24},{24,16},{1,9},{9,1},{17,25},{25,17},{2,10},{10... | collective-permute-start | bytes 1572872 | tf_op jit(solution)/shard_map/ppermute | solution.py:784
  37.1 37.0 %collective-permute-start.7 = (bf16[512,768]{1,0:T(8,128)(2,1)}, bf16[512,768]{1,0:T(8,128)(2,1)}, u32[]{:S(2)}, u32[]{:S(2)}) collective-permute-start(bf16[512,768]{1,0:T(8,128)(2,1)} %param.25), channel_id=1, source_target_pairs={{0,8},{8,0},{16,24},{24,16},{1,9},{9,1},{17,25},{25,17},{2,10},{10... | collective-permute-start | bytes 2359304 | tf_op jit(solution)/shard_map/ppermute | solution.py:784
  38.3 35.8 %collective-permute-start.6 = (bf16[2,320,512]{2,1,0:T(8,128)(2,1)}, bf16[2,320,512]{2,1,0:T(8,128)(2,1)}, u32[]{:S(2)}, u32[]{:S(2)}) collective-permute-start(bf16[2,320,512]{2,1,0:T(8,128)(2,1)} %get-tuple-element.336), channel_id=1, source_target_pairs={{0,16},{8,24},{16,0},{24,8},{1,17},{9,25},{17,1},{25,9},{2,18},{10... | collective-permute-start | bytes 1966088 | tf_op jit(solution)/shard_map/ppermute | solution.py:784
  39.1 34.9 %collective-permute-start.5 = (bf16[2,256,512]{2,1,0:T(8,128)(2,1)}, bf16[2,256,512]{2,1,0:T(8,128)(2,1)}, u32[]{:S(2)}, u32[]{:S(2)}) collective-permute-start(bf16[2,256,512]{2,1,0:T(8,128)(2,1)} %get-tuple-element.312), channel_id=1, source_target_pairs={{0,16},{8,24},{16,0},{24,8},{1,17},{9,25},{17,1},{25,9},{2,18},{10... | collective-permute-start | bytes 1572872 | tf_op jit(solution)/shard_map/ppermute | solution.py:784
  40.3 33.7 %collective-permute-start.4 = (bf16[2,256,512]{2,1,0:T(8,128)(2,1)}, bf16[2,256,512]{2,1,0:T(8,128)(2,1)}, u32[]{:S(2)}, u32[]{:S(2)}) collective-permute-start(bf16[2,256,512]{2,1,0:T(8,128)(2,1)} %get-tuple-element.312), channel_id=1, source_target_pairs={{0,6},{1,7},{2,0},{3,1},{4,2},{5,3},{6,4},{7,5},{8,14},{9,15},{10,... | collective-permute-start | bytes 1572872 | tf_op jit(solution)/shard_map/ppermute | solution.py:797
  43.9 30.1 %collective-permute-start.3 = (bf16[2,256,512]{2,1,0:T(8,128)(2,1)}, bf16[2,256,512]{2,1,0:T(8,128)(2,1)}, u32[]{:S(2)}, u32[]{:S(2)}) collective-permute-start(bf16[2,256,512]{2,1,0:T(8,128)(2,1)} %get-tuple-element.312), channel_id=1, source_target_pairs={{0,2},{1,3},{2,4},{3,5},{4,6},{5,7},{6,0},{7,1},{8,10},{9,11},{10,... | collective-permute-start | bytes 1572872 | tf_op jit(solution)/shard_map/ppermute | solution.py:797
  74.0 27.7 %copy-start = (bf16[1024,512]{1,0:T(8,128)(2,1)}, bf16[1024,512]{1,0:T(8,128)(2,1)S(1)}, u32[]{:S(2)}) copy-start(bf16[1024,512]{1,0:T(8,128)(2,1)S(1)} %place_words.2.refs_0_) | copy-start | bytes 3145732
  74.0 23.3 %collective-permute-start.8 = (bf16[1024,512]{1,0:T(8,128)(2,1)S(1)}, bf16[1024,512]{1,0:T(8,128)(2,1)}, u32[]{:S(2)}, u32[]{:S(2)}) collective-permute-start(bf16[1024,512]{1,0:T(8,128)(2,1)S(1)} %place_words.3), channel_id=1, source_target_pairs={{0,16},{8,24},{16,0},{24,8},{1,17},{9,25},{17,1},{25,9},{2,18},{10... | collective-permute-start | bytes 3145736 | tf_op jit(solution)/shard_map/ppermute | solution.py:784
  74.1 23.2 %collective-permute-start.9 = (bf16[1024,512]{1,0:T(8,128)(2,1)S(1)}, bf16[1024,512]{1,0:T(8,128)(2,1)S(1)}, u32[]{:S(2)}, u32[]{:S(2)}) collective-permute-start(bf16[1024,512]{1,0:T(8,128)(2,1)S(1)} %place_words.2.refs_0_), channel_id=1, source_target_pairs={{0,8},{8,0},{16,24},{24,16},{1,9},{9,1},{17,25},{25,17},{2,10},{10... | collective-permute-start | bytes 3145736 | tf_op jit(solution)/shard_map/ppermute | solution.py:784
  74.2 23.1 %collective-permute-start.10 = (bf16[2,256,512]{2,1,0:T(8,128)(2,1)S(1)}, bf16[2,256,512]{2,1,0:T(8,128)(2,1)S(1)}, u32[]{:S(2)}, u32[]{:S(2)}) collective-permute-start(bf16[2,256,512]{2,1,0:T(8,128)(2,1)S(1)} %copy-done.65), channel_id=1, source_target_pairs={{0,4},{1,5},{2,6},{3,7},{4,0},{5,1},{6,2},{7,3},{8,12},{9,13},{10,... | collective-permute-start | bytes 1572872 | tf_op jit(solution)/shard_map/ppermute | solution.py:797
  75.3 29.9 %copy-start.92 = (s32[1,16]{1,0:T(1,128)S(1)}, s32[1,16]{1,0:T(1,128)}, u32[]{:S(2)}) copy-start(s32[1,16]{1,0:T(1,128)} %constant.739.clone.1) | copy-start | bytes 196
  75.3 29.9 %copy-start.93 = (s32[1,16]{1,0:T(1,128)S(1)}, s32[1,16]{1,0:T(1,128)}, u32[]{:S(2)}) copy-start(s32[1,16]{1,0:T(1,128)} %constant.738.clone.1) | copy-start | bytes 196
  98.3 35.8 %collective-permute-start.12 = (bf16[3,2,256,512]{3,2,1,0:T(8,128)(2,1)S(1)}, bf16[3,2,256,512]{3,2,1,0:T(8,128)(2,1)}, u32[]{:S(2)}, u32[]{:S(2)}) collective-permute-start(bf16[3,2,256,512]{3,2,1,0:T(8,128)(2,1)S(1)} %bitcast_dynamic-update-slice_fusion.refs_5_.refs_1_), channel_id=1, source_target_pairs={{0,1},{1,0},{2,3},{3,2},{4,5},{5,4},{6,7},{7,6},{8,9},{9,8},{10,11... | collective-permute-start | bytes 4718600 | tf_op jit(solution)/shard_map/ppermute | solution.py:793
  98.3 36.9 %collective-permute-start.11 = (bf16[3,2,256,512]{3,2,1,0:T(8,128)(2,1)S(1)}, bf16[3,2,256,512]{3,2,1,0:T(8,128)(2,1)}, u32[]{:S(2)}, u32[]{:S(2)}) collective-permute-start(bf16[3,2,256,512]{3,2,1,0:T(8,128)(2,1)S(1)} %bitcast_dynamic-update-slice_fusion.refs_5_.refs_1_), channel_id=1, source_target_pairs={{0,16},{8,24},{16,0},{24,8},{1,17},{9,25},{17,1},{25,9},{2,18},{10... | collective-permute-start | bytes 4718600 | tf_op jit(solution)/shard_map/ppermute | solution.py:784
  99.9 34.2 %collective-permute-start.13 = (bf16[1024,512]{1,0:T(8,128)(2,1)}, bf16[1024,512]{1,0:T(8,128)(2,1)}, u32[]{:S(2)}, u32[]{:S(2)}) collective-permute-start(bf16[1024,512]{1,0:T(8,128)(2,1)} %collective-permute-done.8.refs_1_), channel_id=1, source_target_pairs={{0,8},{8,0},{16,24},{24,16},{1,9},{9,1},{17,25},{25,17},{2,10},{10... | collective-permute-start | bytes 3145736 | tf_op jit(solution)/shard_map/ppermute | solution.py:784
  102.1 18.4 %collective-permute-start.15 = (bf16[2,320,512]{2,1,0:T(8,128)(2,1)}, bf16[2,320,512]{2,1,0:T(8,128)(2,1)S(1)}, u32[]{:S(2)}, u32[]{:S(2)}) collective-permute-start(bf16[2,320,512]{2,1,0:T(8,128)(2,1)} %get-tuple-element.336), channel_id=1, source_target_pairs={{0,6},{1,7},{2,0},{3,1},{4,2},{5,3},{6,4},{7,5},{8,14},{9,15},{10,... | collective-permute-start | bytes 1966088 | tf_op jit(solution)/shard_map/ppermute | solution.py:797
  105.0 29.1 %collective-permute-start.14 = (bf16[2,320,512]{2,1,0:T(8,128)(2,1)}, bf16[2,320,512]{2,1,0:T(8,128)(2,1)S(1)}, u32[]{:S(2)}, u32[]{:S(2)}) collective-permute-start(bf16[2,320,512]{2,1,0:T(8,128)(2,1)} %get-tuple-element.336), channel_id=1, source_target_pairs={{0,2},{1,3},{2,4},{3,5},{4,6},{5,7},{6,0},{7,1},{8,10},{9,11},{10,... | collective-permute-start | bytes 1966088 | tf_op jit(solution)/shard_map/ppermute | solution.py:797
  108.4 28.5 %copy-start.23 = (bf16[2,2,256,512]{3,2,1,0:T(8,128)(2,1)}, bf16[2,2,256,512]{3,2,1,0:T(8,128)(2,1)S(1)}, u32[]{:S(2)}) copy-start(bf16[2,2,256,512]{3,2,1,0:T(8,128)(2,1)S(1)} %pad_maximum_fusion.3.refs_4_.refs_0_) | copy-start | bytes 3145732
  120.5 33.5 %copy-start.41 = (bf16[2,320,512]{2,1,0:T(8,128)(2,1)}, bf16[2,320,512]{2,1,0:T(8,128)(2,1)S(1)}, u32[]{:S(2)}) copy-start(bf16[2,320,512]{2,1,0:T(8,128)(2,1)S(1)} %collective-permute-done.15) | copy-start | bytes 1966084
  135.2 5.1 %collective-permute-start.17 = (bf16[3,2,256,512]{3,2,1,0:T(8,128)(2,1)}, bf16[3,2,256,512]{3,2,1,0:T(8,128)(2,1)S(1)}, u32[]{:S(2)}, u32[]{:S(2)}) collective-permute-start(bf16[3,2,256,512]{3,2,1,0:T(8,128)(2,1)} %collective-permute-done.11.refs_6_.refs_2_), channel_id=1, source_target_pairs={{0,1},{1,0},{2,3},{3,2},{4,5},{5,4},{6,7},{7,6},{8,9},{9,8},{10,11... | collective-permute-start | bytes 4718600 | tf_op jit(solution)/shard_map/ppermute | solution.py:793
  135.2 4.5 collective-permute-start.16
  136.9 33.2 %collective-permute-start.19 = (bf16[2,2,320,512]{3,2,1,0:T(8,128)(2,1)}, bf16[2,2,320,512]{3,2,1,0:T(8,128)(2,1)}, u32[]{:S(2)}, u32[]{:S(2)}) collective-permute-start(bf16[2,2,320,512]{3,2,1,0:T(8,128)(2,1)} %pad_maximum_fusion.2), channel_id=1, source_target_pairs={{0,16},{8,24},{16,0},{24,8},{1,17},{9,25},{17,1},{25,9},{2,18},{10... | collective-permute-start | bytes 3932168 | tf_op jit(solution)/shard_map/ppermute | solution.py:784
  138.5 31.6 %collective-permute-start.18 = (bf16[2,320,512]{2,1,0:T(8,128)(2,1)}, bf16[2,320,512]{2,1,0:T(8,128)(2,1)}, u32[]{:S(2)}, u32[]{:S(2)}) collective-permute-start(bf16[2,320,512]{2,1,0:T(8,128)(2,1)} %get-tuple-element.336), channel_id=1, source_target_pairs={{0,4},{1,5},{2,6},{3,7},{4,0},{5,1},{6,2},{7,3},{8,12},{9,13},{10,... | collective-permute-start | bytes 1966088 | tf_op jit(solution)/shard_map/ppermute | solution.py:797
  154.0 32.7 %collective-permute-start.21 = (bf16[512,1024]{1,0:T(8,128)(2,1)}, bf16[512,1024]{1,0:T(8,128)(2,1)S(1)}, u32[]{:S(2)}, u32[]{:S(2)}) collective-permute-start(bf16[512,1024]{1,0:T(8,128)(2,1)} %get-tuple-element.335.own.refs_0_), channel_id=1, source_target_pairs={{0,8},{8,0},{16,24},{24,16},{1,9},{9,1},{17,25},{25,17},{2,10},{10... | collective-permute-start | bytes 3145736 | tf_op jit(solution)/shard_map/ppermute | solution.py:784
  170.1 16.5 %collective-permute-start.20 = (bf16[2,320,512]{2,1,0:T(8,128)(2,1)}, bf16[2,320,512]{2,1,0:T(8,128)(2,1)S(1)}, u32[]{:S(2)}, u32[]{:S(2)}) collective-permute-start(bf16[2,320,512]{2,1,0:T(8,128)(2,1)} %collective-permute-done.18), channel_id=1, source_target_pairs={{0,16},{8,24},{16,0},{24,8},{1,17},{9,25},{17,1},{25,9},{2,18},{10... | collective-permute-start | bytes 1966088 | tf_op jit(solution)/shard_map/ppermute | solution.py:784
  172.2 18.7 %collective-permute-start.22 = (bf16[4,2,320,512]{3,2,1,0:T(8,128)(2,1)S(1)}, bf16[4,2,320,512]{3,2,1,0:T(8,128)(2,1)S(1)}, u32[]{:S(2)}, u32[]{:S(2)}) collective-permute-start(bf16[4,2,320,512]{3,2,1,0:T(8,128)(2,1)S(1)} %pad_maximum_fusion.refs_0_), channel_id=1, source_target_pairs={{0,1},{1,0},{2,3},{3,2},{4,5},{5,4},{6,7},{7,6},{8,9},{9,8},{10,11... | collective-permute-start | bytes 7864328 | tf_op jit(solution)/shard_map/ppermute | solution.py:793
  188.9 5.1 %collective-permute-start.23 = (bf16[4,2,320,512]{3,2,1,0:T(8,128)(2,1)S(1)}, bf16[4,2,320,512]{3,2,1,0:T(8,128)(2,1)}, u32[]{:S(2)}, u32[]{:S(2)}) collective-permute-start(bf16[4,2,320,512]{3,2,1,0:T(8,128)(2,1)S(1)} %pad_maximum_fusion.1.refs_1_), channel_id=1, source_target_pairs={{0,1},{1,0},{2,3},{3,2},{4,5},{5,4},{6,7},{7,6},{8,9},{9,8},{10,11... | collective-permute-start | bytes 7864328 | tf_op jit(solution)/shard_map/ppermute | solution.py:793
  189.0 26.0 %collective-permute-start.24 = (bf16[512,1024]{1,0:T(8,128)(2,1)S(1)}, bf16[512,1024]{1,0:T(8,128)(2,1)S(1)}, u32[]{:S(2)}, u32[]{:S(2)}) collective-permute-start(bf16[512,1024]{1,0:T(8,128)(2,1)S(1)} %copy-done.37), channel_id=1, source_target_pairs={{0,8},{8,0},{16,24},{24,16},{1,9},{9,1},{17,25},{25,17},{2,10},{10... | collective-permute-start | bytes 3145736 | tf_op jit(solution)/shard_map/ppermute | solution.py:784
  210.7 40.0 %collective-permute-start.25 = (bf16[512,1024]{1,0:T(8,128)(2,1)}, bf16[512,1024]{1,0:T(8,128)(2,1)}, u32[]{:S(2)}, u32[]{:S(2)}) collective-permute-start(bf16[512,1024]{1,0:T(8,128)(2,1)} %get-tuple-element.357), channel_id=1, source_target_pairs={{0,8},{8,0},{16,24},{24,16},{1,9},{9,1},{17,25},{25,17},{2,10},{10... | collective-permute-start | bytes 3145736 | tf_op jit(solution)/shard_map/ppermute | solution.py:784
  233.1 26.5 %collective-permute-start.26 = (bf16[512,1024]{1,0:T(8,128)(2,1)}, bf16[512,1024]{1,0:T(8,128)(2,1)S(1)}, u32[]{:S(2)}, u32[]{:S(2)}) collective-permute-start(bf16[512,1024]{1,0:T(8,128)(2,1)} %get-tuple-element.369), channel_id=1, source_target_pairs={{0,8},{8,0},{16,24},{24,16},{1,9},{9,1},{17,25},{25,17},{2,10},{10... | collective-permute-start | bytes 3145736 | tf_op jit(solution)/shard_map/ppermute | solution.py:784
  259.6 8.2 %collective-permute-start.27 = (bf16[2,4,2,256,512]{4,3,2,1,0:T(8,128)(2,1)}, bf16[2,4,2,256,512]{4,3,2,1,0:T(8,128)(2,1)}, u32[]{:S(2)}, u32[]{:S(2)}) collective-permute-start(bf16[2,4,2,256,512]{4,3,2,1,0:T(8,128)(2,1)} %get-tuple-element.375), channel_id=1, source_target_pairs={{0,1},{1,0},{2,3},{3,2},{4,5},{5,4},{6,7},{7,6},{8,9},{9,8},{10,11... | collective-permute-start | bytes 12582920 | tf_op jit(solution)/shard_map/ppermute | solution.py:793
  271.5 49.8 %collective-permute-start.30 = (bf16[4,2,256,512]{3,2,1,0:T(8,128)(2,1)}, bf16[4,2,256,512]{3,2,1,0:T(8,128)(2,1)}, u32[]{:S(2)}, u32[]{:S(2)}) collective-permute-start(bf16[4,2,256,512]{3,2,1,0:T(8,128)(2,1)} %fusion), channel_id=1, source_target_pairs={{0,16},{8,24},{16,0},{24,8},{1,17},{9,25},{17,1},{25,9},{2,18},{10... | collective-permute-start | bytes 6291464 | tf_op jit(solution)/shard_map/ppermute | solution.py:784
  272.0 32.9 %collective-permute-start.28 = (bf16[512,1024]{1,0:T(8,128)(2,1)S(1)}, bf16[512,1024]{1,0:T(8,128)(2,1)S(1)}, u32[]{:S(2)}, u32[]{:S(2)}) collective-permute-start(bf16[512,1024]{1,0:T(8,128)(2,1)S(1)} %copy-done.94), channel_id=1, source_target_pairs={{0,8},{8,0},{16,24},{24,16},{1,9},{9,1},{17,25},{25,17},{2,10},{10... | collective-permute-start | bytes 3145736 | tf_op jit(solution)/shard_map/ppermute | solution.py:784
  289.2 31.1 %collective-permute-start.29 = (bf16[512,1024]{1,0:T(8,128)(2,1)}, bf16[512,1024]{1,0:T(8,128)(2,1)S(1)}, u32[]{:S(2)}, u32[]{:S(2)}) collective-permute-start(bf16[512,1024]{1,0:T(8,128)(2,1)} %get-tuple-element.410), channel_id=1, source_target_pairs={{0,8},{8,0},{16,24},{24,16},{1,9},{9,1},{17,25},{25,17},{2,10},{10... | collective-permute-start | bytes 3145736 | tf_op jit(solution)/shard_map/ppermute | solution.py:784
  321.3 11.7 %collective-permute-start.32 = (bf16[2,4,2,256,512]{4,3,2,1,0:T(8,128)(2,1)}, bf16[2,4,2,256,512]{4,3,2,1,0:T(8,128)(2,1)S(1)}, u32[]{:S(2)}, u32[]{:S(2)}) collective-permute-start(bf16[2,4,2,256,512]{4,3,2,1,0:T(8,128)(2,1)} %get-tuple-element.431), channel_id=1, source_target_pairs={{0,1},{1,0},{2,3},{3,2},{4,5},{5,4},{6,7},{7,6},{8,9},{9,8},{10,11... | collective-permute-start | bytes 12582920 | tf_op jit(solution)/shard_map/ppermute | solution.py:793
  326.2 49.9 %collective-permute-start.33 = (bf16[2,256,512]{2,1,0:T(8,128)(2,1)}, bf16[2,256,512]{2,1,0:T(8,128)(2,1)}, u32[]{:S(2)}, u32[]{:S(2)}) collective-permute-start(bf16[2,256,512]{2,1,0:T(8,128)(2,1)} %get-tuple-element.445), channel_id=1, source_target_pairs={{0,4},{1,5},{2,6},{3,7},{4,0},{5,1},{6,2},{7,3},{8,12},{9,13},{10,... | collective-permute-start | bytes 1572872 | tf_op jit(solution)/shard_map/ppermute | solution.py:797
  326.2 49.8 %collective-permute-start.34 = (bf16[2,256,512]{2,1,0:T(8,128)(2,1)}, bf16[2,256,512]{2,1,0:T(8,128)(2,1)}, u32[]{:S(2)}, u32[]{:S(2)}) collective-permute-start(bf16[2,256,512]{2,1,0:T(8,128)(2,1)} %get-tuple-element.446), channel_id=1, source_target_pairs={{0,2},{1,3},{2,4},{3,5},{4,6},{5,7},{6,0},{7,1},{8,10},{9,11},{10,... | collective-permute-start | bytes 1572872 | tf_op jit(solution)/shard_map/ppermute | solution.py:797
  329.1 47.0 %collective-permute-start.35 = (bf16[2,256,512]{2,1,0:T(8,128)(2,1)}, bf16[2,256,512]{2,1,0:T(8,128)(2,1)}, u32[]{:S(2)}, u32[]{:S(2)}) collective-permute-start(bf16[2,256,512]{2,1,0:T(8,128)(2,1)} %get-tuple-element.447), channel_id=1, source_target_pairs={{0,6},{1,7},{2,0},{3,1},{4,2},{5,3},{6,4},{7,5},{8,14},{9,15},{10,... | collective-permute-start | bytes 1572872 | tf_op jit(solution)/shard_map/ppermute | solution.py:797
  331.3 26.1 %collective-permute-start.31 = (bf16[1024,512]{1,0:T(8,128)(2,1)S(1)}, bf16[1024,512]{1,0:T(8,128)(2,1)S(1)}, u32[]{:S(2)}, u32[]{:S(2)}) collective-permute-start(bf16[1024,512]{1,0:T(8,128)(2,1)S(1)} %pad_maximum_fusion.5), channel_id=1, source_target_pairs={{0,16},{8,24},{16,0},{24,8},{1,17},{9,25},{17,1},{25,9},{2,18},{10... | collective-permute-start | bytes 3145736 | tf_op jit(solution)/shard_map/ppermute | solution.py:784
  335.6 43.2 %collective-permute-start.36 = (bf16[2,2,256,512]{3,2,1,0:T(8,128)(2,1)}, bf16[2,2,256,512]{3,2,1,0:T(8,128)(2,1)S(1)}, u32[]{:S(2)}, u32[]{:S(2)}) collective-permute-start(bf16[2,2,256,512]{3,2,1,0:T(8,128)(2,1)} %get-tuple-element.553), channel_id=1, source_target_pairs={{0,16},{8,24},{16,0},{24,8},{1,17},{9,25},{17,1},{25,9},{2,18},{10... | collective-permute-start | bytes 3145736 | tf_op jit(solution)/shard_map/ppermute | solution.py:784
  341.8 37.1 %copy-start.52 = (bf16[4,2,256,512]{3,2,1,0:T(8,128)(2,1)S(1)}, bf16[4,2,256,512]{3,2,1,0:T(8,128)(2,1)}, u32[]{:S(2)}) copy-start(bf16[4,2,256,512]{3,2,1,0:T(8,128)(2,1)} %get-tuple-element.451) | copy-start | bytes 6291460
  380.3 30.3 %collective-permute-start.39 = (bf16[2,2,256,512]{3,2,1,0:T(8,128)(2,1)S(1)}, bf16[2,2,256,512]{3,2,1,0:T(8,128)(2,1)S(1)}, u32[]{:S(2)}, u32[]{:S(2)}) collective-permute-start(bf16[2,2,256,512]{3,2,1,0:T(8,128)(2,1)S(1)} %copy-done.55), channel_id=1, source_target_pairs={{0,16},{8,24},{16,0},{24,8},{1,17},{9,25},{17,1},{25,9},{2,18},{10... | collective-permute-start | bytes 3145736 | tf_op jit(solution)/shard_map/ppermute | solution.py:784
  381.9 28.7 %collective-permute-start.40 = (bf16[512,768]{1,0:T(8,128)(2,1)}, bf16[512,768]{1,0:T(8,128)(2,1)S(1)}, u32[]{:S(2)}, u32[]{:S(2)}) collective-permute-start(bf16[512,768]{1,0:T(8,128)(2,1)} %select_convert_fusion), channel_id=1, source_target_pairs={{0,8},{8,0},{16,24},{24,16},{1,9},{9,1},{17,25},{25,17},{2,10},{10... | collective-permute-start | bytes 2359304 | tf_op jit(solution)/shard_map/ppermute | solution.py:784
  383.7 26.9 %collective-permute-start.37 = (bf16[2,256,512]{2,1,0:T(8,128)(2,1)}, bf16[2,256,512]{2,1,0:T(8,128)(2,1)}, u32[]{:S(2)}, u32[]{:S(2)}) collective-permute-start(bf16[2,256,512]{2,1,0:T(8,128)(2,1)} %get-tuple-element.464), channel_id=1, source_target_pairs={{0,4},{1,5},{2,6},{3,7},{4,0},{5,1},{6,2},{7,3},{8,12},{9,13},{10,... | collective-permute-start | bytes 1572872 | tf_op jit(solution)/shard_map/ppermute | solution.py:797
  384.5 26.1 %collective-permute-start.38 = (bf16[2,256,512]{2,1,0:T(8,128)(2,1)}, bf16[2,256,512]{2,1,0:T(8,128)(2,1)}, u32[]{:S(2)}, u32[]{:S(2)}) collective-permute-start(bf16[2,256,512]{2,1,0:T(8,128)(2,1)} %get-tuple-element.465), channel_id=1, source_target_pairs={{0,6},{1,7},{2,0},{3,1},{4,2},{5,3},{6,4},{7,5},{8,14},{9,15},{10,... | collective-permute-start | bytes 1572872 | tf_op jit(solution)/shard_map/ppermute | solution.py:797
  410.6 26.8 %collective-permute-start.42 = (bf16[512,768]{1,0:T(8,128)(2,1)}, bf16[512,768]{1,0:T(8,128)(2,1)}, u32[]{:S(2)}, u32[]{:S(2)}) collective-permute-start(bf16[512,768]{1,0:T(8,128)(2,1)} %slice.344), channel_id=1, source_target_pairs={{0,16},{8,24},{16,0},{24,8},{1,17},{9,25},{17,1},{25,9},{2,18},{10... | collective-permute-start | bytes 2359304 | tf_op jit(solution)/shard_map/ppermute | solution.py:784
  413.7 22.9 %collective-permute-start.41 = (bf16[2,256,512]{2,1,0:T(8,128)(2,1)S(1)}, bf16[2,256,512]{2,1,0:T(8,128)(2,1)S(1)}, u32[]{:S(2)}, u32[]{:S(2)}) collective-permute-start(bf16[2,256,512]{2,1,0:T(8,128)(2,1)S(1)} %get-tuple-element.479), channel_id=1, source_target_pairs={{0,2},{1,3},{2,4},{3,5},{4,6},{5,7},{6,0},{7,1},{8,10},{9,11},{10,... | collective-permute-start | bytes 1572872 | tf_op jit(solution)/shard_map/ppermute | solution.py:797
  437.6 4.9 collective-permute-start.43
  442.6 6.9 %collective-permute-start.44 = (bf16[640,128]{0,1:T(8,128)(2,1)S(1)}, bf16[640,128]{0,1:T(8,128)(2,1)S(1)}, u32[]{:S(2)}, u32[]{:S(2)}) collective-permute-start(bf16[640,128]{0,1:T(8,128)(2,1)S(1)} %convert_element_type.491), channel_id=1, source_target_pairs={{0,2},{1,3},{2,0},{3,1},{4,6},{5,7},{6,4},{7,5},{8,10},{9,11},{10,... | collective-permute-start | bytes 491528 | tf_op jit(solution)/shard_map/ppermute | solution.py:894
  445.7 13.9 %collective-permute-start.49 = (bf16[4,64,768]{2,1,0:T(8,128)(2,1)S(1)}, bf16[4,64,768]{2,1,0:T(8,128)(2,1)S(1)}, u32[]{:S(2)}, u32[]{:S(2)}) collective-permute-start(bf16[4,64,768]{2,1,0:T(8,128)(2,1)S(1)} %fusion.11), channel_id=1, source_target_pairs={{0,1},{1,0},{2,3},{3,2},{4,5},{5,4},{6,7},{7,6},{8,9},{9,8},{10,11... | collective-permute-start | bytes 1179656 | tf_op jit(solution)/shard_map/ppermute | solution.py:793
  446.0 14.8 %collective-permute-start.46 = (bf16[2,256,512]{2,1,0:T(8,128)(2,1)S(1)}, bf16[2,256,512]{2,1,0:T(8,128)(2,1)S(1)}, u32[]{:S(2)}, u32[]{:S(2)}) collective-permute-start(bf16[2,256,512]{2,1,0:T(8,128)(2,1)S(1)} %copy-done.97), channel_id=1, source_target_pairs={{0,8},{8,0},{16,24},{24,16},{1,9},{9,1},{17,25},{25,17},{2,10},{10... | collective-permute-start | bytes 1572872 | tf_op jit(solution)/shard_map/ppermute | solution.py:784
  447.1 25.1 %collective-permute-start.47 = (bf16[2,256,512]{2,1,0:T(8,128)(2,1)S(1)}, bf16[2,256,512]{2,1,0:T(8,128)(2,1)S(1)}, u32[]{:S(2)}, u32[]{:S(2)}) collective-permute-start(bf16[2,256,512]{2,1,0:T(8,128)(2,1)S(1)} %copy-done.96), channel_id=1, source_target_pairs={{0,16},{8,24},{16,0},{24,8},{1,17},{9,25},{17,1},{25,9},{2,18},{10... | collective-permute-start | bytes 1572872 | tf_op jit(solution)/shard_map/ppermute | solution.py:784
  447.5 24.7 %collective-permute-start.48 = (bf16[2,256,512]{2,1,0:T(8,128)(2,1)S(1)}, bf16[2,256,512]{2,1,0:T(8,128)(2,1)S(1)}, u32[]{:S(2)}, u32[]{:S(2)}) collective-permute-start(bf16[2,256,512]{2,1,0:T(8,128)(2,1)S(1)} %copy-done.95), channel_id=1, source_target_pairs={{0,24},{8,16},{16,8},{24,0},{1,25},{9,17},{17,9},{25,1},{2,26},{10... | collective-permute-start | bytes 1572872 | tf_op jit(solution)/shard_map/ppermute | solution.py:784
  449.5 10.1 %collective-permute-start.45 = (bf16[640,128]{0,1:T(8,128)(2,1)S(1)}, bf16[640,128]{0,1:T(8,128)(2,1)S(1)}, u32[]{:S(2)}, u32[]{:S(2)}) collective-permute-start(bf16[640,128]{0,1:T(8,128)(2,1)S(1)} %fusion.22), channel_id=1, source_target_pairs={{0,4},{1,5},{2,6},{3,7},{4,0},{5,1},{6,2},{7,3},{8,12},{9,13},{10,... | collective-permute-start | bytes 491528 | tf_op jit(solution)/shard_map/ppermute | solution.py:894
  452.4 21.9 %copy-start.61 = (f32[112,512]{1,0:T(8,128)S(1)}, f32[112,512]{1,0:T(8,128)}, u32[]{:S(2)}) copy-start(f32[112,512]{1,0:T(8,128)} %param.28) | copy-start | bytes 688132
  452.4 21.9 %copy-start.68 = (f32[112,512]{1,0:T(8,128)S(1)}, f32[112,512]{1,0:T(8,128)}, u32[]{:S(2)}) copy-start(f32[112,512]{1,0:T(8,128)} %param.35) | copy-start | bytes 688132
  452.4 21.9 %copy-start.69 = (f32[112,512]{1,0:T(8,128)S(1)}, f32[112,512]{1,0:T(8,128)}, u32[]{:S(2)}) copy-start(f32[112,512]{1,0:T(8,128)} %param.36) | copy-start | bytes 688132
  452.4 21.9 %copy-start.89 = (s32[112]{0:T(128)S(1)}, s32[112]{0:T(128)}, u32[]{:S(2)}) copy-start(s32[112]{0:T(128)} %copy-done.88) | copy-start | bytes 1348
  472.2 12.0 %collective-permute-start.50 = (f32[128,128]{0,1:T(8,128)S(1)}, f32[128,128]{0,1:T(8,128)S(1)}, u32[]{:S(2)}, u32[]{:S(2)}) collective-permute-start(f32[128,128]{0,1:T(8,128)S(1)} %slice.278), channel_id=1, source_target_pairs={{0,8},{8,0},{16,24},{24,16},{1,9},{9,1},{17,25},{25,17},{2,10},{10... | collective-permute-start | bytes 196616 | tf_op jit(solution)/shard_map/ppermute | solution.py:784
  473.4 10.9 %collective-permute-start.51 = (bf16[2,64,768]{2,1,0:T(8,128)(2,1)S(1)}, bf16[2,64,768]{2,1,0:T(8,128)(2,1)S(1)}, u32[]{:S(2)}, u32[]{:S(2)}) collective-permute-start(bf16[2,64,768]{2,1,0:T(8,128)(2,1)S(1)} %fusion.24), channel_id=1, source_target_pairs={{0,4},{1,5},{2,6},{3,7},{4,0},{5,1},{6,2},{7,3},{8,12},{9,13},{10,... | collective-permute-start | bytes 589832 | tf_op jit(solution)/shard_map/ppermute | solution.py:894
  484.2 9.7 %collective-permute-start.52 = (f32[128,128]{0,1:T(8,128)S(1)}, f32[128,128]{0,1:T(8,128)S(1)}, u32[]{:S(2)}, u32[]{:S(2)}) collective-permute-start(f32[128,128]{0,1:T(8,128)S(1)} %slice_add_fusion.1), channel_id=1, source_target_pairs={{0,16},{8,24},{16,0},{24,8},{1,17},{9,25},{17,1},{25,9},{2,18},{10... | collective-permute-start | bytes 196616 | tf_op jit(solution)/shard_map/ppermute | solution.py:784
  484.9 9.1 %collective-permute-start.53 = (bf16[1,64,768]{2,1,0:T(8,128)(2,1)S(1)}, bf16[1,64,768]{2,1,0:T(8,128)(2,1)S(1)}, u32[]{:S(2)}, u32[]{:S(2)}) collective-permute-start(bf16[1,64,768]{2,1,0:T(8,128)(2,1)S(1)} %dynamic-slice_convert_fusion.6), channel_id=1, source_target_pairs={{0,2},{1,3},{2,0},{3,1},{4,6},{5,7},{6,4},{7,5},{8,10},{9,11},{10,... | collective-permute-start | bytes 294920 | tf_op jit(solution)/shard_map/ppermute | solution.py:894
  (89 other events, 717.0 us)

commit v4 on v3

--- a/solution.py
+++ b/solution.py
@@ -171,9 +171,9 @@
         out_specs=[column(channels), column(channels), column(ID_ROWS), column(SLOTS_E * CHAR_DIM)],
         out_shape=[
             jax.ShapeDtypeStruct((channels, span), BF16),
-            jax.ShapeDtypeStruct((channels, span), F32),
-            jax.ShapeDtypeStruct((ID_ROWS, span), F32),
-            jax.ShapeDtypeStruct((SLOTS_E * CHAR_DIM, span), BF16),
+            pltpu.HBM((channels, span), F32),
+            pltpu.HBM((ID_ROWS, span), F32),
+            pltpu.HBM((SLOTS_E * CHAR_DIM, span), BF16),
         ],
         scratch_shapes=[
             pltpu.VMEM((cblock, tile), F32),
@@ -302,7 +302,7 @@
         compiler_params=pltpu.CompilerParams(vmem_limit_bytes=48 * MIB),
         cost_estimate=lasting(15),
         name="conv_backward",
-    )(narrow, ids, embedded, conv_t, conv_back, widths, lse, *ranks, *grads, so_far)
+    )(narrow, ids, pltpu.with_memory_space_constraint(embedded, pltpu.HBM), conv_t, conv_back, widths, lse, *ranks, *grads, so_far)
 
 
 def word_order(lengths):
@@ -532,7 +532,7 @@
 
 
 SMEM_SPEC = pl.BlockSpec(memory_space=pltpu.SMEM)
-ANY_SPEC = pl.BlockSpec(memory_space=pl.ANY)
+HBM_SPEC = pl.BlockSpec(memory_space=pltpu.HBM)
 
 
 def whole(array):
@@ -561,7 +561,7 @@
     return pl.pallas_call(
         functools.partial(forward_kernel, len(own), len(pieces), block_rows, width),
         grid=(steps,),
-        in_specs=[SMEM_SPEC, whole(bias)] + [tile] * (2 * len(own)) + [ANY_SPEC] * len(pieces),
+        in_specs=[SMEM_SPEC, whole(bias)] + [tile] * (2 * len(own)) + [HBM_SPEC] * len(pieces),
         out_specs=[out] * 5,
         out_shape=[jax.ShapeDtypeStruct((words, half), kind) for kind in (F32, BF16, BF16, BF16, BF16)],
         scratch_shapes=[pltpu.VMEM((2, 2 * half, half), BF16), pltpu.SemaphoreType.DMA((count_of(pieces),))],
@@ -585,7 +585,7 @@
         grid=(words // rows,),
         in_specs=[SMEM_SPEC, whole(bias), tile, tile, tile, by_rows(rows, out_width)]
         + ([] if packed else [whole(proj)])
-        + [ANY_SPEC] * len(pieces),
+        + [HBM_SPEC] * len(pieces),
         out_specs=[tile] * 5 + [by_rows(rows, out_width), pl.BlockSpec((2, half), lambda i: (0, 0))],
         out_shape=[jax.ShapeDtypeStruct((words, half), kind) for kind in (BF16, BF16, BF16, F32, BF16)]
         + [jax.ShapeDtypeStruct((words, out_width), F32), jax.ShapeDtypeStruct((2, half), F32)],
@@ -603,7 +603,7 @@
     return pl.pallas_call(
         functools.partial(slope_kernel, len(pieces), block_rows, width),
         grid=(words // rows,),
-        in_specs=[SMEM_SPEC] + [tile] * 5 + [ANY_SPEC] * len(pieces),
+        in_specs=[SMEM_SPEC] + [tile] * 5 + [HBM_SPEC] * len(pieces),
         out_specs=[tile, tile, tile, tile, pl.BlockSpec((2, half), lambda i: (0, 0))],
         out_shape=[jax.ShapeDtypeStruct((words, half), kind) for kind in (BF16, BF16, F32, BF16)] + [jax.ShapeDtypeStruct((2, half), F32)],
         scratch_shapes=[pltpu.VMEM((2, half, half), BF16), pltpu.SemaphoreType.DMA((count_of(pieces),))],
@@ -620,7 +620,7 @@
     return pl.pallas_call(
         functools.partial(back_kernel, len(pieces), block_rows),
         grid=(words // rows,),
-        in_specs=[SMEM_SPEC, tile, tile, tile] + [ANY_SPEC] * len(pieces),
+        in_specs=[SMEM_SPEC, tile, tile, tile] + [HBM_SPEC] * len(pieces),
         out_specs=tile,
         out_shape=jax.ShapeDtypeStruct((words, width), F32),
         scratch_shapes=[pltpu.VMEM((2, width, width), BF16), pltpu.SemaphoreType.DMA((count_of(pieces),))],
@@ -666,10 +666,10 @@
     grads, refs = refs[:n_grads], refs[n_grads:]
     weight, one, two, average = refs[:4]
     grad, second, new, average_new = refs[-4:]
-    width = grads[0].shape[2]
+    width = grads[0].shape[1]
     for j, ref in enumerate(grads):
         at = pl.ds(pl.multiple_of(at_ref[j], LANES), width)
-        grad[:, :, at] = ref[...].astype(F32)
+        grad[0, :, at] = ref[...].astype(F32)
     second_new, updated = adam_update(weight[...], grad[...], one[...], two[...], 0.02)
     second[...] = second_new
     new[...] = updated
@@ -677,7 +677,7 @@
 
 
 def owner_update(slot, at, grads, weight, one, two, average, so_far=()):
-    slots, rows, width = grads[0].shape
+    rows, width = grads[0].shape
     part = min(64, rows)
     block = pl.BlockSpec((1, part, weight.shape[2]), lambda i: (slot, i, 0))
     given = len(grads) + 5
@@ -685,9 +685,9 @@
         functools.partial(owner_kernel, len(grads)),
         grid=(rows // part,),
         in_specs=[SMEM_SPEC]
-        + [pl.BlockSpec((1, part, width), lambda i: (slot, i, 0))] * len(grads)
+        + [pl.BlockSpec((part, width), lambda i: (i, 0))] * len(grads)
         + [block] * 4
-        + [ANY_SPEC] * len(so_far),
+        + [HBM_SPEC] * len(so_far),
         out_specs=[block] * 4,
         out_shape=[jax.ShapeDtypeStruct(weight.shape, F32)] * 4,
         input_output_aliases={given + n: n for n in range(len(so_far))},
@@ -737,8 +737,10 @@
 def return_kernel(counts, owner_ref, *refs):
     layers = (refs[: counts[0]], refs[counts[0] : counts[0] + counts[1]])
     here = lax.axis_index("filt")
-    for step, out in enumerate(refs[counts[0] + counts[1] :]):
+    outs = refs[counts[0] + counts[1] :]
+    for step in range(len(outs) // SLOTS):
         for slot in range(SLOTS):
+            out = outs[SLOTS * step + slot]
             taken = -1
             for unit in range(UNITS):
                 fits = (owner_ref[unit] ^ here == step) & (slot_of(owner_ref, unit) == slot)
@@ -746,12 +748,12 @@
             for unit in range(UNITS):
 
                 @pl.when(taken == unit)
-                def _(unit=unit, out=out, slot=slot):
-                    out[slot] = sum(ref[unit % 2].astype(F32) for ref in layers[unit // 2]).astype(BF16)
+                def _(unit=unit, out=out):
+                    out[...] = sum(ref[unit % 2].astype(F32) for ref in layers[unit // 2]).astype(BF16)
 
             @pl.when(taken < 0)
-            def _(out=out, slot=slot):
-                out[slot] = jnp.zeros(out.shape[1:], BF16)
+            def _(out=out):
+                out[...] = jnp.zeros(out.shape, BF16)
 
 
 def return_units(owners, layers, count):
@@ -763,8 +765,8 @@
         functools.partial(return_kernel, [len(layer) for layer in layers]),
         grid=(shape[1] // part,),
         in_specs=[SMEM_SPEC] + [block] * len(terms),
-        out_specs=[block] * count,
-        out_shape=[jax.ShapeDtypeStruct(shape, BF16)] * count,
+        out_specs=[pl.BlockSpec((part, shape[2]), lambda i: (i, 0))] * (SLOTS * count),
+        out_shape=[jax.ShapeDtypeStruct(shape[1:], BF16)] * (SLOTS * count),
         compiler_params=params(),
         cost_estimate=lasting(3),
         name="return_units",
@@ -1180,29 +1182,33 @@
     optimizer = (highway_weight, highway_moment_one, highway_moment_two, highway_average)
     columns = (place.f ^ jnp.arange(n_filt, dtype=jnp.int32)) * width
     if direct:
-        slot_grads, small, proj_y, vectors_arrived = settle(slot_grads, small, proj_y, vectors_arrived)
+        slot_grads, proj_y, vectors_arrived = settle(slot_grads, proj_y, vectors_arrived)
         proj_rows = rows_over_core(place, proj_here + proj_y.astype(F32))
-        arrived_slots = [place.over_filt(slot_grads[step], step) for step in range(1, n_filt)]
+        by_slot = [slot_grads[slot::SLOTS] for slot in range(SLOTS)]
+        to_owner = lambda grads: [grads[0]] + [place.over_filt(grads[step], step) for step in range(1, n_filt)]
+        by_slot[0] = to_owner(by_slot[0])
         small = small + swap_z(place, small.astype(BF16), 1).astype(F32)
+        by_slot, small, proj_rows = settle(by_slot, small, proj_rows)
+        by_slot[1] = to_owner(by_slot[1])
         small = small + swap_z(place, small.astype(BF16), 2).astype(F32)
-        small, arrived_slots, proj_rows = settle(small, arrived_slots, proj_rows)
+        proj_rows = swap_rows(place, proj_rows[0] + proj_rows[1].astype(F32), 2)
+        updates = owner_update(0, columns, by_slot[0], *optimizer)
+        updates, small, proj_rows, by_slot[1] = settle(updates, small, proj_rows, by_slot[1])
         conv_sums, small = small[:width], small[width:]
-        slot_grads = [slot_grads[0]] + arrived_slots
-        small = small + over_x(small)
-        proj_rows = swap_rows(place, proj_rows[0] + proj_rows[1].astype(F32), 2)
-        updates = owner_update(0, columns, slot_grads, *optimizer)
-        updates, small, proj_rows, slot_grads = settle(updates, small, proj_rows, slot_grads)
-        small = small + over_y(small, 1)
+        others = [place.over_filt(small, step) for step in range(1, n_filt)]
         proj_rows = swap_rows(place, proj_rows[0] + proj_rows[1].astype(F32), 1)
-        updates = owner_update(1, columns, slot_grads, *optimizer, updates)
-        updates, small, proj_rows = settle(updates, small, proj_rows)
+        updates = owner_update(1, columns, by_slot[1], *optimizer, updates)
+        updates, others, proj_rows = settle(updates, others, proj_rows)
+        small = (small + others[0]) + (others[1] + others[2])
         proj_grad = (proj_rows[0] + proj_rows[1].astype(F32)).reshape(rows_proj, out_width)
     else:
         slot_grads = return_units(highway_owner, [[sum_zero], [sum_one]], n_filt)
-        slot_grads = [slot_grads[0]] + [place.over_filt(slot_grads[step], step) for step in range(1, n_filt)]
         conv_sums, small = small[:width], small[width:]
-        updates = owner_update(0, columns, slot_grads, *optimizer)
-        updates = owner_update(1, columns, slot_grads, *optimizer, updates)
+        updates = ()
+        for slot in range(SLOTS):
+            grads = slot_grads[slot::SLOTS]
+            grads = [grads[0]] + [place.over_filt(grads[step], step) for step in range(1, n_filt)]
+            updates = owner_update(slot, columns, grads, *optimizer, updates)
     highway_grad, highway_second, highway_new, highway_average_new = updates
     word_vectors = vectors_here + vectors_arrived.astype(F32) + bias_float[UNITS * width_full :]
     conv_grad, conv_bias_grad = conv_sums[:, :TAPS].T * tap_mask, conv_sums[:, TAPS]

time: 504 us -> 499 us (0.990)
  waiting for transfers between devices: 104 us -> 91 us
    ppermute x29 -> x33, waiting for transfers between devices: 49.1 us -> 38 us  [over_filt(): lax.ppermute(value, 'filt', [(i, i ^ step) for i in range(self.n_filt)])]
    ppermute x29 -> x33, starting transfers between devices: 34.5 us -> 39.8 us  [over_filt(): lax.ppermute(value, 'filt', [(i, i ^ step) for i in range(self.n_filt)])]
    unnamed x204 -> x196, local copies, waits for them, and re-layouts: 13.2 us -> 9.38 us
  transfers between devices with their start and end apart: 54 -> 58, of which waited for: 16 -> 16; matrix products, arithmetic and copies ran while one was open for 8% -> 8% of each run, Pallas kernels for 52% -> 53%
where the time goes in v4:
time: 499 us; the launch traced here: 492 us
  Pallas kernels  265 us (53%)
  waiting for transfers between devices  91 us (18%)
  starting transfers between devices  68 us (14%)
  other arithmetic  45.3 us (9%)
  local copies, waits for them, and re-layouts  17.4 us (3%)
    pallas_call x4, Pallas kernels, conv_backward(): pl.pallas_call(functools.partial(conv_backward_kernel, cblock, len(ranks)...  59.1 us
    ppermute x12, waiting for transfers between devices, over_z(): return lax.ppermute(value, 'dp', pairs)  43.7 us
    pallas_call x4, Pallas kernels, conv_forward(): pl.pallas_call(functools.partial(conv_forward_kernel, cblock, base), grid...  42.4 us
    ppermute x33, starting transfers between devices, over_filt(): lax.ppermute(value, 'filt', [(i, i ^ step) for i in range(self.n_filt)])  39.8 us
    ppermute x33, waiting for transfers between devices, over_filt(): lax.ppermute(value, 'filt', [(i, i ^ step) for i in range(self.n_filt)])  38 us
    pallas_call x2, Pallas kernels, highway_turn(): pl.pallas_call(functools.partial(turn_kernel, len(pieces), block_rows, wi...  33.5 us
    pallas_call x4, Pallas kernels, highway_back(): pl.pallas_call(functools.partial(back_kernel, len(pieces), block_rows), g...  31 us
    pallas_call x2, Pallas kernels, highway_weight_grad(): pl.pallas_call(functools.partial(weight_grad_kernel, len(xs), len(xs[0]),...  30.3 us
  transfers between devices with their start and end apart: 58, of which 16 were waited for; matrix products, arithmetic and copies ran while one was open for 8% of the time, Pallas kernels for 53%

profile of v4, /device:TPU:0, one launch (start us, length us, event | category | flops | bytes accessed | tf_op | source)
XLA Modules:
  0.0 492.2 jit_solution(9495541500365684677)
XLA Ops:
  0.7 3.7 dynamic-slice_convert_fusion
  4.4 3.9 collective-permute-start.2
  9.3 1.8 convert_reduce_fusion
  12.5 7.8 %conv_forward.5 = (bf16[512,256]{1,0:T(8,128)(2,1)S(1)}, f32[512,256]{1,0:T(8,128)}, f32[64,256]{1,0:T(8,128)}, bf16[1024,256]{1,0:T(8,128)(2,1)}) custom-call(s32[2]{0:T(128)S(1)} %slice.229.narrow_ref, s32[2048,1]{1,0:T(8,128)S(1)} %copy.97.rank_ref, bf16[64,2048]{1,0:T(8,128)(2,1)S(1)} %fusion.12.data_ref, f32[16,384]{1,0:T(8,128)S(1)} %pad.19.table_ref, ...), custom_call_target="tpu_custom_call" | custom-call | flops 110000000 | bytes 330000 | tf_op jit(solution)/shard_map/conv_forward/pallas_call | solution.py:160
  20.3 12.7 %conv_forward.4 = (bf16[512,256]{1,0:T(8,128)(2,1)S(1)}, f32[512,256]{1,0:T(8,128)}, f32[64,256]{1,0:T(8,128)}, bf16[1024,256]{1,0:T(8,128)(2,1)}) custom-call(s32[2]{0:T(128)S(1)} %slice.229.narrow_ref, s32[2048,1]{1,0:T(8,128)S(1)} %copy.97.rank_ref, bf16[64,2048]{1,0:T(8,128)(2,1)S(1)} %fusion.12.data_ref, f32[16,384]{1,0:T(8,128)S(1)} %pad.19.table_ref, ...), custom_call_target="tpu_custom_call" | custom-call | flops 110000000 | bytes 330000 | tf_op jit(solution)/shard_map/conv_forward/pallas_call | solution.py:160
  35.4 2.8 choose_units.1
  41.4 3.6 collective-permute-start.4
  45.6 10.6 %conv_forward.6 = (bf16[512,512]{1,0:T(8,128)(2,1)S(1)}, f32[512,512]{1,0:T(8,128)}, f32[64,512]{1,0:T(8,128)}, bf16[1024,512]{1,0:T(8,128)(2,1)}) custom-call(s32[2]{0:T(128)S(1)} %slice.229.narrow_ref, s32[2048,1]{1,0:T(8,128)S(1)} %copy.97.rank_ref, bf16[64,2048]{1,0:T(8,128)(2,1)S(1)} %fusion.12.data_ref, f32[16,384]{1,0:T(8,128)S(1)} %pad.19.table_ref, ...), custom_call_target="tpu_custom_call" | custom-call | flops 110000000 | bytes 330000 | tf_op jit(solution)/shard_map/conv_forward/pallas_call | solution.py:160
  56.2 11.3 %conv_forward.7 = (bf16[512,1024]{1,0:T(8,128)(2,1)S(1)}, f32[512,1024]{1,0:T(8,128)}, f32[64,1024]{1,0:T(8,128)}, bf16[1024,1024]{1,0:T(8,128)(2,1)}) custom-call(s32[2]{0:T(128)S(1)} %slice.229.narrow_ref, s32[2048,1]{1,0:T(8,128)S(1)} %copy.97.rank_ref, bf16[64,2048]{1,0:T(8,128)(2,1)S(1)} %fusion.12.data_ref, f32[16,384]{1,0:T(8,128)S(1)} %pad.19.table_ref, ...), custom_call_target="tpu_custom_call" | custom-call | flops 110000000 | bytes 330000 | tf_op jit(solution)/shard_map/conv_forward/pallas_call | solution.py:160
  67.5 3.0 place_words.3
  70.6 3.0 place_words.2.refs_0_
  75.4 2.5 maximum_maximum_fusion
  77.9 20.2 %collective-permute-done.10 = bf16[2,256,512]{2,1,0:T(8,128)(2,1)S(1)} collective-permute-done((bf16[2,256,512]{2,1,0:T(8,128)(2,1)S(1)}, bf16[2,256,512]{2,1,0:T(8,128)(2,1)S(1)}, u32[]{:S(2)}, u32[]{:S(2)}) %collective-permute-start.10) | collective-permute-done | bytes 524320 | tf_op jit(solution)/shard_map/ppermute | solution.py:799
  100.7 1.7 collective-permute-start.13
  102.8 1.9 collective-permute-start.15
  106.4 1.9 convert_reduce_fusion.1
  109.6 3.0 broadcast_select_fusion
  112.6 7.7 %collective-permute-done.15 = bf16[2,320,512]{2,1,0:T(8,128)(2,1)S(1)} collective-permute-done((bf16[2,320,512]{2,1,0:T(8,128)(2,1)}, bf16[2,320,512]{2,1,0:T(8,128)(2,1)S(1)}, u32[]{:S(2)}, u32[]{:S(2)}) %collective-permute-start.15) | collective-permute-done | bytes 655392 | tf_op jit(solution)/shard_map/ppermute | solution.py:799
  120.2 13.6 %collective-permute-done.14 = bf16[2,320,512]{2,1,0:T(8,128)(2,1)S(1)} collective-permute-done((bf16[2,320,512]{2,1,0:T(8,128)(2,1)}, bf16[2,320,512]{2,1,0:T(8,128)(2,1)S(1)}, u32[]{:S(2)}, u32[]{:S(2)}) %collective-permute-start.14) | collective-permute-done | bytes 655392 | tf_op jit(solution)/shard_map/ppermute | solution.py:799
  133.9 2.3 collective-permute-done.11.refs_6_.refs_2_
  143.0 12.0 %highway_forward.2 = (f32[512,1024]{1,0:T(8,128)}, bf16[512,1024]{1,0:T(8,128)(2,1)}, bf16[512,1024]{1,0:T(8,128)(2,1)}, bf16[512,1024]{1,0:T(8,128)(2,1)}, bf16[512,1024]{1,0:T(8,128)(2,1)}) custom-call(s32[3,16]{1,0:T(4,128)} %get-tuple-element.332.table_ref, f32[2,1024]{1,0:T(2,128)} %pad_maximum_fusion.6.bias_ref, bf16[1024,512]{1,0:T(8,128)(2,1)} %copy-done, ...), custom_call_target="tpu_custom_call" | custom-call | flops 100000000 | bytes 300000 | tf_op jit(solution)/shard_map/highway_forward/pallas_call | solution.py:561
  155.0 1.7 collective-permute-start.21
  156.7 12.1 %highway_forward.3 = (f32[512,1024]{1,0:T(8,128)}, bf16[512,1024]{1,0:T(8,128)(2,1)}, bf16[512,1024]{1,0:T(8,128)(2,1)}, bf16[512,1024]{1,0:T(8,128)(2,1)}, bf16[512,1024]{1,0:T(8,128)(2,1)}) custom-call(s32[3,16]{1,0:T(4,128)} %get-tuple-element.332.table_ref, f32[2,1024]{1,0:T(2,128)} %pad_maximum_fusion.6.bias_ref, bf16[1024,512]{1,0:T(8,128)(2,1)} %copy-done, ...), custom_call_target="tpu_custom_call" | custom-call | flops 100000000 | bytes 300000 | tf_op jit(solution)/shard_map/highway_forward/pallas_call | solution.py:561
  168.8 2.1 collective-permute-done.18
  172.9 14.2 %collective-permute-done.20 = bf16[2,320,512]{2,1,0:T(8,128)(2,1)S(1)} collective-permute-done((bf16[2,320,512]{2,1,0:T(8,128)(2,1)}, bf16[2,320,512]{2,1,0:T(8,128)(2,1)S(1)}, u32[]{:S(2)}, u32[]{:S(2)}) %collective-permute-start.20) | collective-permute-done | bytes 655392 | tf_op jit(solution)/shard_map/ppermute | solution.py:786
  187.0 2.2 pad_maximum_fusion.1.refs_1_
  189.4 1.8 collective-permute-start.24
  192.7 1.7 collective-permute-done.23.refs_3_
  194.4 16.6 %highway_turn.2 = (bf16[512,1024]{1,0:T(8,128)(2,1)}, bf16[512,1024]{1,0:T(8,128)(2,1)}, bf16[512,1024]{1,0:T(8,128)(2,1)}, f32[512,1024]{1,0:T(8,128)}, bf16[51...) custom-call(s32[3,16]{1,0:T(4,128)} %get-tuple-element.333.table_ref, ...), custom_call_target="tpu_custom_call" | custom-call | flops 160000000 | bytes 480000 | tf_op jit(solution)/shard_map/highway_turn/pallas_call | solution.py:583
  211.0 1.8 collective-permute-start.25
  212.8 2.7 collective-permute-done.24.mate.refs_3_
  216.4 17.0 %highway_turn.3 = (bf16[512,1024]{1,0:T(8,128)(2,1)}, bf16[512,1024]{1,0:T(8,128)(2,1)}, bf16[512,1024]{1,0:T(8,128)(2,1)}, f32[512,1024]{1,0:T(8,128)}, bf16[51...) custom-call(s32[3,16]{1,0:T(4,128)} %get-tuple-element.333.table_ref, ...), custom_call_target="tpu_custom_call" | custom-call | flops 160000000 | bytes 480000 | tf_op jit(solution)/shard_map/highway_turn/pallas_call | solution.py:583
  233.4 1.8 collective-permute-start.26
  235.8 15.2 %highway_weight_grad.2 = (bf16[4,2,256,512]{3,2,1,0:T(8,128)(2,1)}, bf16[4,2,256,512]{3,2,1,0:T(8,128)(2,1)}, bf16[2,4,2,256,512]{4,3,2,1,0:T(8,128)(2,1)}) custom-call(s32[2,4]{1,0:T(2,128)} %pad_add_fusion.2.table_ref, bf16[512,1024]{1,0:T(8,128)(2,1)} %get-tuple-element.349.own.refs_0_, bf16[512,1024]{1,0:T(8,128)(2,1)} %copy-done.27, ...), custom_call_target="tpu_custom_call" | custom-call | flops 150000000 | bytes 450000 | tf_op jit(solution)/shard_map/highway_weight_grad/pallas_call | solution.py:640
  251.0 7.9 %highway_back.4.partial = f32[512,1024]{1,0:T(8,128)} custom-call(s32[3,16]{1,0:T(4,128)} %get-tuple-element.333.table_ref, bf16[512,1024]{1,0:T(8,128)(2,1)} %get-tuple-element.366.refs_4_.d_first, bf16[512,1024]{1,0:T(8,128)(2,1)} %get-tuple-element.367.refs_6_.d_gate, f32[512,1024]{1,0:T(8,128)} %get-tuple-element.382.up, ...), custom_call_target="tpu_custom_call" | custom-call | flops 60000000 | bytes 180000 | tf_op jit(solution)/shard_map/highway_back/pallas_call | solution.py:620
  260.0 7.8 %highway_slopes.2 = (bf16[512,1024]{1,0:T(8,128)(2,1)}, bf16[512,1024]{1,0:T(8,128)(2,1)}, f32[512,1024]{1,0:T(8,128)}, bf16[512,1024]{1,0:T(8,128)(2,1)}, f32[2,1024]{1,0:T(2,128)}) custom-call(s32[3,16]{1,0:T(4,128)} %get-tuple-element.332.table_ref, f32[512,1024]{1,0:T(8,128)} %highway_back.4.partial, bf16[512,1024]{1,0:T(8,128)(2,1)} %copy-done.43, ...), custom_call_target="tpu_custom_call" | custom-call | flops 80000000 | bytes 240000 | tf_op jit(solution)/shard_map/highway_slopes/pallas_call | solution.py:603
  267.9 5.2 %fusion = bf16[4,2,256,512]{3,2,1,0:T(8,128)(2,1)} fusion(bf16[4,2,256,512]{3,2,1,0:T(8,128)(2,1)} %get-tuple-element.403, bf16[2,4,2,256,512]{4,3,2,1,0:T(8,128)(2,1)S(1)} %collective-permute-done.27), kind=kLoop, calls=%fused_computation.2 | loop fusion | flops 4194304 | bytes 6291456 | tf_op jit(solution)/shard_map/convert_element_type | solution.py:858
  275.2 7.7 %highway_back.5.partial = f32[512,1024]{1,0:T(8,128)} custom-call(s32[3,16]{1,0:T(4,128)} %get-tuple-element.333.table_ref, bf16[512,1024]{1,0:T(8,128)(2,1)} %get-tuple-element.377.refs_5_.d_first, bf16[512,1024]{1,0:T(8,128)(2,1)} %get-tuple-element.378.refs_7_.d_gate, f32[512,1024]{1,0:T(8,128)} %get-tuple-element.406.up, ...), custom_call_target="tpu_custom_call" | custom-call | flops 60000000 | bytes 180000 | tf_op jit(solution)/shard_map/highway_back/pallas_call | solution.py:620
  282.9 7.9 %highway_slopes.3 = (bf16[512,1024]{1,0:T(8,128)(2,1)}, bf16[512,1024]{1,0:T(8,128)(2,1)}, f32[512,1024]{1,0:T(8,128)}, bf16[512,1024]{1,0:T(8,128)(2,1)}, f32[2,1024]{1,0:T(2,128)}) custom-call(s32[3,16]{1,0:T(4,128)} %get-tuple-element.332.table_ref, f32[512,1024]{1,0:T(8,128)} %highway_back.5.partial, bf16[512,1024]{1,0:T(8,128)(2,1)} %collective-permute-done.26.arrived, ...), custom_call_target="tpu_custom_call" | custom-call | flops 80000000 | bytes 240000 | tf_op jit(solution)/shard_map/highway_slopes/pallas_call | solution.py:603
  291.2 15.2 %highway_weight_grad.3 = (bf16[4,2,256,512]{3,2,1,0:T(8,128)(2,1)}, bf16[4,2,256,512]{3,2,1,0:T(8,128)(2,1)}, bf16[2,4,2,256,512]{4,3,2,1,0:T(8,128)(2,1)}) custom-call(s32[2,4]{1,0:T(2,128)} %pad_add_fusion.2.table_ref, bf16[1024,512]{1,0:T(8,128)(2,1)} %copy-done, bf16[1024,512]{1,0:T(8,128)(2,1)} %copy-done.16, bf16[1024,512]{1,0:T(8,128)(2,1)} %copy-done.17, ...), custom_call_target="tpu_custom_call" | custom-call | flops 150000000 | bytes 450000 | tf_op jit(solution)/shard_map/highway_weight_grad/pallas_call | solution.py:640
  306.4 7.6 %highway_back.6 = f32[512,1024]{1,0:T(8,128)} custom-call(s32[3,16]{1,0:T(4,128)} %get-tuple-element.332.table_ref, bf16[512,1024]{1,0:T(8,128)(2,1)} %get-tuple-element.401.refs_4_.d_first, bf16[512,1024]{1,0:T(8,128)(2,1)} %get-tuple-element.402.refs_6_.d_gate, f32[512,1024]{1,0:T(8,128)} %get-tuple-element.419.up, bf16[2,2,256,512]{3,2,1,0:T(8,128)(2,1)} %copy-done.12, ...), custom_call_target="tpu_custom_call" | custom-call | flops 60000000 | bytes 180000 | tf_op jit(solution)/shard_map/highway_back/pallas_call | solution.py:620
  314.1 7.8 %highway_back.7 = f32[512,1024]{1,0:T(8,128)} custom-call(s32[3,16]{1,0:T(4,128)} %get-tuple-element.332.table_ref, bf16[512,1024]{1,0:T(8,128)(2,1)} %get-tuple-element.411.refs_5_.d_first, bf16[512,1024]{1,0:T(8,128)(2,1)} %get-tuple-element.412.refs_7_.d_gate, f32[512,1024]{1,0:T(8,128)} %get-tuple-element.420.up, bf16[2,2,256,512]{3,2,1,0:T(8,128)(2,1)} %copy-done.12, ...), custom_call_target="tpu_custom_call" | custom-call | flops 60000000 | bytes 180000 | tf_op jit(solution)/shard_map/highway_back/pallas_call | solution.py:620
  322.4 4.5 convert_add_fusion.11
  326.9 2.8 collective-permute-start.34
  333.6 2.5 fusion.1
  343.3 14.7 %collective-permute-done.31.refs_3_ = bf16[1024,512]{1,0:T(8,128)(2,1)S(1)} collective-permute-done((bf16[1024,512]{1,0:T(8,128)(2,1)S(1)}, bf16[1024,512]{1,0:T(8,128)(2,1)S(1)}, u32[]{:S(2)}, u32[]{:S(2)}) %collective-permute-start.31) | collective-permute-done | bytes 1048608 | tf_op jit(solution)/shard_map/ppermute | solution.py:786
  358.0 19.5 %conv_backward.4.refs_4_ = f32[640,128]{1,0:T(8,128)S(1)} custom-call(s32[2]{0:T(128)S(1)} %slice.229.narrow_ref, f32[64,256]{1,0:T(8,128)S(1)} %copy-done.8, bf16[1024,256]{1,0:T(8,128)(2,1)} %get-tuple-element.451.e_ref, bf16[512,128]{1,0:T(8,128)(2,1)S(1)} %copy.98.conv_ref, bf16[128,512]{1,0:T(8,128)(2,1)S(1)} %pad.21.back_ref, ...), custom_call_target="tpu_custom_call" | custom-call | flops 150000000 | bytes 450000 | tf_op jit(solution)/shard_map/conv_backward/pallas_call | solution.py:277
  377.5 2.0 collective-permute-done.36
  379.6 2.7 fusion.4
  383.9 1.8 collective-permute-start.40
  386.4 1.9 collective-permute-start.38
  388.4 11.2 %conv_backward.5.refs_4_ = f32[640,128]{1,0:T(8,128)S(1)} custom-call(s32[2]{0:T(128)S(1)} %slice.229.narrow_ref, f32[64,256]{1,0:T(8,128)S(1)} %copy-done.7, bf16[1024,256]{1,0:T(8,128)(2,1)} %get-tuple-element.475.e_ref, bf16[512,128]{1,0:T(8,128)(2,1)S(1)} %copy.98.conv_ref, bf16[128,512]{1,0:T(8,128)(2,1)S(1)} %pad.21.back_ref, ...), custom_call_target="tpu_custom_call" | custom-call | flops 150000000 | bytes 450000 | tf_op jit(solution)/shard_map/conv_backward/pallas_call | solution.py:277
  399.6 14.4 %conv_backward.6.refs_4_ = f32[640,128]{1,0:T(8,128)S(1)} custom-call(s32[2]{0:T(128)S(1)} %slice.229.narrow_ref, f32[64,512]{1,0:T(8,128)S(1)} %copy-done.6, bf16[1024,512]{1,0:T(8,128)(2,1)} %get-tuple-element.472.e_ref, bf16[512,128]{1,0:T(8,128)(2,1)S(1)} %copy.98.conv_ref, bf16[128,512]{1,0:T(8,128)(2,1)S(1)} %pad.21.back_ref, ...), custom_call_target="tpu_custom_call" | custom-call | flops 150000000 | bytes 450000 | tf_op jit(solution)/shard_map/conv_backward/pallas_call | solution.py:277
  415.8 8.2 %collective-permute-start.41 = (bf16[2,256,512]{2,1,0:T(8,128)(2,1)}, bf16[2,256,512]{2,1,0:T(8,128)(2,1)}, u32[]{:S(2)}, u32[]{:S(2)}) collective-permute-start(bf16[2,256,512]{2,1,0:T(8,128)(2,1)} %get-tuple-element.493), channel_id=1, source_target_pairs={{0,2},{1,3},{2,4},{3,5},{4,6},{5,7},{6,0},{7,1},{8,10},{9,11},{10,... | collective-permute-start | bytes 1572872 | tf_op jit(solution)/shard_map/ppermute | solution.py:799
  426.1 14.0 %conv_backward.7 = f32[640,128]{1,0:T(8,128)S(1)} custom-call(s32[2]{0:T(128)S(1)} %slice.229.narrow_ref, f32[64,1024]{1,0:T(8,128)S(1)} %copy-done.5, bf16[1024,1024]{1,0:T(8,128)(2,1)} %get-tuple-element.490.e_ref, bf16[512,128]{1,0:T(8,128)(2,1)S(1)} %copy.98.conv_ref, bf16[128,512]{1,0:T(8,128)(2,1)S(1)} %pad.21.back_ref, ...), custom_call_target="tpu_custom_call" | custom-call | flops 150000000 | bytes 450000 | tf_op jit(solution)/shard_map/conv_backward/pallas_call | solution.py:277
  440.1 4.1 return_units.1
  444.8 2.9 collective-permute-start.45
  448.0 1.9 slice_add_fusion
  453.3 3.5 collective-permute-done.47
  458.1 1.7 collective-permute-start.51
  461.7 2.9 collective-permute-start.50
  464.6 8.2 %owner_update.2 = (f32[2,256,2048]{2,1,0:T(8,128)}, f32[2,256,2048]{2,1,0:T(8,128)}, f32[2,256,2048]{2,1,0:T(8,128)}, f32[2,256,2048]{2,1,0:T(8,128)}) custom-call(s32[4]{0:T(128)} %xor_multiply_fusion.at_ref, bf16[256,512]{1,0:T(8,128)(2,1)} %get-tuple-element.521.refs_0_, bf16[256,512]{1,0:T(8,128)(2,1)} %copy-done.58, bf16[256,512]{1,0:T(8,128)(2,1)} %copy-done.59, ...), custom_call_target="tpu_custom_call" | custom-call | flops 80000000 | bytes 240000 | tf_op jit(solution)/shard_map/owner_update/pallas_call | solution.py:684
  472.9 2.4 collective-permute-done.50
  480.9 8.3 %owner_update.3 = (f32[2,256,2048]{2,1,0:T(8,128)}, f32[2,256,2048]{2,1,0:T(8,128)}, f32[2,256,2048]{2,1,0:T(8,128)}, f32[2,256,2048]{2,1,0:T(8,128)}) custom-call(s32[4]{0:T(128)} %xor_multiply_fusion.at_ref, bf16[256,512]{1,0:T(8,128)(2,1)} %get-tuple-element.537.refs_0_, ...), custom_call_target="tpu_custom_call", output_to_operand_aliasing={{0}: (9, {}), {1}: (10, {}), {2}: (11, {}), {3}: (12, {})} | custom-call | flops 80000000 | bytes 240000 | tf_op jit(solution)/shard_map/owner_update/pallas_call | solution.py:684
  (375 shorter events, 64.6 us)
Async XLA Ops:
  4.4 30.0 %collective-permute-start.2 = (bf16[2,256,512]{2,1,0:T(8,128)(2,1)}, bf16[2,256,512]{2,1,0:T(8,128)(2,1)S(1)}, u32[]{:S(2)}, u32[]{:S(2)}) collective-permute-start(bf16[2,256,512]{2,1,0:T(8,128)(2,1)} %get-tuple-element.585), channel_id=1, source_target_pairs={{0,24},{8,16},{16,8},{24,0},{1,25},{9,17},{17,9},{25,1},{2,26},{10... | collective-permute-start | bytes 1572872 | tf_op jit(solution)/shard_map/ppermute | solution.py:786
  8.3 26.1 %collective-permute-start.1 = (bf16[2,256,512]{2,1,0:T(8,128)(2,1)}, bf16[2,256,512]{2,1,0:T(8,128)(2,1)S(1)}, u32[]{:S(2)}, u32[]{:S(2)}) collective-permute-start(bf16[2,256,512]{2,1,0:T(8,128)(2,1)} %get-tuple-element.586), channel_id=1, source_target_pairs={{0,16},{8,24},{16,0},{24,8},{1,17},{9,25},{17,1},{25,9},{2,18},{10... | collective-permute-start | bytes 1572872 | tf_op jit(solution)/shard_map/ppermute | solution.py:786
  8.8 25.7 %collective-permute-start = (bf16[2,256,512]{2,1,0:T(8,128)(2,1)}, bf16[2,256,512]{2,1,0:T(8,128)(2,1)}, u32[]{:S(2)}, u32[]{:S(2)}) collective-permute-start(bf16[2,256,512]{2,1,0:T(8,128)(2,1)} %get-tuple-element.587), channel_id=1, source_target_pairs={{0,8},{8,0},{16,24},{24,16},{1,9},{9,1},{17,25},{25,17},{2,10},{10... | collective-permute-start | bytes 1572872 | tf_op jit(solution)/shard_map/ppermute | solution.py:786
  33.0 23.2 %copy-start.73 = (f32[8960]{0:T(1024)}, f32[8960]{0:T(1024)S(1)}, u32[]{:S(2)}) copy-start(f32[8960]{0:T(1024)S(1)} %reduce_precision.19) | copy-start | bytes 107524
  38.2 35.4 %collective-permute-start.7 = (bf16[512,768]{1,0:T(8,128)(2,1)}, bf16[512,768]{1,0:T(8,128)(2,1)}, u32[]{:S(2)}, u32[]{:S(2)}) collective-permute-start(bf16[512,768]{1,0:T(8,128)(2,1)} %param.25), channel_id=1, source_target_pairs={{0,8},{8,0},{16,24},{24,16},{1,9},{9,1},{17,25},{25,17},{2,10},{10... | collective-permute-start | bytes 2359304 | tf_op jit(solution)/shard_map/ppermute | solution.py:786
  39.3 34.3 %collective-permute-start.6 = (bf16[2,320,512]{2,1,0:T(8,128)(2,1)}, bf16[2,320,512]{2,1,0:T(8,128)(2,1)}, u32[]{:S(2)}, u32[]{:S(2)}) collective-permute-start(bf16[2,320,512]{2,1,0:T(8,128)(2,1)} %get-tuple-element.350), channel_id=1, source_target_pairs={{0,16},{8,24},{16,0},{24,8},{1,17},{9,25},{17,1},{25,9},{2,18},{10... | collective-permute-start | bytes 1966088 | tf_op jit(solution)/shard_map/ppermute | solution.py:786
  40.2 33.4 %collective-permute-start.5 = (bf16[2,256,512]{2,1,0:T(8,128)(2,1)}, bf16[2,256,512]{2,1,0:T(8,128)(2,1)}, u32[]{:S(2)}, u32[]{:S(2)}) collective-permute-start(bf16[2,256,512]{2,1,0:T(8,128)(2,1)} %get-tuple-element.326), channel_id=1, source_target_pairs={{0,16},{8,24},{16,0},{24,8},{1,17},{9,25},{17,1},{25,9},{2,18},{10... | collective-permute-start | bytes 1572872 | tf_op jit(solution)/shard_map/ppermute | solution.py:786
  41.4 32.3 %collective-permute-start.4 = (bf16[2,256,512]{2,1,0:T(8,128)(2,1)}, bf16[2,256,512]{2,1,0:T(8,128)(2,1)}, u32[]{:S(2)}, u32[]{:S(2)}) collective-permute-start(bf16[2,256,512]{2,1,0:T(8,128)(2,1)} %get-tuple-element.326), channel_id=1, source_target_pairs={{0,6},{1,7},{2,0},{3,1},{4,2},{5,3},{6,4},{7,5},{8,14},{9,15},{10,... | collective-permute-start | bytes 1572872 | tf_op jit(solution)/shard_map/ppermute | solution.py:799
  45.0 28.7 %collective-permute-start.3 = (bf16[2,256,512]{2,1,0:T(8,128)(2,1)}, bf16[2,256,512]{2,1,0:T(8,128)(2,1)}, u32[]{:S(2)}, u32[]{:S(2)}) collective-permute-start(bf16[2,256,512]{2,1,0:T(8,128)(2,1)} %get-tuple-element.326), channel_id=1, source_target_pairs={{0,2},{1,3},{2,4},{3,5},{4,6},{5,7},{6,0},{7,1},{8,10},{9,11},{10,... | collective-permute-start | bytes 1572872 | tf_op jit(solution)/shard_map/ppermute | solution.py:799
  73.6 28.8 %copy-start = (bf16[1024,512]{1,0:T(8,128)(2,1)}, bf16[1024,512]{1,0:T(8,128)(2,1)S(1)}, u32[]{:S(2)}) copy-start(bf16[1024,512]{1,0:T(8,128)(2,1)S(1)} %place_words.2.refs_0_) | copy-start | bytes 3145732
  73.7 24.5 %collective-permute-start.8 = (bf16[1024,512]{1,0:T(8,128)(2,1)S(1)}, bf16[1024,512]{1,0:T(8,128)(2,1)S(1)}, u32[]{:S(2)}, u32[]{:S(2)}) collective-permute-start(bf16[1024,512]{1,0:T(8,128)(2,1)S(1)} %place_words.3), channel_id=1, source_target_pairs={{0,16},{8,24},{16,0},{24,8},{1,17},{9,25},{17,1},{25,9},{2,18},{10... | collective-permute-start | bytes 3145736 | tf_op jit(solution)/shard_map/ppermute | solution.py:786
  73.7 24.4 %collective-permute-start.9 = (bf16[1024,512]{1,0:T(8,128)(2,1)S(1)}, bf16[1024,512]{1,0:T(8,128)(2,1)S(1)}, u32[]{:S(2)}, u32[]{:S(2)}) collective-permute-start(bf16[1024,512]{1,0:T(8,128)(2,1)S(1)} %place_words.2.refs_0_), channel_id=1, source_target_pairs={{0,8},{8,0},{16,24},{24,16},{1,9},{9,1},{17,25},{25,17},{2,10},{10... | collective-permute-start | bytes 3145736 | tf_op jit(solution)/shard_map/ppermute | solution.py:786
  73.8 24.3 %collective-permute-start.10 = (bf16[2,256,512]{2,1,0:T(8,128)(2,1)S(1)}, bf16[2,256,512]{2,1,0:T(8,128)(2,1)S(1)}, u32[]{:S(2)}, u32[]{:S(2)}) collective-permute-start(bf16[2,256,512]{2,1,0:T(8,128)(2,1)S(1)} %copy-done.54), channel_id=1, source_target_pairs={{0,4},{1,5},{2,6},{3,7},{4,0},{5,1},{6,2},{7,3},{8,12},{9,13},{10,... | collective-permute-start | bytes 1572872 | tf_op jit(solution)/shard_map/ppermute | solution.py:799
  99.1 34.8 %collective-permute-start.12 = (bf16[3,2,256,512]{3,2,1,0:T(8,128)(2,1)}, bf16[3,2,256,512]{3,2,1,0:T(8,128)(2,1)}, u32[]{:S(2)}, u32[]{:S(2)}) collective-permute-start(bf16[3,2,256,512]{3,2,1,0:T(8,128)(2,1)} %bitcast_dynamic-update-slice_fusion.refs_5_.refs_1_), channel_id=1, source_target_pairs={{0,1},{1,0},{2,3},{3,2},{4,5},{5,4},{6,7},{7,6},{8,9},{9,8},{10,11... | collective-permute-start | bytes 4718600 | tf_op jit(solution)/shard_map/ppermute | solution.py:795
  99.1 37.1 %collective-permute-start.11 = (bf16[3,2,256,512]{3,2,1,0:T(8,128)(2,1)}, bf16[3,2,256,512]{3,2,1,0:T(8,128)(2,1)}, u32[]{:S(2)}, u32[]{:S(2)}) collective-permute-start(bf16[3,2,256,512]{3,2,1,0:T(8,128)(2,1)} %bitcast_dynamic-update-slice_fusion.refs_5_.refs_1_), channel_id=1, source_target_pairs={{0,16},{8,24},{16,0},{24,8},{1,17},{9,25},{17,1},{25,9},{2,18},{10... | collective-permute-start | bytes 4718600 | tf_op jit(solution)/shard_map/ppermute | solution.py:786
  100.7 33.2 %collective-permute-start.13 = (bf16[1024,512]{1,0:T(8,128)(2,1)S(1)}, bf16[1024,512]{1,0:T(8,128)(2,1)}, u32[]{:S(2)}, u32[]{:S(2)}) collective-permute-start(bf16[1024,512]{1,0:T(8,128)(2,1)S(1)} %collective-permute-done.8.refs_1_), channel_id=1, source_target_pairs={{0,8},{8,0},{16,24},{24,16},{1,9},{9,1},{17,25},{25,17},{2,10},{10... | collective-permute-start | bytes 3145736 | tf_op jit(solution)/shard_map/ppermute | solution.py:786
  102.8 17.4 %collective-permute-start.15 = (bf16[2,320,512]{2,1,0:T(8,128)(2,1)}, bf16[2,320,512]{2,1,0:T(8,128)(2,1)S(1)}, u32[]{:S(2)}, u32[]{:S(2)}) collective-permute-start(bf16[2,320,512]{2,1,0:T(8,128)(2,1)} %get-tuple-element.350), channel_id=1, source_target_pairs={{0,6},{1,7},{2,0},{3,1},{4,2},{5,3},{6,4},{7,5},{8,14},{9,15},{10,... | collective-permute-start | bytes 1966088 | tf_op jit(solution)/shard_map/ppermute | solution.py:799
  104.8 29.1 %collective-permute-start.14 = (bf16[2,320,512]{2,1,0:T(8,128)(2,1)}, bf16[2,320,512]{2,1,0:T(8,128)(2,1)S(1)}, u32[]{:S(2)}, u32[]{:S(2)}) collective-permute-start(bf16[2,320,512]{2,1,0:T(8,128)(2,1)} %get-tuple-element.350), channel_id=1, source_target_pairs={{0,2},{1,3},{2,4},{3,5},{4,6},{5,7},{6,0},{7,1},{8,10},{9,11},{10,... | collective-permute-start | bytes 1966088 | tf_op jit(solution)/shard_map/ppermute | solution.py:799
  109.6 28.3 %copy-start.12 = (bf16[2,2,256,512]{3,2,1,0:T(8,128)(2,1)}, bf16[2,2,256,512]{3,2,1,0:T(8,128)(2,1)S(1)}, u32[]{:S(2)}) copy-start(bf16[2,2,256,512]{3,2,1,0:T(8,128)(2,1)S(1)} %pad_maximum_fusion.3.refs_4_.refs_0_) | copy-start | bytes 3145732
  112.6 26.9 %copy-start.51 = (bf16[2,320,512]{2,1,0:T(8,128)(2,1)S(1)}, bf16[2,320,512]{2,1,0:T(8,128)(2,1)}, u32[]{:S(2)}) copy-start(bf16[2,320,512]{2,1,0:T(8,128)(2,1)} %get-tuple-element.350) | copy-start | bytes 1966084
  120.2 34.7 %copy-start.32 = (bf16[2,320,512]{2,1,0:T(8,128)(2,1)}, bf16[2,320,512]{2,1,0:T(8,128)(2,1)S(1)}, u32[]{:S(2)}) copy-start(bf16[2,320,512]{2,1,0:T(8,128)(2,1)S(1)} %collective-permute-done.15) | copy-start | bytes 1966084
  136.2 5.1 %collective-permute-start.17 = (bf16[3,2,256,512]{3,2,1,0:T(8,128)(2,1)}, bf16[3,2,256,512]{3,2,1,0:T(8,128)(2,1)S(1)}, u32[]{:S(2)}, u32[]{:S(2)}) collective-permute-start(bf16[3,2,256,512]{3,2,1,0:T(8,128)(2,1)} %collective-permute-done.11.refs_6_.refs_2_), channel_id=1, source_target_pairs={{0,1},{1,0},{2,3},{3,2},{4,5},{5,4},{6,7},{7,6},{8,9},{9,8},{10,11... | collective-permute-start | bytes 4718600 | tf_op jit(solution)/shard_map/ppermute | solution.py:795
  136.2 4.5 collective-permute-start.16
  137.9 33.0 %collective-permute-start.19 = (bf16[2,2,320,512]{3,2,1,0:T(8,128)(2,1)}, bf16[2,2,320,512]{3,2,1,0:T(8,128)(2,1)S(1)}, u32[]{:S(2)}, u32[]{:S(2)}) collective-permute-start(bf16[2,2,320,512]{3,2,1,0:T(8,128)(2,1)} %pad_maximum_fusion.2), channel_id=1, source_target_pairs={{0,16},{8,24},{16,0},{24,8},{1,17},{9,25},{17,1},{25,9},{2,18},{10... | collective-permute-start | bytes 3932168 | tf_op jit(solution)/shard_map/ppermute | solution.py:786
  139.5 31.4 %collective-permute-start.18 = (bf16[2,320,512]{2,1,0:T(8,128)(2,1)S(1)}, bf16[2,320,512]{2,1,0:T(8,128)(2,1)}, u32[]{:S(2)}, u32[]{:S(2)}) collective-permute-start(bf16[2,320,512]{2,1,0:T(8,128)(2,1)S(1)} %copy-done.51), channel_id=1, source_target_pairs={{0,4},{1,5},{2,6},{3,7},{4,0},{5,1},{6,2},{7,3},{8,12},{9,13},{10,... | collective-permute-start | bytes 1966088 | tf_op jit(solution)/shard_map/ppermute | solution.py:799
  155.0 32.1 %collective-permute-start.21 = (bf16[512,1024]{1,0:T(8,128)(2,1)}, bf16[512,1024]{1,0:T(8,128)(2,1)S(1)}, u32[]{:S(2)}, u32[]{:S(2)}) collective-permute-start(bf16[512,1024]{1,0:T(8,128)(2,1)} %get-tuple-element.349.own.refs_0_), channel_id=1, source_target_pairs={{0,8},{8,0},{16,24},{24,16},{1,9},{9,1},{17,25},{25,17},{2,10},{10... | collective-permute-start | bytes 3145736 | tf_op jit(solution)/shard_map/ppermute | solution.py:786
  170.9 16.1 %collective-permute-start.20 = (bf16[2,320,512]{2,1,0:T(8,128)(2,1)}, bf16[2,320,512]{2,1,0:T(8,128)(2,1)S(1)}, u32[]{:S(2)}, u32[]{:S(2)}) collective-permute-start(bf16[2,320,512]{2,1,0:T(8,128)(2,1)} %collective-permute-done.18), channel_id=1, source_target_pairs={{0,16},{8,24},{16,0},{24,8},{1,17},{9,25},{17,1},{25,9},{2,18},{10... | collective-permute-start | bytes 1966088 | tf_op jit(solution)/shard_map/ppermute | solution.py:786
  172.8 18.4 %collective-permute-start.22 = (bf16[4,2,320,512]{3,2,1,0:T(8,128)(2,1)S(1)}, bf16[4,2,320,512]{3,2,1,0:T(8,128)(2,1)S(1)}, u32[]{:S(2)}, u32[]{:S(2)}) collective-permute-start(bf16[4,2,320,512]{3,2,1,0:T(8,128)(2,1)S(1)} %pad_maximum_fusion.refs_0_), channel_id=1, source_target_pairs={{0,1},{1,0},{2,3},{3,2},{4,5},{5,4},{6,7},{7,6},{8,9},{9,8},{10,11... | collective-permute-start | bytes 7864328 | tf_op jit(solution)/shard_map/ppermute | solution.py:795
  189.3 5.1 %collective-permute-start.23 = (bf16[4,2,320,512]{3,2,1,0:T(8,128)(2,1)S(1)}, bf16[4,2,320,512]{3,2,1,0:T(8,128)(2,1)}, u32[]{:S(2)}, u32[]{:S(2)}) collective-permute-start(bf16[4,2,320,512]{3,2,1,0:T(8,128)(2,1)S(1)} %pad_maximum_fusion.1.refs_1_), channel_id=1, source_target_pairs={{0,1},{1,0},{2,3},{3,2},{4,5},{5,4},{6,7},{7,6},{8,9},{9,8},{10,11... | collective-permute-start | bytes 7864328 | tf_op jit(solution)/shard_map/ppermute | solution.py:795
  189.4 26.0 %collective-permute-start.24 = (bf16[512,1024]{1,0:T(8,128)(2,1)S(1)}, bf16[512,1024]{1,0:T(8,128)(2,1)S(1)}, u32[]{:S(2)}, u32[]{:S(2)}) collective-permute-start(bf16[512,1024]{1,0:T(8,128)(2,1)S(1)} %copy-done.28), channel_id=1, source_target_pairs={{0,8},{8,0},{16,24},{24,16},{1,9},{9,1},{17,25},{25,17},{2,10},{10... | collective-permute-start | bytes 3145736 | tf_op jit(solution)/shard_map/ppermute | solution.py:786
  211.0 40.0 %collective-permute-start.25 = (bf16[512,1024]{1,0:T(8,128)(2,1)}, bf16[512,1024]{1,0:T(8,128)(2,1)S(1)}, u32[]{:S(2)}, u32[]{:S(2)}) collective-permute-start(bf16[512,1024]{1,0:T(8,128)(2,1)} %get-tuple-element.371), channel_id=1, source_target_pairs={{0,8},{8,0},{16,24},{24,16},{1,9},{9,1},{17,25},{25,17},{2,10},{10... | collective-permute-start | bytes 3145736 | tf_op jit(solution)/shard_map/ppermute | solution.py:786
  233.4 26.6 %collective-permute-start.26 = (bf16[512,1024]{1,0:T(8,128)(2,1)}, bf16[512,1024]{1,0:T(8,128)(2,1)}, u32[]{:S(2)}, u32[]{:S(2)}) collective-permute-start(bf16[512,1024]{1,0:T(8,128)(2,1)} %get-tuple-element.383), channel_id=1, source_target_pairs={{0,8},{8,0},{16,24},{24,16},{1,9},{9,1},{17,25},{25,17},{2,10},{10... | collective-permute-start | bytes 3145736 | tf_op jit(solution)/shard_map/ppermute | solution.py:786
  260.0 7.9 %collective-permute-start.27 = (bf16[2,4,2,256,512]{4,3,2,1,0:T(8,128)(2,1)}, bf16[2,4,2,256,512]{4,3,2,1,0:T(8,128)(2,1)S(1)}, u32[]{:S(2)}, u32[]{:S(2)}) collective-permute-start(bf16[2,4,2,256,512]{4,3,2,1,0:T(8,128)(2,1)} %get-tuple-element.389), channel_id=1, source_target_pairs={{0,1},{1,0},{2,3},{3,2},{4,5},{5,4},{6,7},{7,6},{8,9},{9,8},{10,11... | collective-permute-start | bytes 12582920 | tf_op jit(solution)/shard_map/ppermute | solution.py:795
  273.1 48.8 %collective-permute-start.30 = (bf16[4,2,256,512]{3,2,1,0:T(8,128)(2,1)}, bf16[4,2,256,512]{3,2,1,0:T(8,128)(2,1)}, u32[]{:S(2)}, u32[]{:S(2)}) collective-permute-start(bf16[4,2,256,512]{3,2,1,0:T(8,128)(2,1)} %fusion), channel_id=1, source_target_pairs={{0,16},{8,24},{16,0},{24,8},{1,17},{9,25},{17,1},{25,9},{2,18},{10... | collective-permute-start | bytes 6291464 | tf_op jit(solution)/shard_map/ppermute | solution.py:786
  273.5 32.9 %collective-permute-start.28 = (bf16[512,1024]{1,0:T(8,128)(2,1)}, bf16[512,1024]{1,0:T(8,128)(2,1)S(1)}, u32[]{:S(2)}, u32[]{:S(2)}) collective-permute-start(bf16[512,1024]{1,0:T(8,128)(2,1)} %get-tuple-element.418), channel_id=1, source_target_pairs={{0,8},{8,0},{16,24},{24,16},{1,9},{9,1},{17,25},{25,17},{2,10},{10... | collective-permute-start | bytes 3145736 | tf_op jit(solution)/shard_map/ppermute | solution.py:786
  290.8 31.1 %collective-permute-start.29 = (bf16[512,1024]{1,0:T(8,128)(2,1)}, bf16[512,1024]{1,0:T(8,128)(2,1)S(1)}, u32[]{:S(2)}, u32[]{:S(2)}) collective-permute-start(bf16[512,1024]{1,0:T(8,128)(2,1)} %get-tuple-element.424), channel_id=1, source_target_pairs={{0,8},{8,0},{16,24},{24,16},{1,9},{9,1},{17,25},{25,17},{2,10},{10... | collective-permute-start | bytes 3145736 | tf_op jit(solution)/shard_map/ppermute | solution.py:786
  321.9 11.6 %collective-permute-start.32 = (bf16[2,4,2,256,512]{4,3,2,1,0:T(8,128)(2,1)}, bf16[2,4,2,256,512]{4,3,2,1,0:T(8,128)(2,1)S(1)}, u32[]{:S(2)}, u32[]{:S(2)}) collective-permute-start(bf16[2,4,2,256,512]{4,3,2,1,0:T(8,128)(2,1)} %get-tuple-element.445), channel_id=1, source_target_pairs={{0,1},{1,0},{2,3},{3,2},{4,5},{5,4},{6,7},{7,6},{8,9},{9,8},{10,11... | collective-permute-start | bytes 12582920 | tf_op jit(solution)/shard_map/ppermute | solution.py:795
  326.9 50.6 %collective-permute-start.33 = (bf16[2,256,512]{2,1,0:T(8,128)(2,1)}, bf16[2,256,512]{2,1,0:T(8,128)(2,1)}, u32[]{:S(2)}, u32[]{:S(2)}) collective-permute-start(bf16[2,256,512]{2,1,0:T(8,128)(2,1)} %get-tuple-element.459), channel_id=1, source_target_pairs={{0,4},{1,5},{2,6},{3,7},{4,0},{5,1},{6,2},{7,3},{8,12},{9,13},{10,... | collective-permute-start | bytes 1572872 | tf_op jit(solution)/shard_map/ppermute | solution.py:799
  326.9 50.6 %collective-permute-start.34 = (bf16[2,256,512]{2,1,0:T(8,128)(2,1)S(1)}, bf16[2,256,512]{2,1,0:T(8,128)(2,1)}, u32[]{:S(2)}, u32[]{:S(2)}) collective-permute-start(bf16[2,256,512]{2,1,0:T(8,128)(2,1)S(1)} %get-tuple-element.460), channel_id=1, source_target_pairs={{0,2},{1,3},{2,4},{3,5},{4,6},{5,7},{6,0},{7,1},{8,10},{9,11},{10,... | collective-permute-start | bytes 1572872 | tf_op jit(solution)/shard_map/ppermute | solution.py:799
  329.7 47.8 %collective-permute-start.35 = (bf16[2,256,512]{2,1,0:T(8,128)(2,1)S(1)}, bf16[2,256,512]{2,1,0:T(8,128)(2,1)}, u32[]{:S(2)}, u32[]{:S(2)}) collective-permute-start(bf16[2,256,512]{2,1,0:T(8,128)(2,1)S(1)} %get-tuple-element.461), channel_id=1, source_target_pairs={{0,6},{1,7},{2,0},{3,1},{4,2},{5,3},{6,4},{7,5},{8,14},{9,15},{10,... | collective-permute-start | bytes 1572872 | tf_op jit(solution)/shard_map/ppermute | solution.py:799
  331.9 26.1 %collective-permute-start.31 = (bf16[1024,512]{1,0:T(8,128)(2,1)S(1)}, bf16[1024,512]{1,0:T(8,128)(2,1)S(1)}, u32[]{:S(2)}, u32[]{:S(2)}) collective-permute-start(bf16[1024,512]{1,0:T(8,128)(2,1)S(1)} %pad_maximum_fusion.5), channel_id=1, source_target_pairs={{0,16},{8,24},{16,0},{24,8},{1,17},{9,25},{17,1},{25,9},{2,18},{10... | collective-permute-start | bytes 3145736 | tf_op jit(solution)/shard_map/ppermute | solution.py:786
  336.2 43.3 %collective-permute-start.36 = (bf16[2,2,256,512]{3,2,1,0:T(8,128)(2,1)}, bf16[2,2,256,512]{3,2,1,0:T(8,128)(2,1)}, u32[]{:S(2)}, u32[]{:S(2)}) collective-permute-start(bf16[2,2,256,512]{3,2,1,0:T(8,128)(2,1)} %get-tuple-element.583), channel_id=1, source_target_pairs={{0,16},{8,24},{16,0},{24,8},{1,17},{9,25},{17,1},{25,9},{2,18},{10... | collective-permute-start | bytes 3145736 | tf_op jit(solution)/shard_map/ppermute | solution.py:786
  342.3 37.2 %copy-start.39 = (bf16[4,2,256,512]{3,2,1,0:T(8,128)(2,1)S(1)}, bf16[4,2,256,512]{3,2,1,0:T(8,128)(2,1)}, u32[]{:S(2)}) copy-start(bf16[4,2,256,512]{3,2,1,0:T(8,128)(2,1)} %get-tuple-element.465) | copy-start | bytes 6291460
  382.3 31.9 %collective-permute-start.39 = (bf16[2,2,256,512]{3,2,1,0:T(8,128)(2,1)S(1)}, bf16[2,2,256,512]{3,2,1,0:T(8,128)(2,1)S(1)}, u32[]{:S(2)}, u32[]{:S(2)}) collective-permute-start(bf16[2,2,256,512]{3,2,1,0:T(8,128)(2,1)S(1)} %copy-done.41), channel_id=1, source_target_pairs={{0,16},{8,24},{16,0},{24,8},{1,17},{9,25},{17,1},{25,9},{2,18},{10... | collective-permute-start | bytes 3145736 | tf_op jit(solution)/shard_map/ppermute | solution.py:786
  383.9 30.2 %collective-permute-start.40 = (bf16[512,768]{1,0:T(8,128)(2,1)}, bf16[512,768]{1,0:T(8,128)(2,1)S(1)}, u32[]{:S(2)}, u32[]{:S(2)}) collective-permute-start(bf16[512,768]{1,0:T(8,128)(2,1)} %select_convert_fusion), channel_id=1, source_target_pairs={{0,8},{8,0},{16,24},{24,16},{1,9},{9,1},{17,25},{25,17},{2,10},{10... | collective-permute-start | bytes 2359304 | tf_op jit(solution)/shard_map/ppermute | solution.py:786
  385.7 28.4 %collective-permute-start.37 = (bf16[2,256,512]{2,1,0:T(8,128)(2,1)}, bf16[2,256,512]{2,1,0:T(8,128)(2,1)S(1)}, u32[]{:S(2)}, u32[]{:S(2)}) collective-permute-start(bf16[2,256,512]{2,1,0:T(8,128)(2,1)} %get-tuple-element.478), channel_id=1, source_target_pairs={{0,4},{1,5},{2,6},{3,7},{4,0},{5,1},{6,2},{7,3},{8,12},{9,13},{10,... | collective-permute-start | bytes 1572872 | tf_op jit(solution)/shard_map/ppermute | solution.py:799
  386.4 27.6 %collective-permute-start.38 = (bf16[2,256,512]{2,1,0:T(8,128)(2,1)}, bf16[2,256,512]{2,1,0:T(8,128)(2,1)S(1)}, u32[]{:S(2)}, u32[]{:S(2)}) collective-permute-start(bf16[2,256,512]{2,1,0:T(8,128)(2,1)} %get-tuple-element.479), channel_id=1, source_target_pairs={{0,6},{1,7},{2,0},{3,1},{4,2},{5,3},{6,4},{7,5},{8,14},{9,15},{10,... | collective-permute-start | bytes 1572872 | tf_op jit(solution)/shard_map/ppermute | solution.py:799
  414.1 26.0 %collective-permute-start.42 = (bf16[512,768]{1,0:T(8,128)(2,1)}, bf16[512,768]{1,0:T(8,128)(2,1)}, u32[]{:S(2)}, u32[]{:S(2)}) collective-permute-start(bf16[512,768]{1,0:T(8,128)(2,1)} %slice.346), channel_id=1, source_target_pairs={{0,16},{8,24},{16,0},{24,8},{1,17},{9,25},{17,1},{25,9},{2,18},{10... | collective-permute-start | bytes 2359304 | tf_op jit(solution)/shard_map/ppermute | solution.py:786
  415.8 24.3 %collective-permute-start.41 = (bf16[2,256,512]{2,1,0:T(8,128)(2,1)}, bf16[2,256,512]{2,1,0:T(8,128)(2,1)}, u32[]{:S(2)}, u32[]{:S(2)}) collective-permute-start(bf16[2,256,512]{2,1,0:T(8,128)(2,1)} %get-tuple-element.493), channel_id=1, source_target_pairs={{0,2},{1,3},{2,4},{3,5},{4,6},{5,7},{6,0},{7,1},{8,10},{9,11},{10,... | collective-permute-start | bytes 1572872 | tf_op jit(solution)/shard_map/ppermute | solution.py:799
  444.2 12.6 %collective-permute-start.43 = (bf16[256,512]{1,0:T(8,128)(2,1)}, bf16[256,512]{1,0:T(8,128)(2,1)S(1)}, u32[]{:S(2)}, u32[]{:S(2)}) collective-permute-start(bf16[256,512]{1,0:T(8,128)(2,1)} %get-tuple-element.512), channel_id=1, source_target_pairs={{0,8},{8,0},{16,24},{24,16},{1,9},{9,1},{17,25},{25,17},{2,10},{10... | collective-permute-start | bytes 786440 | tf_op jit(solution)/shard_map/ppermute | solution.py:786
  444.3 13.6 %collective-permute-start.44 = (bf16[256,512]{1,0:T(8,128)(2,1)}, bf16[256,512]{1,0:T(8,128)(2,1)S(1)}, u32[]{:S(2)}, u32[]{:S(2)}) collective-permute-start(bf16[256,512]{1,0:T(8,128)(2,1)} %get-tuple-element.513), channel_id=1, source_target_pairs={{0,16},{8,24},{16,0},{24,8},{1,17},{9,25},{17,1},{25,9},{2,18},{10... | collective-permute-start | bytes 786440 | tf_op jit(solution)/shard_map/ppermute | solution.py:786
  444.8 13.0 %collective-permute-start.45 = (bf16[256,512]{1,0:T(8,128)(2,1)}, bf16[256,512]{1,0:T(8,128)(2,1)S(1)}, u32[]{:S(2)}, u32[]{:S(2)}) collective-permute-start(bf16[256,512]{1,0:T(8,128)(2,1)} %get-tuple-element.514), channel_id=1, source_target_pairs={{0,24},{8,16},{16,8},{24,0},{1,25},{9,17},{17,9},{25,1},{2,26},{10... | collective-permute-start | bytes 786440 | tf_op jit(solution)/shard_map/ppermute | solution.py:786
  447.9 2.5 collective-permute-start.46
  450.0 7.8 %collective-permute-start.48 = (bf16[4,64,768]{2,1,0:T(8,128)(2,1)S(1)}, bf16[4,64,768]{2,1,0:T(8,128)(2,1)S(1)}, u32[]{:S(2)}, u32[]{:S(2)}) collective-permute-start(bf16[4,64,768]{2,1,0:T(8,128)(2,1)S(1)} %fusion.11), channel_id=1, source_target_pairs={{0,1},{1,0},{2,3},{3,2},{4,5},{5,4},{6,7},{7,6},{8,9},{9,8},{10,11... | collective-permute-start | bytes 1179656 | tf_op jit(solution)/shard_map/ppermute | solution.py:795
  450.4 6.3 %collective-permute-start.47 = (bf16[640,128]{0,1:T(8,128)(2,1)S(1)}, bf16[640,128]{0,1:T(8,128)(2,1)S(1)}, u32[]{:S(2)}, u32[]{:S(2)}) collective-permute-start(bf16[640,128]{0,1:T(8,128)(2,1)S(1)} %get-tuple-element.573), channel_id=1, source_target_pairs={{0,2},{1,3},{2,0},{3,1},{4,6},{5,7},{6,4},{7,5},{8,10},{9,11},{10,... | collective-permute-start | bytes 491528 | tf_op jit(solution)/shard_map/ppermute | solution.py:896
  457.9 15.0 %collective-permute-start.49 = (bf16[640,128]{0,1:T(8,128)(2,1)S(1)}, bf16[640,128]{0,1:T(8,128)(2,1)S(1)}, u32[]{:S(2)}, u32[]{:S(2)}) collective-permute-start(bf16[640,128]{0,1:T(8,128)(2,1)S(1)} %convert_element_type.496), channel_id=1, source_target_pairs={{0,4},{1,5},{2,6},{3,7},{4,0},{5,1},{6,2},{7,3},{8,12},{9,13},{10,... | collective-permute-start | bytes 491528 | tf_op jit(solution)/shard_map/ppermute | solution.py:896
  458.1 17.2 %collective-permute-start.51 = (bf16[256,512]{1,0:T(8,128)(2,1)S(1)}, bf16[256,512]{1,0:T(8,128)(2,1)S(1)}, u32[]{:S(2)}, u32[]{:S(2)}) collective-permute-start(bf16[256,512]{1,0:T(8,128)(2,1)S(1)} %copy-done.93), channel_id=1, source_target_pairs={{0,8},{8,0},{16,24},{24,16},{1,9},{9,1},{17,25},{25,17},{2,10},{10... | collective-permute-start | bytes 786440 | tf_op jit(solution)/shard_map/ppermute | solution.py:786
  459.7 15.5 %collective-permute-start.52 = (bf16[256,512]{1,0:T(8,128)(2,1)S(1)}, bf16[256,512]{1,0:T(8,128)(2,1)S(1)}, u32[]{:S(2)}, u32[]{:S(2)}) collective-permute-start(bf16[256,512]{1,0:T(8,128)(2,1)S(1)} %copy-done.92), channel_id=1, source_target_pairs={{0,16},{8,24},{16,0},{24,8},{1,17},{9,25},{17,1},{25,9},{2,18},{10... | collective-permute-start | bytes 786440 | tf_op jit(solution)/shard_map/ppermute | solution.py:786
  460.1 15.2 %collective-permute-start.53 = (bf16[256,512]{1,0:T(8,128)(2,1)S(1)}, bf16[256,512]{1,0:T(8,128)(2,1)S(1)}, u32[]{:S(2)}, u32[]{:S(2)}) collective-permute-start(bf16[256,512]{1,0:T(8,128)(2,1)S(1)} %copy-done.91), channel_id=1, source_target_pairs={{0,24},{8,16},{16,8},{24,0},{1,25},{9,17},{17,9},{25,1},{2,26},{10... | collective-permute-start | bytes 786440 | tf_op jit(solution)/shard_map/ppermute | solution.py:786
  461.7 13.5 %collective-permute-start.50 = (bf16[2,64,768]{2,1,0:T(8,128)(2,1)S(1)}, bf16[2,64,768]{2,1,0:T(8,128)(2,1)S(1)}, u32[]{:S(2)}, u32[]{:S(2)}) collective-permute-start(bf16[2,64,768]{2,1,0:T(8,128)(2,1)S(1)} %fusion.23), channel_id=1, source_target_pairs={{0,4},{1,5},{2,6},{3,7},{4,0},{5,1},{6,2},{7,3},{8,12},{9,13},{10,... | collective-permute-start | bytes 589832 | tf_op jit(solution)/shard_map/ppermute | solution.py:896
  475.3 13.9 %collective-permute-start.56 = (f32[128,128]{0,1:T(8,128)S(1)}, f32[128,128]{0,1:T(8,128)S(1)}, u32[]{:S(2)}, u32[]{:S(2)}) collective-permute-start(f32[128,128]{0,1:T(8,128)S(1)} %slice.278), channel_id=1, source_target_pairs={{0,24},{8,16},{16,8},{24,0},{1,25},{9,17},{17,9},{25,1},{2,26},{10... | collective-permute-start | bytes 196616 | tf_op jit(solution)/shard_map/ppermute | solution.py:786
  476.9 12.3 %collective-permute-start.55 = (f32[128,128]{0,1:T(8,128)S(1)}, f32[128,128]{0,1:T(8,128)S(1)}, u32[]{:S(2)}, u32[]{:S(2)}) collective-permute-start(f32[128,128]{0,1:T(8,128)S(1)} %slice.278), channel_id=1, source_target_pairs={{0,16},{8,24},{16,0},{24,8},{1,17},{9,25},{17,1},{25,9},{2,18},{10... | collective-permute-start | bytes 196616 | tf_op jit(solution)/shard_map/ppermute | solution.py:786
  477.9 11.3 %collective-permute-start.54 = (f32[128,128]{0,1:T(8,128)S(1)}, f32[128,128]{0,1:T(8,128)S(1)}, u32[]{:S(2)}, u32[]{:S(2)}) collective-permute-start(f32[128,128]{0,1:T(8,128)S(1)} %slice.278), channel_id=1, source_target_pairs={{0,8},{8,0},{16,24},{24,16},{1,9},{9,1},{17,25},{25,17},{2,10},{10... | collective-permute-start | bytes 196616 | tf_op jit(solution)/shard_map/ppermute | solution.py:786
  479.0 10.3 %collective-permute-start.57 = (bf16[1,64,768]{2,1,0:T(8,128)(2,1)S(1)}, bf16[1,64,768]{2,1,0:T(8,128)(2,1)S(1)}, u32[]{:S(2)}, u32[]{:S(2)}) collective-permute-start(bf16[1,64,768]{2,1,0:T(8,128)(2,1)S(1)} %dynamic-slice_convert_fusion.6), channel_id=1, source_target_pairs={{0,2},{1,3},{2,0},{3,1},{4,6},{5,7},{6,4},{7,5},{8,10},{9,11},{10,... | collective-permute-start | bytes 294920 | tf_op jit(solution)/shard_map/ppermute | solution.py:896
  (89 other events, 640.2 us)

commit v5 on v4

--- a/solution.py
+++ b/solution.py
@@ -344,6 +344,16 @@
     return widths
 
 
+def packing(height, under, cols):
+    rest, half = height - under, cols // 2
+    return [
+        (0, 0, under, 0, 0, 0, cols),
+        (1, 0, rest, 0, under, 0, cols),
+        (1, rest, height // 2, 0, 0, cols, half),
+        (1, rest, height // 2, half, height // 2, cols, half),
+    ]
+
+
 def load_pieces(table_ref, pieces, rows, dest, sems, half=None, proj=None):
     cols = pieces[0].shape[3]
     depth = dest.shape[1]
@@ -365,12 +375,12 @@
                 else:
                     pl.when((row >= 0) & (row < depth))(go)
                 if proj is not None:
-                    under = ref.shape[2] - rows
-                    part = proj[0].shape[1] // 2
-                    to = pl.ds(pl.multiple_of(table_ref[2, at], under), under)
-                    for side in range(2):
-                        source = ref.at[j, side, rows:, :part]
-                        act(pltpu.make_async_copy(source, proj[0].at[to, side * part : (side + 1) * part], proj[1].at[2 * at + side]))
+                    under, height = ref.shape[2] - rows, proj[2]
+                    first = pl.multiple_of(table_ref[2, at], height)
+                    for n, (side, begin, count, left, row, out_left, wide) in enumerate(packing(height, under, cols)):
+                        source = ref.at[j, side, rows + begin : rows + begin + count, left : left + wide]
+                        to = proj[0].at[pl.ds(first + row, count), out_left : out_left + wide]
+                        act(pltpu.make_async_copy(source, to, proj[1].at[4 * at + n]))
                 at += 1
 
     each(lambda copy: copy.start())
@@ -441,7 +451,7 @@
     if packed:
         pieces, refs = refs[:n_pieces], refs[n_pieces:]
         low_ref, d_first_ref, d_gate_ref, up_ref, leaving_ref, vectors_ref, sums_ref, weight, sems, proj, proj_sems = refs
-        proj_rows = (proj, proj_sems)
+        proj_rows = (proj, proj_sems, proj.shape[0] // table_ref.shape[1])
     else:
         proj, pieces, refs = refs[0], refs[1 : n_pieces + 1], refs[n_pieces + 1 :]
         low_ref, d_first_ref, d_gate_ref, up_ref, leaving_ref, vectors_ref, sums_ref, weight, sems = refs
@@ -579,7 +589,7 @@
     packed = proj is None
     scratch = [pltpu.VMEM((2, 2 * half, half), BF16), pltpu.SemaphoreType.DMA((count_of(pieces),))]
     if packed:
-        scratch += [pltpu.VMEM((half, out_width), BF16), pltpu.SemaphoreType.DMA((2 * count_of(pieces),))]
+        scratch += [pltpu.VMEM((half, out_width), BF16), pltpu.SemaphoreType.DMA((4 * count_of(pieces),))]
     return pl.pallas_call(
         functools.partial(turn_kernel, len(pieces), block_rows, width, packed),
         grid=(words // rows,),
@@ -712,16 +722,16 @@
             def _(ref=ref, unit=unit):
                 outs[unit // 2][unit % 2, :rows, :] = ref[slot_of(owner_ref, unit)]
 
-    under, part = proj.shape[0], proj.shape[1] // 2
-    if outs[1].shape[1] > rows:
-        outs[1][:, rows:, :] = jnp.zeros((2, under, width), BF16)
-        for side in range(2):
-            outs[1][side, rows:, :part] = proj[:, side * part : (side + 1) * part].astype(BF16)
+    under = outs[1].shape[1] - rows
+    if under:
+        for side, begin, count, left, row, out_left, wide in packing(proj.shape[0], under, width):
+            value = proj[row : row + count, out_left : out_left + wide].astype(BF16)
+            outs[1][side, rows + begin : rows + begin + count, left : left + wide] = value
 
 
 def choose_units(owners, arrived, proj, packed):
     slots, rows, width = arrived[0].shape
-    shapes = [(2, rows, width), (2, rows + (proj.shape[0] if packed else 0), width)]
+    shapes = [(2, rows, width), (2, rows + (proj.size // (2 * width) if packed else 0), width)]
     return pl.pallas_call(
         functools.partial(choose_kernel, len(arrived)),
         grid=(1,),
@@ -847,9 +857,12 @@
     return jnp.stack([jnp.stack(at_rows), jnp.stack(at_cols), jnp.stack(at_proj)]).astype(jnp.int32)
 
 
+Z_SEQUENCE = (1, 3, 2, 0)
+
+
 def sum_table(place, rows, width):
     z = jnp.arange(place.n_z, dtype=jnp.int32)
-    z, c = ((place.z + z) % place.n_z, place.c) if place.direct else (z, 0)
+    z, c = ((place.z + jnp.asarray(Z_SEQUENCE, jnp.int32)) % place.n_z, place.c) if place.direct else (z, 0)
     return jnp.stack([place.row_of(z * 2 + c, rows, width), place.row_of(z * 2 + (1 - c), rows, width)]).astype(jnp.int32)
 
 
@@ -1078,7 +1091,7 @@
     sums_zero = sums[0] + sums[1]
     blocks = highway_weight_grad(targets, [own + mate], d_first, d_gate, rows, width)
     blocks, up, arrived_zero[0] = settle(blocks, up, arrived_zero[0])
-    groups = [slice(2, 4), slice(0, 2)]
+    groups = [slice(0, 2), slice(2, 4)]
     if not direct:
         sum_zero = sum_general(place, blocks)
     partial = [highway_back(*gathered[0], d_first[chunk], d_gate[chunk], up[chunk]) for chunk in chunks]
@@ -1087,11 +1100,11 @@
         zero = (blocks[:2], over_core(blocks[2]))
     if direct:
         one_here = kept_over_y(one, one_y, slice(0, place.n_z))
-        one_sent = [one_here[k].astype(BF16) for k in (2, 1, 3)]
-        one_here = one_here[0]
+        one_sent = [one_here[n].astype(BF16) for n in (2, 0, 1)]
+        one_here = one_here[3]
         one_sent, one_here, partial = settle(one_sent, one_here, partial)
         one_z = [over_z(value, k) for value, k in zip(one_sent, (2, 1, 3))]
-    groups = [slice(2, 4), slice(0, 2)]
+    groups = [slice(0, 2), slice(2, 4)]
     if not direct:
         sum_zero = sum_general(place, blocks)
     partial = [highway_back(*gathered[0], d_first[chunk], d_gate[chunk], up[chunk]) for chunk in chunks]
@@ -1106,7 +1119,7 @@
                 [(partial[chunk][:, cols] + arrived_zero[chunk][:, cols].astype(F32)).astype(BF16) for chunk in chunks]
             )
         )
-    groups = [slice(2, 4), slice(0, 2)]
+    groups = [slice(0, 2), slice(2, 4)]
     returned = [over_y(value, step) if step else value for step, value in enumerate(feature_grad)]
     if direct:
         returned[0], x_two_low, vectors = settle(returned[0], x_two_low, vectors)
@@ -1155,51 +1168,49 @@
             )
             zero_here = kept_over_y(zero, zero_y[0], groups[0])
             zero_z, zero_sent, narrow = settle([value.astype(BF16) for value in zero_here], zero_sent, narrow)
-            zero_z = [over_z(value, k) for value, k in zip(zero_z, (2, 3))]
+            zero_z = [over_z(value, k) for value, k in zip(zero_z, (1, 3))]
             zero_y.append(over_y(zero_sent, 1))
+        if direct and n == 2:
+            back, zero_z, narrow, zero_y, vectors_away, proj_away = settle(back, zero_z, narrow, zero_y, vectors_away, proj_away)
             vectors_arrived = over_x(vectors_away)
-        if direct and n == 2:
-            back, zero_z, narrow, zero_y, vectors_arrived, proj_away = settle(back, zero_z, narrow, zero_y, vectors_arrived, proj_away)
-            zero_here, last = kept_over_y(zero, zero_y[1], groups[1])
+            last, zero_here = kept_over_y(zero, zero_y[1], groups[1])
             last, zero_here, narrow = settle(last.astype(BF16), zero_here, narrow)
-            last = over_z(last, 1)
+            last = over_z(last, 2)
             proj_y = over_y(proj_away[0], 1)
     if direct:
-        back, last, proj_y = settle(back, last, proj_y)
+        small = back + over_core(back)
+        last, proj_y, small = settle(last, proj_y, small)
+        small = small + swap_z(place, small.astype(BF16), 1).astype(F32)
         slot_grads = return_units(highway_owner, [[zero_here] + zero_z + [last], [one_here] + one_z], n_filt)
     else:
         proj_y = [over_y(value, step) for value, step in zip(proj_away, steps_y)]
         proj_grad = lax.psum_scatter(proj_here + sum(value.astype(F32) for value in proj_y), "dp", scatter_dimension=0, tiled=True)
     if not direct:
         vectors_arrived = over_x(vectors_away)
-    small = back
-    if direct:
-        small = small + over_core(small)
-    else:
-        small = lax.psum(small, "dp")
+    if not direct:
+        small = lax.psum(back, "dp")
         small = jnp.concatenate([small[:width], sum_filt(place, small[width:])])
 
     optimizer = (highway_weight, highway_moment_one, highway_moment_two, highway_average)
     columns = (place.f ^ jnp.arange(n_filt, dtype=jnp.int32)) * width
     if direct:
-        slot_grads, proj_y, vectors_arrived = settle(slot_grads, proj_y, vectors_arrived)
+        slot_grads, proj_y, vectors_arrived, small = settle(slot_grads, proj_y, vectors_arrived, small)
         proj_rows = rows_over_core(place, proj_here + proj_y.astype(F32))
         by_slot = [slot_grads[slot::SLOTS] for slot in range(SLOTS)]
         to_owner = lambda grads: [grads[0]] + [place.over_filt(grads[step], step) for step in range(1, n_filt)]
         by_slot[0] = to_owner(by_slot[0])
-        small = small + swap_z(place, small.astype(BF16), 1).astype(F32)
+        small = small + swap_z(place, small.astype(BF16), 2).astype(F32)
         by_slot, small, proj_rows = settle(by_slot, small, proj_rows)
         by_slot[1] = to_owner(by_slot[1])
-        small = small + swap_z(place, small.astype(BF16), 2).astype(F32)
+        conv_sums, small = small[:width], small[width:]
+        small = small + over_x(small)
         proj_rows = swap_rows(place, proj_rows[0] + proj_rows[1].astype(F32), 2)
         updates = owner_update(0, columns, by_slot[0], *optimizer)
         updates, small, proj_rows, by_slot[1] = settle(updates, small, proj_rows, by_slot[1])
-        conv_sums, small = small[:width], small[width:]
-        others = [place.over_filt(small, step) for step in range(1, n_filt)]
+        small = small + over_y(small, 1)
         proj_rows = swap_rows(place, proj_rows[0] + proj_rows[1].astype(F32), 1)
         updates = owner_update(1, columns, by_slot[1], *optimizer, updates)
-        updates, others, proj_rows = settle(updates, others, proj_rows)
-        small = (small + others[0]) + (others[1] + others[2])
+        updates, small, proj_rows = settle(updates, small, proj_rows)
         proj_grad = (proj_rows[0] + proj_rows[1].astype(F32)).reshape(rows_proj, out_width)
     else:
         slot_grads = return_units(highway_owner, [[sum_zero], [sum_one]], n_filt)

time: 499 us -> 496 us (level)
  waiting for transfers between devices: 91 us -> 103 us
  starting transfers between devices: 68 us -> 57.2 us
    ppermute x12, waiting for transfers between devices: 43.7 us -> 52 us  [over_z(): return lax.ppermute(value, 'dp', pairs)]
    ppermute x12, starting transfers between devices: 22.5 us -> 15.2 us  [over_z(): return lax.ppermute(value, 'dp', pairs)]
    ppermute x33 -> x32, waiting for transfers between devices: 38 us -> 43.9 us  [over_filt(): lax.ppermute(value, 'filt', [(i, i ^ step) for i in range(self.n_filt)])]
    ppermute x33 -> x32, starting transfers between devices: 39.8 us -> 37.5 us  [over_filt(): lax.ppermute(value, 'filt', [(i, i ^ step) for i in range(self.n_filt)])]
  transfers between devices with their start and end apart: 58 -> 57, of which waited for: 16 -> 20; matrix products, arithmetic and copies ran while one was open for 8% -> 8% of each run, Pallas kernels for 53% -> 54%
where the time goes in v5:
time: 496 us; the launch traced here: 490 us
  Pallas kernels  266 us (54%)
  waiting for transfers between devices  103 us (21%)
  starting transfers between devices  57.2 us (12%)
  other arithmetic  40.8 us (8%)
  local copies, waits for them, and re-layouts  16.8 us (3%)
    pallas_call x4, Pallas kernels, conv_backward(): pl.pallas_call(functools.partial(conv_backward_kernel, cblock, len(ranks)...  59.3 us
    ppermute x12, waiting for transfers between devices, over_z(): return lax.ppermute(value, 'dp', pairs)  52 us
    ppermute x32, waiting for transfers between devices, over_filt(): lax.ppermute(value, 'filt', [(i, i ^ step) for i in range(self.n_filt)])  43.9 us
    pallas_call x4, Pallas kernels, conv_forward(): pl.pallas_call(functools.partial(conv_forward_kernel, cblock, base), grid...  42.5 us
    ppermute x32, starting transfers between devices, over_filt(): lax.ppermute(value, 'filt', [(i, i ^ step) for i in range(self.n_filt)])  37.5 us
    pallas_call x2, Pallas kernels, highway_turn(): pl.pallas_call(functools.partial(turn_kernel, len(pieces), block_rows, wi...  34.3 us
    pallas_call x4, Pallas kernels, highway_back(): pl.pallas_call(functools.partial(back_kernel, len(pieces), block_rows), g...  30.8 us
    pallas_call x2, Pallas kernels, highway_weight_grad(): pl.pallas_call(functools.partial(weight_grad_kernel, len(xs), len(xs[0]),...  30.3 us
  transfers between devices with their start and end apart: 57, of which 20 were waited for; matrix products, arithmetic and copies ran while one was open for 8% of the time, Pallas kernels for 54%

profile of v5, /device:TPU:0, one launch (start us, length us, event | category | flops | bytes accessed | tf_op | source)
XLA Modules:
  0.0 489.6 jit_solution(13556017202818311247)
XLA Ops:
  0.7 3.7 dynamic-slice_convert_fusion
  4.4 3.9 collective-permute-start.2
  9.3 1.8 convert_reduce_fusion
  12.5 7.8 %conv_forward.5 = (bf16[512,256]{1,0:T(8,128)(2,1)S(1)}, f32[512,256]{1,0:T(8,128)}, f32[64,256]{1,0:T(8,128)}, bf16[1024,256]{1,0:T(8,128)(2,1)}) custom-call(s32[2]{0:T(128)S(1)} %slice.229.narrow_ref, s32[2048,1]{1,0:T(8,128)S(1)} %copy.98.rank_ref, bf16[64,2048]{1,0:T(8,128)(2,1)S(1)} %fusion.12.data_ref, f32[16,384]{1,0:T(8,128)S(1)} %pad.19.table_ref, ...), custom_call_target="tpu_custom_call" | custom-call | flops 110000000 | bytes 330000 | tf_op jit(solution)/shard_map/conv_forward/pallas_call | solution.py:160
  20.3 12.7 %conv_forward.4 = (bf16[512,256]{1,0:T(8,128)(2,1)S(1)}, f32[512,256]{1,0:T(8,128)}, f32[64,256]{1,0:T(8,128)}, bf16[1024,256]{1,0:T(8,128)(2,1)}) custom-call(s32[2]{0:T(128)S(1)} %slice.229.narrow_ref, s32[2048,1]{1,0:T(8,128)S(1)} %copy.98.rank_ref, bf16[64,2048]{1,0:T(8,128)(2,1)S(1)} %fusion.12.data_ref, f32[16,384]{1,0:T(8,128)S(1)} %pad.19.table_ref, ...), custom_call_target="tpu_custom_call" | custom-call | flops 110000000 | bytes 330000 | tf_op jit(solution)/shard_map/conv_forward/pallas_call | solution.py:160
  35.4 2.8 choose_units.1
  41.4 3.6 collective-permute-start.4
  45.6 10.6 %conv_forward.6 = (bf16[512,512]{1,0:T(8,128)(2,1)S(1)}, f32[512,512]{1,0:T(8,128)}, f32[64,512]{1,0:T(8,128)}, bf16[1024,512]{1,0:T(8,128)(2,1)}) custom-call(s32[2]{0:T(128)S(1)} %slice.229.narrow_ref, s32[2048,1]{1,0:T(8,128)S(1)} %copy.98.rank_ref, bf16[64,2048]{1,0:T(8,128)(2,1)S(1)} %fusion.12.data_ref, f32[16,384]{1,0:T(8,128)S(1)} %pad.19.table_ref, ...), custom_call_target="tpu_custom_call" | custom-call | flops 110000000 | bytes 330000 | tf_op jit(solution)/shard_map/conv_forward/pallas_call | solution.py:160
  56.3 11.4 %conv_forward.7 = (bf16[512,1024]{1,0:T(8,128)(2,1)S(1)}, f32[512,1024]{1,0:T(8,128)}, f32[64,1024]{1,0:T(8,128)}, bf16[1024,1024]{1,0:T(8,128)(2,1)}) custom-call(s32[2]{0:T(128)S(1)} %slice.229.narrow_ref, s32[2048,1]{1,0:T(8,128)S(1)} %copy.98.rank_ref, bf16[64,2048]{1,0:T(8,128)(2,1)S(1)} %fusion.12.data_ref, f32[16,384]{1,0:T(8,128)S(1)} %pad.19.table_ref, ...), custom_call_target="tpu_custom_call" | custom-call | flops 110000000 | bytes 330000 | tf_op jit(solution)/shard_map/conv_forward/pallas_call | solution.py:160
  67.6 3.0 place_words.3
  70.6 3.0 place_words.2.refs_0_
  76.0 22.2 %collective-permute-done.10 = bf16[2,256,512]{2,1,0:T(8,128)(2,1)S(1)} collective-permute-done((bf16[2,256,512]{2,1,0:T(8,128)(2,1)S(1)}, bf16[2,256,512]{2,1,0:T(8,128)(2,1)S(1)}, u32[]{:S(2)}, u32[]{:S(2)}) %collective-permute-start.10) | collective-permute-done | bytes 524320 | tf_op jit(solution)/shard_map/ppermute | solution.py:809
  99.2 1.6 collective-permute-start.11
  100.8 1.7 collective-permute-start.13
  103.0 2.3 collective-permute-start.15
  106.1 1.9 convert_reduce_fusion.1
  109.3 3.0 broadcast_select_fusion
  112.3 7.7 %collective-permute-done.15 = bf16[2,304,512]{2,1,0:T(8,128)(2,1)S(1)} collective-permute-done((bf16[2,304,512]{2,1,0:T(8,128)(2,1)}, bf16[2,304,512]{2,1,0:T(8,128)(2,1)S(1)}, u32[]{:S(2)}, u32[]{:S(2)}) %collective-permute-start.15) | collective-permute-done | bytes 622624 | tf_op jit(solution)/shard_map/ppermute | solution.py:809
  120.0 12.9 %collective-permute-done.14 = bf16[2,304,512]{2,1,0:T(8,128)(2,1)S(1)} collective-permute-done((bf16[2,304,512]{2,1,0:T(8,128)(2,1)}, bf16[2,304,512]{2,1,0:T(8,128)(2,1)S(1)}, u32[]{:S(2)}, u32[]{:S(2)}) %collective-permute-start.14) | collective-permute-done | bytes 622624 | tf_op jit(solution)/shard_map/ppermute | solution.py:809
  133.0 3.2 collective-permute-done.11.refs_6_.refs_2_
  142.8 12.1 %highway_forward.2 = (f32[512,1024]{1,0:T(8,128)}, bf16[512,1024]{1,0:T(8,128)(2,1)}, bf16[512,1024]{1,0:T(8,128)(2,1)}, bf16[512,1024]{1,0:T(8,128)(2,1)}, bf16[512,1024]{1,0:T(8,128)(2,1)}) custom-call(s32[3,16]{1,0:T(4,128)} %get-tuple-element.331.table_ref, f32[2,1024]{1,0:T(2,128)} %pad_maximum_fusion.6.bias_ref, bf16[1024,512]{1,0:T(8,128)(2,1)} %copy-done, ...), custom_call_target="tpu_custom_call" | custom-call | flops 100000000 | bytes 300000 | tf_op jit(solution)/shard_map/highway_forward/pallas_call | solution.py:571
  154.9 1.7 collective-permute-start.21
  156.6 12.0 %highway_forward.3 = (f32[512,1024]{1,0:T(8,128)}, bf16[512,1024]{1,0:T(8,128)(2,1)}, bf16[512,1024]{1,0:T(8,128)(2,1)}, bf16[512,1024]{1,0:T(8,128)(2,1)}, bf16[512,1024]{1,0:T(8,128)(2,1)}) custom-call(s32[3,16]{1,0:T(4,128)} %get-tuple-element.331.table_ref, f32[2,1024]{1,0:T(2,128)} %pad_maximum_fusion.6.bias_ref, bf16[1024,512]{1,0:T(8,128)(2,1)} %copy-done, ...), custom_call_target="tpu_custom_call" | custom-call | flops 100000000 | bytes 300000 | tf_op jit(solution)/shard_map/highway_forward/pallas_call | solution.py:571
  172.1 12.9 %collective-permute-done.20 = bf16[2,304,512]{2,1,0:T(8,128)(2,1)S(1)} collective-permute-done((bf16[2,304,512]{2,1,0:T(8,128)(2,1)}, bf16[2,304,512]{2,1,0:T(8,128)(2,1)S(1)}, u32[]{:S(2)}, u32[]{:S(2)}) %collective-permute-start.20) | collective-permute-done | bytes 622624 | tf_op jit(solution)/shard_map/ppermute | solution.py:796
  185.0 2.2 pad_maximum_fusion.1.refs_1_
  187.3 2.2 collective-permute-start.24
  192.2 16.9 %highway_turn.2 = (bf16[512,1024]{1,0:T(8,128)(2,1)}, bf16[512,1024]{1,0:T(8,128)(2,1)}, bf16[512,1024]{1,0:T(8,128)(2,1)}, f32[512,1024]{1,0:T(8,128)}, bf16[51...) custom-call(s32[3,16]{1,0:T(4,128)} %get-tuple-element.332.table_ref, ...), custom_call_target="tpu_custom_call" | custom-call | flops 160000000 | bytes 480000 | tf_op jit(solution)/shard_map/highway_turn/pallas_call | solution.py:593
  209.1 2.2 collective-permute-start.25
  211.3 2.2 collective-permute-done.24.mate.refs_3_
  214.5 17.4 %highway_turn.3 = (bf16[512,1024]{1,0:T(8,128)(2,1)}, bf16[512,1024]{1,0:T(8,128)(2,1)}, bf16[512,1024]{1,0:T(8,128)(2,1)}, f32[512,1024]{1,0:T(8,128)}, bf16[51...) custom-call(s32[3,16]{1,0:T(4,128)} %get-tuple-element.332.table_ref, ...), custom_call_target="tpu_custom_call" | custom-call | flops 160000000 | bytes 480000 | tf_op jit(solution)/shard_map/highway_turn/pallas_call | solution.py:593
  231.9 2.0 collective-permute-start.26
  234.5 15.2 %highway_weight_grad.2 = (bf16[4,2,256,512]{3,2,1,0:T(8,128)(2,1)}, bf16[4,2,256,512]{3,2,1,0:T(8,128)(2,1)}, bf16[2,4,2,256,512]{4,3,2,1,0:T(8,128)(2,1)}) custom-call(s32[2,4]{1,0:T(2,128)} %pad_add_fusion.2.table_ref, bf16[512,1024]{1,0:T(8,128)(2,1)} %get-tuple-element.348.own.refs_0_, bf16[512,1024]{1,0:T(8,128)(2,1)} %copy-done.26, ...), custom_call_target="tpu_custom_call" | custom-call | flops 150000000 | bytes 450000 | tf_op jit(solution)/shard_map/highway_weight_grad/pallas_call | solution.py:650
  249.7 7.9 %highway_back.4.partial = f32[512,1024]{1,0:T(8,128)} custom-call(s32[3,16]{1,0:T(4,128)} %get-tuple-element.332.table_ref, bf16[512,1024]{1,0:T(8,128)(2,1)} %get-tuple-element.365.refs_4_.d_first, bf16[512,1024]{1,0:T(8,128)(2,1)} %get-tuple-element.366.refs_6_.d_gate, f32[512,1024]{1,0:T(8,128)} %get-tuple-element.381.up, ...), custom_call_target="tpu_custom_call" | custom-call | flops 60000000 | bytes 180000 | tf_op jit(solution)/shard_map/highway_back/pallas_call | solution.py:630
  258.3 7.9 %highway_slopes.2 = (bf16[512,1024]{1,0:T(8,128)(2,1)}, bf16[512,1024]{1,0:T(8,128)(2,1)}, f32[512,1024]{1,0:T(8,128)}, bf16[512,1024]{1,0:T(8,128)(2,1)}, f32[2,1024]{1,0:T(2,128)}) custom-call(s32[3,16]{1,0:T(4,128)} %get-tuple-element.331.table_ref, f32[512,1024]{1,0:T(8,128)} %highway_back.4.partial, bf16[512,1024]{1,0:T(8,128)(2,1)} %copy-done.33, ...), custom_call_target="tpu_custom_call" | custom-call | flops 80000000 | bytes 240000 | tf_op jit(solution)/shard_map/highway_slopes/pallas_call | solution.py:613
  266.2 3.6 fusion
  271.9 7.7 %highway_back.5.partial = f32[512,1024]{1,0:T(8,128)} custom-call(s32[3,16]{1,0:T(4,128)} %get-tuple-element.332.table_ref, bf16[512,1024]{1,0:T(8,128)(2,1)} %get-tuple-element.376.refs_5_.d_first, bf16[512,1024]{1,0:T(8,128)(2,1)} %get-tuple-element.377.refs_7_.d_gate, f32[512,1024]{1,0:T(8,128)} %get-tuple-element.405.up, ...), custom_call_target="tpu_custom_call" | custom-call | flops 60000000 | bytes 180000 | tf_op jit(solution)/shard_map/highway_back/pallas_call | solution.py:630
  279.6 7.9 %highway_slopes.3 = (bf16[512,1024]{1,0:T(8,128)(2,1)}, bf16[512,1024]{1,0:T(8,128)(2,1)}, f32[512,1024]{1,0:T(8,128)}, bf16[512,1024]{1,0:T(8,128)(2,1)}, f32[2,1024]{1,0:T(2,128)}) custom-call(s32[3,16]{1,0:T(4,128)} %get-tuple-element.331.table_ref, f32[512,1024]{1,0:T(8,128)} %highway_back.5.partial, bf16[512,1024]{1,0:T(8,128)(2,1)} %collective-permute-done.26.arrived, ...), custom_call_target="tpu_custom_call" | custom-call | flops 80000000 | bytes 240000 | tf_op jit(solution)/shard_map/highway_slopes/pallas_call | solution.py:613
  288.8 15.2 %highway_weight_grad.3 = (bf16[4,2,256,512]{3,2,1,0:T(8,128)(2,1)}, bf16[4,2,256,512]{3,2,1,0:T(8,128)(2,1)}, bf16[2,4,2,256,512]{4,3,2,1,0:T(8,128)(2,1)}) custom-call(s32[2,4]{1,0:T(2,128)} %pad_add_fusion.2.table_ref, bf16[1024,512]{1,0:T(8,128)(2,1)} %copy-done, bf16[1024,512]{1,0:T(8,128)(2,1)} %collective-permute-done.8.refs_1_, ...), custom_call_target="tpu_custom_call" | custom-call | flops 150000000 | bytes 450000 | tf_op jit(solution)/shard_map/highway_weight_grad/pallas_call | solution.py:650
  304.0 7.5 %highway_back.6 = f32[512,1024]{1,0:T(8,128)} custom-call(s32[3,16]{1,0:T(4,128)} %get-tuple-element.331.table_ref, bf16[512,1024]{1,0:T(8,128)(2,1)} %get-tuple-element.400.refs_4_.d_first, bf16[512,1024]{1,0:T(8,128)(2,1)} %get-tuple-element.401.refs_6_.d_gate, f32[512,1024]{1,0:T(8,128)} %get-tuple-element.418.up, bf16[2,2,256,512]{3,2,1,0:T(8,128)(2,1)} %copy-done.13, ...), custom_call_target="tpu_custom_call" | custom-call | flops 60000000 | bytes 180000 | tf_op jit(solution)/shard_map/highway_back/pallas_call | solution.py:630
  311.6 7.6 %highway_back.7 = f32[512,1024]{1,0:T(8,128)} custom-call(s32[3,16]{1,0:T(4,128)} %get-tuple-element.331.table_ref, bf16[512,1024]{1,0:T(8,128)(2,1)} %get-tuple-element.410.refs_5_.d_first, bf16[512,1024]{1,0:T(8,128)(2,1)} %get-tuple-element.411.refs_7_.d_gate, f32[512,1024]{1,0:T(8,128)} %get-tuple-element.419.up, bf16[2,2,256,512]{3,2,1,0:T(8,128)(2,1)} %copy-done.13, ...), custom_call_target="tpu_custom_call" | custom-call | flops 60000000 | bytes 180000 | tf_op jit(solution)/shard_map/highway_back/pallas_call | solution.py:630
  319.7 4.6 convert_add_fusion.11
  324.3 2.8 collective-permute-start.34
  328.8 1.6 add_convert_fusion
  336.9 1.7 copy-done.23
  339.6 17.1 %collective-permute-done.31.refs_3_ = bf16[1024,512]{1,0:T(8,128)(2,1)S(1)} collective-permute-done((bf16[1024,512]{1,0:T(8,128)(2,1)S(1)}, bf16[1024,512]{1,0:T(8,128)(2,1)S(1)}, u32[]{:S(2)}, u32[]{:S(2)}) %collective-permute-start.31) | collective-permute-done | bytes 1048608 | tf_op jit(solution)/shard_map/ppermute | solution.py:796
  356.7 19.5 %conv_backward.4.refs_4_ = f32[640,128]{1,0:T(8,128)S(1)} custom-call(s32[2]{0:T(128)S(1)} %slice.229.narrow_ref, f32[64,256]{1,0:T(8,128)S(1)} %copy-done.8, bf16[1024,256]{1,0:T(8,128)(2,1)} %get-tuple-element.450.e_ref, bf16[512,128]{1,0:T(8,128)(2,1)S(1)} %copy.99.conv_ref, bf16[128,512]{1,0:T(8,128)(2,1)S(1)} %pad.21.back_ref, ...), custom_call_target="tpu_custom_call" | custom-call | flops 150000000 | bytes 450000 | tf_op jit(solution)/shard_map/conv_backward/pallas_call | solution.py:277
  376.2 1.9 collective-permute-done.36
  380.6 3.6 collective-permute-start.38
  384.2 11.5 %conv_backward.5.refs_4_ = f32[640,128]{1,0:T(8,128)S(1)} custom-call(s32[2]{0:T(128)S(1)} %slice.229.narrow_ref, f32[64,256]{1,0:T(8,128)S(1)} %copy-done.7, bf16[1024,256]{1,0:T(8,128)(2,1)} %get-tuple-element.474.e_ref, bf16[512,128]{1,0:T(8,128)(2,1)S(1)} %copy.99.conv_ref, bf16[128,512]{1,0:T(8,128)(2,1)S(1)} %pad.21.back_ref, ...), custom_call_target="tpu_custom_call" | custom-call | flops 150000000 | bytes 450000 | tf_op jit(solution)/shard_map/conv_backward/pallas_call | solution.py:277
  395.7 14.4 %conv_backward.6.refs_4_ = f32[640,128]{1,0:T(8,128)S(1)} custom-call(s32[2]{0:T(128)S(1)} %slice.229.narrow_ref, f32[64,512]{1,0:T(8,128)S(1)} %copy-done.6, bf16[1024,512]{1,0:T(8,128)(2,1)} %get-tuple-element.471.e_ref, bf16[512,128]{1,0:T(8,128)(2,1)S(1)} %copy.99.conv_ref, bf16[128,512]{1,0:T(8,128)(2,1)S(1)} %pad.21.back_ref, ...), custom_call_target="tpu_custom_call" | custom-call | flops 150000000 | bytes 450000 | tf_op jit(solution)/shard_map/conv_backward/pallas_call | solution.py:277
  412.6 14.0 %conv_backward.7 = f32[640,128]{1,0:T(8,128)S(1)} custom-call(s32[2]{0:T(128)S(1)} %slice.229.narrow_ref, f32[64,1024]{1,0:T(8,128)S(1)} %copy-done.5, bf16[1024,1024]{1,0:T(8,128)(2,1)} %get-tuple-element.491.e_ref, bf16[512,128]{1,0:T(8,128)(2,1)S(1)} %copy.99.conv_ref, bf16[128,512]{1,0:T(8,128)(2,1)S(1)} %pad.21.back_ref, ...), custom_call_target="tpu_custom_call" | custom-call | flops 150000000 | bytes 450000 | tf_op jit(solution)/shard_map/conv_backward/pallas_call | solution.py:277
  426.8 1.6 collective-permute-done.42
  428.4 8.1 %collective-permute-done.40.refs_3_ = bf16[2,256,512]{2,1,0:T(8,128)(2,1)} collective-permute-done((bf16[2,256,512]{2,1,0:T(8,128)(2,1)S(1)}, bf16[2,256,512]{2,1,0:T(8,128)(2,1)}, u32[]{:S(2)}, u32[]{:S(2)}) %collective-permute-start.40) | collective-permute-done | bytes 524320 | tf_op jit(solution)/shard_map/ppermute | solution.py:809
  437.2 4.2 return_units.1
  444.7 1.8 collective-permute-start.46
  446.5 1.7 collective-permute-start.47
  448.3 2.6 add_add_fusion
  451.1 2.2 collective-permute-done.48
  453.9 3.5 collective-permute-done.46.refs_2_
  457.4 1.8 collective-permute-done.47.refs_3_
  466.5 8.2 %owner_update.2 = (f32[2,256,2048]{2,1,0:T(8,128)}, f32[2,256,2048]{2,1,0:T(8,128)}, f32[2,256,2048]{2,1,0:T(8,128)}, f32[2,256,2048]{2,1,0:T(8,128)}) custom-call(s32[4]{0:T(128)} %xor_multiply_fusion.at_ref, bf16[256,512]{1,0:T(8,128)(2,1)} %get-tuple-element.521.refs_0_, bf16[256,512]{1,0:T(8,128)(2,1)} %copy-done.45, bf16[256,512]{1,0:T(8,128)(2,1)} %copy-done.46, ...), custom_call_target="tpu_custom_call" | custom-call | flops 80000000 | bytes 240000 | tf_op jit(solution)/shard_map/owner_update/pallas_call | solution.py:694
  474.8 1.8 collective-permute-start.55
  476.8 1.7 collective-permute-start.56
  478.5 8.2 %owner_update.3 = (f32[2,256,2048]{2,1,0:T(8,128)}, f32[2,256,2048]{2,1,0:T(8,128)}, f32[2,256,2048]{2,1,0:T(8,128)}, f32[2,256,2048]{2,1,0:T(8,128)}) custom-call(s32[4]{0:T(128)} %xor_multiply_fusion.at_ref, bf16[256,512]{1,0:T(8,128)(2,1)} %get-tuple-element.536.refs_0_, ...), custom_call_target="tpu_custom_call", output_to_operand_aliasing={{0}: (9, {}), {1}: (10, {}), {2}: (11, {}), {3}: (12, {})} | custom-call | flops 80000000 | bytes 240000 | tf_op jit(solution)/shard_map/owner_update/pallas_call | solution.py:694
  (362 shorter events, 61.7 us)
Async XLA Ops:
  4.4 30.1 %collective-permute-start.2 = (bf16[2,256,512]{2,1,0:T(8,128)(2,1)}, bf16[2,256,512]{2,1,0:T(8,128)(2,1)S(1)}, u32[]{:S(2)}, u32[]{:S(2)}) collective-permute-start(bf16[2,256,512]{2,1,0:T(8,128)(2,1)} %get-tuple-element.583), channel_id=1, source_target_pairs={{0,24},{8,16},{16,8},{24,0},{1,25},{9,17},{17,9},{25,1},{2,26},{10... | collective-permute-start | bytes 1572872 | tf_op jit(solution)/shard_map/ppermute | solution.py:796
  8.3 26.2 %collective-permute-start.1 = (bf16[2,256,512]{2,1,0:T(8,128)(2,1)}, bf16[2,256,512]{2,1,0:T(8,128)(2,1)S(1)}, u32[]{:S(2)}, u32[]{:S(2)}) collective-permute-start(bf16[2,256,512]{2,1,0:T(8,128)(2,1)} %get-tuple-element.584), channel_id=1, source_target_pairs={{0,16},{8,24},{16,0},{24,8},{1,17},{9,25},{17,1},{25,9},{2,18},{10... | collective-permute-start | bytes 1572872 | tf_op jit(solution)/shard_map/ppermute | solution.py:796
  8.8 25.7 %collective-permute-start = (bf16[2,256,512]{2,1,0:T(8,128)(2,1)}, bf16[2,256,512]{2,1,0:T(8,128)(2,1)}, u32[]{:S(2)}, u32[]{:S(2)}) collective-permute-start(bf16[2,256,512]{2,1,0:T(8,128)(2,1)} %get-tuple-element.585), channel_id=1, source_target_pairs={{0,8},{8,0},{16,24},{24,16},{1,9},{9,1},{17,25},{25,17},{2,10},{10... | collective-permute-start | bytes 1572872 | tf_op jit(solution)/shard_map/ppermute | solution.py:796
  12.4 20.6 %copy-start.56 = (f32[8960]{0:T(1024)S(1)}, f32[8960]{0:T(1024)}, u32[]{:S(2)}) copy-start(f32[8960]{0:T(1024)} %param.33) | copy-start | bytes 107524
  38.2 35.5 %collective-permute-start.7 = (bf16[512,768]{1,0:T(8,128)(2,1)}, bf16[512,768]{1,0:T(8,128)(2,1)}, u32[]{:S(2)}, u32[]{:S(2)}) collective-permute-start(bf16[512,768]{1,0:T(8,128)(2,1)} %param.26), channel_id=1, source_target_pairs={{0,8},{8,0},{16,24},{24,16},{1,9},{9,1},{17,25},{25,17},{2,10},{10... | collective-permute-start | bytes 2359304 | tf_op jit(solution)/shard_map/ppermute | solution.py:796
  39.4 34.4 %collective-permute-start.6 = (bf16[2,304,512]{2,1,0:T(8,128)(2,1)}, bf16[2,304,512]{2,1,0:T(8,128)(2,1)}, u32[]{:S(2)}, u32[]{:S(2)}) collective-permute-start(bf16[2,304,512]{2,1,0:T(8,128)(2,1)} %get-tuple-element.349), channel_id=1, source_target_pairs={{0,16},{8,24},{16,0},{24,8},{1,17},{9,25},{17,1},{25,9},{2,18},{10... | collective-permute-start | bytes 1867784 | tf_op jit(solution)/shard_map/ppermute | solution.py:796
  40.2 33.5 %collective-permute-start.5 = (bf16[2,256,512]{2,1,0:T(8,128)(2,1)}, bf16[2,256,512]{2,1,0:T(8,128)(2,1)}, u32[]{:S(2)}, u32[]{:S(2)}) collective-permute-start(bf16[2,256,512]{2,1,0:T(8,128)(2,1)} %get-tuple-element.325), channel_id=1, source_target_pairs={{0,16},{8,24},{16,0},{24,8},{1,17},{9,25},{17,1},{25,9},{2,18},{10... | collective-permute-start | bytes 1572872 | tf_op jit(solution)/shard_map/ppermute | solution.py:796
  41.4 32.3 %collective-permute-start.4 = (bf16[2,256,512]{2,1,0:T(8,128)(2,1)}, bf16[2,256,512]{2,1,0:T(8,128)(2,1)}, u32[]{:S(2)}, u32[]{:S(2)}) collective-permute-start(bf16[2,256,512]{2,1,0:T(8,128)(2,1)} %get-tuple-element.325), channel_id=1, source_target_pairs={{0,6},{1,7},{2,0},{3,1},{4,2},{5,3},{6,4},{7,5},{8,14},{9,15},{10,... | collective-permute-start | bytes 1572872 | tf_op jit(solution)/shard_map/ppermute | solution.py:809
  45.0 28.7 %collective-permute-start.3 = (bf16[2,256,512]{2,1,0:T(8,128)(2,1)}, bf16[2,256,512]{2,1,0:T(8,128)(2,1)}, u32[]{:S(2)}, u32[]{:S(2)}) collective-permute-start(bf16[2,256,512]{2,1,0:T(8,128)(2,1)} %get-tuple-element.325), channel_id=1, source_target_pairs={{0,2},{1,3},{2,4},{3,5},{4,6},{5,7},{6,0},{7,1},{8,10},{9,11},{10,... | collective-permute-start | bytes 1572872 | tf_op jit(solution)/shard_map/ppermute | solution.py:809
  73.7 28.9 %copy-start = (bf16[1024,512]{1,0:T(8,128)(2,1)}, bf16[1024,512]{1,0:T(8,128)(2,1)S(1)}, u32[]{:S(2)}) copy-start(bf16[1024,512]{1,0:T(8,128)(2,1)S(1)} %place_words.2.refs_0_) | copy-start | bytes 3145732
  73.7 24.5 %collective-permute-start.8 = (bf16[1024,512]{1,0:T(8,128)(2,1)S(1)}, bf16[1024,512]{1,0:T(8,128)(2,1)}, u32[]{:S(2)}, u32[]{:S(2)}) collective-permute-start(bf16[1024,512]{1,0:T(8,128)(2,1)S(1)} %place_words.3), channel_id=1, source_target_pairs={{0,16},{8,24},{16,0},{24,8},{1,17},{9,25},{17,1},{25,9},{2,18},{10... | collective-permute-start | bytes 3145736 | tf_op jit(solution)/shard_map/ppermute | solution.py:796
  73.8 24.4 %collective-permute-start.9 = (bf16[1024,512]{1,0:T(8,128)(2,1)S(1)}, bf16[1024,512]{1,0:T(8,128)(2,1)S(1)}, u32[]{:S(2)}, u32[]{:S(2)}) collective-permute-start(bf16[1024,512]{1,0:T(8,128)(2,1)S(1)} %place_words.2.refs_0_), channel_id=1, source_target_pairs={{0,8},{8,0},{16,24},{24,16},{1,9},{9,1},{17,25},{25,17},{2,10},{10... | collective-permute-start | bytes 3145736 | tf_op jit(solution)/shard_map/ppermute | solution.py:796
  73.9 24.3 %collective-permute-start.10 = (bf16[2,256,512]{2,1,0:T(8,128)(2,1)S(1)}, bf16[2,256,512]{2,1,0:T(8,128)(2,1)S(1)}, u32[]{:S(2)}, u32[]{:S(2)}) collective-permute-start(bf16[2,256,512]{2,1,0:T(8,128)(2,1)S(1)} %copy-done.41), channel_id=1, source_target_pairs={{0,4},{1,5},{2,6},{3,7},{4,0},{5,1},{6,2},{7,3},{8,12},{9,13},{10,... | collective-permute-start | bytes 1572872 | tf_op jit(solution)/shard_map/ppermute | solution.py:809
  74.6 30.9 %copy-start.78 = (s32[1,16]{1,0:T(1,128)S(1)}, s32[1,16]{1,0:T(1,128)}, u32[]{:S(2)}) copy-start(s32[1,16]{1,0:T(1,128)} %constant.741.clone.1) | copy-start | bytes 196
  74.6 30.9 %copy-start.79 = (s32[1,16]{1,0:T(1,128)S(1)}, s32[1,16]{1,0:T(1,128)}, u32[]{:S(2)}) copy-start(s32[1,16]{1,0:T(1,128)} %constant.740.clone.1) | copy-start | bytes 196
  99.2 33.7 %collective-permute-start.12 = (bf16[3,2,256,512]{3,2,1,0:T(8,128)(2,1)S(1)}, bf16[3,2,256,512]{3,2,1,0:T(8,128)(2,1)}, u32[]{:S(2)}, u32[]{:S(2)}) collective-permute-start(bf16[3,2,256,512]{3,2,1,0:T(8,128)(2,1)S(1)} %bitcast_dynamic-update-slice_fusion.refs_5_.refs_1_), channel_id=1, source_target_pairs={{0,1},{1,0},{2,3},{3,2},{4,5},{5,4},{6,7},{7,6},{8,9},{9,8},{10,11... | collective-permute-start | bytes 4718600 | tf_op jit(solution)/shard_map/ppermute | solution.py:805
  99.2 36.9 %collective-permute-start.11 = (bf16[3,2,256,512]{3,2,1,0:T(8,128)(2,1)S(1)}, bf16[3,2,256,512]{3,2,1,0:T(8,128)(2,1)}, u32[]{:S(2)}, u32[]{:S(2)}) collective-permute-start(bf16[3,2,256,512]{3,2,1,0:T(8,128)(2,1)S(1)} %bitcast_dynamic-update-slice_fusion.refs_5_.refs_1_), channel_id=1, source_target_pairs={{0,16},{8,24},{16,0},{24,8},{1,17},{9,25},{17,1},{25,9},{2,18},{10... | collective-permute-start | bytes 4718600 | tf_op jit(solution)/shard_map/ppermute | solution.py:796
  100.8 32.1 %collective-permute-start.13 = (bf16[1024,512]{1,0:T(8,128)(2,1)}, bf16[1024,512]{1,0:T(8,128)(2,1)}, u32[]{:S(2)}, u32[]{:S(2)}) collective-permute-start(bf16[1024,512]{1,0:T(8,128)(2,1)} %collective-permute-done.8.refs_1_), channel_id=1, source_target_pairs={{0,8},{8,0},{16,24},{24,16},{1,9},{9,1},{17,25},{25,17},{2,10},{10... | collective-permute-start | bytes 3145736 | tf_op jit(solution)/shard_map/ppermute | solution.py:796
  103.0 17.0 %collective-permute-start.15 = (bf16[2,304,512]{2,1,0:T(8,128)(2,1)}, bf16[2,304,512]{2,1,0:T(8,128)(2,1)S(1)}, u32[]{:S(2)}, u32[]{:S(2)}) collective-permute-start(bf16[2,304,512]{2,1,0:T(8,128)(2,1)} %get-tuple-element.349), channel_id=1, source_target_pairs={{0,6},{1,7},{2,0},{3,1},{4,2},{5,3},{6,4},{7,5},{8,14},{9,15},{10,... | collective-permute-start | bytes 1867784 | tf_op jit(solution)/shard_map/ppermute | solution.py:809
  105.3 27.7 %collective-permute-start.14 = (bf16[2,304,512]{2,1,0:T(8,128)(2,1)}, bf16[2,304,512]{2,1,0:T(8,128)(2,1)S(1)}, u32[]{:S(2)}, u32[]{:S(2)}) collective-permute-start(bf16[2,304,512]{2,1,0:T(8,128)(2,1)} %get-tuple-element.349), channel_id=1, source_target_pairs={{0,2},{1,3},{2,4},{3,5},{4,6},{5,7},{6,0},{7,1},{8,10},{9,11},{10,... | collective-permute-start | bytes 1867784 | tf_op jit(solution)/shard_map/ppermute | solution.py:809
  109.3 28.6 %copy-start.13 = (bf16[2,2,256,512]{3,2,1,0:T(8,128)(2,1)}, bf16[2,2,256,512]{3,2,1,0:T(8,128)(2,1)S(1)}, u32[]{:S(2)}) copy-start(bf16[2,2,256,512]{3,2,1,0:T(8,128)(2,1)S(1)} %pad_maximum_fusion.3.refs_4_.refs_0_) | copy-start | bytes 3145732
  136.2 5.1 %collective-permute-start.17 = (bf16[3,2,256,512]{3,2,1,0:T(8,128)(2,1)}, bf16[3,2,256,512]{3,2,1,0:T(8,128)(2,1)S(1)}, u32[]{:S(2)}, u32[]{:S(2)}) collective-permute-start(bf16[3,2,256,512]{3,2,1,0:T(8,128)(2,1)} %collective-permute-done.11.refs_6_.refs_2_), channel_id=1, source_target_pairs={{0,1},{1,0},{2,3},{3,2},{4,5},{5,4},{6,7},{7,6},{8,9},{9,8},{10,11... | collective-permute-start | bytes 4718600 | tf_op jit(solution)/shard_map/ppermute | solution.py:805
  136.2 4.5 collective-permute-start.16
  137.8 31.8 %collective-permute-start.19 = (bf16[2,2,304,512]{3,2,1,0:T(8,128)(2,1)}, bf16[2,2,304,512]{3,2,1,0:T(8,128)(2,1)}, u32[]{:S(2)}, u32[]{:S(2)}) collective-permute-start(bf16[2,2,304,512]{3,2,1,0:T(8,128)(2,1)} %pad_maximum_fusion.2), channel_id=1, source_target_pairs={{0,16},{8,24},{16,0},{24,8},{1,17},{9,25},{17,1},{25,9},{2,18},{10... | collective-permute-start | bytes 3735560 | tf_op jit(solution)/shard_map/ppermute | solution.py:796
  139.4 30.2 %collective-permute-start.18 = (bf16[2,304,512]{2,1,0:T(8,128)(2,1)}, bf16[2,304,512]{2,1,0:T(8,128)(2,1)}, u32[]{:S(2)}, u32[]{:S(2)}) collective-permute-start(bf16[2,304,512]{2,1,0:T(8,128)(2,1)} %get-tuple-element.349), channel_id=1, source_target_pairs={{0,4},{1,5},{2,6},{3,7},{4,0},{5,1},{6,2},{7,3},{8,12},{9,13},{10,... | collective-permute-start | bytes 1867784 | tf_op jit(solution)/shard_map/ppermute | solution.py:809
  154.9 30.1 %collective-permute-start.21 = (bf16[512,1024]{1,0:T(8,128)(2,1)}, bf16[512,1024]{1,0:T(8,128)(2,1)S(1)}, u32[]{:S(2)}, u32[]{:S(2)}) collective-permute-start(bf16[512,1024]{1,0:T(8,128)(2,1)} %get-tuple-element.348.own.refs_0_), channel_id=1, source_target_pairs={{0,8},{8,0},{16,24},{24,16},{1,9},{9,1},{17,25},{25,17},{2,10},{10... | collective-permute-start | bytes 3145736 | tf_op jit(solution)/shard_map/ppermute | solution.py:796
  169.6 15.4 %collective-permute-start.20 = (bf16[2,304,512]{2,1,0:T(8,128)(2,1)}, bf16[2,304,512]{2,1,0:T(8,128)(2,1)S(1)}, u32[]{:S(2)}, u32[]{:S(2)}) collective-permute-start(bf16[2,304,512]{2,1,0:T(8,128)(2,1)} %collective-permute-done.18), channel_id=1, source_target_pairs={{0,16},{8,24},{16,0},{24,8},{1,17},{9,25},{17,1},{25,9},{2,18},{10... | collective-permute-start | bytes 1867784 | tf_op jit(solution)/shard_map/ppermute | solution.py:796
  172.0 17.5 %collective-permute-start.22 = (bf16[4,2,304,512]{3,2,1,0:T(8,128)(2,1)S(1)}, bf16[4,2,304,512]{3,2,1,0:T(8,128)(2,1)S(1)}, u32[]{:S(2)}, u32[]{:S(2)}) collective-permute-start(bf16[4,2,304,512]{3,2,1,0:T(8,128)(2,1)S(1)} %pad_maximum_fusion.refs_0_), channel_id=1, source_target_pairs={{0,1},{1,0},{2,3},{3,2},{4,5},{5,4},{6,7},{7,6},{8,9},{9,8},{10,11... | collective-permute-start | bytes 7471112 | tf_op jit(solution)/shard_map/ppermute | solution.py:805
  187.2 4.9 %collective-permute-start.23 = (bf16[4,2,304,512]{3,2,1,0:T(8,128)(2,1)S(1)}, bf16[4,2,304,512]{3,2,1,0:T(8,128)(2,1)}, u32[]{:S(2)}, u32[]{:S(2)}) collective-permute-start(bf16[4,2,304,512]{3,2,1,0:T(8,128)(2,1)S(1)} %pad_maximum_fusion.1.refs_1_), channel_id=1, source_target_pairs={{0,1},{1,0},{2,3},{3,2},{4,5},{5,4},{6,7},{7,6},{8,9},{9,8},{10,11... | collective-permute-start | bytes 7471112 | tf_op jit(solution)/shard_map/ppermute | solution.py:805
  187.3 26.2 %collective-permute-start.24 = (bf16[512,1024]{1,0:T(8,128)(2,1)S(1)}, bf16[512,1024]{1,0:T(8,128)(2,1)S(1)}, u32[]{:S(2)}, u32[]{:S(2)}) collective-permute-start(bf16[512,1024]{1,0:T(8,128)(2,1)S(1)} %copy-done.27), channel_id=1, source_target_pairs={{0,8},{8,0},{16,24},{24,16},{1,9},{9,1},{17,25},{25,17},{2,10},{10... | collective-permute-start | bytes 3145736 | tf_op jit(solution)/shard_map/ppermute | solution.py:796
  209.1 40.6 %collective-permute-start.25 = (bf16[512,1024]{1,0:T(8,128)(2,1)}, bf16[512,1024]{1,0:T(8,128)(2,1)S(1)}, u32[]{:S(2)}, u32[]{:S(2)}) collective-permute-start(bf16[512,1024]{1,0:T(8,128)(2,1)} %get-tuple-element.370), channel_id=1, source_target_pairs={{0,8},{8,0},{16,24},{24,16},{1,9},{9,1},{17,25},{25,17},{2,10},{10... | collective-permute-start | bytes 3145736 | tf_op jit(solution)/shard_map/ppermute | solution.py:796
  214.5 19.4 %copy-start.80 = (s32[4]{0:T(128)S(1)}, s32[4]{0:T(128)}, u32[]{:S(2)}) copy-start(s32[4]{0:T(128)} %constant.752.clone) | copy-start | bytes 52
  231.9 26.4 %collective-permute-start.26 = (bf16[512,1024]{1,0:T(8,128)(2,1)}, bf16[512,1024]{1,0:T(8,128)(2,1)}, u32[]{:S(2)}, u32[]{:S(2)}) collective-permute-start(bf16[512,1024]{1,0:T(8,128)(2,1)} %get-tuple-element.382), channel_id=1, source_target_pairs={{0,8},{8,0},{16,24},{24,16},{1,9},{9,1},{17,25},{25,17},{2,10},{10... | collective-permute-start | bytes 3145736 | tf_op jit(solution)/shard_map/ppermute | solution.py:796
  258.3 7.9 %collective-permute-start.27 = (bf16[2,4,2,256,512]{4,3,2,1,0:T(8,128)(2,1)}, bf16[2,4,2,256,512]{4,3,2,1,0:T(8,128)(2,1)S(1)}, u32[]{:S(2)}, u32[]{:S(2)}) collective-permute-start(bf16[2,4,2,256,512]{4,3,2,1,0:T(8,128)(2,1)} %get-tuple-element.388), channel_id=1, source_target_pairs={{0,1},{1,0},{2,3},{3,2},{4,5},{5,4},{6,7},{7,6},{8,9},{9,8},{10,11... | collective-permute-start | bytes 12582920 | tf_op jit(solution)/shard_map/ppermute | solution.py:805
  269.8 49.4 %collective-permute-start.30 = (bf16[4,2,256,512]{3,2,1,0:T(8,128)(2,1)}, bf16[4,2,256,512]{3,2,1,0:T(8,128)(2,1)}, u32[]{:S(2)}, u32[]{:S(2)}) collective-permute-start(bf16[4,2,256,512]{3,2,1,0:T(8,128)(2,1)} %fusion), channel_id=1, source_target_pairs={{0,16},{8,24},{16,0},{24,8},{1,17},{9,25},{17,1},{25,9},{2,18},{10... | collective-permute-start | bytes 6291464 | tf_op jit(solution)/shard_map/ppermute | solution.py:796
  271.1 32.9 %collective-permute-start.28 = (bf16[512,1024]{1,0:T(8,128)(2,1)}, bf16[512,1024]{1,0:T(8,128)(2,1)S(1)}, u32[]{:S(2)}, u32[]{:S(2)}) collective-permute-start(bf16[512,1024]{1,0:T(8,128)(2,1)} %get-tuple-element.417), channel_id=1, source_target_pairs={{0,8},{8,0},{16,24},{24,16},{1,9},{9,1},{17,25},{25,17},{2,10},{10... | collective-permute-start | bytes 3145736 | tf_op jit(solution)/shard_map/ppermute | solution.py:796
  287.5 31.7 %collective-permute-start.29 = (bf16[512,1024]{1,0:T(8,128)(2,1)}, bf16[512,1024]{1,0:T(8,128)(2,1)}, u32[]{:S(2)}, u32[]{:S(2)}) collective-permute-start(bf16[512,1024]{1,0:T(8,128)(2,1)} %get-tuple-element.423), channel_id=1, source_target_pairs={{0,8},{8,0},{16,24},{24,16},{1,9},{9,1},{17,25},{25,17},{2,10},{10... | collective-permute-start | bytes 3145736 | tf_op jit(solution)/shard_map/ppermute | solution.py:796
  319.2 12.5 %collective-permute-start.32 = (bf16[2,4,2,256,512]{4,3,2,1,0:T(8,128)(2,1)}, bf16[2,4,2,256,512]{4,3,2,1,0:T(8,128)(2,1)S(1)}, u32[]{:S(2)}, u32[]{:S(2)}) collective-permute-start(bf16[2,4,2,256,512]{4,3,2,1,0:T(8,128)(2,1)} %get-tuple-element.444), channel_id=1, source_target_pairs={{0,1},{1,0},{2,3},{3,2},{4,5},{5,4},{6,7},{7,6},{8,9},{9,8},{10,11... | collective-permute-start | bytes 12582920 | tf_op jit(solution)/shard_map/ppermute | solution.py:805
  324.3 51.9 %collective-permute-start.33 = (bf16[2,256,512]{2,1,0:T(8,128)(2,1)}, bf16[2,256,512]{2,1,0:T(8,128)(2,1)}, u32[]{:S(2)}, u32[]{:S(2)}) collective-permute-start(bf16[2,256,512]{2,1,0:T(8,128)(2,1)} %get-tuple-element.458), channel_id=1, source_target_pairs={{0,4},{1,5},{2,6},{3,7},{4,0},{5,1},{6,2},{7,3},{8,12},{9,13},{10,... | collective-permute-start | bytes 1572872 | tf_op jit(solution)/shard_map/ppermute | solution.py:809
  324.3 51.9 %collective-permute-start.34 = (bf16[2,256,512]{2,1,0:T(8,128)(2,1)}, bf16[2,256,512]{2,1,0:T(8,128)(2,1)}, u32[]{:S(2)}, u32[]{:S(2)}) collective-permute-start(bf16[2,256,512]{2,1,0:T(8,128)(2,1)} %get-tuple-element.459), channel_id=1, source_target_pairs={{0,2},{1,3},{2,4},{3,5},{4,6},{5,7},{6,0},{7,1},{8,10},{9,11},{10,... | collective-permute-start | bytes 1572872 | tf_op jit(solution)/shard_map/ppermute | solution.py:809
  327.1 49.1 %collective-permute-start.35 = (bf16[2,256,512]{2,1,0:T(8,128)(2,1)}, bf16[2,256,512]{2,1,0:T(8,128)(2,1)}, u32[]{:S(2)}, u32[]{:S(2)}) collective-permute-start(bf16[2,256,512]{2,1,0:T(8,128)(2,1)} %get-tuple-element.460), channel_id=1, source_target_pairs={{0,6},{1,7},{2,0},{3,1},{4,2},{5,3},{6,4},{7,5},{8,14},{9,15},{10,... | collective-permute-start | bytes 1572872 | tf_op jit(solution)/shard_map/ppermute | solution.py:809
  330.6 26.1 %collective-permute-start.31 = (bf16[1024,512]{1,0:T(8,128)(2,1)S(1)}, bf16[1024,512]{1,0:T(8,128)(2,1)S(1)}, u32[]{:S(2)}, u32[]{:S(2)}) collective-permute-start(bf16[1024,512]{1,0:T(8,128)(2,1)S(1)} %pad_maximum_fusion.5), channel_id=1, source_target_pairs={{0,16},{8,24},{16,0},{24,8},{1,17},{9,25},{17,1},{25,9},{2,18},{10... | collective-permute-start | bytes 3145736 | tf_op jit(solution)/shard_map/ppermute | solution.py:796
  332.6 45.5 %collective-permute-start.36 = (bf16[2,2,256,512]{3,2,1,0:T(8,128)(2,1)S(1)}, bf16[2,2,256,512]{3,2,1,0:T(8,128)(2,1)S(1)}, u32[]{:S(2)}, u32[]{:S(2)}) collective-permute-start(bf16[2,2,256,512]{3,2,1,0:T(8,128)(2,1)S(1)} %get-tuple-element.581), channel_id=1, source_target_pairs={{0,16},{8,24},{16,0},{24,8},{1,17},{9,25},{17,1},{25,9},{2,18},{10... | collective-permute-start | bytes 3145736 | tf_op jit(solution)/shard_map/ppermute | solution.py:796
  356.7 21.4 %copy-start.31 = (bf16[4,2,256,512]{3,2,1,0:T(8,128)(2,1)S(1)}, bf16[4,2,256,512]{3,2,1,0:T(8,128)(2,1)}, u32[]{:S(2)}) copy-start(bf16[4,2,256,512]{3,2,1,0:T(8,128)(2,1)} %get-tuple-element.464) | copy-start | bytes 6291460
  379.6 30.6 %collective-permute-start.39 = (bf16[2,2,256,512]{3,2,1,0:T(8,128)(2,1)S(1)}, bf16[2,2,256,512]{3,2,1,0:T(8,128)(2,1)S(1)}, u32[]{:S(2)}, u32[]{:S(2)}) collective-permute-start(bf16[2,2,256,512]{3,2,1,0:T(8,128)(2,1)S(1)} %get-tuple-element.479), channel_id=1, source_target_pairs={{0,16},{8,24},{16,0},{24,8},{1,17},{9,25},{17,1},{25,9},{2,18},{10... | collective-permute-start | bytes 3145736 | tf_op jit(solution)/shard_map/ppermute | solution.py:796
  380.4 29.8 %collective-permute-start.37 = (bf16[2,256,512]{2,1,0:T(8,128)(2,1)}, bf16[2,256,512]{2,1,0:T(8,128)(2,1)S(1)}, u32[]{:S(2)}, u32[]{:S(2)}) collective-permute-start(bf16[2,256,512]{2,1,0:T(8,128)(2,1)} %get-tuple-element.477), channel_id=1, source_target_pairs={{0,2},{1,3},{2,4},{3,5},{4,6},{5,7},{6,0},{7,1},{8,10},{9,11},{10,... | collective-permute-start | bytes 1572872 | tf_op jit(solution)/shard_map/ppermute | solution.py:809
  380.6 29.6 %collective-permute-start.38 = (bf16[2,256,512]{2,1,0:T(8,128)(2,1)}, bf16[2,256,512]{2,1,0:T(8,128)(2,1)S(1)}, u32[]{:S(2)}, u32[]{:S(2)}) collective-permute-start(bf16[2,256,512]{2,1,0:T(8,128)(2,1)} %get-tuple-element.478), channel_id=1, source_target_pairs={{0,6},{1,7},{2,0},{3,1},{4,2},{5,3},{6,4},{7,5},{8,14},{9,15},{10,... | collective-permute-start | bytes 1572872 | tf_op jit(solution)/shard_map/ppermute | solution.py:809
  411.1 25.4 %collective-permute-start.41 = (bf16[512,768]{1,0:T(8,128)(2,1)}, bf16[512,768]{1,0:T(8,128)(2,1)}, u32[]{:S(2)}, u32[]{:S(2)}) collective-permute-start(bf16[512,768]{1,0:T(8,128)(2,1)} %slice.344), channel_id=1, source_target_pairs={{0,16},{8,24},{16,0},{24,8},{1,17},{9,25},{17,1},{25,9},{2,18},{10... | collective-permute-start | bytes 2359304 | tf_op jit(solution)/shard_map/ppermute | solution.py:796
  412.5 24.0 %collective-permute-start.40 = (bf16[2,256,512]{2,1,0:T(8,128)(2,1)S(1)}, bf16[2,256,512]{2,1,0:T(8,128)(2,1)}, u32[]{:S(2)}, u32[]{:S(2)}) collective-permute-start(bf16[2,256,512]{2,1,0:T(8,128)(2,1)S(1)} %get-tuple-element.487), channel_id=1, source_target_pairs={{0,4},{1,5},{2,6},{3,7},{4,0},{5,1},{6,2},{7,3},{8,12},{9,13},{10,... | collective-permute-start | bytes 1572872 | tf_op jit(solution)/shard_map/ppermute | solution.py:809
  412.5 29.8 %collective-permute-start.43 = (bf16[512,768]{1,0:T(8,128)(2,1)}, bf16[512,768]{1,0:T(8,128)(2,1)}, u32[]{:S(2)}, u32[]{:S(2)}) collective-permute-start(bf16[512,768]{1,0:T(8,128)(2,1)} %select_convert_fusion), channel_id=1, source_target_pairs={{0,8},{8,0},{16,24},{24,16},{1,9},{9,1},{17,25},{25,17},{2,10},{10... | collective-permute-start | bytes 2359304 | tf_op jit(solution)/shard_map/ppermute | solution.py:796
  426.7 1.7 collective-permute-start.42
  436.5 5.8 %collective-permute-start.44 = (bf16[640,128]{0,1:T(8,128)(2,1)S(1)}, bf16[640,128]{0,1:T(8,128)(2,1)S(1)}, u32[]{:S(2)}, u32[]{:S(2)}) collective-permute-start(bf16[640,128]{0,1:T(8,128)(2,1)S(1)} %convert_element_type.490), channel_id=1, source_target_pairs={{0,2},{1,3},{2,0},{3,1},{4,6},{5,7},{6,4},{7,5},{8,10},{9,11},{10,... | collective-permute-start | bytes 491528 | tf_op jit(solution)/shard_map/ppermute | solution.py:909
  443.9 9.3 %collective-permute-start.48 = (bf16[640,128]{0,1:T(8,128)(2,1)S(1)}, bf16[640,128]{0,1:T(8,128)(2,1)S(1)}, u32[]{:S(2)}, u32[]{:S(2)}) collective-permute-start(bf16[640,128]{0,1:T(8,128)(2,1)S(1)} %convert_element_type.493), channel_id=1, source_target_pairs={{0,4},{1,5},{2,6},{3,7},{4,0},{5,1},{6,2},{7,3},{8,12},{9,13},{10,... | collective-permute-start | bytes 491528 | tf_op jit(solution)/shard_map/ppermute | solution.py:909
  444.7 9.2 %collective-permute-start.45 = (bf16[256,512]{1,0:T(8,128)(2,1)S(1)}, bf16[256,512]{1,0:T(8,128)(2,1)S(1)}, u32[]{:S(2)}, u32[]{:S(2)}) collective-permute-start(bf16[256,512]{1,0:T(8,128)(2,1)S(1)} %copy-done.86), channel_id=1, source_target_pairs={{0,8},{8,0},{16,24},{24,16},{1,9},{9,1},{17,25},{25,17},{2,10},{10... | collective-permute-start | bytes 786440 | tf_op jit(solution)/shard_map/ppermute | solution.py:796
  444.7 12.7 %collective-permute-start.46 = (bf16[256,512]{1,0:T(8,128)(2,1)S(1)}, bf16[256,512]{1,0:T(8,128)(2,1)S(1)}, u32[]{:S(2)}, u32[]{:S(2)}) collective-permute-start(bf16[256,512]{1,0:T(8,128)(2,1)S(1)} %copy-done.85), channel_id=1, source_target_pairs={{0,16},{8,24},{16,0},{24,8},{1,17},{9,25},{17,1},{25,9},{2,18},{10... | collective-permute-start | bytes 786440 | tf_op jit(solution)/shard_map/ppermute | solution.py:796
  446.5 12.7 %collective-permute-start.47 = (bf16[256,512]{1,0:T(8,128)(2,1)S(1)}, bf16[256,512]{1,0:T(8,128)(2,1)S(1)}, u32[]{:S(2)}, u32[]{:S(2)}) collective-permute-start(bf16[256,512]{1,0:T(8,128)(2,1)S(1)} %copy-done.84), channel_id=1, source_target_pairs={{0,24},{8,16},{16,8},{24,0},{1,25},{9,17},{17,9},{25,1},{2,26},{10... | collective-permute-start | bytes 786440 | tf_op jit(solution)/shard_map/ppermute | solution.py:796
  448.2 11.0 %collective-permute-start.49 = (bf16[4,64,768]{2,1,0:T(8,128)(2,1)S(1)}, bf16[4,64,768]{2,1,0:T(8,128)(2,1)S(1)}, u32[]{:S(2)}, u32[]{:S(2)}) collective-permute-start(bf16[4,64,768]{2,1,0:T(8,128)(2,1)S(1)} %fusion.11), channel_id=1, source_target_pairs={{0,1},{1,0},{2,3},{3,2},{4,5},{5,4},{6,7},{7,6},{8,9},{9,8},{10,11... | collective-permute-start | bytes 1179656 | tf_op jit(solution)/shard_map/ppermute | solution.py:805
  459.3 15.4 %collective-permute-start.50 = (f32[128,128]{0,1:T(8,128)S(1)}, f32[128,128]{0,1:T(8,128)S(1)}, u32[]{:S(2)}, u32[]{:S(2)}) collective-permute-start(f32[128,128]{0,1:T(8,128)S(1)} %slice.278), channel_id=1, source_target_pairs={{0,8},{8,0},{16,24},{24,16},{1,9},{9,1},{17,25},{25,17},{2,10},{10... | collective-permute-start | bytes 196616 | tf_op jit(solution)/shard_map/ppermute | solution.py:796
  459.9 14.8 %collective-permute-start.52 = (bf16[256,512]{1,0:T(8,128)(2,1)S(1)}, bf16[256,512]{1,0:T(8,128)(2,1)S(1)}, u32[]{:S(2)}, u32[]{:S(2)}) collective-permute-start(bf16[256,512]{1,0:T(8,128)(2,1)S(1)} %copy-done.83), channel_id=1, source_target_pairs={{0,8},{8,0},{16,24},{24,16},{1,9},{9,1},{17,25},{25,17},{2,10},{10... | collective-permute-start | bytes 786440 | tf_op jit(solution)/shard_map/ppermute | solution.py:796
  461.4 13.4 %collective-permute-start.53 = (bf16[256,512]{1,0:T(8,128)(2,1)S(1)}, bf16[256,512]{1,0:T(8,128)(2,1)S(1)}, u32[]{:S(2)}, u32[]{:S(2)}) collective-permute-start(bf16[256,512]{1,0:T(8,128)(2,1)S(1)} %copy-done.82), channel_id=1, source_target_pairs={{0,16},{8,24},{16,0},{24,8},{1,17},{9,25},{17,1},{25,9},{2,18},{10... | collective-permute-start | bytes 786440 | tf_op jit(solution)/shard_map/ppermute | solution.py:796
  462.0 12.8 %collective-permute-start.54 = (bf16[256,512]{1,0:T(8,128)(2,1)S(1)}, bf16[256,512]{1,0:T(8,128)(2,1)S(1)}, u32[]{:S(2)}, u32[]{:S(2)}) collective-permute-start(bf16[256,512]{1,0:T(8,128)(2,1)S(1)} %copy-done.81), channel_id=1, source_target_pairs={{0,24},{8,16},{16,8},{24,0},{1,25},{9,17},{17,9},{25,1},{2,26},{10... | collective-permute-start | bytes 786440 | tf_op jit(solution)/shard_map/ppermute | solution.py:796
  463.6 11.2 %collective-permute-start.51 = (bf16[2,64,768]{2,1,0:T(8,128)(2,1)S(1)}, bf16[2,64,768]{2,1,0:T(8,128)(2,1)S(1)}, u32[]{:S(2)}, u32[]{:S(2)}) collective-permute-start(bf16[2,64,768]{2,1,0:T(8,128)(2,1)S(1)} %fusion.23), channel_id=1, source_target_pairs={{0,4},{1,5},{2,6},{3,7},{4,0},{5,1},{6,2},{7,3},{8,12},{9,13},{10,... | collective-permute-start | bytes 589832 | tf_op jit(solution)/shard_map/ppermute | solution.py:909
  474.8 11.9 %collective-permute-start.55 = (f32[128,128]{0,1:T(8,128)S(1)}, f32[128,128]{0,1:T(8,128)S(1)}, u32[]{:S(2)}, u32[]{:S(2)}) collective-permute-start(f32[128,128]{0,1:T(8,128)S(1)} %slice_add_fusion.1), channel_id=1, source_target_pairs={{0,16},{8,24},{16,0},{24,8},{1,17},{9,25},{17,1},{25,9},{2,18},{10... | collective-permute-start | bytes 196616 | tf_op jit(solution)/shard_map/ppermute | solution.py:796
  476.8 9.9 %collective-permute-start.56 = (bf16[1,64,768]{2,1,0:T(8,128)(2,1)S(1)}, bf16[1,64,768]{2,1,0:T(8,128)(2,1)S(1)}, u32[]{:S(2)}, u32[]{:S(2)}) collective-permute-start(bf16[1,64,768]{2,1,0:T(8,128)(2,1)S(1)} %dynamic-slice_convert_fusion.6), channel_id=1, source_target_pairs={{0,2},{1,3},{2,0},{3,1},{4,6},{5,7},{6,4},{7,5},{8,10},{9,11},{10,... | collective-permute-start | bytes 294920 | tf_op jit(solution)/shard_map/ppermute | solution.py:909
  (81 other events, 587.7 us)
